TPU v7x, 32 devices: a whole 2x2x4 slice. The times are simulated.
32 devices in a mesh: seq: 16 (over z, y, x), state: 2 (over core).
Axes of the slice: x: 2, y: 2, z: 4, core: 2. Of those that a mesh axis runs over, the one named last changes fastest.
Arguments:
- tokens: bfloat16 [4, 4096, 512], P(None, 'seq', 'state'), may hold values from -6 to 6
- batchnorm_gain: bfloat16 [2, 512], P(None, 'state'), may hold values from 0.5 to 1.5
- batchnorm_bias: bfloat16 [2, 512], P(None, 'state'), may hold values from -3 to 3
- in_proj: bfloat16 [2, 512, 2, 256], P(None, None, None, 'state'), may hold values from -0.25 to 0.25
- out_proj: bfloat16 [2, 2, 256, 512], P(None, None, 'state'), may hold values from -0.25 to 0.25
- rate_log: bfloat16 [2, 256], P(None, 'state'), may hold values from -13 to -2
- angle_log: bfloat16 [2, 256], P(None, 'state'), may hold values from -4.59375 to 1
- skip_gain: bfloat16 [2, 512], P(None, 'state'), may hold values from -4 to 4
- glu_lin: bfloat16 [2, 512, 512], P(None, None, 'state'), may hold values from -0.25 to 0.25
- glu_gate: bfloat16 [2, 512, 512], P(None, None, 'state'), may hold values from -0.25 to 0.25
- positions: int32 [4, 16], replicated, may hold values from 0 to 4095, as said below
- cotangent: bfloat16 [4, 4096, 512], P(None, 'seq', 'state'), may hold values from -6 to 6
Outputs:
- block_out: bfloat16 [4, 4096, 512], P(None, 'seq', 'state')
- input_grad: float32 [4, 4096, 512], P(None, 'seq', 'state')
- norm_gain_gradient: float32 [2, 512], P(None, 'state')
- bias_grad: float32 [2, 512], P(None, 'state')
- in_grad: float32 [2, 512, 2, 256], P(None, None, None, 'state')
- out_grad: float32 [2, 2, 256, 512], P(None, None, 'state')
- rate_grad: float32 [2, 256], P(None, 'state')
- angle_grad: float32 [2, 256], P(None, 'state')
- skip_grad: float32 [2, 512], P(None, 'state')
- lin_grad: float32 [2, 512, 512], P(None, None, 'state')
- gate_grad: float32 [2, 512, 512], P(None, None, 'state')
Inputs may be any that keep to these rules, and one draw needn't show every extreme that they name: Each row lists 16 positions at which a document starts, in order, the first 0; repeats may occur. In one row all are 0.
All inputs are finite; a program needn't handle non-finite values.
Results may differ from a plain program's by a relative error of at most 0.02.
Values may be sent and summed in bfloat16 or wider, within the bound.
No kernel may reach another device: no remote copies, remote signals or barrier semaphores. Data moves between devices by JAX's collectives and lax.ppermute only.
A program may use at most 128 MiB of HBM per device.

v0:
```python
import jax
import jax.numpy as jnp
from jax import lax
from jax.sharding import PartitionSpec as P

norm_eps = 1e-05


def carried_in(value, axis, combine, identity, reverse):
    peers, position = (lax.axis_size(axis), lax.axis_index(axis))
    everything = jax.tree.map(lambda part: lax.all_gather(part, axis), value)
    start = jax.tree.map(
        lambda part, zero: jnp.broadcast_to(jnp.asarray(zero, part.dtype), part.shape),
        value,
        identity,
    )

    def step(k, before):
        at = peers - 1 - k if reverse else k
        reached = at > position if reverse else at < position
        new = combine(before, jax.tree.map(lambda part: part[at], everything))
        return jax.tree.map(lambda a, b: jnp.where(reached, a, b), new, before)

    return lax.fori_loop(0, peers, step, start)


def decay_terms(rate_log, angle_log):
    rate_now = jnp.exp(rate_log)
    modulus = jnp.exp(-rate_now)
    angle_now = jnp.exp(angle_log)
    return (
        modulus * jnp.cos(angle_now),
        modulus * jnp.sin(angle_now),
        jnp.sqrt(1.0 - modulus * modulus),
    )


def compose(earlier, latter):
    early_ar, early_ai, early_br, early_bi = earlier
    late_ar, late_ai, late_br, late_bi = latter
    return (
        late_ar * early_ar - late_ai * early_ai,
        late_ar * early_ai + late_ai * early_ar,
        late_ar * early_br - late_ai * early_bi + late_br,
        late_ar * early_bi + late_ai * early_br + late_bi,
    )


def gelu_tanh(values):
    return jax.nn.gelu(values, approximate=True)


def local_chain(coef_re, coef_im, drive_re, drive_im, reverse):
    return lax.associative_scan(
        compose, (coef_re, coef_im, drive_re, drive_im), reverse=reverse, axis=1
    )


def chain_summary(local, reverse):
    edge_at = 0 if reverse else local[0].shape[1] - 1
    return tuple((member[:, edge_at, :] for member in local))


def state_carry_in(local, reverse):
    summary = chain_summary(local, reverse)
    sample = summary[0]
    found = carried_in(
        (summary[0], summary[1], summary[2], summary[3]),
        "seq",
        compose,
        (
            jnp.ones_like(sample),
            jnp.zeros_like(sample),
            jnp.zeros_like(sample),
            jnp.zeros_like(sample),
        ),
        reverse,
    )
    return (found[2], found[3])


def adjoint_carry_in(local, reverse):
    summary = chain_summary(local, reverse)
    sample = summary[0]
    found = carried_in(
        (summary[0], summary[1], summary[2], summary[3]),
        "seq",
        compose,
        (
            jnp.ones_like(sample),
            jnp.zeros_like(sample),
            jnp.zeros_like(sample),
            jnp.zeros_like(sample),
        ),
        reverse,
    )
    return (found[2], found[3])


def apply_carry(local, carried_along):
    acc_re, acc_im, part_re, part_im = local
    carry_re = carried_along[0][:, None, :]
    carry_im = carried_along[1][:, None, :]
    return (
        part_re + acc_re * carry_re - acc_im * carry_im,
        part_im + acc_re * carry_im + acc_im * carry_re,
    )


def norm_totals(first_sum, second_sum):
    running_totals = lax.psum((first_sum, second_sum), "seq")
    return running_totals


def spread_normed(values):
    return lax.all_gather(values, "state", axis=2, tiled=True)


def spread_active(values):
    return lax.all_gather(values, "state", axis=2, tiled=True)


def spread_grad(values):
    return lax.all_gather(values, "state", axis=2, tiled=True)


def reduce_mix(values):
    return lax.psum_scatter(values, "state", scatter_dimension=2, tiled=True)


def reduce_active(values):
    return lax.psum_scatter(
        values.astype(jnp.bfloat16), "state", scatter_dimension=2, tiled=True
    ).astype(jnp.float32)


def reduce_normed(values):
    return lax.psum_scatter(
        values.astype(jnp.bfloat16), "state", scatter_dimension=2, tiled=True
    ).astype(jnp.float32)


def project_in(normed_all_rows, in_proj):
    row_count, time_len, full_width = normed_all_rows.shape
    flat_rows = normed_all_rows.reshape(row_count * time_len, full_width)
    result = jnp.dot(flat_rows, in_proj.reshape(full_width, -1), preferred_element_type=jnp.float32)
    return result.reshape(row_count, time_len, -1)


def block_forward(block_inputs, weights, masks, reverse, element_count):
    (
        batchnorm_gain,
        batchnorm_bias,
        in_proj,
        out_proj,
        rate_log,
        angle_log,
        skip_gain,
        glu_lin,
        glu_gate,
    ) = weights
    row_count, time_len, width_here = block_inputs.shape
    full_width = in_proj.shape[0]
    state_count = in_proj.shape[2]
    token_count = row_count * time_len
    running_totals = norm_totals(
        jnp.sum(block_inputs, axis=(0, 1)), jnp.sum(block_inputs * block_inputs, axis=(0, 1))
    )
    batch_mean = running_totals[0] / element_count
    reciprocal_deviation = lax.rsqrt(
        running_totals[1] / element_count - batch_mean * batch_mean + norm_eps
    )
    centered_input = (block_inputs - batch_mean) * reciprocal_deviation
    normed_rows = centered_input * batchnorm_gain.astype(jnp.float32) + batchnorm_bias.astype(
        jnp.float32
    )
    normed_all_rows = spread_normed(normed_rows.astype(jnp.bfloat16))
    projected = project_in(normed_all_rows, in_proj)
    lam_re, lam_im, scale_in = decay_terms(
        rate_log.astype(jnp.float32), angle_log.astype(jnp.float32)
    )
    keep_here = masks[1] if reverse else masks[0]
    local = local_chain(
        lam_re * keep_here,
        lam_im * keep_here,
        scale_in * projected[..., :state_count],
        scale_in * projected[..., state_count:],
        reverse,
    )
    carried_along = state_carry_in(local, reverse)
    h_re, h_im = apply_carry(local, carried_along)
    states_low = jnp.concatenate([h_re, h_im], axis=2).astype(jnp.bfloat16)
    mixed_part = jnp.dot(
        states_low.reshape(token_count, 2 * state_count),
        out_proj.reshape(2 * state_count, full_width),
        preferred_element_type=jnp.float32,
    ).reshape(row_count, time_len, full_width)
    mixed_output = reduce_mix(mixed_part) + skip_gain.astype(jnp.float32) * normed_rows
    active_all_rows = spread_active(gelu_tanh(mixed_output).astype(jnp.bfloat16))
    active_rows = active_all_rows.reshape(token_count, full_width)
    linear = jnp.dot(active_rows, glu_lin, preferred_element_type=jnp.float32)
    gating = jnp.dot(active_rows, glu_gate, preferred_element_type=jnp.float32)
    block_outputs = block_inputs + (linear * jax.nn.sigmoid(gating)).reshape(
        row_count, time_len, width_here
    )
    return (
        block_outputs,
        (
            centered_input,
            reciprocal_deviation,
            normed_rows,
            normed_all_rows,
            carried_along,
            mixed_output,
            active_all_rows,
            None,
        ),
    )


def block_backward(grad_out, weights, masks, reverse, element_count, saved_values):
    (
        batchnorm_gain,
        batchnorm_bias,
        in_proj,
        out_proj,
        rate_log,
        angle_log,
        skip_gain,
        glu_lin,
        glu_gate,
    ) = weights
    (
        centered_input,
        reciprocal_deviation,
        normed_rows,
        normed_all_rows,
        carried_along,
        mixed_output,
        active_all_rows,
        saved_states,
    ) = saved_values
    row_count, time_len, width_here = grad_out.shape
    full_width = in_proj.shape[0]
    state_count = in_proj.shape[2]
    token_count = row_count * time_len
    active_rows = active_all_rows.reshape(token_count, full_width)
    linear = jnp.dot(active_rows, glu_lin, preferred_element_type=jnp.float32)
    gating = jnp.dot(active_rows, glu_gate, preferred_element_type=jnp.float32)
    gate_sig = jax.nn.sigmoid(gating)
    upstream = grad_out.reshape(token_count, width_here)
    d_linear = (upstream * gate_sig).astype(jnp.bfloat16)
    d_gating = (upstream * linear * gate_sig * (1.0 - gate_sig)).astype(jnp.bfloat16)
    lin_grad = jnp.einsum("ta,tb->ab", active_rows, d_linear, preferred_element_type=jnp.float32)
    gate_grad = jnp.einsum("ta,tb->ab", active_rows, d_gating, preferred_element_type=jnp.float32)
    d_active = jnp.einsum(
        "tb,ab->ta", d_linear, glu_lin, preferred_element_type=jnp.float32
    ) + jnp.einsum("tb,ab->ta", d_gating, glu_gate, preferred_element_type=jnp.float32)
    d_active = reduce_active(d_active.reshape(row_count, time_len, full_width))
    gelu_value, gelu_pull = jax.vjp(gelu_tanh, mixed_output)
    d_mixed = gelu_pull(d_active)[0]
    skip_grad = jnp.sum(d_mixed * normed_rows, axis=(0, 1))
    normed_grad = d_mixed * skip_gain.astype(jnp.float32)
    d_mixed_full = spread_grad(d_mixed.astype(jnp.bfloat16))
    d_mixed_rows = d_mixed_full.reshape(token_count, full_width)
    out_matrix = out_proj.reshape(2 * state_count, full_width)
    d_states = jnp.einsum("ta,sa->ts", d_mixed_rows, out_matrix, preferred_element_type=jnp.float32)
    d_states = d_states.reshape(row_count, time_len, 2 * state_count)
    projected = project_in(normed_all_rows, in_proj)
    lam_re, lam_im, scale_in = decay_terms(
        rate_log.astype(jnp.float32), angle_log.astype(jnp.float32)
    )
    keep_here = masks[1] if reverse else masks[0]
    keep_adjoint = masks[0] if reverse else masks[1]
    local = local_chain(
        lam_re * keep_here,
        lam_im * keep_here,
        scale_in * projected[..., :state_count],
        scale_in * projected[..., state_count:],
        reverse,
    )
    h_re, h_im = apply_carry(local, carried_along)
    states_low = jnp.concatenate([h_re, h_im], axis=2).astype(jnp.bfloat16)
    out_grad = jnp.einsum(
        "ts,ta->sa",
        states_low.reshape(token_count, 2 * state_count),
        d_mixed_rows,
        preferred_element_type=jnp.float32,
    ).reshape(2, state_count, full_width)
    adjoint_reverse = not reverse
    adjoint_local = local_chain(
        lam_re * keep_adjoint,
        -lam_im * keep_adjoint,
        d_states[..., :state_count],
        d_states[..., state_count:],
        adjoint_reverse,
    )
    adj_re, adj_im = apply_carry(adjoint_local, adjoint_carry_in(adjoint_local, adjoint_reverse))
    if reverse:
        prior_re = jnp.concatenate([h_re[:, 1:], carried_along[0][:, None, :]], axis=1)
        prior_im = jnp.concatenate([h_im[:, 1:], carried_along[1][:, None, :]], axis=1)
    else:
        prior_re = jnp.concatenate([carried_along[0][:, None, :], h_re[:, :-1]], axis=1)
        prior_im = jnp.concatenate([carried_along[1][:, None, :], h_im[:, :-1]], axis=1)
    d_lam_re = jnp.sum(keep_here * (adj_re * prior_re + adj_im * prior_im), axis=(0, 1))
    d_lam_im = jnp.sum(keep_here * (adj_im * prior_re - adj_re * prior_im), axis=(0, 1))
    d_scale = jnp.sum(
        adj_re * projected[..., :state_count] + adj_im * projected[..., state_count:], axis=(0, 1)
    )
    decay_value, decay_pull = jax.vjp(
        decay_terms, rate_log.astype(jnp.float32), angle_log.astype(jnp.float32)
    )
    rate_grad, angle_grad = decay_pull((d_lam_re, d_lam_im, d_scale))
    d_projected = jnp.concatenate([scale_in * adj_re, scale_in * adj_im], axis=2).astype(
        jnp.bfloat16
    )
    d_projected = d_projected.reshape(token_count, 2 * state_count)
    in_grad = jnp.einsum(
        "ta,ts->as",
        normed_all_rows.reshape(token_count, full_width),
        d_projected,
        preferred_element_type=jnp.float32,
    ).reshape(full_width, 2, state_count)
    d_back = jnp.einsum(
        "ts,as->ta",
        d_projected,
        in_proj.reshape(full_width, 2 * state_count),
        preferred_element_type=jnp.float32,
    ).reshape(row_count, time_len, full_width)
    normed_grad = normed_grad + reduce_normed(d_back)
    norm_gain_gradient = jnp.sum(normed_grad * centered_input, axis=(0, 1))
    bias_grad = jnp.sum(normed_grad, axis=(0, 1))
    partials = (
        norm_gain_gradient,
        bias_grad,
        in_grad,
        out_grad,
        rate_grad,
        angle_grad,
        skip_grad,
        lin_grad,
        gate_grad,
    )
    running_totals = lax.psum(
        (
            partials[0],
            partials[1],
            partials[2],
            partials[3],
            partials[4],
            partials[5],
            partials[6],
            partials[7],
            partials[8],
        ),
        "seq",
    )
    gain_current = batchnorm_gain.astype(jnp.float32)
    centered_grad = normed_grad * gain_current
    d_inputs = grad_out + reciprocal_deviation * (
        centered_grad
        - gain_current * running_totals[1] / element_count
        - centered_input * gain_current * running_totals[0] / element_count
    )
    return (d_inputs, running_totals)


def body(
    tokens,
    batchnorm_gain,
    batchnorm_bias,
    in_proj,
    out_proj,
    rate_log,
    angle_log,
    skip_gain,
    glu_lin,
    glu_gate,
    positions,
    cotangent,
):
    element_count = float(positions.shape[0] * tokens.shape[1] * lax.axis_size("seq"))
    weights = (
        batchnorm_gain,
        batchnorm_bias,
        in_proj,
        out_proj,
        rate_log,
        angle_log,
        skip_gain,
        glu_lin,
        glu_gate,
    )
    time_len = tokens.shape[1]
    time_index = lax.axis_index("seq") * time_len + jnp.arange(time_len, dtype=jnp.int32)
    hit_now = jnp.any(positions[:, None, :] == time_index[None, :, None], axis=2)
    hit_next = jnp.any(positions[:, None, :] == time_index[None, :, None] + 1, axis=2)
    mask_fwd = jnp.where(hit_now, 0.0, 1.0).astype(jnp.float32)[:, :, None]
    mask_bwd = jnp.where(hit_next, 0.0, 1.0).astype(jnp.float32)[:, :, None]
    masks = (mask_fwd, mask_bwd)
    first_weights = tuple((member[0] for member in weights))
    second_weights = tuple((member[1] for member in weights))
    first_out, first_kept = block_forward(
        tokens.astype(jnp.float32), first_weights, masks, False, element_count
    )
    second_out, second_kept = block_forward(first_out, second_weights, masks, True, element_count)
    middle_grad, second_totals = block_backward(
        cotangent.astype(jnp.float32), second_weights, masks, True, element_count, second_kept
    )
    input_grad, first_totals = block_backward(
        middle_grad, first_weights, masks, False, element_count, first_kept
    )
    grads = tuple(
        (
            jnp.stack([first_grad, second_grad])
            for first_grad, second_grad in zip(first_totals, second_totals)
        )
    )
    block_out = second_out.astype(jnp.bfloat16)
    return (
        block_out,
        input_grad,
        grads[0],
        grads[1],
        grads[2],
        grads[3],
        grads[4],
        grads[5],
        grads[6],
        grads[7],
        grads[8],
    )


def solution(mesh):
    placed = (
        P(None, "seq", "state"),
        P(None, "state"),
        P(None, "state"),
        P(None, None, None, "state"),
        P(None, None, "state", None),
        P(None, "state"),
        P(None, "state"),
        P(None, "state"),
        P(None, None, "state"),
        P(None, None, "state"),
        P(),
        P(None, "seq", "state"),
    )
    return jax.shard_map(
        body,
        mesh=mesh,
        in_specs=placed,
        out_specs=(
            P(None, "seq", "state"),
            P(None, "seq", "state"),
            P(None, "state"),
            P(None, "state"),
            P(None, None, None, "state"),
            P(None, None, "state", None),
            P(None, "state"),
            P(None, "state"),
            P(None, "state"),
            P(None, None, "state"),
            P(None, None, "state"),
        ),
        check_vma=False,
    )
```

profile of v0, /device:TPU:0, one launch (start us, length us, event | category | flops | bytes accessed | tf_op | source)
XLA Modules:
  0.0 1639.8 jit_solution(7077188708286047563)
XLA Ops:
  10.6 43.5 %all-reduce.259 = (f32[256]{0:T(256)S(1)}, f32[256]{0:T(256)S(1)}) all-reduce(f32[256]{0:T(256)S(1)} %get-tuple-element.853, f32[256]{0:T(256)S(1)} %get-tuple-element.852), channel_id=1, replica_groups=mesh['seq'=16,'state'=2] {'seq'}, use_global_device_ids=true, to_apply=%region_3.4 | all-reduce | flops 512 | bytes 4096 | tf_op jit(solution)/shard_map/psum | solution.py:111
  110.5 37.4 %all-gather = f32[64,1,128]{2,1,0:T(1,128)S(1)} all-gather(f32[4,1,128]{2,1,0:T(1,128)S(1)} %slice_add_fusion.123), channel_id=2, replica_groups=mesh['seq'=16,'state'=2] {'seq'}, dimensions={0}, use_global_device_ids=true | all-gather | bytes 34816 | tf_op jit(solution)/shard_map/all_gather | solution.py:11
  147.8 3.8 pad.973
  152.4 35.9 %all-gather.1 = f32[64,1,128]{2,1,0:T(1,128)S(1)} all-gather(f32[4,1,128]{2,1,0:T(1,128)S(1)} %slice_add_fusion.122), channel_id=3, replica_groups=mesh['seq'=16,'state'=2] {'seq'}, dimensions={0}, use_global_device_ids=true | all-gather | bytes 34816 | tf_op jit(solution)/shard_map/all_gather | solution.py:11
  189.9 3.8 pad.974
  193.7 3.8 pad.941
  198.3 37.4 %all-gather.2 = f32[64,1,128]{2,1,0:T(1,128)S(1)} all-gather(f32[4,1,128]{2,1,0:T(1,128)S(1)} %slice_add_fusion.121), channel_id=4, replica_groups=mesh['seq'=16,'state'=2] {'seq'}, dimensions={0}, use_global_device_ids=true | all-gather | bytes 34816 | tf_op jit(solution)/shard_map/all_gather | solution.py:11
  235.6 3.8 pad.975
  240.2 35.9 %all-gather.3 = f32[64,1,128]{2,1,0:T(1,128)S(1)} all-gather(f32[4,1,128]{2,1,0:T(1,128)S(1)} %slice_add_fusion.120), channel_id=5, replica_groups=mesh['seq'=16,'state'=2] {'seq'}, dimensions={0}, use_global_device_ids=true | all-gather | bytes 34816 | tf_op jit(solution)/shard_map/all_gather | solution.py:11
  282.3 6.6 reduce-scatter.7.cloned.1.call-done
  291.6 10.3 all-gather.25.cloned.1.call-done
  305.4 42.0 %all-reduce.258 = (f32[256]{0:T(256)S(1)}, f32[256]{0:T(256)S(1)}) all-reduce(f32[256]{0:T(256)S(1)} %get-tuple-element.851, f32[256]{0:T(256)S(1)} %get-tuple-element.850), channel_id=1, replica_groups=mesh['seq'=16,'state'=2] {'seq'}, use_global_device_ids=true, to_apply=%region_11.12 | all-reduce | flops 512 | bytes 4096 | tf_op jit(solution)/shard_map/psum | solution.py:111
  476.0 3.8 pad.1035
  486.5 3.8 pad.1037
  534.6 3.8 pad.1005
  544.5 3.8 pad.1039
  551.0 4.8 rev.17
  555.8 35.6 %all-gather.4 = f32[64,1,128]{2,1,0:T(1,128)S(1)} all-gather(f32[4,1,128]{2,1,0:T(1,128)S(1)} %copy-done.199), channel_id=6, replica_groups=mesh['seq'=16,'state'=2] {'seq'}, dimensions={0}, use_global_device_ids=true | all-gather | bytes 34816 | tf_op jit(solution)/shard_map/all_gather | solution.py:11
  591.4 4.7 rev.18
  596.2 37.6 %all-gather.5 = f32[64,1,128]{2,1,0:T(1,128)S(1)} all-gather(f32[4,1,128]{2,1,0:T(1,128)S(1)} %copy-done.201), channel_id=7, replica_groups=mesh['seq'=16,'state'=2] {'seq'}, dimensions={0}, use_global_device_ids=true | all-gather | bytes 34816 | tf_op jit(solution)/shard_map/all_gather | solution.py:11
  636.4 35.6 %all-gather.6 = f32[64,1,128]{2,1,0:T(1,128)S(1)} all-gather(f32[4,1,128]{2,1,0:T(1,128)S(1)} %slice_add_fusion.113), channel_id=8, replica_groups=mesh['seq'=16,'state'=2] {'seq'}, dimensions={0}, use_global_device_ids=true | all-gather | bytes 34816 | tf_op jit(solution)/shard_map/all_gather | solution.py:11
  672.0 4.7 rev.19
  676.7 37.6 %all-gather.7 = f32[64,1,128]{2,1,0:T(1,128)S(1)} all-gather(f32[4,1,128]{2,1,0:T(1,128)S(1)} %slice_add_fusion.112), channel_id=9, replica_groups=mesh['seq'=16,'state'=2] {'seq'}, dimensions={0}, use_global_device_ids=true | all-gather | bytes 34816 | tf_op jit(solution)/shard_map/all_gather | solution.py:11
  720.9 5.5 reduce-scatter.9.cloned.1.call-done
  729.1 10.3 all-gather.29.cloned.1.call-done
  745.0 9.7 reduce-scatter.11.cloned.1.call-done
  904.8 3.9 pad.1098
  910.4 3.8 pad.1100
  914.2 3.8 pad.1099
  918.8 41.0 %all-gather.8 = f32[64,1,128]{2,1,0:T(1,128)S(1)} all-gather(f32[4,1,128]{2,1,0:T(1,128)S(1)} %slice_add_fusion.107), channel_id=10, replica_groups=mesh['seq'=16,'state'=2] {'seq'}, dimensions={0}, use_global_device_ids=true | all-gather | bytes 34816 | tf_op jit(solution)/shard_map/all_gather | solution.py:11
  959.8 3.9 pad.1101
  964.4 35.6 %all-gather.9 = f32[64,1,128]{2,1,0:T(1,128)S(1)} all-gather(f32[4,1,128]{2,1,0:T(1,128)S(1)} %slice_add_fusion.106), channel_id=11, replica_groups=mesh['seq'=16,'state'=2] {'seq'}, dimensions={0}, use_global_device_ids=true | all-gather | bytes 34816 | tf_op jit(solution)/shard_map/all_gather | solution.py:11
  1001.6 3.8 pad.1102
  1005.4 3.8 pad.1069
  1010.0 37.6 %all-gather.10 = f32[64,1,128]{2,1,0:T(1,128)S(1)} all-gather(f32[4,1,128]{2,1,0:T(1,128)S(1)} %slice_add_fusion.105), channel_id=12, replica_groups=mesh['seq'=16,'state'=2] {'seq'}, dimensions={0}, use_global_device_ids=true | all-gather | bytes 34816 | tf_op jit(solution)/shard_map/all_gather | solution.py:11
  1050.2 35.6 %all-gather.11 = f32[64,1,128]{2,1,0:T(1,128)S(1)} all-gather(f32[4,1,128]{2,1,0:T(1,128)S(1)} %slice_add_fusion.104), channel_id=13, replica_groups=mesh['seq'=16,'state'=2] {'seq'}, dimensions={0}, use_global_device_ids=true | all-gather | bytes 34816 | tf_op jit(solution)/shard_map/all_gather | solution.py:11
  1086.5 4.6 broadcast_multiply_fusion.3
  1093.5 6.4 reduce-scatter.13.cloned.1.call-done
  1102.0 41.9 %all-reduce.257 = (f32[256]{0:T(256)S(1)}, f32[256]{0:T(256)S(1)}) all-reduce(f32[256]{0:T(256)S(1)} %get-tuple-element.843, f32[256]{0:T(256)S(1)} %get-tuple-element.847), channel_id=1, replica_groups=mesh['seq'=16,'state'=2] {'seq'}, use_global_device_ids=true, to_apply=%region_23.24 | all-reduce | flops 512 | bytes 4096 | tf_op jit(solution)/shard_map/psum | solution.py:344
  1151.2 4.3 reduce-scatter.15.cloned.1.call-done
  1264.5 41.1 %all-gather.12 = f32[64,1,128]{2,1,0:T(1,128)S(1)} all-gather(f32[4,1,128]{2,1,0:T(1,128)S(1)} %copy-done.198), channel_id=14, replica_groups=mesh['seq'=16,'state'=2] {'seq'}, dimensions={0}, use_global_device_ids=true | all-gather | bytes 34816 | tf_op jit(solution)/shard_map/all_gather | solution.py:11
  1305.6 4.7 rev.22
  1310.4 35.6 %all-gather.13 = f32[64,1,128]{2,1,0:T(1,128)S(1)} all-gather(f32[4,1,128]{2,1,0:T(1,128)S(1)} %copy-done.200), channel_id=15, replica_groups=mesh['seq'=16,'state'=2] {'seq'}, dimensions={0}, use_global_device_ids=true | all-gather | bytes 34816 | tf_op jit(solution)/shard_map/all_gather | solution.py:11
  1346.0 4.7 rev.20
  1350.7 37.6 %all-gather.14 = f32[64,1,128]{2,1,0:T(1,128)S(1)} all-gather(f32[4,1,128]{2,1,0:T(1,128)S(1)} %slice_add_fusion.97), channel_id=16, replica_groups=mesh['seq'=16,'state'=2] {'seq'}, dimensions={0}, use_global_device_ids=true | all-gather | bytes 34816 | tf_op jit(solution)/shard_map/all_gather | solution.py:11
  1390.9 35.6 %all-gather.15 = f32[64,1,128]{2,1,0:T(1,128)S(1)} all-gather(f32[4,1,128]{2,1,0:T(1,128)S(1)} %slice_add_fusion.96), channel_id=17, replica_groups=mesh['seq'=16,'state'=2] {'seq'}, dimensions={0}, use_global_device_ids=true | all-gather | bytes 34816 | tf_op jit(solution)/shard_map/all_gather | solution.py:11
  1458.7 42.0 %all-reduce.256 = (f32[256]{0:T(256)S(1)}, f32[256]{0:T(256)S(1)}, f32[1,128]{1,0:T(1,128)S(1)}, f32[1,128]{1,0:T(1,128)S(1)}, f32[1,128]{1,0:T(1,128)S(1)}, /*i...) all-reduce(f32[256]{0:T(256)S(1)} %get-tuple-element.845, ...), channel_id=1, replica_groups=mesh['seq'=16,'state'=2] {'seq'}, use_global_device_ids=true, to_apply=%region_31.32 | all-reduce | flops 1536 | bytes 12288 | tf_op jit(solution)/shard_map/psum | solution.py:344
  1505.0 121.6 %all-reduce.263.cloned.1.call-done = (f32[1,512,2,128]{3,1,2,0:T(8,128)}, f32[1,512,2,128]{3,1,2,0:T(8,128)}, f32[1,2,128,512]{3,2,1,0:T(8,128)}, f32[1,2,128,51...) async-done(((f32[1,512,2,128]{3,1,2,0:T(8,128)}, f32[1,512,2,128]{3,1,2,0:T(8,128)}, ...) | async-done | bytes 4194320 | tf_op jit(solution)/shard_map/psum | solution.py:344
  (1642 shorter events, 602.8 us)
Async XLA Ops:
  7.2 49.0 %copy-start.225 = (s32[4,16]{1,0:T(4,128)S(1)}, s32[4,16]{1,0:T(4,128)}, u32[]{:S(2)}) copy-start(s32[4,16]{1,0:T(4,128)} %param.30) | copy-start | bytes 772
  7.2 49.2 %copy-start.207 = (bf16[2,128]{1,0:T(2,128)(2,1)S(1)}, bf16[2,128]{1,0:T(2,128)(2,1)}, u32[]{:S(2)}) copy-start(bf16[2,128]{1,0:T(2,128)(2,1)} %param.26) | copy-start | bytes 1540
  7.2 49.2 %copy-start.209 = (bf16[2,128]{1,0:T(2,128)(2,1)S(1)}, bf16[2,128]{1,0:T(2,128)(2,1)}, u32[]{:S(2)}) copy-start(bf16[2,128]{1,0:T(2,128)(2,1)} %param.25) | copy-start | bytes 1540
  7.2 57.6 %all-gather.23.cloned.1.call-start = ((), (), s32[]{:S(2)}) async-start(), calls=%async_computation.6 | async-start | bytes 1572864 | tf_op jit(solution)/shard_map/all_gather | solution.py:116
  8.0 280.9 %copy-start.138 = (f32[1,256]{1,0:T(1,128)}, f32[1,256]{1,0:T(1,128)S(1)}, u32[]{:S(2)}) copy-start(f32[1,256]{1,0:T(1,128)S(1)} %get-tuple-element.1338) | copy-start | bytes 3076
  8.0 339.4 %copy-start.141 = (f32[1,256]{1,0:T(1,128)}, f32[1,256]{1,0:T(1,128)S(1)}, u32[]{:S(2)}) copy-start(f32[1,256]{1,0:T(1,128)S(1)} %get-tuple-element.1337) | copy-start | bytes 3076
  9.3 47.7 %copy-start.164 = (f32[1,256]{1,0:T(1,128)}, f32[1,256]{1,0:T(1,128)S(1)}, u32[]{:S(2)}) copy-start(f32[1,256]{1,0:T(1,128)S(1)} %get-tuple-element.1340) | copy-start | bytes 3076
  56.1 232.8 %reduce-scatter.7.cloned.1.call-start = ((), (), s32[]{:S(2)}) async-start(), calls=%async_computation.7 | async-start | bytes 3145728 | tf_op jit(solution)/shard_map/reduce_scatter | solution.py:128
  107.7 80.5 %copy-start.179 = (f32[4,1,128]{2,1,0:T(1,128)S(1)}, f32[4,1,128]{2,1,0:T(1,128)}, u32[]{:S(2)}) copy-start(f32[4,1,128]{2,1,0:T(1,128)} %slice.3147) | copy-start | bytes 6148
  110.4 166.3 %copy-start.44 = (f32[4,256,128]{2,1,0:T(8,128)}, f32[4,256,128]{2,1,0:T(8,128)S(1)}, u32[]{:S(2)}) copy-start(f32[4,256,128]{2,1,0:T(8,128)S(1)} %pad.971) | copy-start | bytes 1572868
  281.6 20.3 %copy-start.104 = (bf16[2,512,256]{2,1,0:T(8,128)(2,1)S(1)}, bf16[2,512,256]{2,1,0:T(8,128)(2,1)}, u32[]{:S(2)}) copy-start(bf16[2,512,256]{2,1,0:T(8,128)(2,1)} %param.29) | copy-start | bytes 1572868
  281.7 20.2 %all-gather.25.cloned.1.call-start = ((), (), s32[]{:S(2)}) async-start(), calls=%async_computation.8 | async-start | bytes 1572864 | tf_op jit(solution)/shard_map/all_gather | solution.py:120
  282.3 21.4 %copy-start.161 = (f32[1,256]{1,0:T(1,128)}, f32[1,256]{1,0:T(1,128)S(1)}, u32[]{:S(2)}) copy-start(f32[1,256]{1,0:T(1,128)S(1)} %get-tuple-element.1334) | copy-start | bytes 3076
  291.6 74.4 %all-gather.27.cloned.1.call-start = ((), (), s32[]{:S(2)}) async-start(), calls=%async_computation.9 | async-start | bytes 1572864 | tf_op jit(solution)/shard_map/all_gather | solution.py:116
  305.2 42.2 %copy-start.168 = (f32[1,256]{1,0:T(1,128)S(1)}, f32[1,256]{1,0:T(1,128)}, u32[]{:S(2)}) copy-start(f32[1,256]{1,0:T(1,128)} %get-tuple-element.1339) | copy-start | bytes 3076
  348.4 378.0 %reduce-scatter.9.cloned.1.call-start = ((), (), s32[]{:S(2)}) async-start(), calls=%async_computation.10 | async-start | bytes 3145728 | tf_op jit(solution)/shard_map/reduce_scatter | solution.py:128
  451.0 20.5 %copy-start.22 = (f32[4,127,128]{2,1,0:T(8,128)S(1)}, f32[4,127,128]{2,1,0:T(8,128)}, u32[]{:S(2)}) copy-start(f32[4,127,128]{2,1,0:T(8,128)} %slice.2673) | copy-start | bytes 780292
  451.0 20.5 %copy-start.23 = (f32[4,127,128]{2,1,0:T(8,128)S(1)}, f32[4,127,128]{2,1,0:T(8,128)}, u32[]{:S(2)}) copy-start(f32[4,127,128]{2,1,0:T(8,128)} %slice.2553) | copy-start | bytes 780292
  544.5 51.6 %copy-start.201 = (f32[4,1,128]{2,1,0:T(1,128)S(1)}, f32[4,1,128]{2,1,0:T(1,128)}, u32[]{:S(2)}) copy-start(f32[4,1,128]{2,1,0:T(1,128)} %slice_add_fusion.114) | copy-start | bytes 6148
  551.0 82.8 %copy-start.47 = (f32[4,256,128]{2,1,0:T(8,128)S(1)}, f32[4,256,128]{2,1,0:T(8,128)}, u32[]{:S(2)}) copy-start(f32[4,256,128]{2,1,0:T(8,128)} %add.2402) | copy-start | bytes 1572868
  551.0 163.3 %copy-start.130 = (f32[4,128]{1,0:T(4,128)S(1)}, f32[4,128]{1,0:T(4,128)}, u32[]{:S(2)}) copy-start(f32[4,128]{1,0:T(4,128)} %custom-call.3) | copy-start | bytes 6148
  551.0 163.3 %copy-start.131 = (f32[4,128]{1,0:T(4,128)S(1)}, f32[4,128]{1,0:T(4,128)}, u32[]{:S(2)}) copy-start(f32[4,128]{1,0:T(4,128)} %custom-call.2) | copy-start | bytes 6148
  720.8 18.5 %all-gather.29.cloned.1.call-start = ((), (), s32[]{:S(2)}) async-start(), calls=%async_computation.11 | async-start | bytes 1572864 | tf_op jit(solution)/shard_map/all_gather | solution.py:120
  729.0 25.7 %reduce-scatter.11.cloned.1.call-start = ((), (), s32[]{:S(2)}) async-start(), calls=%async_computation.12 | async-start | bytes 1572864 | tf_op jit(solution)/shard_map/reduce_scatter | solution.py:132
  744.8 26.6 %all-gather.31.cloned.1.call-start = ((), (), s32[]{:S(2)}) async-start(), calls=%async_computation.13 | async-start | bytes 1572864 | tf_op jit(solution)/shard_map/all_gather | solution.py:124
  758.1 341.8 %reduce-scatter.13.cloned.1.call-start = ((), (), s32[]{:S(2)}) async-start(), calls=%async_computation.14 | async-start | bytes 1572864 | tf_op jit(solution)/shard_map/reduce_scatter | solution.py:138
  819.8 21.4 %copy-start.83 = (f32[4,31,128]{2,1,0:T(8,128)S(1)}, f32[4,31,128]{2,1,0:T(8,128)}, u32[]{:S(2)}) copy-start(f32[4,31,128]{2,1,0:T(8,128)} %slice.2821) | copy-start | bytes 190468
  819.9 21.3 %copy-start.84 = (f32[4,31,128]{2,1,0:T(8,128)S(1)}, f32[4,31,128]{2,1,0:T(8,128)}, u32[]{:S(2)}) copy-start(f32[4,31,128]{2,1,0:T(8,128)} %slice.2742) | copy-start | bytes 190468
  866.2 24.3 %copy-start.90 = (f32[4,64,128]{2,1,0:T(8,128)S(1)}, f32[4,64,128]{2,1,0:T(8,128)}, u32[]{:S(2)}) copy-start(f32[4,64,128]{2,1,0:T(8,128)} %add.2496) | copy-start | bytes 393220
  902.9 106.4 %copy-start.43 = (f32[4,256,128]{2,1,0:T(8,128)}, f32[4,256,128]{2,1,0:T(8,128)S(1)}, u32[]{:S(2)}) copy-start(f32[4,256,128]{2,1,0:T(8,128)S(1)} %pad.1068) | copy-start | bytes 1572868
  902.9 97.0 %copy-start.196 = (f32[4,1,128]{2,1,0:T(1,128)S(1)}, f32[4,1,128]{2,1,0:T(1,128)}, u32[]{:S(2)}) copy-start(f32[4,1,128]{2,1,0:T(1,128)} %get-tuple-element.1010) | copy-start | bytes 6148
  1049.4 37.0 %copy-start.45 = (f32[4,256,128]{2,1,0:T(8,128)}, f32[4,256,128]{2,1,0:T(8,128)S(1)}, u32[]{:S(2)}) copy-start(f32[4,256,128]{2,1,0:T(8,128)S(1)} %pad.1103) | copy-start | bytes 1572868
  1093.5 62.0 %reduce-scatter.15.cloned.1.call-start = ((), (), s32[]{:S(2)}) async-start(), calls=%async_computation.15 | async-start | bytes 1572864 | tf_op jit(solution)/shard_map/reduce_scatter | solution.py:132
  1150.9 25.4 %all-gather.33.cloned.1.call-start = ((), (), s32[]{:S(2)}) async-start(), calls=%async_computation.16 | async-start | bytes 1572864 | tf_op jit(solution)/shard_map/all_gather | solution.py:124
  1158.4 298.7 %reduce-scatter.17.cloned.1.call-start = ((), (), s32[]{:S(2)}) async-start(), calls=%async_computation.17 | async-start | bytes 1572864 | tf_op jit(solution)/shard_map/reduce_scatter | solution.py:138
  1259.2 51.2 %copy-start.200 = (f32[4,1,128]{2,1,0:T(1,128)S(1)}, f32[4,1,128]{2,1,0:T(1,128)}, u32[]{:S(2)}) copy-start(f32[4,1,128]{2,1,0:T(1,128)} %slice_add_fusion.98) | copy-start | bytes 6148
  1261.8 164.7 %copy-start.132 = (f32[4,128]{1,0:T(4,128)S(1)}, f32[4,128]{1,0:T(4,128)}, u32[]{:S(2)}) copy-start(f32[4,128]{1,0:T(4,128)} %custom-call.7) | copy-start | bytes 6148
  1261.8 164.7 %copy-start.133 = (f32[4,128]{1,0:T(4,128)S(1)}, f32[4,128]{1,0:T(4,128)}, u32[]{:S(2)}) copy-start(f32[4,128]{1,0:T(4,128)} %custom-call.6) | copy-start | bytes 6148
  1264.5 123.9 %copy-start.48 = (f32[4,256,128]{2,1,0:T(8,128)S(1)}, f32[4,256,128]{2,1,0:T(8,128)}, u32[]{:S(2)}) copy-start(f32[4,256,128]{2,1,0:T(8,128)} %add.2628) | copy-start | bytes 1572868
  1264.5 162.8 %copy-start.2 = (f32[4,256,256]{2,1,0:T(8,128)S(1)}, f32[4,256,256]{2,1,0:T(8,128)}, u32[]{:S(2)}) copy-start(f32[4,256,256]{2,1,0:T(8,128)} %copy-done.1) | copy-start | bytes 3145732
  1264.5 162.8 %copy-start.127 = (f32[4,128]{1,0:T(4,128)S(1)}, f32[4,128]{1,0:T(4,128)}, u32[]{:S(2)}) copy-start(f32[4,128]{1,0:T(4,128)} %copy-done.126) | copy-start | bytes 6148
  1264.5 162.8 %copy-start.129 = (f32[4,128]{1,0:T(4,128)S(1)}, f32[4,128]{1,0:T(4,128)}, u32[]{:S(2)}) copy-start(f32[4,128]{1,0:T(4,128)} %copy-done.128) | copy-start | bytes 6148
  1264.5 162.8 %copy-start.160 = (f32[4,256]{1,0:T(4,128)S(1)}, f32[4,256]{1,0:T(4,128)}, u32[]{:S(2)}) copy-start(f32[4,256]{1,0:T(4,128)} %copy-done.159) | copy-start | bytes 12292
  1431.2 195.3 %all-reduce.263.cloned.1.call-start = ((), (), s32[]{:S(2)}) async-start(), calls=%async_computation.18 | async-start | bytes 8388608 | tf_op jit(solution)/shard_map/psum | solution.py:344
  1456.3 45.4 %copy-start.221 = (f32[256]{0:T(256)S(1)}, f32[256]{0:T(256)}, u32[]{:S(2)}) copy-start(f32[256]{0:T(256)} %copy-done.220) | copy-start | bytes 3076
  1456.3 46.0 %copy-start.218 = (f32[256]{0:T(256)S(1)}, f32[256]{0:T(256)}, u32[]{:S(2)}) copy-start(f32[256]{0:T(256)} %copy-done.217) | copy-start | bytes 3076
  1456.4 47.2 %copy-start.4 = (f32[4,256,256]{2,1,0:T(8,128)S(1)}, f32[4,256,256]{2,1,0:T(8,128)}, u32[]{:S(2)}) copy-start(f32[4,256,256]{2,1,0:T(8,128)} %copy-done.3) | copy-start | bytes 3145732
  1457.0 46.5 %copy-start.49 = (bf16[4,256,256]{2,1,0:T(8,128)(2,1)S(1)}, bf16[4,256,256]{2,1,0:T(8,128)(2,1)}, u32[]{:S(2)}) copy-start(bf16[4,256,256]{2,1,0:T(8,128)(2,1)} %reduce-scatter.17.cloned.1.call-done) | copy-start | bytes 1572868
  (191 other events, 1265.0 us)
Sparse Core Ops, SparseCore 0:
  56.3 4.8 all-gather.22
  281.8 7.1 reduce-scatter.6
  291.7 10.1 all-gather.24
  348.5 4.8 all-gather.26
  720.9 5.4 reduce-scatter.8
  729.1 10.1 all-gather.28
  744.9 9.7 reduce-scatter.10
  758.3 10.1 all-gather.30
  1093.6 6.3 reduce-scatter.12
  1151.0 4.4 reduce-scatter.14
  1158.5 10.1 all-gather.32
  1431.4 6.3 reduce-scatter.16
  1456.4 170.0 all-reduce.262
where the time goes:
time: 1660 us; the launch traced here: 1640 us
  blocking collectives  762 us (46%)
  local copies, waits for them, and re-layouts  424 us (26%)
  other arithmetic  216 us (13%)
  waiting for transfers between devices  175 us (11%)
  matrix products  40.4 us (2%)
  between operations  19.7 us (1%)
    all_gather x16, blocking collectives, carried_in(): everything = jax.tree.map(lambda part: lax.all_gather(part, axis), value)  593 us
    slice x450, local copies, waits for them, and re-layouts, local_chain(): lax.associative_scan(compose, (coef_re, coef_im, drive_re, drive_im), rev...  200 us
    pad x224, local copies, waits for them, and re-layouts, local_chain(): lax.associative_scan(compose, (coef_re, coef_im, drive_re, drive_im), rev...  168 us
    psum x1, waiting for transfers between devices, block_backward(): lax.psum((partials[0], partials[1], partials[2], partials[3], partials[4]...  122 us
    psum x2, blocking collectives, norm_totals(): running_totals = lax.psum((first_sum, second_sum), 'seq')  85.5 us
    psum x2, blocking collectives, block_backward(): lax.psum((partials[0], partials[1], partials[2], partials[3], partials[4]...  83.9 us
    add x136, other arithmetic, local_chain(): lax.associative_scan(compose, (coef_re, coef_im, drive_re, drive_im), rev...  66.9 us
    concatenate x112, other arithmetic, local_chain(): lax.associative_scan(compose, (coef_re, coef_im, drive_re, drive_im), rev...  50.7 us
  transfers between devices with their start and end apart: 13, of which 8 were waited for; matrix products, arithmetic and copies ran while one was open for 5% of the time, Pallas kernels for 0%

commit v1 on v0

v1 whole, which is shorter than its diff:
```python
import functools

import jax
import jax.numpy as jnp
from jax import lax
from jax.experimental import pallas as pl
from jax.experimental.pallas import tpu as pltpu
from jax.sharding import PartitionSpec as P

f32, bf16 = jnp.float32, jnp.bfloat16
norm_eps = 1e-05
CHUNKS = 8
SLAB = 2 * CHUNKS


def mm(a, b):
    return jnp.dot(a, b, preferred_element_type=f32)


def mm_nt(a, b):
    return lax.dot_general(a, b, (((1,), (1,)), ((), ())), preferred_element_type=f32)


def mm_tn(a, b):
    return lax.dot_general(a, b, (((0,), (0,)), ((), ())), preferred_element_type=f32)


def wide(row):
    return jnp.broadcast_to(row, (CHUNKS, 128))


def cmul(ar, ai, br, bi):
    return ar * br - ai * bi, ar * bi + ai * br


def row_of_tiles(tiles):
    return jnp.concatenate([tiles[i : i + 1, :] for i in range(tiles.shape[0])], axis=1)


def channel_row(core, own, oth, at):
    mine, other = own[at : at + 2, :], oth[at : at + 2, :]
    low = jnp.where(core == 0, mine, other)
    high = jnp.where(core == 0, other, mine)
    return jnp.concatenate([low[0:1], low[1:2], high[0:1], high[1:2]], axis=1)


def own_cols(core, width):
    return pl.ds(pl.multiple_of(core * width, width), width)


def oth_cols(core, width):
    return pl.ds(pl.multiple_of((1 - core) * width, width), width)


def scan(drive, lams, keep_ref, which, steps, reverse, start, visit):
    order = range(steps - 1, -1, -1) if reverse else range(steps)
    state = dict(start)
    for s in order:
        for row in range(2):
            at = s * SLAB + row * CHUNKS
            keep = keep_ref[which, at : at + CHUNKS, :]
            for half in range(2):
                lr, li = lams[half]
                hr, hi = state[half, row]
                hr, hi = keep * hr, keep * hi
                dr, di = drive(s, row, half)
                state[half, row] = (lr * hr - li * hi + dr, lr * hi + li * hr + di)
        visit(s, state, keep_ref)
    return state


def keep_products(keep_ref, which, steps):
    out = []
    for row in range(2):
        total = keep_ref[which, row * CHUNKS : (row + 1) * CHUNKS, :]
        for s in range(1, steps):
            at = s * SLAB + row * CHUNKS
            total = total * keep_ref[which, at : at + CHUNKS, :]
        out.append(total)
    return out


def chunk_scan(ends, keeps, powers, reverse, comp_ref, packed):
    index = lax.broadcasted_iota(jnp.int32, (CHUNKS, 128), 0)

    def shifted(value, by, fill):
        turned = pltpu.roll(value, CHUNKS - by if reverse else by, 0)
        valid = index < CHUNKS - by if reverse else index >= by
        return jnp.where(valid, turned, fill)

    for half in range(2):
        for row in range(2):
            er, ei = ends[half, row]
            pr, pi = powers[half][0] * keeps[row], powers[half][1] * keeps[row]
            for by in (1, 2, 4):
                tr, ti = cmul(pr, pi, shifted(er, by, 0.0), shifted(ei, by, 0.0))
                er, ei = er + tr, ei + ti
                pr, pi = cmul(pr, pi, shifted(pr, by, 1.0), shifted(pi, by, 0.0))
            edge = 0 if reverse else CHUNKS - 1
            q = row * 2 + half
            packed[q : q + 1, :] = er[edge : edge + 1, :]
            packed[4 + q : 5 + q, :] = ei[edge : edge + 1, :]
            base = (half * 2 + row) * 4
            comp_ref[base] = shifted(er, 1, 0.0)
            comp_ref[base + 1] = shifted(ei, 1, 0.0)
            comp_ref[base + 2] = shifted(pr, 1, 1.0)
            comp_ref[base + 3] = shifted(pi, 1, 0.0)


def device_carry(me, peers, got_ref, dk_ref, which, own, oth, base, conj, reverse, packed):
    index = lax.broadcasted_iota(jnp.int32, (CHUNKS, 128), 0)
    is_own = index % 2 == 0
    sign = jnp.where(index < 4, -1.0, 1.0) * (-1.0 if conj else 1.0)
    ar = jnp.where(is_own, wide(own[base + 11 : base + 12, :]), wide(oth[base + 11 : base + 12, :]))
    ai = jnp.where(is_own, wide(own[base + 12 : base + 13, :]), wide(oth[base + 12 : base + 13, :]))
    ai = ai * sign

    def step(k, held):
        at = peers - 1 - k if reverse else k
        reached = at > me if reverse else at < me
        new = dk_ref[which, at] * (ar * held + ai * pltpu.roll(held, 4, 0)) + got_ref[at]
        return jnp.where(reached, new, held)

    packed[...] = lax.fori_loop(0, peers, step, jnp.zeros((8, 128), f32), unroll=peers <= 16)


def entries(comp_ref, packed):
    start = {}
    for half in range(2):
        for row in range(2):
            base, q = (half * 2 + row) * 4, row * 2 + half
            hr, hi = wide(packed[q : q + 1, :]), wide(packed[4 + q : 5 + q, :])
            tr, ti = cmul(comp_ref[base + 2], comp_ref[base + 3], hr, hi)
            start[half, row] = (comp_ref[base] + tr, comp_ref[base + 1] + ti)
    return start


def decay(own, oth, base, at, conj=False):
    sign = -1.0 if conj else 1.0
    return [(wide(r[base + at : base + at + 1, :]), sign * wide(r[base + at + 1 : base + at + 2, :])) for r in (own, oth)]


def scales(own, oth, base):
    return [wide(r[base + 8 : base + 9, :]) for r in (own, oth)]


def nothing(*_):
    return None


def zeros_start():
    zero = jnp.zeros((CHUNKS, 128), f32)
    return {(half, row): (zero, zero) for half in range(2) for row in range(2)}


def part(s, row):
    at = s * SLAB + row * CHUNKS
    return slice(at, at + CHUNKS)


def cols(half, im):
    at = half * 256 + im * 128
    return slice(at, at + 128)


def spread(out_ref, packed):
    out_ref[...] = jnp.broadcast_to(packed[...][None], out_ref.shape)


def prep_kernel(peers, steps, info, pos, tokens, gain, bias, skip, rate_log, angle_log, stats, small, keep, dk, perm):
    seq, core = info[0], info[1]
    rows, span, _ = tokens.shape
    docs = pos.shape[1]
    s1 = s2 = 0.0
    for r in range(rows):
        x = tokens[r].astype(f32)
        s1 = s1 + jnp.sum(x, axis=0, keepdims=True)
        s2 = s2 + jnp.sum(x * x, axis=0, keepdims=True)
    for i in range(2):
        stats[0, i : i + 1, :] = s1[:, 128 * i : 128 * (i + 1)]
        stats[0, 2 + i : 3 + i, :] = s2[:, 128 * i : 128 * (i + 1)]
    stats[...] = jnp.broadcast_to(stats[0][None], stats.shape)

    small[...] = jnp.zeros_like(small)
    for k in range(2):
        at = 16 * k
        for j, ref in enumerate((gain, bias, skip)):
            v = ref[...].astype(f32)
            small[at + 2 * j : at + 2 * j + 1, :] = v[k : k + 1, :128]
            small[at + 2 * j + 1 : at + 2 * j + 2, :] = v[k : k + 1, 128:]
        rate = jnp.exp(rate_log[...].astype(f32)[k : k + 1, :])
        angle = jnp.exp(angle_log[...].astype(f32)[k : k + 1, :])
        modulus = jnp.exp(-rate)
        lr, li = modulus * jnp.cos(angle), modulus * jnp.sin(angle)
        small[at + 6 : at + 7, :] = lr
        small[at + 7 : at + 8, :] = li
        small[at + 8 : at + 9, :] = jnp.sqrt(1.0 - modulus * modulus)
        power = 1
        while power < span:
            lr, li = cmul(lr, li, lr, li)
            power *= 2
            if power == steps:
                small[at + 9 : at + 10, :] = lr
                small[at + 10 : at + 11, :] = li
        small[at + 11 : at + 12, :] = lr
        small[at + 12 : at + 13, :] = li

    chunk = lax.broadcasted_iota(jnp.int32, (CHUNKS, 128), 0) * steps + seq * span
    for row in range(2):
        targets = [pos[core * 2 + row, d] - chunk for d in range(docs)]
        for s in range(steps + 1):
            hit = targets[0] == s
            for t in targets[1:]:
                hit = jnp.logical_or(hit, t == s)
            value = jnp.where(hit, 0.0, 1.0)
            at = s * SLAB + row * CHUNKS
            if s < steps:
                keep[0, at : at + CHUNKS, :] = value
            if s >= 1:
                keep[1, at - SLAB : at - SLAB + CHUNKS, :] = value

    first_row = (lax.broadcasted_iota(jnp.int32, (CHUNKS, 128), 0) // 2) % 2 == 0
    owners = ([], [])
    for d in range(docs):
        a, b = pos[core * 2, d], pos[core * 2 + 1, d]
        owners[0].append(jnp.where(first_row, a // span, b // span))
        owners[1].append(jnp.where(first_row, (a + span - 1) // span - 1, (b + span - 1) // span - 1))

    def mark(j, _):
        for m in range(2):
            hit = owners[m][0] == j
            for o in owners[m][1:]:
                hit = jnp.logical_or(hit, o == j)
            dk[m, j] = jnp.where(hit, 0.0, 1.0)
        return 0

    lax.fori_loop(0, peers, mark, 0)

    count = perm.shape[0]
    p = lax.broadcasted_iota(jnp.int32, (count, count), 0)
    q = lax.broadcasted_iota(jnp.int32, (count, count), 1)
    source = ((p >> 3) & 1) * span + (p & 7) * steps + (p >> 4)
    perm[...] = jnp.where(q == source, 1.0, 0.0).astype(bf16)


def norm_rows(total, squares, count, core, own, oth, base, nrm):
    mean = total / count
    inv = lax.rsqrt(squares / count - mean * mean + norm_eps)
    nrm[0:1, :] = mean
    nrm[1:2, :] = inv
    nrm[2:3, :] = channel_row(core, own, oth, base)
    nrm[3:4, :] = channel_row(core, own, oth, base + 2)
    nrm[4:5, :] = channel_row(core, own, oth, base + 4)
    nrm[5:8, :] = jnp.zeros_like(nrm[5:8, :])


def normalized(x, nrm):
    xhat = (x - nrm[0:1, :]) * nrm[1:2, :]
    return xhat, xhat * nrm[2:3, :] + nrm[3:4, :]


def project_and_scan(steps, base, which, reverse, own, oth, keep, win_own, win_oth, nl, proj, comp, summ, packed):
    proj[:, :256] = mm(nl[...], win_own[...])
    proj[:, 256:] = mm(nl[...], win_oth[...])
    lams, sc = decay(own, oth, base, 6), scales(own, oth, base)

    def drive(s, row, half):
        return sc[half] * proj[part(s, row), cols(half, 0)], sc[half] * proj[part(s, row), cols(half, 1)]

    ends = scan(drive, lams, keep, which, steps, reverse, zeros_start(), nothing)
    chunk_scan(ends, keep_products(keep, which, steps), decay(own, oth, base, 9), reverse, comp, packed)
    spread(summ, packed)


def enter_first_kernel(peers, steps, count, info, got, x_own, x_oth, perm, own, oth, keep, win_own, win_oth,
                       xp, nl, proj, comp, summ, nrm, packed):
    core = info[1]
    sums = got[0:2]
    for j in range(1, peers):
        sums = sums + got[2 * j : 2 * j + 2]
    total = jnp.concatenate([sums[0, 0:1], sums[0, 1:2], sums[1, 0:1], sums[1, 1:2]], axis=1)
    squares = jnp.concatenate([sums[0, 2:3], sums[0, 3:4], sums[1, 2:3], sums[1, 3:4]], axis=1)
    norm_rows(total, squares, count, core, own, oth, 0, nrm)
    xp[:, own_cols(core, 256)] = mm(perm[...], x_own[...]).astype(bf16)
    xp[:, oth_cols(core, 256)] = mm(perm[...], x_oth[...]).astype(bf16)
    _, normed = normalized(xp[...].astype(f32), nrm)
    nl[...] = normed.astype(bf16)
    project_and_scan(steps, 0, 0, False, own, oth, keep, win_own, win_oth, nl, proj, comp, summ, packed)


def sum_peers(got):
    total = got[0]
    for j in range(1, got.shape[0]):
        total = total + got[j]
    return total


def enter_second_kernel(peers, steps, count, info, got, x, own, oth, keep, win_own, win_oth,
                        nl, proj, comp, summ, nrm, packed):
    core = info[1]
    sums = sum_peers(got)
    norm_rows(row_of_tiles(sums[0:4]), row_of_tiles(sums[4:8]), count, core, own, oth, 16, nrm)
    _, normed = normalized(x[...], nrm)
    nl[...] = normed.astype(bf16)
    project_and_scan(steps, 16, 1, True, own, oth, keep, win_own, win_oth, nl, proj, comp, summ, packed)


def states_of(peers, steps, base, which, reverse, info, got, comp, dk, own, oth, keep, proj, hx, sl, packed):
    device_carry(info[0], peers, got, dk, which, own, oth, base, False, reverse, packed)
    start = entries(comp, packed)
    lams, sc = decay(own, oth, base, 6), scales(own, oth, base)
    shift = 0 if reverse else 1
    first = steps if reverse else 0
    for (half, row), (hr, hi) in start.items():
        hx[part(first, row), cols(half, 0)] = hr
        hx[part(first, row), cols(half, 1)] = hi

    def drive(s, row, half):
        return sc[half] * proj[part(s, row), cols(half, 0)], sc[half] * proj[part(s, row), cols(half, 1)]

    def visit(s, state, _):
        for half in range(2):
            for im in range(2):
                both = jnp.concatenate([state[half, row][im] for row in range(2)], axis=0)
                at = (s + shift) * SLAB
                hx[at : at + SLAB, cols(half, im)] = both
                sl[s * SLAB : (s + 1) * SLAB, cols(half, im)] = both.astype(bf16)

    scan(drive, lams, keep, which, steps, reverse, start, visit)


def mix_and_gate(core, x, nrm, sl, wout_own, wout_oth, lin_own, lin_oth, gate_own, gate_oth, gp, act, sig, qv, y):
    _, normed = normalized(x[...].astype(f32), nrm)
    mixed = mm(sl[:, :256], wout_own[...]) + mm(sl[:, 256:], wout_oth[...]) + nrm[4:5, :] * normed
    c = 0.7978845608028654
    sq = mixed * mixed
    t = jnp.tanh(c * (mixed + 0.044715 * sq * mixed))
    act[...] = (0.5 * mixed * (1.0 + t)).astype(bf16)
    gp[...] = 0.5 * (1.0 + t) + 0.5 * mixed * (1.0 - t * t) * (c * (1.0 + 3 * 0.044715 * sq))
    for w_lin, w_gate, at in ((lin_own, gate_own, own_cols(core, 256)), (lin_oth, gate_oth, oth_cols(core, 256))):
        linear = mm(act[...], w_lin[...])
        gating = mm(act[...], w_gate[...])
        sg = 0.5 + 0.5 * jnp.tanh(0.5 * gating)
        out = linear * sg
        sig[:, at] = sg
        qv[:, at] = out * (1.0 - sg)
        y[:, at] = x[:, at].astype(f32) + out


def leave_first_kernel(peers, steps, info, got, comp, dk, own, oth, keep, proj, x, nrm, wout_own, wout_oth,
                       lin_own, lin_oth, gate_own, gate_oth, hx, sl, gp, act, sig, qv, y, stats, packed):
    states_of(peers, steps, 0, 0, False, info, got, comp, dk, own, oth, keep, proj, hx, sl, packed)
    mix_and_gate(info[1], x, nrm, sl, wout_own, wout_oth, lin_own, lin_oth, gate_own, gate_oth, gp, act, sig, qv, y)
    out = y[...]
    pack_two(jnp.sum(out, axis=0, keepdims=True), jnp.sum(out * out, axis=0, keepdims=True), packed)
    spread(stats, packed)


def pack_two(a, b, packed):
    for i in range(4):
        packed[i : i + 1, :] = a[:, 128 * i : 128 * (i + 1)]
        packed[4 + i : 5 + i, :] = b[:, 128 * i : 128 * (i + 1)]


def glu_backward(steps, base, adj_which, adj_reverse, core, d_out, nrm, x, sl, gp, act, sig, qv, own, oth, keep, wout_own, wout_oth,
                 lin_own, lin_oth, gate_own, gate_oth, g_own, g_oth, skip_row, dmix, dst, comp, summ, packed, dl, dg, dml):
    dl[...] = (d_out * sig[...]).astype(bf16)
    dg[...] = (d_out * qv[...]).astype(bf16)
    mine, other = own_cols(core, 256), oth_cols(core, 256)
    d_active = (mm_nt(dl[:, mine], lin_own[...]) + mm_nt(dg[:, mine], gate_own[...])
                + mm_nt(dl[:, other], lin_oth[...]) + mm_nt(dg[:, other], gate_oth[...]))
    d_mixed = d_active * gp[...]
    dmix[...] = d_mixed
    _, normed = normalized(x[...].astype(f32), nrm)
    skip_row[0:1, :] = jnp.sum(d_mixed * normed, axis=0, keepdims=True)
    dml[...] = d_mixed.astype(bf16)
    dst[:, :256] = mm_nt(dml[...], wout_own[...])
    dst[:, 256:] = mm_nt(dml[...], wout_oth[...])
    lams = decay(own, oth, base, 6, conj=True)

    def drive(s, row, half):
        return dst[part(s, row), cols(half, 0)], dst[part(s, row), cols(half, 1)]

    ends = scan(drive, lams, keep, adj_which, steps, adj_reverse, zeros_start(), nothing)
    chunk_scan(ends, keep_products(keep, adj_which, steps), decay(own, oth, base, 9, conj=True), adj_reverse, comp, packed)
    spread(summ, packed)
    g_own[0:512, :] = mm_tn(act[...], dl[:, mine])
    g_oth[0:512, :] = mm_tn(act[...], dl[:, other]).astype(bf16)
    g_own[512:1024, :] = mm_tn(act[...], dg[:, mine])
    g_oth[512:1024, :] = mm_tn(act[...], dg[:, other]).astype(bf16)
    out_grad = mm_tn(sl[...], dml[...])
    for i in range(2):
        g_own[1024 + 256 * i : 1280 + 256 * i, :] = out_grad[:256, 256 * i : 256 * (i + 1)]
        g_oth[1024 + 256 * i : 1280 + 256 * i, :] = out_grad[256:, 256 * i : 256 * (i + 1)].astype(bf16)


def turn_kernel(peers, steps, info, got, comp_in, dk, own, oth, keep, proj, x, nrm, wout_own, wout_oth,
                lin_own, lin_oth, gate_own, gate_oth, perm, cot_own, cot_oth,
                hx, bo_own, bo_oth, d_out, g_own, g_oth, skip_row, dmix, dst, comp, summ,
                packed, sl, gp, act, sig, qv, y, dl, dg, dml):
    core = info[1]
    states_of(peers, steps, 16, 1, True, info, got, comp_in, dk, own, oth, keep, proj, hx, sl, packed)
    mix_and_gate(core, x, nrm, sl, wout_own, wout_oth, lin_own, lin_oth, gate_own, gate_oth, gp, act, sig, qv, y)
    low = y[...].astype(bf16)
    natural = mm_tn(perm[...], low)
    y[...] = natural
    bo_own[...] = y[:, own_cols(core, 256)].astype(bf16)
    bo_oth[...] = y[:, oth_cols(core, 256)].astype(bf16)
    d_out[:, own_cols(core, 256)] = mm(perm[...], cot_own[...])
    d_out[:, oth_cols(core, 256)] = mm(perm[...], cot_oth[...])
    glu_backward(steps, 16, 0, False, core, d_out[...], nrm, x, sl, gp, act, sig, qv, own, oth, keep, wout_own, wout_oth,
                 lin_own, lin_oth, gate_own, gate_oth, g_own, g_oth, skip_row, dmix, dst, comp, summ, packed, dl, dg, dml)


def adjoint_part(peers, steps, base, keep_which, adj_which, adj_reverse, info, got, comp, dk, own, oth, keep, proj, x, nrm, nl,
                 hx, dst, dmix, win_own, win_oth, skip_row, g_own, g_oth, small_own, small_oth, at, packed, dp):
    core = info[1]
    device_carry(info[0], peers, got, dk, adj_which, own, oth, base, True, adj_reverse, packed)
    start = entries(comp, packed)
    lams, sc = decay(own, oth, base, 6, conj=True), scales(own, oth, base)
    zero = jnp.zeros((CHUNKS, 128), f32)
    acc = {half: [zero, zero, zero] for half in range(2)}
    shift = 0 if adj_reverse else 1

    def drive(s, row, half):
        return dst[part(s, row), cols(half, 0)], dst[part(s, row), cols(half, 1)]

    def visit(s, state, _):
        for half in range(2):
            for row in range(2):
                ar, ai = state[half, row]
                pr, pi = hx[part(s + shift, row), cols(half, 0)], hx[part(s + shift, row), cols(half, 1)]
                keep_here = keep[keep_which, part(s, row), :]
                acc[half][0] = acc[half][0] + keep_here * (ar * pr + ai * pi)
                acc[half][1] = acc[half][1] + keep_here * (ai * pr - ar * pi)
                acc[half][2] = acc[half][2] + (ar * proj[part(s, row), cols(half, 0)] + ai * proj[part(s, row), cols(half, 1)])
            for im in range(2):
                both = jnp.concatenate([sc[half] * state[half, row][im] for row in range(2)], axis=0)
                dp[s * SLAB : (s + 1) * SLAB, cols(half, im)] = both.astype(bf16)

    scan(drive, lams, keep, adj_which, steps, adj_reverse, start, visit)

    d_normed = dmix[...] * nrm[4:5, :] + mm_nt(dp[:, :256], win_own[...]) + mm_nt(dp[:, 256:], win_oth[...])
    xhat, _ = normalized(x[...].astype(f32), nrm)
    bias_row = jnp.sum(d_normed, axis=0, keepdims=True)
    gain_row = jnp.sum(d_normed * xhat, axis=0, keepdims=True)
    pack_two(bias_row, gain_row, packed)

    for ref, half, flip in ((small_own, 0, 0), (small_oth, 1, 1)):
        ref[at : at + 16, :] = jnp.zeros((16, 128), f32)
        for j, row in enumerate((skip_row[0:1, :], bias_row, gain_row)):
            low = (core == 0) if flip == 0 else (core == 1)
            pick = jnp.where(low, row[:, :256], row[:, 256:])
            ref[at + 2 * j : at + 2 * j + 1, :] = pick[:, :128]
            ref[at + 2 * j + 1 : at + 2 * j + 2, :] = pick[:, 128:]
        for j in range(3):
            ref[at + 6 + j : at + 7 + j, :] = jnp.sum(acc[half][j], axis=0, keepdims=True)

    g_own[...] = mm_tn(nl[...], dp[:, :256])
    g_oth[...] = mm_tn(nl[...], dp[:, 256:]).astype(bf16)
    return d_normed


def adjoint_second_kernel(peers, steps, info, got, comp, dk, own, oth, keep, proj, x, nrm, nl, hx, dst, dmix, win_own, win_oth, skip_row,
                          g_own, g_oth, small_own, small_oth, dn, stats, packed, dp):
    dn[...] = adjoint_part(peers, steps, 16, 1, 0, False, info, got, comp, dk, own, oth, keep, proj, x, nrm, nl,
                           hx, dst, dmix, win_own, win_oth, skip_row, g_own, g_oth, small_own, small_oth, 0, packed, dp)
    spread(stats, packed)


def back_first_kernel(steps, count, info, got, dn, x2, nrm2, d_out2, own, oth, keep, x, nrm, sl, gp, act, sig, qv,
                      wout_own, wout_oth, lin_own, lin_oth, gate_own, gate_oth,
                      d_out, g_own, g_oth, skip_row, dmix, dst, comp, summ, packed, dl, dg, dml):
    sums = sum_peers(got)
    bias_row, gain_row = row_of_tiles(sums[0:4]), row_of_tiles(sums[4:8])
    xhat, _ = normalized(x2[...], nrm2)
    gain = nrm2[2:3, :]
    d_in = d_out2[...] + nrm2[1:2, :] * (dn[...] * gain - gain * bias_row / count - xhat * (gain * gain_row / count))
    d_out[...] = d_in
    glu_backward(steps, 0, 1, True, info[1], d_in, nrm, x, sl, gp, act, sig, qv, own, oth, keep, wout_own, wout_oth,
                 lin_own, lin_oth, gate_own, gate_oth, g_own, g_oth, skip_row, dmix, dst, comp, summ, packed, dl, dg, dml)


def adjoint_first_kernel(peers, steps, info, got, comp, dk, own, oth, keep, proj, x, nrm, nl, hx, dst, dmix, win_own, win_oth, skip_row,
                         d_out, perm, small1_own, small1_oth,
                         g_own, g_oth, small_own, small_oth, a_own, a_oth, packed, dp, tmp):
    core = info[1]
    d_normed = adjoint_part(peers, steps, 0, 0, 1, True, info, got, comp, dk, own, oth, keep, proj, x, nrm, nl,
                            hx, dst, dmix, win_own, win_oth, skip_row, g_own, g_oth, small_own, small_oth, 0, packed, dp)
    small_own[16:32, :] = small1_own[...]
    small_oth[16:32, :] = small1_oth[...]
    partial = d_out[...] + nrm[1:2, :] * nrm[2:3, :] * d_normed
    tmp[...] = mm_tn(perm[...], partial.astype(bf16))
    a_own[...] = tmp[:, own_cols(core, 256)].astype(bf16)
    a_oth[...] = tmp[:, oth_cols(core, 256)].astype(bf16)


def finish_kernel(count, info, got, a_mine, a_other, tokens, nrm, rate_log, angle_log,
                  d_in, ngg, bias, skip, rate_grad, angle_grad, packed, held):
    core = info[1]
    packed[...] = sum_peers(got)
    for k in range(2):
        at = 16 * k
        for ref, j in ((skip, 0), (bias, 2), (ngg, 4)):
            ref[k : k + 1, :128] = packed[at + j : at + j + 1, :]
            ref[k : k + 1, 128:] = packed[at + j + 1 : at + j + 2, :]
        rate = jnp.exp(rate_log[...].astype(f32)[k : k + 1, :])
        angle = jnp.exp(angle_log[...].astype(f32)[k : k + 1, :])
        modulus = jnp.exp(-rate)
        scale = jnp.sqrt(1.0 - modulus * modulus)
        cos, sin = jnp.cos(angle), jnp.sin(angle)
        dr, di, ds = (packed[at + j : at + j + 1, :] for j in (6, 7, 8))
        g_mod = dr * cos + di * sin - ds * modulus / scale
        rate_grad[k : k + 1, :] = -g_mod * modulus * rate
        angle_grad[k : k + 1, :] = modulus * (di * cos - dr * sin) * angle
    mine = nrm[:, own_cols(core, 256)]
    mean, inv, gain = mine[0:1, :], mine[1:2, :], mine[2:3, :]
    bias_row, gain_row = bias[0:1, :], ngg[0:1, :]
    flat = inv * gain / count
    for r in range(4):
        held_rows = jnp.where(core == r // 2, a_mine[r % 2].astype(f32), a_other[r % 2].astype(f32))
        xhat = (tokens[r].astype(f32) - mean) * inv
        d_in[r] = held_rows - flat * (bias_row + xhat * gain_row)


def swap(value):
    return lax.ppermute(value, "state", [(0, 1), (1, 0)])


def to_all(value):
    axes = ("seq", "state") if value.shape[0] != lax.axis_size("seq") else "seq"
    return lax.all_to_all(value, axes, 0, 0)


def partner(value, mask):
    size = lax.axis_size("seq")
    return lax.ppermute(value, "seq", [(i, i ^ mask) for i in range(size)])


def halves_down(value, masks):
    me = lax.axis_index("seq")
    for m in masks:
        half = value.shape[0] // 2
        bit = (me // m) % 2
        mine = lax.dynamic_slice_in_dim(value, bit * half, half, 0)
        other = lax.dynamic_slice_in_dim(value, (1 - bit) * half, half, 0)
        value = (mine.astype(f32) + partner(other, m).astype(f32)).astype(bf16)
    return value


def halves_up(value, masks):
    me = lax.axis_index("seq")
    for m in reversed(masks):
        bit = (me // m) % 2
        got = partner(value, m)
        value = jnp.concatenate([jnp.where(bit == 0, value, got), jnp.where(bit == 0, got, value)], axis=0)
    return value


def sum_over_seq(value):
    masks = []
    m = 1
    while m < lax.axis_size("seq"):
        masks.append(m)
        m *= 2
    turned = masks[len(masks) // 2 :] + masks[: len(masks) // 2]
    half = value.shape[0] // 2
    parts = [halves_up(halves_down(v, ms), ms) for v, ms in ((value[:half], masks), (value[half:], turned))]
    return jnp.concatenate(parts, axis=0)


def run(kernel, outs, args, scratch=(), n_smem=1):
    return pl.pallas_call(
        kernel,
        out_shape=[jax.ShapeDtypeStruct(s, d) for s, d in outs],
        in_specs=[pl.BlockSpec(memory_space=pltpu.SMEM)] * n_smem + [pl.BlockSpec(memory_space=pltpu.VMEM)] * (len(args) - n_smem),
        out_specs=[pl.BlockSpec(memory_space=pltpu.VMEM)] * len(outs),
        scratch_shapes=[pltpu.VMEM(s, d) for s, d in scratch],
        compiler_params=pltpu.CompilerParams(vmem_limit_bytes=48 * 2**20),
    )(*args)


def body(tokens, gain, bias, in_proj, out_proj, rate_log, angle_log, skip, glu_lin, glu_gate, positions, cotangent):
    peers = lax.axis_size("seq")
    seq, core = lax.axis_index("seq"), lax.axis_index("state")
    rows, span, width = tokens.shape
    steps = span // CHUNKS
    n = 2 * span
    count = float(rows * span * peers)
    info = jnp.stack([seq, core]).astype(jnp.int32)
    packed = ((8, 128), f32)

    def cut(value):
        value = value.reshape(2, 2 * span, width)
        return (lax.dynamic_index_in_dim(value, core, 0, False), swap(lax.dynamic_index_in_dim(value, 1 - core, 0, False)))

    x_own, x_oth = cut(tokens)
    cot_own, cot_oth = cut(cotangent)
    w_in = in_proj.reshape(2, 512, 256)
    w_out = out_proj.reshape(2, 256, 512)
    in_oth, out_oth, lin_oth, gate_oth = (swap(w) for w in (w_in, w_out, glu_lin, glu_gate))

    stats, own, keep, dk, perm = run(
        functools.partial(prep_kernel, peers, steps),
        [((2 * peers, 4, 128), f32), ((32, 128), f32), ((2, n, 128), f32), ((2, peers, 8, 128), f32), ((n, n), bf16)],
        (info, positions, tokens, gain, bias, skip, rate_log, angle_log), n_smem=2)
    oth = swap(own)

    scan_outs = [((n, 512), bf16), ((n, 512), f32), ((16, 8, 128), f32), ((peers, 8, 128), f32), ((8, 512), f32)]
    xp, nl0, proj0, comp, summ, nrm0 = run(
        functools.partial(enter_first_kernel, peers, steps, count), [((n, 512), bf16)] + scan_outs,
        (info, to_all(stats), x_own, x_oth, perm, own, oth, keep, w_in[0], in_oth[0]), [packed])
    hx0, sl0, gp0, act0, sig0, qv0, y0, stats = run(
        functools.partial(leave_first_kernel, peers, steps),
        [((n + SLAB, 512), f32), ((n, 512), bf16), ((n, 512), f32), ((n, 512), bf16), ((n, 512), f32), ((n, 512), f32), ((n, 512), f32),
         ((2 * peers, 8, 128), f32)],
        (info, to_all(summ), comp, dk, own, oth, keep, proj0, xp, nrm0, w_out[0], out_oth[0], glu_lin[0], lin_oth[0], glu_gate[0], gate_oth[0]),
        [packed])
    nl1, proj1, comp, summ, nrm1 = run(
        functools.partial(enter_second_kernel, peers, steps, count), scan_outs,
        (info, to_all(stats), y0, own, oth, keep, w_in[1], in_oth[1]), [packed])
    grad_outs = [((1536, 256), f32), ((1536, 256), bf16), ((8, 512), f32), ((n, 512), f32), ((n, 512), f32), ((16, 8, 128), f32),
                 ((peers, 8, 128), f32)]
    low = ((n, 512), bf16)
    full = ((n, 512), f32)
    hx1, bo_own, bo_oth, d_out1, g1_own, g1_oth, skip1, dmix, dst, comp, summ = run(
        functools.partial(turn_kernel, peers, steps),
        [((n + SLAB, 512), f32), ((n, 256), bf16), ((n, 256), bf16), full] + grad_outs,
        (info, to_all(summ), comp, dk, own, oth, keep, proj1, y0, nrm1, w_out[1], out_oth[1], glu_lin[1], lin_oth[1], glu_gate[1], gate_oth[1],
         perm, cot_own, cot_oth),
        [packed, low, full, low, full, full, full, low, low, low])
    bo_got = swap(bo_oth)
    adj_outs = [((512, 256), f32), ((512, 256), bf16)]
    i1_own, i1_oth, s1_own, s1_oth, dn, stats = run(
        functools.partial(adjoint_second_kernel, peers, steps),
        adj_outs + [((16, 128), f32), ((16, 128), f32), full, ((2 * peers, 8, 128), f32)],
        (info, to_all(summ), comp, dk, own, oth, keep, proj1, y0, nrm1, nl1, hx1, dst, dmix, w_in[1], in_oth[1], skip1),
        [packed, low])
    d_out0, g0_own, g0_oth, skip0, dmix, dst, comp, summ = run(
        functools.partial(back_first_kernel, steps, count),
        [full] + grad_outs,
        (info, to_all(stats), dn, y0, nrm1, d_out1, own, oth, keep, xp, nrm0, sl0, gp0, act0, sig0, qv0,
         w_out[0], out_oth[0], glu_lin[0], lin_oth[0], glu_gate[0], gate_oth[0]),
        [packed, low, low, low])
    i0_own, i0_oth, s_own, s_oth, a_own, a_oth = run(
        functools.partial(adjoint_first_kernel, peers, steps),
        adj_outs + [((32, 128), f32), ((32, 128), f32), ((n, 256), bf16), ((n, 256), bf16)],
        (info, to_all(summ), comp, dk, own, oth, keep, proj0, xp, nrm0, nl0, hx0, dst, dmix, w_in[0], in_oth[0], skip0,
         d_out0, perm, s1_own, s1_oth),
        [packed, low, full])
    a_got = swap(a_oth)
    s_all = s_own + swap(s_oth)
    got = to_all(jnp.broadcast_to(s_all[None], (peers, 32, 128)))
    pair = (2, span, width)
    d_in, ngg, bias_grad, skip_grad, rate_grad, angle_grad = run(
        functools.partial(finish_kernel, count),
        [((rows, span, width), f32), ((2, 256), f32), ((2, 256), f32), ((2, 256), f32), ((2, 128), f32), ((2, 128), f32)],
        (info, got, a_own.reshape(pair), a_got.reshape(pair), tokens, nrm0, rate_log, angle_log),
        [((32, 128), f32), ((8, 256), f32)])

    def weight_sum(g_own, g_oth, i_own, i_oth):
        mine = jnp.concatenate([g_own, i_own], axis=0)
        return sum_over_seq((mine + swap(jnp.concatenate([g_oth, i_oth], axis=0)).astype(f32)).astype(bf16))

    total1 = weight_sum(g1_own, g1_oth, i1_own, i1_oth).astype(f32)
    total0 = weight_sum(g0_own, g0_oth, i0_own, i0_oth).astype(f32)
    both = jnp.stack([total0, total1])
    lin_grad, gate_grad = both[:, :512], both[:, 512:1024]
    out_grad = jnp.concatenate([both[:, 1024:1280], both[:, 1280:1536]], axis=2).reshape(2, 2, 128, 512)
    in_grad = both[:, 1536:].reshape(2, 512, 2, 128)
    mine, other = bo_own.reshape(pair), bo_got.reshape(pair)
    block_out = jnp.concatenate([jnp.where(core == 0, mine, other), jnp.where(core == 0, other, mine)], axis=0)
    return (block_out, d_in, ngg, bias_grad, in_grad, out_grad, rate_grad, angle_grad, skip_grad, lin_grad, gate_grad)


def solution(mesh):
    placed = (
        P(None, "seq", "state"),
        P(None, "state"),
        P(None, "state"),
        P(None, None, None, "state"),
        P(None, None, "state", None),
        P(None, "state"),
        P(None, "state"),
        P(None, "state"),
        P(None, None, "state"),
        P(None, None, "state"),
        P(),
        P(None, "seq", "state"),
    )
    return jax.shard_map(
        body,
        mesh=mesh,
        in_specs=placed,
        out_specs=(
            P(None, "seq", "state"),
            P(None, "seq", "state"),
            P(None, "state"),
            P(None, "state"),
            P(None, None, None, "state"),
            P(None, None, "state", None),
            P(None, "state"),
            P(None, "state"),
            P(None, "state"),
            P(None, None, "state"),
            P(None, None, "state"),
        ),
        check_vma=False,
    )
```

time: 1660 us -> 263 us (0.16); the launches traced: 1640 us -> 262 us
  blocking collectives: 762 us -> 20.2 us
  local copies, waits for them, and re-layouts: 424 us -> 55.6 us
  other arithmetic: 216 us -> 12.9 us
  waiting for transfers between devices: 175 us -> 67.5 us
  starting transfers between devices: 1.64 us -> 67.9 us
  matrix products: 40.4 us -> 0 us
  Pallas kernels: 0 us -> 35.8 us
  between operations: 19.7 us -> 1.83 us
    all_gather x16 -> x0, blocking collectives: 593 us -> none  [carried_in(): everything = jax.tree.map(lambda part: lax.all_gather(part, axis), value)]
    slice x456 -> x5, local copies, waits for them, and re-layouts: 208 us -> 3.84 us  [the longest x1 1.78 us: body(): w_out[1]]
    psum x4 -> x0, blocking collectives: 169 us -> none  [the longest x2 85.5 us: norm_totals(): running_totals = lax.psum((first_sum, second_sum), 'seq')]
    pad x224 -> x0, local copies, waits for them, and re-layouts: 168 us -> none  [local_chain(): lax.associative_scan(compose, (coef_re, coef_im, drive_re, drive_im), rev...]
    psum x1 -> x0, waiting for transfers between devices: 122 us -> none  [block_backward(): lax.psum((partials[0], partials[1], partials[2], partials[3], partials[4]...]
    add x225 -> x1, other arithmetic: 114 us -> 0.01 us  [body(): s_all = s_own + swap(s_oth)]
    concatenate x112 -> x20, other arithmetic: 50.7 us -> 4.59 us  [the longest x2 2.07 us: weight_sum(): jnp.concatenate([g_oth, i_oth], axis=0)]
    ppermute x0 -> x44, waiting for transfers between devices: none -> 41.2 us  [the longest x32 41.2 us: partner(): return lax.ppermute(value, 'seq', [(i, i ^ mask) for i in range(size)])]
  transfers between devices with their start and end apart: 13 -> 50, of which waited for: 8 -> 23; matrix products, arithmetic and copies ran while one was open for 5% -> 9% of each run, Pallas kernels for 0% -> 8%
where the time goes in v1:
time: 263 us; the launch traced here: 262 us
  starting transfers between devices  67.9 us (26%)
  waiting for transfers between devices  67.5 us (26%)
  local copies, waits for them, and re-layouts  55.6 us (21%)
  Pallas kernels  35.8 us (14%)
  blocking collectives  20.2 us (8%)
  other arithmetic  12.9 us (5%)
    ppermute x32, waiting for transfers between devices, partner(): return lax.ppermute(value, 'seq', [(i, i ^ mask) for i in range(size)])  41.2 us
    unnamed x176, local copies, waits for them, and re-layouts  37.5 us
    ppermute x32, starting transfers between devices, partner(): return lax.ppermute(value, 'seq', [(i, i ^ mask) for i in range(size)])  36.8 us
    pallas_call x9, Pallas kernels, run(): pl.pallas_call(kernel, out_shape=[jax.ShapeDtypeStruct(s, d) for s, d in...  35.8 us
    all_to_all x6, starting transfers between devices, to_all(): return lax.all_to_all(value, axes, 0, 0)  28.3 us
    all_to_all x6, waiting for transfers between devices, to_all(): return lax.all_to_all(value, axes, 0, 0)  26.3 us
    all_to_all x2, blocking collectives, to_all(): return lax.all_to_all(value, axes, 0, 0)  20.2 us
  transfers between devices with their start and end apart: 50, of which 23 were waited for; matrix products, arithmetic and copies ran while one was open for 9% of the time, Pallas kernels for 8%

profile of v1, /device:TPU:0, one launch (start us, length us, event | category | flops | bytes accessed | tf_op | source)
XLA Modules:
  0.0 261.7 jit_solution(8735984880401119844)
XLA Ops:
  0.7 1.8 dynamic-slice_bitcast_fusion.2
  8.1 2.3 shard_map.203
  10.5 7.3 %all-to-all-start = ((f32[32,4,128]{2,1,0:T(4,128)}), f32[32,4,128]{2,1,0:T(4,128)S(1)}, u32[]{:S(2)}, u32[]{:S(2)}) async-start(f32[32,4,128]{2,1,0:T(4,128)} %get-tuple-element.72), calls=%async_computation | async-start | bytes 131072 | tf_op jit(solution)/shard_map/all_to_all | solution.py:532
  19.0 2.2 slice_bitcast_fusion.8
  22.2 1.8 fusion.4
  25.2 2.2 shard_map.204
  29.8 6.1 %all-to-all-start.1 = ((f32[16,8,128]{2,1,0:T(8,128)}), f32[16,8,128]{2,1,0:T(8,128)}, u32[]{:S(2)}, u32[]{:S(2)}) async-start(f32[16,8,128]{2,1,0:T(8,128)} %get-tuple-element.76), calls=%async_computation.1 | async-start | bytes 131072 | tf_op jit(solution)/shard_map/all_to_all | solution.py:532
  35.9 1.8 slice_bitcast_fusion
  37.7 1.9 slice_bitcast_fusion.1
  39.6 1.9 slice_bitcast_fusion.2
  41.4 2.1 all-to-all-done.1.got
  46.9 4.9 %shard_map.205 = (f32[528,512]{1,0:T(8,128)}, bf16[512,512]{1,0:T(8,128)(2,1)S(1)}, f32[512,512]{1,0:T(8,128)S(1)}, bf16[512,512]{1,0:T(8,128)(2,1)S(1)}, f32[51...) custom-call(s32[2]{0:T(128)S(1)} %pad_add_fusion.info, ...), custom_call_target="tpu_custom_call" | custom-call | tf_op jit(solution)/shard_map/pallas_call | solution.py:573
  56.8 3.9 %all-to-all-start.2 = ((f32[32,8,128]{2,1,0:T(8,128)}), f32[32,8,128]{2,1,0:T(8,128)}, u32[]{:S(2)}, u32[]{:S(2)}) async-start(f32[32,8,128]{2,1,0:T(8,128)} %copy-done.66), calls=%async_computation.2 | async-start | bytes 262144 | tf_op jit(solution)/shard_map/all_to_all | solution.py:532
  60.7 1.9 dynamic-slice_bitcast_fusion
  63.8 5.1 %all-to-all-done.2.got = f32[32,8,128]{2,1,0:T(8,128)} async-done(((f32[32,8,128]{2,1,0:T(8,128)}), f32[32,8,128]{2,1,0:T(8,128)}, u32[]{:S(2)}, u32[]{:S(2)}) %all-to-all-start.2) | async-done | bytes 131104 | tf_op jit(solution)/shard_map/all_to_all | solution.py:532
  70.3 1.7 shard_map.206
  75.6 3.7 %all-to-all-start.3 = ((f32[16,8,128]{2,1,0:T(8,128)}), f32[16,8,128]{2,1,0:T(8,128)S(1)}, u32[]{:S(2)}, u32[]{:S(2)}) async-start(f32[16,8,128]{2,1,0:T(8,128)} %copy-done.69), calls=%async_computation.3 | async-start | bytes 131072 | tf_op jit(solution)/shard_map/all_to_all | solution.py:532
  79.3 7.3 %all-to-all-done.3.got = f32[16,8,128]{2,1,0:T(8,128)S(1)} async-done(((f32[16,8,128]{2,1,0:T(8,128)}), f32[16,8,128]{2,1,0:T(8,128)S(1)}, u32[]{:S(2)}, u32[]{:S(2)}) %all-to-all-start.3) | async-done | bytes 65568 | tf_op jit(solution)/shard_map/all_to_all | solution.py:532
  97.7 7.9 %shard_map.207 = (f32[528,512]{1,0:T(8,128)}, bf16[512,256]{1,0:T(8,128)(2,1)S(1)}, bf16[512,256]{1,0:T(8,128)(2,1)S(1)}, f32[512,512]{1,0:T(8,128)S(1)}, f32[15...) custom-call(s32[2]{0:T(128)S(1)} %copy-done.72, ...), custom_call_target="tpu_custom_call" | custom-call | tf_op jit(solution)/shard_map/pallas_call | solution.py:573
  107.2 10.1 %all_to_all.40.got = f32[16,8,128]{2,1,0:T(8,128)S(1)} all-to-all(f32[16,8,128]{2,1,0:T(8,128)S(1)} %get-tuple-element.90), channel_id=1, replica_groups=mesh['seq'=16,'state'=2] {'seq'}, dimensions={0} | all-to-all | bytes 131072 | tf_op jit(solution)/shard_map/all_to_all | solution.py:532
  117.4 3.3 %shard_map.208 = (f32[512,256]{1,0:T(8,128)S(1)}, bf16[512,256]{1,0:T(8,128)(2,1)S(1)}, f32[16,128]{1,0:T(8,128)S(1)}, f32[16,128]{1,0:T(8,128)S(1)}, f32[512,512]{1,0:T(8,128)S(1)}, /*index=5*/f32[32,8,128]{2,1,0:T(8,128)S(1)}) custom-call(s32[2]{0:T(128)S(1)} %copy-done.72, f32[16,8,128]{2,1,0:T(8,128)S(1)} %all_to_all.40.got, ...), custom_call_target="tpu_custom_call" | custom-call | tf_op jit(solution)/shard_map/pallas_call | solution.py:573
  121.8 10.0 %all_to_all.41.got = f32[32,8,128]{2,1,0:T(8,128)S(1)} all-to-all(f32[32,8,128]{2,1,0:T(8,128)S(1)} %get-tuple-element.97), channel_id=1, replica_groups=mesh['seq'=16,'state'=2] {'seq','state'}, dimensions={0} | all-to-all | bytes 262144 | tf_op jit(solution)/shard_map/all_to_all | solution.py:532
  132.0 6.9 %shard_map.209 = (f32[512,512]{1,0:T(8,128)S(1)}, f32[1536,256]{1,0:T(8,128)}, bf16[1536,256]{1,0:T(8,128)(2,1)S(1)}, f32[8,512]{1,0:T(8,128)S(1)}, f32[512,512]...) custom-call(s32[2]{0:T(128)S(1)} %copy-done.72, ...), custom_call_target="tpu_custom_call" | custom-call | tf_op jit(solution)/shard_map/pallas_call | solution.py:573
  140.7 3.5 %all-to-all-start.6 = ((f32[16,8,128]{2,1,0:T(8,128)}), f32[16,8,128]{2,1,0:T(8,128)S(1)}, u32[]{:S(2)}, u32[]{:S(2)}) async-start(f32[16,8,128]{2,1,0:T(8,128)} %get-tuple-element.105), calls=%async_computation.6 | async-start | bytes 131072 | tf_op jit(solution)/shard_map/all_to_all | solution.py:532
  144.7 7.0 %all-to-all-done.6.got = f32[16,8,128]{2,1,0:T(8,128)S(1)} async-done(((f32[16,8,128]{2,1,0:T(8,128)}), f32[16,8,128]{2,1,0:T(8,128)S(1)}, u32[]{:S(2)}, u32[]{:S(2)}) %all-to-all-start.6) | async-done | bytes 65568 | tf_op jit(solution)/shard_map/all_to_all | solution.py:532
  152.8 4.6 %shard_map.210 = (f32[512,256]{1,0:T(8,128)S(1)}, bf16[512,256]{1,0:T(8,128)(2,1)S(1)}, f32[32,128]{1,0:T(8,128)S(1)}, f32[32,128]{1,0:T(8,128)S(1)}, bf16[512,2...) custom-call(s32[2]{0:T(128)S(1)} %copy-done.73, f32[16,8,128]{2,1,0:T(8,128)S(1)} %all-to-all-done.6.got, ...), custom_call_target="tpu_custom_call" | custom-call | tf_op jit(solution)/shard_map/pallas_call | solution.py:573
  159.8 3.8 %all-to-all-start.7 = ((f32[16,32,128]{2,1,0:T(8,128)}), f32[16,32,128]{2,1,0:T(8,128)S(1)}, u32[]{:S(2)}, u32[]{:S(2)}) async-start(f32[16,32,128]{2,1,0:T(8,128)} %broadcast_in_dim.2), calls=%async_computation.7 | async-start | bytes 524288 | tf_op jit(solution)/shard_map/all_to_all | solution.py:532
  163.6 1.9 fusion.1
  170.0 4.0 %all-to-all-done.7.got = f32[16,32,128]{2,1,0:T(8,128)S(1)} async-done(((f32[16,32,128]{2,1,0:T(8,128)}), f32[16,32,128]{2,1,0:T(8,128)S(1)}, u32[]{:S(2)}, u32[]{:S(2)}) %all-to-all-start.7) | async-done | bytes 262176 | tf_op jit(solution)/shard_map/all_to_all | solution.py:532
  174.0 2.0 shard_map.211
  179.2 3.9 %collective-permute-done.36 = bf16[512,256]{1,0:T(8,128)(2,1)S(1)} collective-permute-done((bf16[512,256]{1,0:T(8,128)(2,1)S(1)}, bf16[512,256]{1,0:T(8,128)(2,1)S(1)}, u32[]{:S(2)}, u32[]{:S(2)}) %collective-permute-start.36) | collective-permute-done | bytes 262176 | tf_op jit(solution)/shard_map/ppermute | solution.py:537
  192.3 3.9 %collective-permute-done.30 = bf16[128,256]{1,0:T(8,128)(2,1)S(1)} collective-permute-done((bf16[128,256]{1,0:T(8,128)(2,1)S(1)}, bf16[128,256]{1,0:T(8,128)(2,1)S(1)}, u32[]{:S(2)}, u32[]{:S(2)}) %collective-permute-start.30) | collective-permute-done | bytes 65568 | tf_op jit(solution)/shard_map/ppermute | solution.py:537
  198.3 3.1 %collective-permute-done.31 = bf16[64,256]{1,0:T(8,128)(2,1)S(1)} collective-permute-done((bf16[64,256]{1,0:T(8,128)(2,1)S(1)}, bf16[64,256]{1,0:T(8,128)(2,1)S(1)}, u32[]{:S(2)}, u32[]{:S(2)}) %collective-permute-start.31) | collective-permute-done | bytes 32800 | tf_op jit(solution)/shard_map/ppermute | solution.py:537
  203.2 3.4 %collective-permute-done.32 = bf16[64,256]{1,0:T(8,128)(2,1)S(1)} collective-permute-done((bf16[64,256]{1,0:T(8,128)(2,1)S(1)}, bf16[64,256]{1,0:T(8,128)(2,1)S(1)}, u32[]{:S(2)}, u32[]{:S(2)}) %collective-permute-start.32) | collective-permute-done | bytes 32800 | tf_op jit(solution)/shard_map/ppermute | solution.py:537
  208.2 3.4 %collective-permute-done.33 = bf16[128,256]{1,0:T(8,128)(2,1)S(1)} collective-permute-done((bf16[128,256]{1,0:T(8,128)(2,1)S(1)}, bf16[128,256]{1,0:T(8,128)(2,1)S(1)}, u32[]{:S(2)}, u32[]{:S(2)}) %collective-permute-start.33) | collective-permute-done | bytes 65568 | tf_op jit(solution)/shard_map/ppermute | solution.py:537
  212.2 1.9 collective-permute-start.42
  215.1 2.1 collective-permute-start.20
  221.9 2.2 collective-permute-start.21
  224.0 3.0 %collective-permute-done.13 = bf16[128,256]{1,0:T(8,128)(2,1)S(1)} collective-permute-done((bf16[128,256]{1,0:T(8,128)(2,1)S(1)}, bf16[128,256]{1,0:T(8,128)(2,1)S(1)}, u32[]{:S(2)}, u32[]{:S(2)}) %collective-permute-start.13) | collective-permute-done | bytes 65568 | tf_op jit(solution)/shard_map/ppermute | solution.py:537
  227.1 1.9 collective-permute-start.14
  229.8 2.5 collective-permute-done.14
  234.7 2.7 %collective-permute-done.15 = bf16[64,256]{1,0:T(8,128)(2,1)S(1)} collective-permute-done((bf16[64,256]{1,0:T(8,128)(2,1)S(1)}, bf16[64,256]{1,0:T(8,128)(2,1)S(1)}, u32[]{:S(2)}, u32[]{:S(2)}) %collective-permute-start.15) | collective-permute-done | bytes 32800 | tf_op jit(solution)/shard_map/ppermute | solution.py:537
  239.2 2.6 collective-permute-done.16
  243.0 1.8 collective-permute-start.25
  244.9 1.9 collective-permute-done.17
  247.6 2.8 %collective-permute-done.25 = bf16[256,256]{1,0:T(8,128)(2,1)S(1)} collective-permute-done((bf16[256,256]{1,0:T(8,128)(2,1)S(1)}, bf16[256,256]{1,0:T(8,128)(2,1)S(1)}, u32[]{:S(2)}, u32[]{:S(2)}) %collective-permute-start.25) | collective-permute-done | bytes 131104 | tf_op jit(solution)/shard_map/ppermute | solution.py:537
  251.0 2.4 collective-permute-done.18
  253.4 3.4 %collective-permute-done.26 = bf16[512,256]{1,0:T(8,128)(2,1)S(1)} collective-permute-done((bf16[512,256]{1,0:T(8,128)(2,1)S(1)}, bf16[512,256]{1,0:T(8,128)(2,1)S(1)}, u32[]{:S(2)}, u32[]{:S(2)}) %collective-permute-start.26) | collective-permute-done | bytes 262176 | tf_op jit(solution)/shard_map/ppermute | solution.py:537
  (326 shorter events, 86.0 us)
Async XLA Ops:
  2.5 22.7 %collective-permute-start = (bf16[512,256]{1,0:T(8,128)(2,1)}, bf16[512,256]{1,0:T(8,128)(2,1)S(1)}, u32[]{:S(2)}, u32[]{:S(2)}) collective-permute-start(bf16[512,256]{1,0:T(8,128)(2,1)} %get-tuple-element.169), channel_id=1, source_target_pairs={{0,1},{1,0},{2,3},{3,2},{4,5},{5,4},{6,7},{7,6},{8,9},{9,8},{10,11... | collective-permute-start | bytes 786440 | tf_op jit(solution)/shard_map/ppermute | solution.py:527
  10.4 14.0 %collective-permute-start.1 = (f32[32,128]{1,0:T(8,128)S(1)}, f32[32,128]{1,0:T(8,128)S(1)}, u32[]{:S(2)}, u32[]{:S(2)}) collective-permute-start(f32[32,128]{1,0:T(8,128)S(1)} %get-tuple-element.74.own), channel_id=1, source_target_pairs={{0,1},{1,0},{2,3},{3,2},{4,5},{5,4},{6,7},{7,6},{8,9},{9,8},{10,11... | collective-permute-start | bytes 49160 | tf_op jit(solution)/shard_map/ppermute | solution.py:527
  10.5 14.7 %all-to-all-start = ((f32[32,4,128]{2,1,0:T(4,128)}), f32[32,4,128]{2,1,0:T(4,128)S(1)}, u32[]{:S(2)}, u32[]{:S(2)}) async-start(f32[32,4,128]{2,1,0:T(4,128)} %get-tuple-element.72), calls=%async_computation | async-start | bytes 131072 | tf_op jit(solution)/shard_map/all_to_all | solution.py:532
  18.1 5.9 %collective-permute-start.2 = (bf16[2,512,256]{2,1,0:T(8,128)(2,1)S(1)}, bf16[2,512,256]{2,1,0:T(8,128)(2,1)S(1)}, u32[]{:S(2)}, u32[]{:S(2)}) collective-permute-start(bf16[2,512,256]{2,1,0:T(8,128)(2,1)S(1)} %reshape.172), channel_id=1, source_target_pairs={{0,1},{1,0},{2,3},{3,2},{4,5},{5,4},{6,7},{7,6},{8,9},{9,8},{10,11... | collective-permute-start | bytes 1572872 | tf_op jit(solution)/shard_map/ppermute | solution.py:527
  18.5 17.4 %collective-permute-start.5 = (bf16[2,512,256]{2,1,0:T(8,128)(2,1)}, bf16[2,512,256]{2,1,0:T(8,128)(2,1)}, u32[]{:S(2)}, u32[]{:S(2)}) collective-permute-start(bf16[2,512,256]{2,1,0:T(8,128)(2,1)} %param.21), channel_id=1, source_target_pairs={{0,1},{1,0},{2,3},{3,2},{4,5},{5,4},{6,7},{7,6},{8,9},{9,8},{10,11... | collective-permute-start | bytes 1572872 | tf_op jit(solution)/shard_map/ppermute | solution.py:527
  18.7 19.0 %collective-permute-start.4 = (bf16[2,512,256]{2,1,0:T(8,128)(2,1)}, bf16[2,512,256]{2,1,0:T(8,128)(2,1)}, u32[]{:S(2)}, u32[]{:S(2)}) collective-permute-start(bf16[2,512,256]{2,1,0:T(8,128)(2,1)} %param.20), channel_id=1, source_target_pairs={{0,1},{1,0},{2,3},{3,2},{4,5},{5,4},{6,7},{7,6},{8,9},{9,8},{10,11... | collective-permute-start | bytes 1572872 | tf_op jit(solution)/shard_map/ppermute | solution.py:527
  24.0 15.5 %collective-permute-start.3 = (bf16[2,256,512]{2,1,0:T(8,128)(2,1)}, bf16[2,256,512]{2,1,0:T(8,128)(2,1)}, u32[]{:S(2)}, u32[]{:S(2)}) collective-permute-start(bf16[2,256,512]{2,1,0:T(8,128)(2,1)} %bitcast.7), channel_id=1, source_target_pairs={{0,1},{1,0},{2,3},{3,2},{4,5},{5,4},{6,7},{7,6},{8,9},{9,8},{10,11... | collective-permute-start | bytes 1572872 | tf_op jit(solution)/shard_map/ppermute | solution.py:527
  29.8 13.7 %all-to-all-start.1 = ((f32[16,8,128]{2,1,0:T(8,128)}), f32[16,8,128]{2,1,0:T(8,128)}, u32[]{:S(2)}, u32[]{:S(2)}) async-start(f32[16,8,128]{2,1,0:T(8,128)} %get-tuple-element.76), calls=%async_computation.1 | async-start | bytes 131072 | tf_op jit(solution)/shard_map/all_to_all | solution.py:532
  56.8 12.1 %all-to-all-start.2 = ((f32[32,8,128]{2,1,0:T(8,128)}), f32[32,8,128]{2,1,0:T(8,128)}, u32[]{:S(2)}, u32[]{:S(2)}) async-start(f32[32,8,128]{2,1,0:T(8,128)} %copy-done.66), calls=%async_computation.2 | async-start | bytes 262144 | tf_op jit(solution)/shard_map/all_to_all | solution.py:532
  62.6 16.7 %collective-permute-start.6 = (bf16[512,256]{1,0:T(8,128)(2,1)}, bf16[512,256]{1,0:T(8,128)(2,1)}, u32[]{:S(2)}, u32[]{:S(2)}) collective-permute-start(bf16[512,256]{1,0:T(8,128)(2,1)} %get-tuple-element.151), channel_id=1, source_target_pairs={{0,1},{1,0},{2,3},{3,2},{4,5},{5,4},{6,7},{7,6},{8,9},{9,8},{10,11... | collective-permute-start | bytes 786440 | tf_op jit(solution)/shard_map/ppermute | solution.py:527
  75.6 11.0 %all-to-all-start.3 = ((f32[16,8,128]{2,1,0:T(8,128)}), f32[16,8,128]{2,1,0:T(8,128)S(1)}, u32[]{:S(2)}, u32[]{:S(2)}) async-start(f32[16,8,128]{2,1,0:T(8,128)} %copy-done.69), calls=%async_computation.3 | async-start | bytes 131072 | tf_op jit(solution)/shard_map/all_to_all | solution.py:532
  121.8 41.8 %collective-permute-start.27 = (bf16[2048,256]{1,0:T(8,128)(2,1)}, bf16[2048,256]{1,0:T(8,128)(2,1)}, u32[]{:S(2)}, u32[]{:S(2)}) collective-permute-start(bf16[2048,256]{1,0:T(8,128)(2,1)} %pad_maximum_fusion.1), channel_id=1, source_target_pairs={{0,1},{1,0},{2,3},{3,2},{4,5},{5,4},{6,7},{7,6},{8,9},{9,8},{10,11... | collective-permute-start | bytes 3145736 | tf_op jit(solution)/shard_map/ppermute | solution.py:527
  140.7 11.0 %all-to-all-start.6 = ((f32[16,8,128]{2,1,0:T(8,128)}), f32[16,8,128]{2,1,0:T(8,128)S(1)}, u32[]{:S(2)}, u32[]{:S(2)}) async-start(f32[16,8,128]{2,1,0:T(8,128)} %get-tuple-element.105), calls=%async_computation.6 | async-start | bytes 131072 | tf_op jit(solution)/shard_map/all_to_all | solution.py:532
  144.4 23.8 %collective-permute-start.7 = (bf16[512,256]{1,0:T(8,128)(2,1)}, bf16[512,256]{1,0:T(8,128)(2,1)}, u32[]{:S(2)}, u32[]{:S(2)}) collective-permute-start(bf16[512,256]{1,0:T(8,128)(2,1)} %copy-done.82), channel_id=1, source_target_pairs={{0,1},{1,0},{2,3},{3,2},{4,5},{5,4},{6,7},{7,6},{8,9},{9,8},{10,11... | collective-permute-start | bytes 786440 | tf_op jit(solution)/shard_map/ppermute | solution.py:527
  158.5 26.3 %collective-permute-start.10 = (bf16[2048,256]{1,0:T(8,128)(2,1)}, bf16[2048,256]{1,0:T(8,128)(2,1)}, u32[]{:S(2)}, u32[]{:S(2)}) collective-permute-start(bf16[2048,256]{1,0:T(8,128)(2,1)} %pad_maximum_fusion), channel_id=1, source_target_pairs={{0,1},{1,0},{2,3},{3,2},{4,5},{5,4},{6,7},{7,6},{8,9},{9,8},{10,11... | collective-permute-start | bytes 3145736 | tf_op jit(solution)/shard_map/ppermute | solution.py:527
  159.0 11.0 %collective-permute-start.9 = (bf16[512,256]{1,0:T(8,128)(2,1)}, bf16[512,256]{1,0:T(8,128)(2,1)S(1)}, u32[]{:S(2)}, u32[]{:S(2)}) collective-permute-start(bf16[512,256]{1,0:T(8,128)(2,1)} %get-tuple-element.118), channel_id=1, source_target_pairs={{0,1},{1,0},{2,3},{3,2},{4,5},{5,4},{6,7},{7,6},{8,9},{9,8},{10,11... | collective-permute-start | bytes 786440 | tf_op jit(solution)/shard_map/ppermute | solution.py:527
  159.8 14.2 %all-to-all-start.7 = ((f32[16,32,128]{2,1,0:T(8,128)}), f32[16,32,128]{2,1,0:T(8,128)S(1)}, u32[]{:S(2)}, u32[]{:S(2)}) async-start(f32[16,32,128]{2,1,0:T(8,128)} %broadcast_in_dim.2), calls=%async_computation.7 | async-start | bytes 524288 | tf_op jit(solution)/shard_map/all_to_all | solution.py:532
  166.5 10.8 %collective-permute-start.28 = (bf16[512,256]{1,0:T(8,128)(2,1)S(1)}, bf16[512,256]{1,0:T(8,128)(2,1)S(1)}, u32[]{:S(2)}, u32[]{:S(2)}) collective-permute-start(bf16[512,256]{1,0:T(8,128)(2,1)S(1)} %constant_dynamic-slice_fusion.7), channel_id=1, source_target_pairs={{0,2},{2,0},{4,6},{6,4},{8,10},{10,8},{12,14},{14,12},{16,18},{18,... | collective-permute-start | bytes 786440 | tf_op jit(solution)/shard_map/ppermute | solution.py:537
  176.1 7.0 %collective-permute-start.36 = (bf16[512,256]{1,0:T(8,128)(2,1)S(1)}, bf16[512,256]{1,0:T(8,128)(2,1)S(1)}, u32[]{:S(2)}, u32[]{:S(2)}) collective-permute-start(bf16[512,256]{1,0:T(8,128)(2,1)S(1)} %constant_dynamic-slice_fusion.3), channel_id=1, source_target_pairs={{0,8},{2,10},{4,12},{6,14},{8,0},{10,2},{12,4},{14,6},{16,24},{18,... | collective-permute-start | bytes 786440 | tf_op jit(solution)/shard_map/ppermute | solution.py:537
  178.4 10.1 %collective-permute-start.29 = (bf16[256,256]{1,0:T(8,128)(2,1)S(1)}, bf16[256,256]{1,0:T(8,128)(2,1)S(1)}, u32[]{:S(2)}, u32[]{:S(2)}) collective-permute-start(bf16[256,256]{1,0:T(8,128)(2,1)S(1)} %constant_dynamic-slice_fusion.6), channel_id=1, source_target_pairs={{0,4},{2,6},{4,0},{6,2},{8,12},{10,14},{12,8},{14,10},{16,20},{18,... | collective-permute-start | bytes 393224 | tf_op jit(solution)/shard_map/ppermute | solution.py:537
  183.2 7.4 %collective-permute-start.37 = (bf16[256,256]{1,0:T(8,128)(2,1)S(1)}, bf16[256,256]{1,0:T(8,128)(2,1)S(1)}, u32[]{:S(2)}, u32[]{:S(2)}) collective-permute-start(bf16[256,256]{1,0:T(8,128)(2,1)S(1)} %constant_dynamic-slice_fusion.2), channel_id=1, source_target_pairs={{0,16},{2,18},{4,20},{6,22},{8,24},{10,26},{12,28},{14,30},{16,0},... | collective-permute-start | bytes 393224 | tf_op jit(solution)/shard_map/ppermute | solution.py:537
  186.4 27.7 %collective-permute-start.11 = (bf16[512,256]{1,0:T(8,128)(2,1)S(1)}, bf16[512,256]{1,0:T(8,128)(2,1)S(1)}, u32[]{:S(2)}, u32[]{:S(2)}) collective-permute-start(bf16[512,256]{1,0:T(8,128)(2,1)S(1)} %constant_dynamic-slice_fusion.15), channel_id=1, source_target_pairs={{0,2},{2,0},{4,6},{6,4},{8,10},{10,8},{12,14},{14,12},{16,18},{18,... | collective-permute-start | bytes 786440 | tf_op jit(solution)/shard_map/ppermute | solution.py:537
  187.6 27.4 %collective-permute-start.19 = (bf16[512,256]{1,0:T(8,128)(2,1)S(1)}, bf16[512,256]{1,0:T(8,128)(2,1)S(1)}, u32[]{:S(2)}, u32[]{:S(2)}) collective-permute-start(bf16[512,256]{1,0:T(8,128)(2,1)S(1)} %constant_dynamic-slice_fusion.11), channel_id=1, source_target_pairs={{0,8},{2,10},{4,12},{6,14},{8,0},{10,2},{12,4},{14,6},{16,24},{18,... | collective-permute-start | bytes 786440 | tf_op jit(solution)/shard_map/ppermute | solution.py:537
  188.5 7.6 %collective-permute-start.30 = (bf16[128,256]{1,0:T(8,128)(2,1)S(1)}, bf16[128,256]{1,0:T(8,128)(2,1)S(1)}, u32[]{:S(2)}, u32[]{:S(2)}) collective-permute-start(bf16[128,256]{1,0:T(8,128)(2,1)S(1)} %constant_dynamic-slice_fusion.5), channel_id=1, source_target_pairs={{0,8},{2,10},{4,12},{6,14},{8,0},{10,2},{12,4},{14,6},{16,24},{18,... | collective-permute-start | bytes 196616 | tf_op jit(solution)/shard_map/ppermute | solution.py:537
  190.7 6.9 %collective-permute-start.38 = (bf16[128,256]{1,0:T(8,128)(2,1)S(1)}, bf16[128,256]{1,0:T(8,128)(2,1)S(1)}, u32[]{:S(2)}, u32[]{:S(2)}) collective-permute-start(bf16[128,256]{1,0:T(8,128)(2,1)S(1)} %constant_dynamic-slice_fusion.1), channel_id=1, source_target_pairs={{0,2},{2,0},{4,6},{6,4},{8,10},{10,8},{12,14},{14,12},{16,18},{18,... | collective-permute-start | bytes 196616 | tf_op jit(solution)/shard_map/ppermute | solution.py:537
  196.2 5.2 %collective-permute-start.31 = (bf16[64,256]{1,0:T(8,128)(2,1)S(1)}, bf16[64,256]{1,0:T(8,128)(2,1)S(1)}, u32[]{:S(2)}, u32[]{:S(2)}) collective-permute-start(bf16[64,256]{1,0:T(8,128)(2,1)S(1)} %constant_dynamic-slice_fusion.4), channel_id=1, source_target_pairs={{0,16},{2,18},{4,20},{6,22},{8,24},{10,26},{12,28},{14,30},{16,0},... | collective-permute-start | bytes 98312 | tf_op jit(solution)/shard_map/ppermute | solution.py:537
  197.7 4.9 %collective-permute-start.39 = (bf16[64,256]{1,0:T(8,128)(2,1)S(1)}, bf16[64,256]{1,0:T(8,128)(2,1)S(1)}, u32[]{:S(2)}, u32[]{:S(2)}) collective-permute-start(bf16[64,256]{1,0:T(8,128)(2,1)S(1)} %constant_dynamic-slice_fusion), channel_id=1, source_target_pairs={{0,4},{2,6},{4,0},{6,2},{8,12},{10,14},{12,8},{14,10},{16,20},{18,... | collective-permute-start | bytes 98312 | tf_op jit(solution)/shard_map/ppermute | solution.py:537
  201.5 5.1 %collective-permute-start.32 = (bf16[64,256]{1,0:T(8,128)(2,1)S(1)}, bf16[64,256]{1,0:T(8,128)(2,1)S(1)}, u32[]{:S(2)}, u32[]{:S(2)}) collective-permute-start(bf16[64,256]{1,0:T(8,128)(2,1)S(1)} %add_convert_fusion.13), channel_id=1, source_target_pairs={{0,16},{2,18},{4,20},{6,22},{8,24},{10,26},{12,28},{14,30},{16,0},... | collective-permute-start | bytes 98312 | tf_op jit(solution)/shard_map/ppermute | solution.py:537
  202.6 4.6 %collective-permute-start.40 = (bf16[64,256]{1,0:T(8,128)(2,1)S(1)}, bf16[64,256]{1,0:T(8,128)(2,1)S(1)}, u32[]{:S(2)}, u32[]{:S(2)}) collective-permute-start(bf16[64,256]{1,0:T(8,128)(2,1)S(1)} %add_convert_fusion.12), channel_id=1, source_target_pairs={{0,4},{2,6},{4,0},{6,2},{8,12},{10,14},{12,8},{14,10},{16,20},{18,... | collective-permute-start | bytes 98312 | tf_op jit(solution)/shard_map/ppermute | solution.py:537
  206.6 5.0 %collective-permute-start.33 = (bf16[128,256]{1,0:T(8,128)(2,1)S(1)}, bf16[128,256]{1,0:T(8,128)(2,1)S(1)}, u32[]{:S(2)}, u32[]{:S(2)}) collective-permute-start(bf16[128,256]{1,0:T(8,128)(2,1)S(1)} %pad_maximum_fusion.14), channel_id=1, source_target_pairs={{0,8},{2,10},{4,12},{6,14},{8,0},{10,2},{12,4},{14,6},{16,24},{18,... | collective-permute-start | bytes 196616 | tf_op jit(solution)/shard_map/ppermute | solution.py:537
  207.2 5.0 %collective-permute-start.41 = (bf16[128,256]{1,0:T(8,128)(2,1)S(1)}, bf16[128,256]{1,0:T(8,128)(2,1)S(1)}, u32[]{:S(2)}, u32[]{:S(2)}) collective-permute-start(bf16[128,256]{1,0:T(8,128)(2,1)S(1)} %pad_maximum_fusion.15), channel_id=1, source_target_pairs={{0,2},{2,0},{4,6},{6,4},{8,10},{10,8},{12,14},{14,12},{16,18},{18,... | collective-permute-start | bytes 196616 | tf_op jit(solution)/shard_map/ppermute | solution.py:537
  211.7 5.5 %collective-permute-start.34 = (bf16[256,256]{1,0:T(8,128)(2,1)S(1)}, bf16[256,256]{1,0:T(8,128)(2,1)S(1)}, u32[]{:S(2)}, u32[]{:S(2)}) collective-permute-start(bf16[256,256]{1,0:T(8,128)(2,1)S(1)} %pad_maximum_fusion.10), channel_id=1, source_target_pairs={{0,4},{2,6},{4,0},{6,2},{8,12},{10,14},{12,8},{14,10},{16,20},{18,... | collective-permute-start | bytes 393224 | tf_op jit(solution)/shard_map/ppermute | solution.py:537
  212.2 7.3 %collective-permute-start.42 = (bf16[256,256]{1,0:T(8,128)(2,1)S(1)}, bf16[256,256]{1,0:T(8,128)(2,1)S(1)}, u32[]{:S(2)}, u32[]{:S(2)}) collective-permute-start(bf16[256,256]{1,0:T(8,128)(2,1)S(1)} %pad_maximum_fusion.11), channel_id=1, source_target_pairs={{0,16},{2,18},{4,20},{6,22},{8,24},{10,26},{12,28},{14,30},{16,0},... | collective-permute-start | bytes 393224 | tf_op jit(solution)/shard_map/ppermute | solution.py:537
  214.2 6.0 %collective-permute-start.12 = (bf16[256,256]{1,0:T(8,128)(2,1)S(1)}, bf16[256,256]{1,0:T(8,128)(2,1)S(1)}, u32[]{:S(2)}, u32[]{:S(2)}) collective-permute-start(bf16[256,256]{1,0:T(8,128)(2,1)S(1)} %constant_dynamic-slice_fusion.14), channel_id=1, source_target_pairs={{0,4},{2,6},{4,0},{6,2},{8,12},{10,14},{12,8},{14,10},{16,20},{18,... | collective-permute-start | bytes 393224 | tf_op jit(solution)/shard_map/ppermute | solution.py:537
  215.1 6.7 %collective-permute-start.20 = (bf16[256,256]{1,0:T(8,128)(2,1)S(1)}, bf16[256,256]{1,0:T(8,128)(2,1)S(1)}, u32[]{:S(2)}, u32[]{:S(2)}) collective-permute-start(bf16[256,256]{1,0:T(8,128)(2,1)S(1)} %constant_dynamic-slice_fusion.10), channel_id=1, source_target_pairs={{0,16},{2,18},{4,20},{6,22},{8,24},{10,26},{12,28},{14,30},{16,0},... | collective-permute-start | bytes 393224 | tf_op jit(solution)/shard_map/ppermute | solution.py:537
  217.2 27.5 %collective-permute-start.35 = (bf16[512,256]{1,0:T(8,128)(2,1)S(1)}, bf16[512,256]{1,0:T(8,128)(2,1)S(1)}, u32[]{:S(2)}, u32[]{:S(2)}) collective-permute-start(bf16[512,256]{1,0:T(8,128)(2,1)S(1)} %pad_maximum_fusion.6), channel_id=1, source_target_pairs={{0,2},{2,0},{4,6},{6,4},{8,10},{10,8},{12,14},{14,12},{16,18},{18,... | collective-permute-start | bytes 786440 | tf_op jit(solution)/shard_map/ppermute | solution.py:537
  219.6 31.3 %collective-permute-start.43 = (bf16[512,256]{1,0:T(8,128)(2,1)S(1)}, bf16[512,256]{1,0:T(8,128)(2,1)S(1)}, u32[]{:S(2)}, u32[]{:S(2)}) collective-permute-start(bf16[512,256]{1,0:T(8,128)(2,1)S(1)} %pad_maximum_fusion.7), channel_id=1, source_target_pairs={{0,8},{2,10},{4,12},{6,14},{8,0},{10,2},{12,4},{14,6},{16,24},{18,... | collective-permute-start | bytes 786440 | tf_op jit(solution)/shard_map/ppermute | solution.py:537
  220.3 6.7 %collective-permute-start.13 = (bf16[128,256]{1,0:T(8,128)(2,1)S(1)}, bf16[128,256]{1,0:T(8,128)(2,1)S(1)}, u32[]{:S(2)}, u32[]{:S(2)}) collective-permute-start(bf16[128,256]{1,0:T(8,128)(2,1)S(1)} %constant_dynamic-slice_fusion.13), channel_id=1, source_target_pairs={{0,8},{2,10},{4,12},{6,14},{8,0},{10,2},{12,4},{14,6},{16,24},{18,... | collective-permute-start | bytes 196616 | tf_op jit(solution)/shard_map/ppermute | solution.py:537
  221.9 7.1 %collective-permute-start.21 = (bf16[128,256]{1,0:T(8,128)(2,1)S(1)}, bf16[128,256]{1,0:T(8,128)(2,1)S(1)}, u32[]{:S(2)}, u32[]{:S(2)}) collective-permute-start(bf16[128,256]{1,0:T(8,128)(2,1)S(1)} %constant_dynamic-slice_fusion.9), channel_id=1, source_target_pairs={{0,2},{2,0},{4,6},{6,4},{8,10},{10,8},{12,14},{14,12},{16,18},{18,... | collective-permute-start | bytes 196616 | tf_op jit(solution)/shard_map/ppermute | solution.py:537
  227.1 5.2 %collective-permute-start.14 = (bf16[64,256]{1,0:T(8,128)(2,1)S(1)}, bf16[64,256]{1,0:T(8,128)(2,1)S(1)}, u32[]{:S(2)}, u32[]{:S(2)}) collective-permute-start(bf16[64,256]{1,0:T(8,128)(2,1)S(1)} %constant_dynamic-slice_fusion.12), channel_id=1, source_target_pairs={{0,16},{2,18},{4,20},{6,22},{8,24},{10,26},{12,28},{14,30},{16,0},... | collective-permute-start | bytes 98312 | tf_op jit(solution)/shard_map/ppermute | solution.py:537
  229.1 4.9 %collective-permute-start.22 = (bf16[64,256]{1,0:T(8,128)(2,1)S(1)}, bf16[64,256]{1,0:T(8,128)(2,1)S(1)}, u32[]{:S(2)}, u32[]{:S(2)}) collective-permute-start(bf16[64,256]{1,0:T(8,128)(2,1)S(1)} %constant_dynamic-slice_fusion.8), channel_id=1, source_target_pairs={{0,4},{2,6},{4,0},{6,2},{8,12},{10,14},{12,8},{14,10},{16,20},{18,... | collective-permute-start | bytes 98312 | tf_op jit(solution)/shard_map/ppermute | solution.py:537
  232.4 5.0 %collective-permute-start.15 = (bf16[64,256]{1,0:T(8,128)(2,1)S(1)}, bf16[64,256]{1,0:T(8,128)(2,1)S(1)}, u32[]{:S(2)}, u32[]{:S(2)}) collective-permute-start(bf16[64,256]{1,0:T(8,128)(2,1)S(1)} %add_convert_fusion.15), channel_id=1, source_target_pairs={{0,16},{2,18},{4,20},{6,22},{8,24},{10,26},{12,28},{14,30},{16,0},... | collective-permute-start | bytes 98312 | tf_op jit(solution)/shard_map/ppermute | solution.py:537
  237.4 4.3 %collective-permute-start.16 = (bf16[128,256]{1,0:T(8,128)(2,1)S(1)}, bf16[128,256]{1,0:T(8,128)(2,1)S(1)}, u32[]{:S(2)}, u32[]{:S(2)}) collective-permute-start(bf16[128,256]{1,0:T(8,128)(2,1)S(1)} %pad_maximum_fusion.12), channel_id=1, source_target_pairs={{0,8},{2,10},{4,12},{6,14},{8,0},{10,2},{12,4},{14,6},{16,24},{18,... | collective-permute-start | bytes 196616 | tf_op jit(solution)/shard_map/ppermute | solution.py:537
  237.9 5.0 %collective-permute-start.24 = (bf16[128,256]{1,0:T(8,128)(2,1)S(1)}, bf16[128,256]{1,0:T(8,128)(2,1)S(1)}, u32[]{:S(2)}, u32[]{:S(2)}) collective-permute-start(bf16[128,256]{1,0:T(8,128)(2,1)S(1)} %pad_maximum_fusion.13), channel_id=1, source_target_pairs={{0,2},{2,0},{4,6},{6,4},{8,10},{10,8},{12,14},{14,12},{16,18},{18,... | collective-permute-start | bytes 196616 | tf_op jit(solution)/shard_map/ppermute | solution.py:537
  241.8 5.0 %collective-permute-start.17 = (bf16[256,256]{1,0:T(8,128)(2,1)S(1)}, bf16[256,256]{1,0:T(8,128)(2,1)S(1)}, u32[]{:S(2)}, u32[]{:S(2)}) collective-permute-start(bf16[256,256]{1,0:T(8,128)(2,1)S(1)} %pad_maximum_fusion.8), channel_id=1, source_target_pairs={{0,4},{2,6},{4,0},{6,2},{8,12},{10,14},{12,8},{14,10},{16,20},{18,... | collective-permute-start | bytes 393224 | tf_op jit(solution)/shard_map/ppermute | solution.py:537
  243.0 7.3 %collective-permute-start.25 = (bf16[256,256]{1,0:T(8,128)(2,1)S(1)}, bf16[256,256]{1,0:T(8,128)(2,1)S(1)}, u32[]{:S(2)}, u32[]{:S(2)}) collective-permute-start(bf16[256,256]{1,0:T(8,128)(2,1)S(1)} %pad_maximum_fusion.9), channel_id=1, source_target_pairs={{0,16},{2,18},{4,20},{6,22},{8,24},{10,26},{12,28},{14,30},{16,0},... | collective-permute-start | bytes 393224 | tf_op jit(solution)/shard_map/ppermute | solution.py:537
  246.9 6.4 %collective-permute-start.18 = (bf16[512,256]{1,0:T(8,128)(2,1)S(1)}, bf16[512,256]{1,0:T(8,128)(2,1)S(1)}, u32[]{:S(2)}, u32[]{:S(2)}) collective-permute-start(bf16[512,256]{1,0:T(8,128)(2,1)S(1)} %pad_maximum_fusion.4), channel_id=1, source_target_pairs={{0,2},{2,0},{4,6},{6,4},{8,10},{10,8},{12,14},{14,12},{16,18},{18,... | collective-permute-start | bytes 786440 | tf_op jit(solution)/shard_map/ppermute | solution.py:537
  250.4 6.4 %collective-permute-start.26 = (bf16[512,256]{1,0:T(8,128)(2,1)S(1)}, bf16[512,256]{1,0:T(8,128)(2,1)S(1)}, u32[]{:S(2)}, u32[]{:S(2)}) collective-permute-start(bf16[512,256]{1,0:T(8,128)(2,1)S(1)} %pad_maximum_fusion.5), channel_id=1, source_target_pairs={{0,8},{2,10},{4,12},{6,14},{8,0},{10,2},{12,4},{14,6},{16,24},{18,... | collective-permute-start | bytes 786440 | tf_op jit(solution)/shard_map/ppermute | solution.py:537
  (89 other events, 558.3 us)

commit v2 on v1

v2 whole, which is shorter than its diff:
```python
import functools

import jax
import jax.numpy as jnp
from jax import lax
from jax.experimental import pallas as pl
from jax.experimental.pallas import tpu as pltpu
from jax.sharding import PartitionSpec as P

f32, bf16 = jnp.float32, jnp.bfloat16
norm_eps = 1e-05
CHUNKS = 8
SLAB = 2 * CHUNKS


def mm(a, b):
    return jnp.dot(a, b, preferred_element_type=f32)


def mm_nt(a, b):
    return lax.dot_general(a, b, (((1,), (1,)), ((), ())), preferred_element_type=f32)


def mm_tn(a, b):
    return lax.dot_general(a, b, (((0,), (0,)), ((), ())), preferred_element_type=f32)


def wide(row):
    return jnp.broadcast_to(row, (CHUNKS, 128))


def cmul(ar, ai, br, bi):
    return ar * br - ai * bi, ar * bi + ai * br


def row_of_tiles(tiles):
    return jnp.concatenate([tiles[i : i + 1, :] for i in range(tiles.shape[0])], axis=1)


def channel_row(core, own, oth, at):
    mine, other = own[at : at + 2, :], oth[at : at + 2, :]
    low = jnp.where(core == 0, mine, other)
    high = jnp.where(core == 0, other, mine)
    return jnp.concatenate([low[0:1], low[1:2], high[0:1], high[1:2]], axis=1)


def own_cols(core, width):
    return pl.ds(pl.multiple_of(core * width, width), width)


def oth_cols(core, width):
    return pl.ds(pl.multiple_of((1 - core) * width, width), width)


def scan(drive, lams, keep_ref, which, steps, reverse, start, visit):
    order = range(steps - 1, -1, -1) if reverse else range(steps)
    state = dict(start)
    for s in order:
        for row in range(2):
            at = s * SLAB + row * CHUNKS
            keep = keep_ref[which, at : at + CHUNKS, :]
            for half in range(2):
                lr, li = lams[half]
                hr, hi = state[half, row]
                hr, hi = keep * hr, keep * hi
                dr, di = drive(s, row, half)
                state[half, row] = (lr * hr - li * hi + dr, lr * hi + li * hr + di)
        visit(s, state, keep_ref)
    return state


def keep_products(keep_ref, which, steps):
    out = []
    for row in range(2):
        total = keep_ref[which, row * CHUNKS : (row + 1) * CHUNKS, :]
        for s in range(1, steps):
            at = s * SLAB + row * CHUNKS
            total = total * keep_ref[which, at : at + CHUNKS, :]
        out.append(total)
    return out


def chunk_scan(ends, keeps, powers, reverse, comp_ref, packed):
    index = lax.broadcasted_iota(jnp.int32, (CHUNKS, 128), 0)

    def shifted(value, by, fill):
        turned = pltpu.roll(value, CHUNKS - by if reverse else by, 0)
        valid = index < CHUNKS - by if reverse else index >= by
        return jnp.where(valid, turned, fill)

    for half in range(2):
        for row in range(2):
            er, ei = ends[half, row]
            pr, pi = powers[half][0] * keeps[row], powers[half][1] * keeps[row]
            for by in (1, 2, 4):
                tr, ti = cmul(pr, pi, shifted(er, by, 0.0), shifted(ei, by, 0.0))
                er, ei = er + tr, ei + ti
                pr, pi = cmul(pr, pi, shifted(pr, by, 1.0), shifted(pi, by, 0.0))
            edge = 0 if reverse else CHUNKS - 1
            q = row * 2 + half
            packed[q : q + 1, :] = er[edge : edge + 1, :]
            packed[4 + q : 5 + q, :] = ei[edge : edge + 1, :]
            base = (half * 2 + row) * 4
            comp_ref[base] = shifted(er, 1, 0.0)
            comp_ref[base + 1] = shifted(ei, 1, 0.0)
            comp_ref[base + 2] = shifted(pr, 1, 1.0)
            comp_ref[base + 3] = shifted(pi, 1, 0.0)


def device_carry(me, peers, got, held, dk_ref, which, own, oth, base, conj, reverse, packed):
    got_ref = arrange(got, held)
    index = lax.broadcasted_iota(jnp.int32, (CHUNKS, 128), 0)
    is_own = index % 2 == 0
    sign = jnp.where(index < 4, -1.0, 1.0) * (-1.0 if conj else 1.0)
    ar = jnp.where(is_own, wide(own[base + 11 : base + 12, :]), wide(oth[base + 11 : base + 12, :]))
    ai = jnp.where(is_own, wide(own[base + 12 : base + 13, :]), wide(oth[base + 12 : base + 13, :]))
    ai = ai * sign

    def step(k, held):
        at = peers - 1 - k if reverse else k
        reached = at > me if reverse else at < me
        new = dk_ref[which, at] * (ar * held + ai * pltpu.roll(held, 4, 0)) + got_ref[at]
        return jnp.where(reached, new, held)

    packed[...] = lax.fori_loop(0, peers, step, jnp.zeros((8, 128), f32), unroll=peers <= 16)


def entries(comp_ref, packed):
    start = {}
    for half in range(2):
        for row in range(2):
            base, q = (half * 2 + row) * 4, row * 2 + half
            hr, hi = wide(packed[q : q + 1, :]), wide(packed[4 + q : 5 + q, :])
            tr, ti = cmul(comp_ref[base + 2], comp_ref[base + 3], hr, hi)
            start[half, row] = (comp_ref[base] + tr, comp_ref[base + 1] + ti)
    return start


def decay(own, oth, base, at, conj=False):
    sign = -1.0 if conj else 1.0
    return [(wide(r[base + at : base + at + 1, :]), sign * wide(r[base + at + 1 : base + at + 2, :])) for r in (own, oth)]


def scales(own, oth, base):
    return [wide(r[base + 8 : base + 9, :]) for r in (own, oth)]


def nothing(*_):
    return None


def zeros_start():
    zero = jnp.zeros((CHUNKS, 128), f32)
    return {(half, row): (zero, zero) for half in range(2) for row in range(2)}


def part(s, row):
    at = s * SLAB + row * CHUNKS
    return slice(at, at + CHUNKS)


def cols(half, im):
    at = half * 256 + im * 128
    return slice(at, at + 128)


def flat_rows(ref):
    value = ref[...]
    return value.reshape(value.shape[0] * value.shape[1], value.shape[2])


def spread(out_ref, packed):
    value = packed[...]
    out_ref[...] = value if len(out_ref.shape) == 2 else jnp.broadcast_to(value[None], out_ref.shape)


def arrange(got, held):
    if len(got) == 1:
        return got[0]
    me = place()[0]
    for m, block in enumerate(got):
        for e in range(4):
            held[(((me >> 2) ^ m) << 2) + ((me & 3) ^ e)] = block[e]
    return held


def place():
    return lax.axis_index("seq"), lax.axis_index("state")


def prep_kernel(peers, steps, pos, tokens, gain, bias, skip, rate_log, angle_log, stats, small, keep, dk, perm):
    seq, core = place()
    rows, span, _ = tokens.shape
    docs = pos.shape[1]

    count = perm.shape[0]
    p = lax.broadcasted_iota(jnp.int32, (count, count), 0)
    q = lax.broadcasted_iota(jnp.int32, (count, count), 1)
    source = ((p >> 3) & 1) * span + (p & 7) * steps + (p >> 4)
    perm[...] = jnp.where(q == source, 1.0, 0.0).astype(bf16)
    s1 = s2 = 0.0
    for r in range(rows):
        x = tokens[r].astype(f32)
        s1 = s1 + jnp.sum(x, axis=0, keepdims=True)
        s2 = s2 + jnp.sum(x * x, axis=0, keepdims=True)
    for i in range(2):
        stats[0, i : i + 1, :] = s1[:, 128 * i : 128 * (i + 1)]
        stats[0, 2 + i : 3 + i, :] = s2[:, 128 * i : 128 * (i + 1)]
    stats[...] = jnp.broadcast_to(stats[0][None], stats.shape)

    small[...] = jnp.zeros_like(small)
    for k in range(2):
        at = 16 * k
        for j, ref in enumerate((gain, bias, skip)):
            v = ref[...].astype(f32)
            small[at + 2 * j : at + 2 * j + 1, :] = v[k : k + 1, :128]
            small[at + 2 * j + 1 : at + 2 * j + 2, :] = v[k : k + 1, 128:]
        rate = jnp.exp(rate_log[...].astype(f32)[k : k + 1, :])
        angle = jnp.exp(angle_log[...].astype(f32)[k : k + 1, :])
        modulus = jnp.exp(-rate)
        lr, li = modulus * jnp.cos(angle), modulus * jnp.sin(angle)
        small[at + 6 : at + 7, :] = lr
        small[at + 7 : at + 8, :] = li
        small[at + 8 : at + 9, :] = jnp.sqrt(1.0 - modulus * modulus)
        power = 1
        while power < span:
            lr, li = cmul(lr, li, lr, li)
            power *= 2
            if power == steps:
                small[at + 9 : at + 10, :] = lr
                small[at + 10 : at + 11, :] = li
        small[at + 11 : at + 12, :] = lr
        small[at + 12 : at + 13, :] = li

    chunk = lax.broadcasted_iota(jnp.int32, (CHUNKS, 128), 0) * steps + seq * span
    for row in range(2):
        targets = [pos[core * 2 + row, d] - chunk for d in range(docs)]
        for s in range(steps + 1):
            hit = targets[0] == s
            for t in targets[1:]:
                hit = jnp.logical_or(hit, t == s)
            value = jnp.where(hit, 0.0, 1.0)
            at = s * SLAB + row * CHUNKS
            if s < steps:
                keep[0, at : at + CHUNKS, :] = value
            if s >= 1:
                keep[1, at - SLAB : at - SLAB + CHUNKS, :] = value

    first_row = (lax.broadcasted_iota(jnp.int32, (CHUNKS, 128), 0) // 2) % 2 == 0
    owners = ([], [])
    for d in range(docs):
        a, b = pos[core * 2, d], pos[core * 2 + 1, d]
        owners[0].append(jnp.where(first_row, a // span, b // span))
        owners[1].append(jnp.where(first_row, (a + span - 1) // span - 1, (b + span - 1) // span - 1))

    def mark(j, _):
        for m in range(2):
            hit = owners[m][0] == j
            for o in owners[m][1:]:
                hit = jnp.logical_or(hit, o == j)
            dk[m, j] = jnp.where(hit, 0.0, 1.0)
        return 0

    lax.fori_loop(0, peers, mark, 0)


def norm_rows(total, squares, count, core, own, oth, base, nrm):
    mean = total / count
    inv = lax.rsqrt(squares / count - mean * mean + norm_eps)
    nrm[0:1, :] = mean
    nrm[1:2, :] = inv
    nrm[2:3, :] = channel_row(core, own, oth, base)
    nrm[3:4, :] = channel_row(core, own, oth, base + 2)
    nrm[4:5, :] = channel_row(core, own, oth, base + 4)
    nrm[5:8, :] = jnp.zeros_like(nrm[5:8, :])


def normalized(x, nrm):
    xhat = (x - nrm[0:1, :]) * nrm[1:2, :]
    return xhat, xhat * nrm[2:3, :] + nrm[3:4, :]


def project_and_scan(steps, base, which, reverse, own, oth, keep, win_own, win_oth, nl, proj, comp, summ, packed):
    proj[:, :256] = mm(nl[...], win_own[...])
    proj[:, 256:] = mm(nl[...], win_oth[...])
    lams, sc = decay(own, oth, base, 6), scales(own, oth, base)

    def drive(s, row, half):
        return sc[half] * proj[part(s, row), cols(half, 0)], sc[half] * proj[part(s, row), cols(half, 1)]

    ends = scan(drive, lams, keep, which, steps, reverse, zeros_start(), nothing)
    chunk_scan(ends, keep_products(keep, which, steps), decay(own, oth, base, 9), reverse, comp, packed)
    spread(summ, packed)


def enter_first_kernel(peers, steps, count, got, x_own, x_oth, perm, own, oth, keep, win_own, win_oth,
                       xp, nl, proj, comp, summ, nrm, packed):
    _, core = place()
    sums = got[0:2]
    for j in range(1, peers):
        sums = sums + got[2 * j : 2 * j + 2]
    total = jnp.concatenate([sums[0, 0:1], sums[0, 1:2], sums[1, 0:1], sums[1, 1:2]], axis=1)
    squares = jnp.concatenate([sums[0, 2:3], sums[0, 3:4], sums[1, 2:3], sums[1, 3:4]], axis=1)
    norm_rows(total, squares, count, core, own, oth, 0, nrm)
    xp[:, own_cols(core, 256)] = mm(perm[...], flat_rows(x_own)).astype(bf16)
    xp[:, oth_cols(core, 256)] = mm(perm[...], flat_rows(x_oth)).astype(bf16)
    _, normed = normalized(xp[...].astype(f32), nrm)
    xp.send()
    nl[...] = normed.astype(bf16)
    nl.send()
    project_and_scan(steps, 0, 0, False, own, oth, keep, win_own, win_oth, nl, proj, comp, summ, packed)


def sum_peers(got):
    if len(got) == 1 and len(got[0].shape) == 3:
        got = [got[0].at[j] for j in range(got[0].shape[0])]
    total = got[0][...]
    for part in got[1:]:
        total = total + part[...]
    return total


def enter_second_kernel(peers, steps, count, got, x, own, oth, keep, win_own, win_oth,
                        nl, proj, comp, summ, nrm, packed):
    _, core = place()
    sums = sum_peers(got)
    norm_rows(row_of_tiles(sums[0:4]), row_of_tiles(sums[4:8]), count, core, own, oth, 16, nrm)
    _, normed = normalized(x[...], nrm)
    nl[...] = normed.astype(bf16)
    project_and_scan(steps, 16, 1, True, own, oth, keep, win_own, win_oth, nl, proj, comp, summ, packed)


def states_of(peers, steps, base, which, reverse, got, comp, dk, own, oth, keep, proj, cin, sl, packed, held):
    device_carry(place()[0], peers, got, held, dk, which, own, oth, base, False, reverse, packed)
    start = entries(comp, packed)
    lams, sc = decay(own, oth, base, 6), scales(own, oth, base)
    for (half, row), (hr, hi) in start.items():
        cin[part(0, row), cols(half, 0)] = hr
        cin[part(0, row), cols(half, 1)] = hi

    def drive(s, row, half):
        return sc[half] * proj[part(s, row), cols(half, 0)], sc[half] * proj[part(s, row), cols(half, 1)]

    def visit(s, state, _):
        for half in range(2):
            for im in range(2):
                both = jnp.concatenate([state[half, row][im] for row in range(2)], axis=0)
                sl[s * SLAB : (s + 1) * SLAB, cols(half, im)] = both.astype(bf16)

    scan(drive, lams, keep, which, steps, reverse, start, visit)
    send(sl)


def send(ref):
    if isinstance(ref, Drained):
        ref.send()


def mix_and_gate(core, x, nrm, sl, wout_own, wout_oth, lin_own, lin_oth, gate_own, gate_oth, gp, act, sig, qv, y):
    _, normed = normalized(x[...].astype(f32), nrm)
    mixed = mm(sl[:, :256], wout_own[...]) + mm(sl[:, 256:], wout_oth[...]) + nrm[4:5, :] * normed
    c = 0.7978845608028654
    sq = mixed * mixed
    t = jnp.tanh(c * (mixed + 0.044715 * sq * mixed))
    act[...] = (0.5 * mixed * (1.0 + t)).astype(bf16)
    send(act)
    gp[...] = (0.5 * (1.0 + t) + 0.5 * mixed * (1.0 - t * t) * (c * (1.0 + 3 * 0.044715 * sq))).astype(gp.dtype)
    send(gp)
    for w_lin, w_gate, at in ((lin_own, gate_own, own_cols(core, 256)), (lin_oth, gate_oth, oth_cols(core, 256))):
        linear = mm(act[...], w_lin[...])
        gating = mm(act[...], w_gate[...])
        sg = 0.5 + 0.5 * jnp.tanh(0.5 * gating)
        out = linear * sg
        sig[:, at] = sg.astype(sig.dtype)
        qv[:, at] = (out * (1.0 - sg)).astype(qv.dtype)
        y[:, at] = x[:, at].astype(f32) + out
    send(sig)
    send(qv)


def leave_first_kernel(peers, steps, got, comp, dk, own, oth, keep, proj, x, nrm, wout_own, wout_oth,
                       lin_own, lin_oth, gate_own, gate_oth, cin, sl, gp, act, sig, qv, y, stats, packed, held):
    states_of(peers, steps, 0, 0, False, got, comp, dk, own, oth, keep, proj, cin, sl, packed, held)
    mix_and_gate(place()[1], x, nrm, sl, wout_own, wout_oth, lin_own, lin_oth, gate_own, gate_oth, gp, act, sig, qv, y)
    out = y[...]
    pack_two(jnp.sum(out, axis=0, keepdims=True), jnp.sum(out * out, axis=0, keepdims=True), packed)
    spread(stats, packed)


def pack_two(a, b, packed):
    for i in range(4):
        packed[i : i + 1, :] = a[:, 128 * i : 128 * (i + 1)]
        packed[4 + i : 5 + i, :] = b[:, 128 * i : 128 * (i + 1)]


def glu_backward(steps, base, adj_which, adj_reverse, core, d_out, nrm, x, gp, sig, qv, own, oth, keep, wout_own, wout_oth,
                 lin_own, lin_oth, gate_own, gate_oth, skip_row, dst, comp, summ, packed, dl, dg, dml):
    dl[...] = (d_out * sig[...].astype(f32)).astype(bf16)
    dg[...] = (d_out * qv[...].astype(f32)).astype(bf16)
    mine, other = own_cols(core, 256), oth_cols(core, 256)
    d_active = (mm_nt(dl[:, mine], lin_own[...]) + mm_nt(dg[:, mine], gate_own[...])
                + mm_nt(dl[:, other], lin_oth[...]) + mm_nt(dg[:, other], gate_oth[...]))
    d_mixed = d_active * gp[...].astype(f32)
    _, normed = normalized(x[...].astype(f32), nrm)
    skip_row[0:1, :] = jnp.sum(d_mixed * normed, axis=0, keepdims=True)
    dml[...] = d_mixed.astype(bf16)
    dst[:, :256] = mm_nt(dml[...], wout_own[...])
    dst[:, 256:] = mm_nt(dml[...], wout_oth[...])
    lams = decay(own, oth, base, 6, conj=True)

    def drive(s, row, half):
        return dst[part(s, row), cols(half, 0)], dst[part(s, row), cols(half, 1)]

    ends = scan(drive, lams, keep, adj_which, steps, adj_reverse, zeros_start(), nothing)
    chunk_scan(ends, keep_products(keep, adj_which, steps), decay(own, oth, base, 9, conj=True), adj_reverse, comp, packed)
    spread(summ, packed)


def mixer_grads(act, dl, dg, sl, dml, g_own, g_oth):
    _, core = place()
    mine, other = own_cols(core, 256), oth_cols(core, 256)
    g_own[0:512, :] = mm_tn(act[...], dl[:, mine])
    g_oth[0:512, :] = mm_tn(act[...], dl[:, other]).astype(bf16)
    g_own[512:1024, :] = mm_tn(act[...], dg[:, mine])
    g_oth[512:1024, :] = mm_tn(act[...], dg[:, other]).astype(bf16)
    out_grad = mm_tn(sl[...], dml[...])
    for i in range(2):
        g_own[1024 + 256 * i : 1280 + 256 * i, :] = out_grad[:256, 256 * i : 256 * (i + 1)]
        g_oth[1024 + 256 * i : 1280 + 256 * i, :] = out_grad[256:, 256 * i : 256 * (i + 1)].astype(bf16)


def in_grads(nl, dp, g_own, g_oth):
    g_own[...] = mm_tn(nl[...], dp[:, :256])
    g_oth[...] = mm_tn(nl[...], dp[:, 256:]).astype(bf16)


def turn_kernel(peers, steps, got, comp_in, dk, own, oth, keep, proj, x, nrm, wout_own, wout_oth,
                lin_own, lin_oth, gate_own, gate_oth, perm, cot_own, cot_oth,
                cin, bo_own, bo_oth, d_out, act, dl, dg, sl, dml, skip_row, dst, comp, summ,
                packed, held, gp, sig, qv, y):
    _, core = place()
    states_of(peers, steps, 16, 1, True, got, comp_in, dk, own, oth, keep, proj, cin, sl, packed, held)
    mix_and_gate(core, x, nrm, sl, wout_own, wout_oth, lin_own, lin_oth, gate_own, gate_oth, gp, act, sig, qv, y)
    low = y[...].astype(bf16)
    natural = mm_tn(perm[...], low)
    y[...] = natural
    bo_own[...] = y[:, own_cols(core, 256)].astype(bf16)
    bo_oth[...] = y[:, oth_cols(core, 256)].astype(bf16)
    send(bo_own)
    send(bo_oth)
    d_out[:, own_cols(core, 256)] = mm(perm[...], flat_rows(cot_own)).astype(bf16)
    d_out[:, oth_cols(core, 256)] = mm(perm[...], flat_rows(cot_oth)).astype(bf16)
    glu_backward(steps, 16, 0, False, core, d_out[...].astype(f32), nrm, x, gp, sig, qv, own, oth, keep, wout_own, wout_oth,
                 lin_own, lin_oth, gate_own, gate_oth, skip_row, dst, comp, summ, packed, dl, dg, dml)


def adjoint_part(peers, steps, base, keep_which, adj_which, adj_reverse, got, comp, dk, own, oth, keep, nl, x, nrm,
                 cin, sl, dst, dml, win_own, win_oth, skip_row, small_own, small_oth, at, packed, held, proj, dp):
    _, core = place()
    device_carry(place()[0], peers, got, held, dk, adj_which, own, oth, base, True, adj_reverse, packed)
    start = entries(comp, packed)
    lams, sc = decay(own, oth, base, 6, conj=True), scales(own, oth, base)
    zero = jnp.zeros((CHUNKS, 128), f32)
    acc = {half: [zero, zero, zero] for half in range(2)}
    proj[:, :256] = mm(nl[...], win_own[...])
    proj[:, 256:] = mm(nl[...], win_oth[...])

    def prior(s, half, im):
        before = s - 1 if adj_reverse else s + 1
        if 0 <= before < steps:
            return sl[before * SLAB : (before + 1) * SLAB, cols(half, im)].astype(f32)
        return cin[:, cols(half, im)]

    def drive(s, row, half):
        return dst[part(s, row), cols(half, 0)], dst[part(s, row), cols(half, 1)]

    def visit(s, state, _):
        for half in range(2):
            prior_re, prior_im = prior(s, half, 0), prior(s, half, 1)
            for row in range(2):
                ar, ai = state[half, row]
                pr, pi = prior_re[part(0, row)], prior_im[part(0, row)]
                keep_here = keep[keep_which, part(s, row), :]
                acc[half][0] = acc[half][0] + keep_here * (ar * pr + ai * pi)
                acc[half][1] = acc[half][1] + keep_here * (ai * pr - ar * pi)
                acc[half][2] = acc[half][2] + (ar * proj[part(s, row), cols(half, 0)] + ai * proj[part(s, row), cols(half, 1)])
            for im in range(2):
                both = jnp.concatenate([sc[half] * state[half, row][im] for row in range(2)], axis=0)
                dp[s * SLAB : (s + 1) * SLAB, cols(half, im)] = both.astype(bf16)

    scan(drive, lams, keep, adj_which, steps, adj_reverse, start, visit)

    d_normed = dml[...].astype(f32) * nrm[4:5, :] + mm_nt(dp[:, :256], win_own[...]) + mm_nt(dp[:, 256:], win_oth[...])
    xhat, _ = normalized(x[...].astype(f32), nrm)
    bias_row = jnp.sum(d_normed, axis=0, keepdims=True)
    gain_row = jnp.sum(d_normed * xhat, axis=0, keepdims=True)
    pack_two(bias_row, gain_row, packed)

    for ref, half, flip in ((small_own, 0, 0), (small_oth, 1, 1)):
        ref[at : at + 16, :] = jnp.zeros((16, 128), f32)
        for j, row in enumerate((skip_row[0:1, :], bias_row, gain_row)):
            low = (core == 0) if flip == 0 else (core == 1)
            pick = jnp.where(low, row[:, :256], row[:, 256:])
            ref[at + 2 * j : at + 2 * j + 1, :] = pick[:, :128]
            ref[at + 2 * j + 1 : at + 2 * j + 2, :] = pick[:, 128:]
        for j in range(3):
            ref[at + 6 + j : at + 7 + j, :] = jnp.sum(acc[half][j], axis=0, keepdims=True)
    return d_normed


def adjoint_second_kernel(peers, steps, got, comp, dk, own, oth, keep, nl, x, nrm, cin, sl, dst, dml, win_own, win_oth, skip_row, act, dl, dg,
                          g_own, g_oth, small_own, small_oth, dn, stats, packed, held, proj, dp):
    dn[...] = adjoint_part(peers, steps, 16, 1, 0, False, got, comp, dk, own, oth, keep, nl, x, nrm,
                           cin, sl, dst, dml, win_own, win_oth, skip_row, small_own, small_oth, 0, packed, held, proj, dp)
    spread(stats, packed)
    mixer_grads(act, dl, dg, sl, dml, g_own, g_oth)
    in_grads(nl, dp, g_own.at[1536:], g_oth.at[1536:])


def back_first_kernel(steps, count, got, dn, x2, nrm2, d_out2, own, oth, keep, x, nrm, gp, sig, qv,
                      wout_own, wout_oth, lin_own, lin_oth, gate_own, gate_oth,
                      act, sl, d_out, dml, g_own, g_oth, skip_row, dst, comp, summ, packed, dl, dg):
    sums = sum_peers(got)
    bias_row, gain_row = row_of_tiles(sums[0:4]), row_of_tiles(sums[4:8])
    xhat, _ = normalized(x2[...], nrm2)
    gain = nrm2[2:3, :]
    d_in = d_out2[...].astype(f32) + nrm2[1:2, :] * (dn[...] * gain - gain * bias_row / count - xhat * (gain * gain_row / count))
    d_out[...] = d_in
    glu_backward(steps, 0, 1, True, place()[1], d_in, nrm, x, gp, sig, qv, own, oth, keep, wout_own, wout_oth,
                 lin_own, lin_oth, gate_own, gate_oth, skip_row, dst, comp, summ, packed, dl, dg, dml)
    mixer_grads(act, dl, dg, sl, dml, g_own, g_oth)


def adjoint_first_kernel(peers, steps, got, comp, dk, own, oth, keep, nl, x, nrm, cin, sl, dst, dml, win_own, win_oth, skip_row,
                         d_out, perm, small1_own, small1_oth,
                         g_own, g_oth, small_own, small_oth, a_own, a_oth, packed, held, proj, tmp, dp):
    _, core = place()
    d_normed = adjoint_part(peers, steps, 0, 0, 1, True, got, comp, dk, own, oth, keep, nl, x, nrm,
                            cin, sl, dst, dml, win_own, win_oth, skip_row, small_own, small_oth, 0, packed, held, proj, dp)
    small_own[16:32, :] = small1_own[...]
    small_oth[16:32, :] = small1_oth[...]
    partial = d_out[...] + nrm[1:2, :] * nrm[2:3, :] * d_normed
    tmp[...] = mm_tn(perm[...], partial.astype(bf16))
    a_own[...] = tmp[:, own_cols(core, 256)].astype(bf16)
    a_oth[...] = tmp[:, oth_cols(core, 256)].astype(bf16)
    in_grads(nl, dp, g_own, g_oth)


def finish_kernel(count, got, a_mine, a_other, tokens, nrm, rate_log, angle_log,
                  d_in, ngg, bias, skip, rate_grad, angle_grad, packed):
    _, core = place()
    packed[...] = sum_peers(got)
    for k in range(2):
        at = 16 * k
        for ref, j in ((skip, 0), (bias, 2), (ngg, 4)):
            ref[k : k + 1, :128] = packed[at + j : at + j + 1, :]
            ref[k : k + 1, 128:] = packed[at + j + 1 : at + j + 2, :]
        rate = jnp.exp(rate_log[...].astype(f32)[k : k + 1, :])
        angle = jnp.exp(angle_log[...].astype(f32)[k : k + 1, :])
        modulus = jnp.exp(-rate)
        scale = jnp.sqrt(1.0 - modulus * modulus)
        cos, sin = jnp.cos(angle), jnp.sin(angle)
        dr, di, ds = (packed[at + j : at + j + 1, :] for j in (6, 7, 8))
        g_mod = dr * cos + di * sin - ds * modulus / scale
        rate_grad[k : k + 1, :] = -g_mod * modulus * rate
        angle_grad[k : k + 1, :] = modulus * (di * cos - dr * sin) * angle
    mine = nrm[:, own_cols(core, 256)]
    mean, inv, gain = mine[0:1, :], mine[1:2, :], mine[2:3, :]
    bias_row, gain_row = bias[0:1, :], ngg[0:1, :]
    flat = inv * gain / count
    for r in range(4):
        held_rows = jnp.where(core == r // 2, a_mine[r % 2].astype(f32), a_other[r % 2].astype(f32))
        xhat = (tokens[r].astype(f32) - mean) * inv
        d_in[r] = held_rows - flat * (bias_row + xhat * gain_row)


def swap(value):
    return lax.ppermute(value, "state", [(0, 1), (1, 0)])


def to_all(value, axes):
    peers = 1
    for a in axes:
        peers *= lax.axis_size(a)
    return lax.all_to_all(jnp.broadcast_to(value[None], (peers,) + value.shape), axes, 0, 0)


def blocking(value, axes, others):
    value, others = lax.optimization_barrier((value, others))
    got, others = lax.optimization_barrier((lax.all_to_all(value, axes, 0, 0), others))
    return (got,), others


def gather_seq(value):
    if lax.axis_size("seq") != 16:
        return (to_all(value, ("seq",)),)
    near = jnp.stack([value] + [partner(value, m) for m in (1, 2, 3)])
    return (near,) + tuple(partner(near, m) for m in (4, 8, 12))


def sum_all(value):
    if lax.axis_size("seq") != 16:
        return (to_all(value, ("seq", "state")),)
    value = value + swap(value)
    near = value + partner(value, 1) + partner(value, 2) + partner(value, 3)
    return (near,) + tuple(partner(near, m) for m in (4, 8, 12))


def partner(value, mask):
    size = lax.axis_size("seq")
    return lax.ppermute(value, "seq", [(i, i ^ mask) for i in range(size)])


def partners(value, masks):
    size = lax.axis_size("seq")
    return lax.ppermute(value, ("seq", "state"), [(2 * i + c, 2 * (i ^ masks[c]) + c) for i in range(size) for c in range(2)])


def tie(value, others):
    return lax.optimization_barrier((value, others))


def bit_of(masks):
    me, core = place()
    return (me // jnp.where(core == 0, masks[0], masks[1])) & 1


def first_halves_kernel(masks, pairs, mine, other):
    bit, at = bit_of(masks), 0
    for own, got in pairs:
        half = own.shape[0] // 2
        for out, which in ((mine, bit), (other, 1 - bit)):
            rows = pl.ds(pl.multiple_of(which * half, half), half)
            out[at : at + half, :] = (own[rows, :] + got[rows, :].astype(f32)).astype(bf16)
        at += half


def next_halves_kernel(masks, held, got, mine, other):
    bit, half = bit_of(masks), mine.shape[0]
    for out, which in ((mine, bit), (other, 1 - bit)):
        rows = pl.ds(pl.multiple_of(which * half, half), half)
        out[...] = (held[rows, :].astype(f32) + got[rows, :].astype(f32)).astype(bf16)


class SeqSum:
    def __init__(self, pairs):
        masks, m = [], 1
        while m < lax.axis_size("seq"):
            masks.append(m)
            m *= 2
        self.masks = list(zip(masks, masks[2:3] + masks[:2] + masks[3:]))
        rows = sum(a.shape[0] for a, _ in pairs) // 2
        shape = ((rows, pairs[0][0].shape[1]), bf16)
        flat = tuple(v for p in pairs for v in p)

        def kernel(refs, mine, other):
            first_halves_kernel(self.masks[0], [(refs[i], refs[i + 1]) for i in range(0, len(refs), 2)], mine, other)

        self.mine, self.other = run(kernel, [shape, shape], (flat,))

    def down(self, beside):
        masks = self.masks
        for i, now in enumerate(masks):
            if i < len(beside):
                self.other = tie(self.other, beside[i]())[0]
            got = partners(self.other, now)
            if i + 1 < len(masks):
                shape = ((got.shape[0] // 2, got.shape[1]), bf16)
                self.mine, self.other = run(functools.partial(next_halves_kernel, masks[i + 1]), [shape, shape], (self.mine, got))
        self.value = (self.mine.astype(f32) + got.astype(f32)).astype(bf16)

    def up(self, beside):
        for i, now in enumerate(self.masks[::-1]):
            if i < len(beside):
                self.value = tie(self.value, beside[i]())[0]
            got = partners(self.value, now)
            if i + 1 < len(self.masks):
                bit = bit_of(now)
                self.value = jnp.concatenate([jnp.where(bit == 0, self.value, got), jnp.where(bit == 0, got, self.value)], axis=0)
        return self.value, got


def unpack_kernel(masks, mine, got, lin, gate, out, entry):
    bit = bit_of(masks)
    cut = 1024
    for ref, which in ((mine, bit), (got, 1 - bit)):
        def piece(at, rows):
            return ref[at : at + rows, :].astype(f32)

        @pl.when(which == 0)
        def _():
            lin[1], gate[1] = piece(0, 512), piece(512, 512)
            lin[0], gate[0, :256], entry[0, :256] = piece(cut, 512), piece(cut + 512, 256), piece(cut + 768, 256)

        @pl.when(which == 1)
        def _():
            out[1, :, :256], out[1, :, 256:], entry[1] = piece(0, 256), piece(256, 256), piece(512, 512)
            gate[0, 256:] = piece(cut, 256)
            out[0, :, :256], out[0, :, 256:], entry[0, 256:] = piece(cut + 256, 256), piece(cut + 512, 256), piece(cut + 768, 256)


class Far:
    def __init__(self, value, at=None, smem=False):
        self.value, self.at, self.smem = value, at, smem
        self.shape = value.shape if at is None else value.shape[1:] if at != "rows" else (2,) + value.shape[1:]

    def source(self, ref):
        if self.at is None:
            return ref
        return ref.at[pl.ds(lax.axis_index("state") * 2, 2)] if self.at == "rows" else ref.at[self.at]


class Held:
    def __init__(self, source, ref, sem):
        self.ref, self.copy, self.shape, self.dtype = ref, pltpu.make_async_copy(source, ref, sem), ref.shape, ref.dtype
        self.copy.start()

    def ready(self):
        if self.copy is not None:
            self.copy.wait()
            self.copy = None

    def __getitem__(self, index):
        self.ready()
        return self.ref[index]


class Drained:
    def __init__(self, ref, target, sem):
        self.ref, self.copy, self.sent = ref, pltpu.make_async_copy(ref, target, sem), False
        self.shape, self.dtype = ref.shape, ref.dtype

    def __getitem__(self, index):
        return self.ref[index]

    def __setitem__(self, index, value):
        self.ref[index] = value

    def send(self):
        if not self.sent:
            self.copy.start()
            self.sent = True


def run(kernel, outs, groups, scratch=(), limit=24, flops=0):
    args = [a for g in groups for a in (g if isinstance(g, tuple) else (g,))]
    far_in = [i for i, a in enumerate(args) if isinstance(a, Far)]
    far_out = [i for i, o in enumerate(outs) if len(o) == 3]
    moved = sum(a.value.size * a.value.dtype.itemsize if isinstance(a, Far) else a.size * a.dtype.itemsize for a in args)

    def whole(*refs):
        ins, results = list(refs[: len(args)]), list(refs[len(args) : len(args) + len(outs)])
        rest = refs[len(args) + len(outs) :]
        own = rest[: len(scratch)]
        if far_in or far_out:
            buffers, sem = rest[len(scratch) : -1], rest[-1]
        for j, i in enumerate(far_in):
            ins[i] = Held(args[i].source(ins[i]), buffers[j], sem.at[j])
        for j, i in enumerate(far_out, len(far_in)):
            results[i] = Drained(buffers[j], results[i], sem.at[j])
        grouped, at = [], 0
        for g in groups:
            if isinstance(g, tuple):
                grouped.append(tuple(ins[at : at + len(g)]))
                at += len(g)
            else:
                grouped.append(ins[at])
                at += 1
        kernel(*grouped, *results, *own)
        for i in far_in:
            ins[i].ready()
        for i in far_out:
            results[i].send()
        for i in far_out:
            results[i].copy.wait()

    def space(far):
        return pl.BlockSpec(memory_space=pltpu.HBM if far else pltpu.VMEM)

    held = [(pltpu.SMEM if args[i].smem else pltpu.VMEM)(args[i].shape, args[i].value.dtype) for i in far_in]
    held += [pltpu.VMEM(outs[i][0], outs[i][1]) for i in far_out]
    if held:
        held.append(pltpu.SemaphoreType.DMA((len(held),)))
    return pl.pallas_call(
        whole,
        out_shape=[jax.ShapeDtypeStruct(o[0], o[1]) for o in outs],
        in_specs=[space(isinstance(a, Far)) for a in args],
        out_specs=[space(len(o) == 3) for o in outs],
        scratch_shapes=[pltpu.VMEM(*s) for s in scratch] + held,
        compiler_params=pltpu.CompilerParams(vmem_limit_bytes=limit * 2**20),
        cost_estimate=pl.CostEstimate(flops=flops, bytes_accessed=moved, transcendentals=0),
    )(*[a.value if isinstance(a, Far) else a for a in args])


def body(tokens, gain, bias, in_proj, out_proj, rate_log, angle_log, skip, glu_lin, glu_gate, positions, cotangent):
    peers = lax.axis_size("seq")
    core = lax.axis_index("state")
    rows, span, width = tokens.shape
    steps = span // CHUNKS
    n = 2 * span
    count = float(rows * span * peers)
    packed = ((8, 128), f32)
    one = 2 * n * 512 * 512
    far = ((n, 512), bf16, "far")
    low = ((n, 512), bf16)
    full = ((n, 512), f32)

    w_in = in_proj.reshape(2, 512, 256)
    w_out = out_proj.reshape(2, 256, 512)
    x_oth, cot_oth, in_oth, out_oth, lin_oth, gate_oth = (swap(w) for w in (tokens, cotangent, w_in, w_out, glu_lin, glu_gate))
    enter = [(Far(w_in, k), Far(in_oth, k)) for k in range(2)]

    stats, own, keep, dk, perm = run(
        functools.partial(prep_kernel, peers, steps),
        [((2 * peers, 4, 128), f32), ((32, 128), f32), ((2, n, 128), f32), ((2, peers, 8, 128), f32), ((n, n), bf16)],
        (Far(positions, smem=True),) + tuple(Far(v) for v in (tokens, gain, bias, skip, rate_log, angle_log)))
    oth = swap(own)
    ordered = ((peers, 8, 128), f32)

    for_seq, for_all = ((peers, 8, 128), f32), ((2 * peers, 8, 128), f32)
    scan_outs = [full, ((16, 8, 128), f32), for_seq, ((8, 512), f32)]
    xp, nl0, proj, comp, summ, nrm0 = run(
        functools.partial(enter_first_kernel, peers, steps, count), [far, far] + scan_outs,
        (lax.all_to_all(stats, ("seq", "state"), 0, 0), Far(tokens, "rows"), Far(x_oth, "rows"), perm, own, oth, keep) + enter[0], [packed], flops=2 * one)
    got, (cot_oth, out_oth, lin_oth, gate_oth) = blocking(summ, "seq", (cot_oth, out_oth, lin_oth, gate_oth))
    glu = [tuple(Far(w, k) for w in (w_out, out_oth, glu_lin, lin_oth, glu_gate, gate_oth)) for k in range(2)]
    cin0, sl0, gp0, act0, sig0, qv0, y0, stats = run(
        functools.partial(leave_first_kernel, peers, steps),
        [((SLAB, 512), f32), far, far, far, far, far, full, for_all],
        (got, comp, dk, own, oth, keep, proj, Far(xp), nrm0) + glu[0], [packed, ordered], flops=3 * one)
    got, _ = blocking(stats, ("seq", "state"), ())
    nl1, proj, comp, summ, nrm1 = run(
        functools.partial(enter_second_kernel, peers, steps, count), [low] + scan_outs,
        (got, y0, own, oth, keep) + enter[1], [packed], flops=one)
    got, _ = blocking(summ, "seq", ())
    turn_outs = [((8, 512), f32), full, ((16, 8, 128), f32)]
    cin1, bo_own, bo_oth, d_out1, act1, dl1, dg1, sl1, dml1, skip1, dst, comp, summ = run(
        functools.partial(turn_kernel, peers, steps),
        [((SLAB, 512), f32), ((n, 256), bf16, "far"), ((n, 256), bf16, "far"), low, low, low, low, low, low] + turn_outs + [for_seq],
        (got, comp, dk, own, oth, keep, proj, y0, nrm1) + glu[1] + (perm, Far(cotangent, "rows"), Far(cot_oth, "rows")),
        [packed, ordered, full, full, full, full], flops=8 * one)
    got, (bo_oth,) = blocking(summ, "seq", (bo_oth,))
    g1_own, g1_oth, s1_own, s1_oth, dn, stats = run(
        functools.partial(adjoint_second_kernel, peers, steps),
        [((2048, 256), f32), ((2048, 256), bf16), ((16, 128), f32), ((16, 128), f32), full, for_all],
        (got, comp, dk, own, oth, keep, nl1, y0, nrm1, cin1, sl1, dst, dml1) + enter[1] + (skip1, act1, dl1, dg1),
        [packed, ordered, full, low], flops=6 * one)
    got, (bo_oth, g1_oth) = blocking(stats, ("seq", "state"), (bo_oth, g1_oth))
    bo_got, g1_got = swap(bo_oth), swap(g1_oth)
    d_out0, dml0, g0_own, g0_oth, skip0, dst, comp, summ = run(
        functools.partial(back_first_kernel, steps, count),
        [full, low, ((1536, 256), f32), ((1536, 256), bf16)] + turn_outs + [for_seq],
        (got, dn, y0, nrm1, d_out1, own, oth, keep, Far(xp), nrm0, Far(gp0), Far(sig0), Far(qv0)) + glu[0] + (Far(act0), Far(sl0)),
        [packed, low, low], flops=6 * one)
    got, (g0_oth, bo_got, g1_got) = blocking(summ, "seq", (g0_oth, bo_got, g1_got))
    g0_got = swap(g0_oth)
    i0_own, i0_oth, s_own, s_oth, a_own, a_oth = run(
        functools.partial(adjoint_first_kernel, peers, steps),
        [((512, 256), f32), ((512, 256), bf16), ((32, 128), f32), ((32, 128), f32), ((n, 256), bf16), ((n, 256), bf16)],
        (got, comp, dk, own, oth, keep, Far(nl0), Far(xp), nrm0, cin0, Far(sl0), dst, dml0) + enter[0]
        + (skip0, d_out0, perm, s1_own, s1_oth),
        [packed, ordered, full, full, low], flops=4 * one)
    i0_got = swap(i0_oth)
    bulk = SeqSum([(g1_own, g1_got), (g0_own, g0_got), (i0_own, i0_got)])
    s_got, a_got = swap(s_oth), swap(a_oth)
    s_all = jnp.broadcast_to((s_own + s_got)[None], (peers, 32, 128))
    got = lax.all_to_all(s_all, "seq", 0, 0)
    pair = (2, span, width)
    d_in, ngg, bias_grad, skip_grad, rate_grad, angle_grad = run(
        functools.partial(finish_kernel, count),
        [((rows, span, width), f32), ((2, 256), f32), ((2, 256), f32), ((2, 256), f32), ((2, 128), f32), ((2, 128), f32)],
        ((got,), a_own.reshape(pair), a_got.reshape(pair), Far(tokens), nrm0, Far(rate_log), Far(angle_log)),
        [((32, 128), f32)])
    bulk.down([lambda: (), lambda: s_all, lambda: got, lambda: d_in])
    mine, other = bulk.up([])
    lin_grad, gate_grad, out_grad, in_grad = run(
        functools.partial(unpack_kernel, bulk.masks[0]),
        [((2, 512, 256), f32), ((2, 512, 256), f32), ((2, 256, 512), f32), ((2, 512, 256), f32)],
        (mine, other))
    out_grad, in_grad = out_grad.reshape(2, 2, 128, 512), in_grad.reshape(2, 512, 2, 128)
    mine, other = bo_own.reshape(pair), bo_got.reshape(pair)
    block_out = jnp.concatenate([jnp.where(core == 0, mine, other), jnp.where(core == 0, other, mine)], axis=0)
    return (block_out, d_in, ngg, bias_grad, in_grad, out_grad, rate_grad, angle_grad, skip_grad, lin_grad, gate_grad)


def solution(mesh):
    placed = (
        P(None, "seq", "state"),
        P(None, "state"),
        P(None, "state"),
        P(None, None, None, "state"),
        P(None, None, "state", None),
        P(None, "state"),
        P(None, "state"),
        P(None, "state"),
        P(None, None, "state"),
        P(None, None, "state"),
        P(),
        P(None, "seq", "state"),
    )
    return jax.shard_map(
        body,
        mesh=mesh,
        in_specs=placed,
        out_specs=(
            P(None, "seq", "state"),
            P(None, "seq", "state"),
            P(None, "state"),
            P(None, "state"),
            P(None, None, None, "state"),
            P(None, None, "state", None),
            P(None, "state"),
            P(None, "state"),
            P(None, "state"),
            P(None, None, "state"),
            P(None, None, "state"),
        ),
        check_vma=False,
    )
```

time: 263 us -> 203 us (0.77)
  blocking collectives: 20.2 us -> 75.1 us
  starting transfers between devices: 67.9 us -> 13.8 us
  local copies, waits for them, and re-layouts: 55.6 us -> 9.83 us
  other arithmetic: 12.9 us -> 1.34 us
  Pallas kernels: 35.8 us -> 32.2 us
    all_to_all x2 -> x7, blocking collectives: 20.2 us -> 75.1 us  [the longest x6 60.7 us: blocking(): lax.all_to_all(value, axes, 0, 0)]
    unnamed x176 -> x34, local copies, waits for them, and re-layouts: 37.5 us -> 6.16 us
    ppermute x32 -> x8, starting transfers between devices: 36.8 us -> 6.89 us  [partners(): lax.ppermute(value, ('seq', 'state'), [(2 * i + c, 2 * (i ^ masks[c]) + c...]
    all_to_all x6 -> x1, starting transfers between devices: 28.3 us -> 3.53 us  [body(): got = lax.all_to_all(s_all, 'seq', 0, 0)]
    all_to_all x6 -> x1, waiting for transfers between devices: 26.3 us -> 2.63 us  [body(): got = lax.all_to_all(s_all, 'seq', 0, 0)]
    ppermute x32 -> x8, waiting for transfers between devices: 41.2 us -> 64.2 us  [partners(): lax.ppermute(value, ('seq', 'state'), [(2 * i + c, 2 * (i ^ masks[c]) + c...]
    squeeze x7 -> x0, local copies, waits for them, and re-layouts: 11.4 us -> none  [the longest x2 3.72 us: cut(): lax.dynamic_index_in_dim(value, 1 - core, 0, False)]
    convert_element_type x18 -> x1, other arithmetic: 4.93 us -> 0.03 us  [down(): self.value = (self.mine.astype(f32) + got.astype(f32)).astype(bf16)]
  transfers between devices with their start and end apart: 50 -> 22, of which waited for: 23 -> 12; matrix products, arithmetic and copies ran while one was open for 9% -> 1% of each run, Pallas kernels for 8% -> 7%
where the time goes in v2:
time: 203 us
  blocking collectives  75.1 us (37%)
  waiting for transfers between devices  69.5 us (34%)
  Pallas kernels  32.2 us (16%)
  starting transfers between devices  13.8 us (7%)
  local copies, waits for them, and re-layouts  9.83 us (5%)
    ppermute x8, waiting for transfers between devices, partners(): lax.ppermute(value, ('seq', 'state'), [(2 * i + c, 2 * (i ^ masks[c]) + c...  64.2 us
    all_to_all x6, blocking collectives, blocking(): lax.all_to_all(value, axes, 0, 0)  60.7 us
    pallas_call x14, Pallas kernels, run(): pl.pallas_call(whole, out_shape=[jax.ShapeDtypeStruct(o[0], o[1]) for o i...  32.2 us
    all_to_all x1, blocking collectives, body(): lax.all_to_all(stats, ('seq', 'state'), 0, 0)  14.4 us
    ppermute x8, starting transfers between devices, partners(): lax.ppermute(value, ('seq', 'state'), [(2 * i + c, 2 * (i ^ masks[c]) + c...  6.89 us
    unnamed x34, local copies, waits for them, and re-layouts  6.16 us
  transfers between devices with their start and end apart: 22, of which 12 were waited for; matrix products, arithmetic and copies ran while one was open for 1% of the time, Pallas kernels for 7%

profile of v2, /device:TPU:0, one launch (start us, length us, event | category | flops | bytes accessed | tf_op | source)
XLA Modules:
  0.0 202.7 jit_solution(7783393336385137592)
XLA Ops:
  1.2 1.5 reshape.47.refs_7_.refs_5_.refs_13_
  2.8 1.0 copy-done
  3.8 0.7 copy-done.6
  4.5 0.7 copy-done.7
  5.1 0.7 copy-done.9
  5.8 0.7 copy-done.11
  6.5 0.7 copy-done.12
  7.1 0.7 copy-done.13
  7.8 1.5 shard_map.203
  11.2 14.4 %all_to_all.40.refs_0_ = f32[32,4,128]{2,1,0:T(4,128)S(1)} all-to-all(f32[32,4,128]{2,1,0:T(4,128)S(1)} %get-tuple-element.117), channel_id=1, replica_groups=mesh['seq'=16,'state'=2] {'seq','state'}, dimensions={0} | all-to-all | bytes 131072 | tf_op jit(solution)/shard_map/all_to_all | solution.py:824
  25.6 1.0 copy-done.1
  26.6 2.3 %shard_map.204 = (bf16[512,512]{1,0:T(8,128)(2,1)S(1)}, bf16[512,512]{1,0:T(8,128)(2,1)S(1)}, f32[512,512]{1,0:T(8,128)S(1)}, f32[16,8,128]{2,1,0:T(8,128)S(1)},...) custom-call(f32[32,4,128]{2,1,0:T(4,128)S(1)} %all_to_all.40.refs_0_, bf16[4,256,256]{2,1,0:T(8,128)(2,1)S(1)} %copy-done.1, ...), custom_call_target="tpu_custom_call" | custom-call | flops 536870912 | bytes 3244032 | tf_op jit(solution)/shard_map/pallas_call | solution.py:784
  28.9 10.1 %all_to_all.41.refs_0_ = f32[16,8,128]{2,1,0:T(8,128)S(1)} all-to-all(f32[16,8,128]{2,1,0:T(8,128)S(1)} %get-tuple-element.122), channel_id=1, replica_groups=mesh['seq'=16,'state'=2] {'seq'}, dimensions={0} | all-to-all | bytes 131072 | tf_op jit(solution)/shard_map/all_to_all | solution.py:590
  39.1 4.3 %shard_map.205 = (f32[16,512]{1,0:T(8,128)S(1)}, bf16[512,512]{1,0:T(8,128)(2,1)S(1)}, bf16[512,512]{1,0:T(8,128)(2,1)S(1)}, bf16[512,512]{1,0:T(8,128)(2,1)S(1)...) custom-call(f32[16,8,128]{2,1,0:T(8,128)S(1)} %all_to_all.41.refs_0_, ...), custom_call_target="tpu_custom_call" | custom-call | flops 805306368 | bytes 5554176 | tf_op jit(solution)/shard_map/pallas_call | solution.py:784
  43.4 10.1 %all_to_all.42.refs_0_ = f32[32,8,128]{2,1,0:T(8,128)S(1)} all-to-all(f32[32,8,128]{2,1,0:T(8,128)S(1)} %get-tuple-element.136), channel_id=1, replica_groups=mesh['seq'=16,'state'=2] {'seq','state'}, dimensions={0} | all-to-all | bytes 262144 | tf_op jit(solution)/shard_map/all_to_all | solution.py:590
  53.5 1.6 shard_map.206
  55.1 10.2 %all_to_all.43.refs_0_ = f32[16,8,128]{2,1,0:T(8,128)S(1)} all-to-all(f32[16,8,128]{2,1,0:T(8,128)S(1)} %get-tuple-element.138), channel_id=1, replica_groups=mesh['seq'=16,'state'=2] {'seq'}, dimensions={0} | all-to-all | bytes 131072 | tf_op jit(solution)/shard_map/all_to_all | solution.py:590
  65.3 6.7 %shard_map.207 = (f32[16,512]{1,0:T(8,128)S(1)}, bf16[512,256]{1,0:T(8,128)(2,1)S(1)}, bf16[512,256]{1,0:T(8,128)(2,1)S(1)}, bf16[512,512]{1,0:T(8,128)(2,1)S(1)...) custom-call(f32[16,8,128]{2,1,0:T(8,128)S(1)} %all_to_all.43.refs_0_, ...), custom_call_target="tpu_custom_call" | custom-call | flops 2147483648 | bytes 7651328 | tf_op jit(solution)/shard_map/pallas_call | solution.py:784
  72.0 10.1 %all_to_all.44.refs_0_ = f32[16,8,128]{2,1,0:T(8,128)S(1)} all-to-all(f32[16,8,128]{2,1,0:T(8,128)S(1)} %get-tuple-element.146), channel_id=1, replica_groups=mesh['seq'=16,'state'=2] {'seq'}, dimensions={0} | all-to-all | bytes 131072 | tf_op jit(solution)/shard_map/all_to_all | solution.py:590
  82.2 2.8 %shard_map.208 = (f32[2048,256]{1,0:T(8,128)S(1)}, bf16[2048,256]{1,0:T(8,128)(2,1)S(1)}, f32[16,128]{1,0:T(8,128)S(1)}, f32[16,128]{1,0:T(8,128)S(1)}, f32[512,...) custom-call(f32[16,8,128]{2,1,0:T(8,128)S(1)} %all_to_all.44.refs_0_, f32[16,8,128]{2,1,0:T(8,128)S(1)} %get-tuple-element.149.refs_1_, ...), custom_call_target="tpu_custom_call" | custom-call | flops 1610612736 | bytes 7176192 | tf_op jit(solution)/shard_map/pallas_call | solution.py:784
  84.9 9.9 %all_to_all.45.refs_0_ = f32[32,8,128]{2,1,0:T(8,128)S(1)} all-to-all(f32[32,8,128]{2,1,0:T(8,128)S(1)} %get-tuple-element.162), channel_id=1, replica_groups=mesh['seq'=16,'state'=2] {'seq','state'}, dimensions={0} | all-to-all | bytes 262144 | tf_op jit(solution)/shard_map/all_to_all | solution.py:590
  95.4 5.0 %shard_map.209 = (f32[512,512]{1,0:T(8,128)S(1)}, bf16[512,512]{1,0:T(8,128)(2,1)S(1)}, f32[1536,256]{1,0:T(8,128)S(1)}, bf16[1536,256]{1,0:T(8,128)(2,1)S(1)}, ...) custom-call(f32[32,8,128]{2,1,0:T(8,128)S(1)} %all_to_all.45.refs_0_, ...), custom_call_target="tpu_custom_call" | custom-call | flops 1610612736 | bytes 9633792 | tf_op jit(solution)/shard_map/pallas_call | solution.py:784
  100.4 10.2 %all_to_all.46.refs_0_ = f32[16,8,128]{2,1,0:T(8,128)S(1)} all-to-all(f32[16,8,128]{2,1,0:T(8,128)S(1)} %get-tuple-element.177), channel_id=1, replica_groups=mesh['seq'=16,'state'=2] {'seq'}, dimensions={0} | all-to-all | bytes 131072 | tf_op jit(solution)/shard_map/all_to_all | solution.py:590
  110.6 3.9 %shard_map.210 = (f32[512,256]{1,0:T(8,128)S(1)}, bf16[512,256]{1,0:T(8,128)(2,1)S(1)}, f32[32,128]{1,0:T(8,128)S(1)}, f32[32,128]{1,0:T(8,128)S(1)}, bf16[512,2...) custom-call(f32[16,8,128]{2,1,0:T(8,128)S(1)} %all_to_all.46.refs_0_, f32[16,8,128]{2,1,0:T(8,128)S(1)} %get-tuple-element.183.refs_1_, ...), custom_call_target="tpu_custom_call" | custom-call | flops 1073741824 | bytes 6668288 | tf_op jit(solution)/shard_map/pallas_call | solution.py:784
  114.5 0.6 collective-permute-start.12
  115.1 1.2 collective-permute-done.12.refs_5_
  116.6 0.9 collective-permute-start.13
  117.5 1.2 collective-permute-done.9
  118.7 12.8 %collective-permute-done.13.refs_1_ = bf16[2048,256]{1,0:T(8,128)(2,1)S(1)} collective-permute-done((bf16[2048,256]{1,0:T(8,128)(2,1)S(1)}, bf16[2048,256]{1,0:T(8,128)(2,1)S(1)}, u32[]{:S(2)}, u32[]{:S(2)}) %collective-permute-start.13) | collective-permute-done | bytes 1048608 | tf_op jit(solution)/shard_map/ppermute | solution.py:616
  131.8 0.7 broadcast_in_dim.2
  132.5 0.7 collective-permute-start.14
  133.1 3.5 %all-to-all-start.7 = ((f32[16,32,128]{2,1,0:T(8,128)}), f32[16,32,128]{2,1,0:T(8,128)S(1)}, u32[]{:S(2)}, u32[]{:S(2)}) async-start(f32[16,32,128]{2,1,0:T(8,128)} %broadcast_in_dim.2), calls=%async_computation.7 | async-start | bytes 524288 | tf_op jit(solution)/shard_map/all_to_all | solution.py:867
  136.8 6.8 %collective-permute-done.14.refs_1_ = bf16[1024,256]{1,0:T(8,128)(2,1)S(1)} collective-permute-done((bf16[1024,256]{1,0:T(8,128)(2,1)S(1)}, bf16[1024,256]{1,0:T(8,128)(2,1)S(1)}, u32[]{:S(2)}, u32[]{:S(2)}) %collective-permute-start.14) | collective-permute-done | bytes 524320 | tf_op jit(solution)/shard_map/ppermute | solution.py:616
  143.7 2.6 %all-to-all-done.7.refs_0_ = f32[16,32,128]{2,1,0:T(8,128)S(1)} async-done(((f32[16,32,128]{2,1,0:T(8,128)}), f32[16,32,128]{2,1,0:T(8,128)S(1)}, u32[]{:S(2)}, u32[]{:S(2)}) %all-to-all-start.7) | async-done | bytes 262176 | tf_op jit(solution)/shard_map/all_to_all | solution.py:867
  146.3 1.2 collective-permute-start.15
  147.6 1.5 shard_map.211
  149.1 3.6 %collective-permute-done.15.refs_1_ = bf16[512,256]{1,0:T(8,128)(2,1)S(1)} collective-permute-done((bf16[512,256]{1,0:T(8,128)(2,1)S(1)}, bf16[512,256]{1,0:T(8,128)(2,1)S(1)}, u32[]{:S(2)}, u32[]{:S(2)}) %collective-permute-start.15) | collective-permute-done | bytes 262176 | tf_op jit(solution)/shard_map/ppermute | solution.py:616
  152.8 0.7 collective-permute-start.16
  153.5 7.2 %collective-permute-done.16 = bf16[256,256]{1,0:T(8,128)(2,1)S(1)} collective-permute-done((bf16[256,256]{1,0:T(8,128)(2,1)S(1)}, bf16[256,256]{1,0:T(8,128)(2,1)S(1)}, u32[]{:S(2)}, u32[]{:S(2)}) %collective-permute-start.16) | collective-permute-done | bytes 131104 | tf_op jit(solution)/shard_map/ppermute | solution.py:616
  160.9 6.8 %collective-permute-done.17 = bf16[256,256]{1,0:T(8,128)(2,1)S(1)} collective-permute-done((bf16[256,256]{1,0:T(8,128)(2,1)S(1)}, bf16[256,256]{1,0:T(8,128)(2,1)S(1)}, u32[]{:S(2)}, u32[]{:S(2)}) %collective-permute-start.17) | collective-permute-done | bytes 131104 | tf_op jit(solution)/shard_map/ppermute | solution.py:616
  167.8 6.3 %collective-permute-done.18 = bf16[512,256]{1,0:T(8,128)(2,1)S(1)} collective-permute-done((bf16[512,256]{1,0:T(8,128)(2,1)S(1)}, bf16[512,256]{1,0:T(8,128)(2,1)S(1)}, u32[]{:S(2)}, u32[]{:S(2)}) %collective-permute-start.18) | collective-permute-done | bytes 262176 | tf_op jit(solution)/shard_map/ppermute | solution.py:616
  174.3 2.7 %collective-permute-start.19 = (bf16[1024,256]{1,0:T(8,128)(2,1)S(1)}, bf16[1024,256]{1,0:T(8,128)(2,1)S(1)}, u32[]{:S(2)}, u32[]{:S(2)}) collective-permute-start(bf16[1024,256]{1,0:T(8,128)(2,1)S(1)} %pad_maximum_fusion.2), channel_id=1, source_target_pairs={{0,4},{1,3},{2,6},{3,1},{4,0},{5,7},{6,2},{7,5},{8,12},{9,11},{10,... | collective-permute-start | bytes 1572872 | tf_op jit(solution)/shard_map/ppermute | solution.py:616
  177.0 7.2 %collective-permute-done.19 = bf16[1024,256]{1,0:T(8,128)(2,1)S(1)} collective-permute-done((bf16[1024,256]{1,0:T(8,128)(2,1)S(1)}, bf16[1024,256]{1,0:T(8,128)(2,1)S(1)}, u32[]{:S(2)}, u32[]{:S(2)}) %collective-permute-start.19) | collective-permute-done | bytes 524320 | tf_op jit(solution)/shard_map/ppermute | solution.py:616
  184.4 0.6 collective-permute-start.20
  185.1 0.8 pad_maximum_fusion.1
  185.9 13.4 %collective-permute-done.20.refs_1_ = bf16[2048,256]{1,0:T(8,128)(2,1)S(1)} collective-permute-done((bf16[2048,256]{1,0:T(8,128)(2,1)S(1)}, bf16[2048,256]{1,0:T(8,128)(2,1)S(1)}, u32[]{:S(2)}, u32[]{:S(2)}) %collective-permute-start.20) | collective-permute-done | bytes 1048608 | tf_op jit(solution)/shard_map/ppermute | solution.py:616
  199.3 1.9 shard_map.216
  201.2 1.5 reshape.51
  (64 shorter events, 4.6 us)
Async XLA Ops:
  0.6 10.4 %collective-permute-start = (bf16[4,256,256]{2,1,0:T(8,128)(2,1)}, bf16[4,256,256]{2,1,0:T(8,128)(2,1)S(1)}, u32[]{:S(2)}, u32[]{:S(2)}) collective-permute-start(bf16[4,256,256]{2,1,0:T(8,128)(2,1)} %refs_3_.3), channel_id=1, source_target_pairs={{0,1},{1,0},{2,3},{3,2},{4,5},{5,4},{6,7},{7,6},{8,9},{9,8},{10,11... | collective-permute-start | bytes 1572872 | tf_op jit(solution)/shard_map/ppermute | solution.py:578
  1.2 37.9 %copy-start.4 = (bf16[2,512,256]{2,1,0:T(8,128)(2,1)S(1)}, bf16[2,512,256]{2,1,0:T(8,128)(2,1)}, u32[]{:S(2)}) copy-start(bf16[2,512,256]{2,1,0:T(8,128)(2,1)} %refs_15_.1) | copy-start | bytes 1572868
  1.2 37.9 %copy-start.5 = (bf16[2,512,256]{2,1,0:T(8,128)(2,1)S(1)}, bf16[2,512,256]{2,1,0:T(8,128)(2,1)}, u32[]{:S(2)}) copy-start(bf16[2,512,256]{2,1,0:T(8,128)(2,1)} %refs_17_.1) | copy-start | bytes 1572868
  2.6 23.0 %collective-permute-start.2 = (bf16[2,512,256]{2,1,0:T(8,128)(2,1)S(1)}, bf16[2,512,256]{2,1,0:T(8,128)(2,1)S(1)}, u32[]{:S(2)}, u32[]{:S(2)}) collective-permute-start(bf16[2,512,256]{2,1,0:T(8,128)(2,1)S(1)} %reshape.47.refs_7_.refs_5_.refs_13_), channel_id=1, source_target_pairs={{0,1},{1,0},{2,3},{3,2},{4,5},{5,4},{6,7},{7,6},{8,9},{9,8},{10,11... | collective-permute-start | bytes 1572872 | tf_op jit(solution)/shard_map/ppermute | solution.py:578
  2.8 1.0 copy-start
  3.8 0.7 copy-start.6
  4.5 0.7 copy-start.7
  5.1 0.7 copy-start.9
  5.8 0.7 copy-start.11
  6.5 0.7 copy-start.12
  7.1 0.7 copy-start.13
  7.8 31.2 %copy-start.3 = (bf16[2,2,128,512]{3,2,1,0:T(8,128)(2,1)S(1)}, bf16[2,2,128,512]{3,2,1,0:T(8,128)(2,1)}, u32[]{:S(2)}) copy-start(bf16[2,2,128,512]{3,2,1,0:T(8,128)(2,1)} %param.16) | copy-start | bytes 1572868
  9.3 1.4 collective-permute-start.1
  9.8 19.1 %collective-permute-start.3 = (bf16[4,256,256]{2,1,0:T(8,128)(2,1)}, bf16[4,256,256]{2,1,0:T(8,128)(2,1)S(1)}, u32[]{:S(2)}, u32[]{:S(2)}) collective-permute-start(bf16[4,256,256]{2,1,0:T(8,128)(2,1)} %refs_16_.1), channel_id=1, source_target_pairs={{0,1},{1,0},{2,3},{3,2},{4,5},{5,4},{6,7},{7,6},{8,9},{9,8},{10,11... | collective-permute-start | bytes 1572872 | tf_op jit(solution)/shard_map/ppermute | solution.py:578
  9.9 19.0 %collective-permute-start.4 = (bf16[2,256,512]{2,1,0:T(8,128)(2,1)}, bf16[2,256,512]{2,1,0:T(8,128)(2,1)S(1)}, u32[]{:S(2)}, u32[]{:S(2)}) collective-permute-start(bf16[2,256,512]{2,1,0:T(8,128)(2,1)} %bitcast.6), channel_id=1, source_target_pairs={{0,1},{1,0},{2,3},{3,2},{4,5},{5,4},{6,7},{7,6},{8,9},{9,8},{10,11... | collective-permute-start | bytes 1572872 | tf_op jit(solution)/shard_map/ppermute | solution.py:578
  10.7 18.3 %collective-permute-start.5 = (bf16[2,512,256]{2,1,0:T(8,128)(2,1)}, bf16[2,512,256]{2,1,0:T(8,128)(2,1)S(1)}, u32[]{:S(2)}, u32[]{:S(2)}) collective-permute-start(bf16[2,512,256]{2,1,0:T(8,128)(2,1)} %refs_15_.1), channel_id=1, source_target_pairs={{0,1},{1,0},{2,3},{3,2},{4,5},{5,4},{6,7},{7,6},{8,9},{9,8},{10,11... | collective-permute-start | bytes 1572872 | tf_op jit(solution)/shard_map/ppermute | solution.py:578
  11.0 17.9 %collective-permute-start.6 = (bf16[2,512,256]{2,1,0:T(8,128)(2,1)}, bf16[2,512,256]{2,1,0:T(8,128)(2,1)S(1)}, u32[]{:S(2)}, u32[]{:S(2)}) collective-permute-start(bf16[2,512,256]{2,1,0:T(8,128)(2,1)} %refs_17_.1), channel_id=1, source_target_pairs={{0,1},{1,0},{2,3},{3,2},{4,5},{5,4},{6,7},{7,6},{8,9},{9,8},{10,11... | collective-permute-start | bytes 1572872 | tf_op jit(solution)/shard_map/ppermute | solution.py:578
  25.6 1.0 copy-start.1
  43.4 21.9 %copy-start.14 = (bf16[4,256,256]{2,1,0:T(8,128)(2,1)S(1)}, bf16[4,256,256]{2,1,0:T(8,128)(2,1)}, u32[]{:S(2)}) copy-start(bf16[4,256,256]{2,1,0:T(8,128)(2,1)} %refs_16_.1) | copy-start | bytes 1572868
  94.8 5.5 %collective-permute-start.8 = (bf16[2048,256]{1,0:T(8,128)(2,1)S(1)}, bf16[2048,256]{1,0:T(8,128)(2,1)S(1)}, u32[]{:S(2)}, u32[]{:S(2)}) collective-permute-start(bf16[2048,256]{1,0:T(8,128)(2,1)S(1)} %get-tuple-element.176), channel_id=1, source_target_pairs={{0,1},{1,0},{2,3},{3,2},{4,5},{5,4},{6,7},{7,6},{8,9},{9,8},{10,11... | collective-permute-start | bytes 3145736 | tf_op jit(solution)/shard_map/ppermute | solution.py:578
  95.1 5.3 %collective-permute-start.7 = (bf16[512,256]{1,0:T(8,128)(2,1)S(1)}, bf16[512,256]{1,0:T(8,128)(2,1)S(1)}, u32[]{:S(2)}, u32[]{:S(2)}) collective-permute-start(bf16[512,256]{1,0:T(8,128)(2,1)S(1)} %get-tuple-element.175), channel_id=1, source_target_pairs={{0,1},{1,0},{2,3},{3,2},{4,5},{5,4},{6,7},{7,6},{8,9},{9,8},{10,11... | collective-permute-start | bytes 786440 | tf_op jit(solution)/shard_map/ppermute | solution.py:578
  100.4 14.1 %copy-start.15 = (bf16[512,256]{1,0:T(8,128)(2,1)}, bf16[512,256]{1,0:T(8,128)(2,1)S(1)}, u32[]{:S(2)}) copy-start(bf16[512,256]{1,0:T(8,128)(2,1)S(1)} %collective-permute-done.7) | copy-start | bytes 786436
  110.6 5.7 %collective-permute-start.11 = (bf16[1536,256]{1,0:T(8,128)(2,1)S(1)}, bf16[1536,256]{1,0:T(8,128)(2,1)S(1)}, u32[]{:S(2)}, u32[]{:S(2)}) collective-permute-start(bf16[1536,256]{1,0:T(8,128)(2,1)S(1)} %get-tuple-element.202), channel_id=1, source_target_pairs={{0,1},{1,0},{2,3},{3,2},{4,5},{5,4},{6,7},{7,6},{8,9},{9,8},{10,11... | collective-permute-start | bytes 2359304 | tf_op jit(solution)/shard_map/ppermute | solution.py:578
  114.5 1.7 collective-permute-start.12
  116.6 30.9 %copy-start.2 = (bf16[4,256,256]{2,1,0:T(8,128)(2,1)S(1)}, bf16[4,256,256]{2,1,0:T(8,128)(2,1)}, u32[]{:S(2)}) copy-start(bf16[4,256,256]{2,1,0:T(8,128)(2,1)} %refs_3_.3) | copy-start | bytes 1572868
  116.6 30.9 %copy-start.8 = (bf16[2,128]{1,0:T(2,128)(2,1)S(1)}, bf16[2,128]{1,0:T(2,128)(2,1)}, u32[]{:S(2)}) copy-start(bf16[2,128]{1,0:T(2,128)(2,1)} %refs_5_.3) | copy-start | bytes 1540
  116.6 30.9 %copy-start.10 = (bf16[2,128]{1,0:T(2,128)(2,1)S(1)}, bf16[2,128]{1,0:T(2,128)(2,1)}, u32[]{:S(2)}) copy-start(bf16[2,128]{1,0:T(2,128)(2,1)} %refs_6_.3) | copy-start | bytes 1540
  116.6 14.9 %collective-permute-start.13 = (bf16[2048,256]{1,0:T(8,128)(2,1)S(1)}, bf16[2048,256]{1,0:T(8,128)(2,1)S(1)}, u32[]{:S(2)}, u32[]{:S(2)}) collective-permute-start(bf16[2048,256]{1,0:T(8,128)(2,1)S(1)} %get-tuple-element.206), channel_id=1, source_target_pairs={{0,2},{1,9},{2,0},{3,11},{4,6},{5,13},{6,4},{7,15},{8,10},{9,1},{1... | collective-permute-start | bytes 3145736 | tf_op jit(solution)/shard_map/ppermute | solution.py:616
  117.5 1.2 collective-permute-start.9
  132.5 11.1 %collective-permute-start.14 = (bf16[1024,256]{1,0:T(8,128)(2,1)S(1)}, bf16[1024,256]{1,0:T(8,128)(2,1)S(1)}, u32[]{:S(2)}, u32[]{:S(2)}) collective-permute-start(bf16[1024,256]{1,0:T(8,128)(2,1)S(1)} %get-tuple-element.209), channel_id=1, source_target_pairs={{0,4},{1,3},{2,6},{3,1},{4,0},{5,7},{6,2},{7,5},{8,12},{9,11},{10,... | collective-permute-start | bytes 1572872 | tf_op jit(solution)/shard_map/ppermute | solution.py:616
  133.1 13.2 %all-to-all-start.7 = ((f32[16,32,128]{2,1,0:T(8,128)}), f32[16,32,128]{2,1,0:T(8,128)S(1)}, u32[]{:S(2)}, u32[]{:S(2)}) async-start(f32[16,32,128]{2,1,0:T(8,128)} %broadcast_in_dim.2), calls=%async_computation.7 | async-start | bytes 524288 | tf_op jit(solution)/shard_map/all_to_all | solution.py:867
  136.7 10.9 %collective-permute-start.10 = (bf16[512,256]{1,0:T(8,128)(2,1)}, bf16[512,256]{1,0:T(8,128)(2,1)S(1)}, u32[]{:S(2)}, u32[]{:S(2)}) collective-permute-start(bf16[512,256]{1,0:T(8,128)(2,1)} %get-tuple-element.195), channel_id=1, source_target_pairs={{0,1},{1,0},{2,3},{3,2},{4,5},{5,4},{6,7},{7,6},{8,9},{9,8},{10,11... | collective-permute-start | bytes 786440 | tf_op jit(solution)/shard_map/ppermute | solution.py:578
  146.3 6.4 %collective-permute-start.15 = (bf16[512,256]{1,0:T(8,128)(2,1)S(1)}, bf16[512,256]{1,0:T(8,128)(2,1)S(1)}, u32[]{:S(2)}, u32[]{:S(2)}) collective-permute-start(bf16[512,256]{1,0:T(8,128)(2,1)S(1)} %get-tuple-element.212), channel_id=1, source_target_pairs={{0,8},{1,5},{2,10},{3,7},{4,12},{5,1},{6,14},{7,3},{8,0},{9,13},{1... | collective-permute-start | bytes 786440 | tf_op jit(solution)/shard_map/ppermute | solution.py:616
  152.8 7.9 %collective-permute-start.16 = (bf16[256,256]{1,0:T(8,128)(2,1)S(1)}, bf16[256,256]{1,0:T(8,128)(2,1)S(1)}, u32[]{:S(2)}, u32[]{:S(2)}) collective-permute-start(bf16[256,256]{1,0:T(8,128)(2,1)S(1)} %get-tuple-element.215), channel_id=1, source_target_pairs={{0,16},{1,17},{2,18},{3,19},{4,20},{5,21},{6,22},{7,23},{8,24},{9,... | collective-permute-start | bytes 393224 | tf_op jit(solution)/shard_map/ppermute | solution.py:616
  160.8 6.9 %collective-permute-start.17 = (bf16[256,256]{1,0:T(8,128)(2,1)S(1)}, bf16[256,256]{1,0:T(8,128)(2,1)S(1)}, u32[]{:S(2)}, u32[]{:S(2)}) collective-permute-start(bf16[256,256]{1,0:T(8,128)(2,1)S(1)} %add_convert_fusion), channel_id=1, source_target_pairs={{0,16},{1,17},{2,18},{3,19},{4,20},{5,21},{6,22},{7,23},{8,24},{9,... | collective-permute-start | bytes 393224 | tf_op jit(solution)/shard_map/ppermute | solution.py:616
  167.7 6.4 %collective-permute-start.18 = (bf16[512,256]{1,0:T(8,128)(2,1)S(1)}, bf16[512,256]{1,0:T(8,128)(2,1)S(1)}, u32[]{:S(2)}, u32[]{:S(2)}) collective-permute-start(bf16[512,256]{1,0:T(8,128)(2,1)S(1)} %pad_maximum_fusion.3), channel_id=1, source_target_pairs={{0,8},{1,5},{2,10},{3,7},{4,12},{5,1},{6,14},{7,3},{8,0},{9,13},{1... | collective-permute-start | bytes 786440 | tf_op jit(solution)/shard_map/ppermute | solution.py:616
  174.3 9.9 %collective-permute-start.19 = (bf16[1024,256]{1,0:T(8,128)(2,1)S(1)}, bf16[1024,256]{1,0:T(8,128)(2,1)S(1)}, u32[]{:S(2)}, u32[]{:S(2)}) collective-permute-start(bf16[1024,256]{1,0:T(8,128)(2,1)S(1)} %pad_maximum_fusion.2), channel_id=1, source_target_pairs={{0,4},{1,3},{2,6},{3,1},{4,0},{5,7},{6,2},{7,5},{8,12},{9,11},{10,... | collective-permute-start | bytes 1572872 | tf_op jit(solution)/shard_map/ppermute | solution.py:616
  177.0 8.0 %copy-start.16 = (bf16[512,256]{1,0:T(8,128)(2,1)S(1)}, bf16[512,256]{1,0:T(8,128)(2,1)}, u32[]{:S(2)}) copy-start(bf16[512,256]{1,0:T(8,128)(2,1)} %copy-done.15) | copy-start | bytes 786436
  184.4 14.9 %collective-permute-start.20 = (bf16[2048,256]{1,0:T(8,128)(2,1)S(1)}, bf16[2048,256]{1,0:T(8,128)(2,1)S(1)}, u32[]{:S(2)}, u32[]{:S(2)}) collective-permute-start(bf16[2048,256]{1,0:T(8,128)(2,1)S(1)} %pad_maximum_fusion.refs_0_), channel_id=1, source_target_pairs={{0,2},{1,9},{2,0},{3,11},{4,6},{5,13},{6,4},{7,15},{8,10},{9,1},{1... | collective-permute-start | bytes 3145736 | tf_op jit(solution)/shard_map/ppermute | solution.py:616

commit v3 on v2

--- a/solution.py
+++ b/solution.py
@@ -11,6 +11,7 @@
 norm_eps = 1e-05
 CHUNKS = 8
 SLAB = 2 * CHUNKS
+TILE = 256
 
 
 def mm(a, b):
@@ -188,18 +189,9 @@
     return lax.axis_index("seq"), lax.axis_index("state")
 
 
-def prep_kernel(peers, steps, pos, tokens, gain, bias, skip, rate_log, angle_log, stats, small, keep, dk, perm):
-    seq, core = place()
-    rows, span, _ = tokens.shape
-    docs = pos.shape[1]
-
-    count = perm.shape[0]
-    p = lax.broadcasted_iota(jnp.int32, (count, count), 0)
-    q = lax.broadcasted_iota(jnp.int32, (count, count), 1)
-    source = ((p >> 3) & 1) * span + (p & 7) * steps + (p >> 4)
-    perm[...] = jnp.where(q == source, 1.0, 0.0).astype(bf16)
+def stats_kernel(tokens, stats):
     s1 = s2 = 0.0
-    for r in range(rows):
+    for r in range(tokens.shape[0]):
         x = tokens[r].astype(f32)
         s1 = s1 + jnp.sum(x, axis=0, keepdims=True)
         s2 = s2 + jnp.sum(x * x, axis=0, keepdims=True)
@@ -208,15 +200,27 @@
         stats[0, 2 + i : 3 + i, :] = s2[:, 128 * i : 128 * (i + 1)]
     stats[...] = jnp.broadcast_to(stats[0][None], stats.shape)
 
+
+def prep_kernel(peers, steps, span, pos, raw, small, keep, dk, perm):
+    seq, core = place()
+    docs = pos.shape[1]
+
+    count = perm.shape[1]
+    p = lax.broadcasted_iota(jnp.int32, (count, count), 0)
+    q = lax.broadcasted_iota(jnp.int32, (count, count), 1)
+    source = ((p >> 3) & 1) * span + (p & 7) * steps + (p >> 4)
+    perm[0] = jnp.where(q == source, 1.0, 0.0).astype(bf16)
+    source = ((q >> 3) & 1) * span + (q & 7) * steps + (q >> 4)
+    perm[1] = jnp.where(p == source, 1.0, 0.0).astype(bf16)
+
     small[...] = jnp.zeros_like(small)
     for k in range(2):
         at = 16 * k
-        for j, ref in enumerate((gain, bias, skip)):
-            v = ref[...].astype(f32)
-            small[at + 2 * j : at + 2 * j + 1, :] = v[k : k + 1, :128]
-            small[at + 2 * j + 1 : at + 2 * j + 2, :] = v[k : k + 1, 128:]
-        rate = jnp.exp(rate_log[...].astype(f32)[k : k + 1, :])
-        angle = jnp.exp(angle_log[...].astype(f32)[k : k + 1, :])
+        values = raw[k : k + 1, :]
+        for j in range(6):
+            small[at + j : at + j + 1, :] = values[:, 128 * j : 128 * (j + 1)]
+        rate = jnp.exp(values[:, 768:896])
+        angle = jnp.exp(values[:, 896:])
         modulus = jnp.exp(-rate)
         lr, li = modulus * jnp.cos(angle), modulus * jnp.sin(angle)
         small[at + 6 : at + 7, :] = lr
@@ -302,12 +306,10 @@
     total = jnp.concatenate([sums[0, 0:1], sums[0, 1:2], sums[1, 0:1], sums[1, 1:2]], axis=1)
     squares = jnp.concatenate([sums[0, 2:3], sums[0, 3:4], sums[1, 2:3], sums[1, 3:4]], axis=1)
     norm_rows(total, squares, count, core, own, oth, 0, nrm)
-    xp[:, own_cols(core, 256)] = mm(perm[...], flat_rows(x_own)).astype(bf16)
-    xp[:, oth_cols(core, 256)] = mm(perm[...], flat_rows(x_oth)).astype(bf16)
+    xp[:, own_cols(core, 256)] = mm(perm[0], flat_rows(x_own)).astype(bf16)
+    xp[:, oth_cols(core, 256)] = mm(perm[0], flat_rows(x_oth)).astype(bf16)
     _, normed = normalized(xp[...].astype(f32), nrm)
-    xp.send()
     nl[...] = normed.astype(bf16)
-    nl.send()
     project_and_scan(steps, 0, 0, False, own, oth, keep, win_own, win_oth, nl, proj, comp, summ, packed)
 
 
@@ -348,42 +350,39 @@
                 sl[s * SLAB : (s + 1) * SLAB, cols(half, im)] = both.astype(bf16)
 
     scan(drive, lams, keep, which, steps, reverse, start, visit)
-    send(sl)
-
-
-def send(ref):
-    if isinstance(ref, Drained):
-        ref.send()
 
 
 def mix_and_gate(core, x, nrm, sl, wout_own, wout_oth, lin_own, lin_oth, gate_own, gate_oth, gp, act, sig, qv, y):
-    _, normed = normalized(x[...].astype(f32), nrm)
-    mixed = mm(sl[:, :256], wout_own[...]) + mm(sl[:, 256:], wout_oth[...]) + nrm[4:5, :] * normed
     c = 0.7978845608028654
-    sq = mixed * mixed
-    t = jnp.tanh(c * (mixed + 0.044715 * sq * mixed))
-    act[...] = (0.5 * mixed * (1.0 + t)).astype(bf16)
-    send(act)
-    gp[...] = (0.5 * (1.0 + t) + 0.5 * mixed * (1.0 - t * t) * (c * (1.0 + 3 * 0.044715 * sq))).astype(gp.dtype)
-    send(gp)
-    for w_lin, w_gate, at in ((lin_own, gate_own, own_cols(core, 256)), (lin_oth, gate_oth, oth_cols(core, 256))):
-        linear = mm(act[...], w_lin[...])
-        gating = mm(act[...], w_gate[...])
-        sg = 0.5 + 0.5 * jnp.tanh(0.5 * gating)
-        out = linear * sg
-        sig[:, at] = sg.astype(sig.dtype)
-        qv[:, at] = (out * (1.0 - sg)).astype(qv.dtype)
-        y[:, at] = x[:, at].astype(f32) + out
-    send(sig)
-    send(qv)
+    for i in range(0, y.shape[0], TILE):
+        rows = slice(i, i + TILE)
+        _, normed = normalized(x[rows, :].astype(f32), nrm)
+        mixed = mm(sl[rows, :256], wout_own[...]) + mm(sl[rows, 256:], wout_oth[...]) + nrm[4:5, :] * normed
+        sq = mixed * mixed
+        t = jnp.tanh(mixed * (c + (c * 0.044715) * sq))
+        upper = 0.5 + 0.5 * t
+        low = (mixed * upper).astype(bf16)
+        act[rows, :] = low
+        gp[rows, :] = (upper + mixed * (upper * (1.0 - t)) * (c + (3 * c * 0.044715) * sq)).astype(gp.dtype)
+        for w_lin, w_gate, at in ((lin_own, gate_own, own_cols(core, 256)), (lin_oth, gate_oth, oth_cols(core, 256))):
+            linear = mm(low, w_lin[...])
+            gating = mm(low, w_gate[...])
+            sg = 0.5 + 0.5 * jnp.tanh(0.5 * gating)
+            out = linear * sg
+            sig[rows, at] = sg.astype(sig.dtype)
+            qv[rows, at] = (out * (1.0 - sg)).astype(qv.dtype)
+            y[rows, at] = x[rows, at].astype(f32) + out
+        yield rows
 
 
 def leave_first_kernel(peers, steps, got, comp, dk, own, oth, keep, proj, x, nrm, wout_own, wout_oth,
                        lin_own, lin_oth, gate_own, gate_oth, cin, sl, gp, act, sig, qv, y, stats, packed, held):
     states_of(peers, steps, 0, 0, False, got, comp, dk, own, oth, keep, proj, cin, sl, packed, held)
-    mix_and_gate(place()[1], x, nrm, sl, wout_own, wout_oth, lin_own, lin_oth, gate_own, gate_oth, gp, act, sig, qv, y)
-    out = y[...]
-    pack_two(jnp.sum(out, axis=0, keepdims=True), jnp.sum(out * out, axis=0, keepdims=True), packed)
+    s1 = s2 = 0.0
+    for rows in mix_and_gate(place()[1], x, nrm, sl, wout_own, wout_oth, lin_own, lin_oth, gate_own, gate_oth, gp, act, sig, qv, y):
+        out = y[rows, :]
+        s1, s2 = s1 + jnp.sum(out, axis=0, keepdims=True), s2 + jnp.sum(out * out, axis=0, keepdims=True)
+    pack_two(s1, s2, packed)
     spread(stats, packed)
 
 
@@ -395,17 +394,23 @@
 
 def glu_backward(steps, base, adj_which, adj_reverse, core, d_out, nrm, x, gp, sig, qv, own, oth, keep, wout_own, wout_oth,
                  lin_own, lin_oth, gate_own, gate_oth, skip_row, dst, comp, summ, packed, dl, dg, dml):
-    dl[...] = (d_out * sig[...].astype(f32)).astype(bf16)
-    dg[...] = (d_out * qv[...].astype(f32)).astype(bf16)
     mine, other = own_cols(core, 256), oth_cols(core, 256)
-    d_active = (mm_nt(dl[:, mine], lin_own[...]) + mm_nt(dg[:, mine], gate_own[...])
-                + mm_nt(dl[:, other], lin_oth[...]) + mm_nt(dg[:, other], gate_oth[...]))
-    d_mixed = d_active * gp[...].astype(f32)
-    _, normed = normalized(x[...].astype(f32), nrm)
-    skip_row[0:1, :] = jnp.sum(d_mixed * normed, axis=0, keepdims=True)
-    dml[...] = d_mixed.astype(bf16)
-    dst[:, :256] = mm_nt(dml[...], wout_own[...])
-    dst[:, 256:] = mm_nt(dml[...], wout_oth[...])
+    total = 0.0
+    for i in range(0, dl.shape[0], TILE):
+        rows = slice(i, i + TILE)
+        grad = d_out(rows)
+        dl[rows, :] = (grad * sig[rows, :].astype(f32)).astype(bf16)
+        dg[rows, :] = (grad * qv[rows, :].astype(f32)).astype(bf16)
+        d_active = (mm_nt(dl[rows, mine], lin_own[...]) + mm_nt(dg[rows, mine], gate_own[...])
+                    + mm_nt(dl[rows, other], lin_oth[...]) + mm_nt(dg[rows, other], gate_oth[...]))
+        d_mixed = d_active * gp[rows, :].astype(f32)
+        _, normed = normalized(x[rows, :].astype(f32), nrm)
+        total = total + jnp.sum(d_mixed * normed, axis=0, keepdims=True)
+        low = d_mixed.astype(bf16)
+        dml[rows, :] = low
+        dst[rows, :256] = mm_nt(low, wout_own[...])
+        dst[rows, 256:] = mm_nt(low, wout_oth[...])
+    skip_row[0:1, :] = total
     lams = decay(own, oth, base, 6, conj=True)
 
     def drive(s, row, half):
@@ -419,19 +424,20 @@
 def mixer_grads(act, dl, dg, sl, dml, g_own, g_oth):
     _, core = place()
     mine, other = own_cols(core, 256), oth_cols(core, 256)
-    g_own[0:512, :] = mm_tn(act[...], dl[:, mine])
-    g_oth[0:512, :] = mm_tn(act[...], dl[:, other]).astype(bf16)
-    g_own[512:1024, :] = mm_tn(act[...], dg[:, mine])
-    g_oth[512:1024, :] = mm_tn(act[...], dg[:, other]).astype(bf16)
-    out_grad = mm_tn(sl[...], dml[...])
-    for i in range(2):
-        g_own[1024 + 256 * i : 1280 + 256 * i, :] = out_grad[:256, 256 * i : 256 * (i + 1)]
-        g_oth[1024 + 256 * i : 1280 + 256 * i, :] = out_grad[256:, 256 * i : 256 * (i + 1)].astype(bf16)
+    left = act[...].T
+    for ref, at in ((dl, 0), (dg, 512)):
+        g_own[at : at + 512, :] = mm(left, ref[:, mine])
+        g_oth[at : at + 512, :] = mm(left, ref[:, other]).astype(bf16)
+    for ref, cut in ((g_own, slice(0, 256)), (g_oth, slice(256, 512))):
+        left = sl[:, cut].T
+        for i in range(2):
+            ref[1024 + 256 * i : 1280 + 256 * i, :] = mm(left, dml[:, 256 * i : 256 * (i + 1)]).astype(ref.dtype)
 
 
 def in_grads(nl, dp, g_own, g_oth):
-    g_own[...] = mm_tn(nl[...], dp[:, :256])
-    g_oth[...] = mm_tn(nl[...], dp[:, 256:]).astype(bf16)
+    left = nl[...].T
+    g_own[...] = mm(left, dp[:, :256])
+    g_oth[...] = mm(left, dp[:, 256:]).astype(bf16)
 
 
 def turn_kernel(peers, steps, got, comp_in, dk, own, oth, keep, proj, x, nrm, wout_own, wout_oth,
@@ -440,22 +446,18 @@
                 packed, held, gp, sig, qv, y):
     _, core = place()
     states_of(peers, steps, 16, 1, True, got, comp_in, dk, own, oth, keep, proj, cin, sl, packed, held)
-    mix_and_gate(core, x, nrm, sl, wout_own, wout_oth, lin_own, lin_oth, gate_own, gate_oth, gp, act, sig, qv, y)
-    low = y[...].astype(bf16)
-    natural = mm_tn(perm[...], low)
-    y[...] = natural
-    bo_own[...] = y[:, own_cols(core, 256)].astype(bf16)
-    bo_oth[...] = y[:, oth_cols(core, 256)].astype(bf16)
-    send(bo_own)
-    send(bo_oth)
-    d_out[:, own_cols(core, 256)] = mm(perm[...], flat_rows(cot_own)).astype(bf16)
-    d_out[:, oth_cols(core, 256)] = mm(perm[...], flat_rows(cot_oth)).astype(bf16)
-    glu_backward(steps, 16, 0, False, core, d_out[...].astype(f32), nrm, x, gp, sig, qv, own, oth, keep, wout_own, wout_oth,
+    for _ in mix_and_gate(core, x, nrm, sl, wout_own, wout_oth, lin_own, lin_oth, gate_own, gate_oth, gp, act, sig, qv, y):
+        pass
+    bo_own[...] = mm(perm[1], y[:, own_cols(core, 256)].astype(bf16)).astype(bf16)
+    bo_oth[...] = mm(perm[1], y[:, oth_cols(core, 256)].astype(bf16)).astype(bf16)
+    d_out[:, own_cols(core, 256)] = mm(perm[0], flat_rows(cot_own)).astype(bf16)
+    d_out[:, oth_cols(core, 256)] = mm(perm[0], flat_rows(cot_oth)).astype(bf16)
+    glu_backward(steps, 16, 0, False, core, lambda rows: d_out[rows, :].astype(f32), nrm, x, gp, sig, qv, own, oth, keep, wout_own, wout_oth,
                  lin_own, lin_oth, gate_own, gate_oth, skip_row, dst, comp, summ, packed, dl, dg, dml)
 
 
 def adjoint_part(peers, steps, base, keep_which, adj_which, adj_reverse, got, comp, dk, own, oth, keep, nl, x, nrm,
-                 cin, sl, dst, dml, win_own, win_oth, skip_row, small_own, small_oth, at, packed, held, proj, dp):
+                 cin, sl, dst, dml, win_own, win_oth, skip_row, small_own, small_oth, at, packed, held, proj, dp, keep_tile):
     _, core = place()
     device_carry(place()[0], peers, got, held, dk, adj_which, own, oth, base, True, adj_reverse, packed)
     start = entries(comp, packed)
@@ -490,10 +492,14 @@
 
     scan(drive, lams, keep, adj_which, steps, adj_reverse, start, visit)
 
-    d_normed = dml[...].astype(f32) * nrm[4:5, :] + mm_nt(dp[:, :256], win_own[...]) + mm_nt(dp[:, 256:], win_oth[...])
-    xhat, _ = normalized(x[...].astype(f32), nrm)
-    bias_row = jnp.sum(d_normed, axis=0, keepdims=True)
-    gain_row = jnp.sum(d_normed * xhat, axis=0, keepdims=True)
+    bias_row = gain_row = 0.0
+    for i in range(0, dp.shape[0], TILE):
+        rows = slice(i, i + TILE)
+        d_normed = dml[rows, :].astype(f32) * nrm[4:5, :] + mm_nt(dp[rows, :256], win_own[...]) + mm_nt(dp[rows, 256:], win_oth[...])
+        xhat, _ = normalized(x[rows, :].astype(f32), nrm)
+        bias_row = bias_row + jnp.sum(d_normed, axis=0, keepdims=True)
+        gain_row = gain_row + jnp.sum(d_normed * xhat, axis=0, keepdims=True)
+        keep_tile(rows, d_normed)
     pack_two(bias_row, gain_row, packed)
 
     for ref, half, flip in ((small_own, 0, 0), (small_oth, 1, 1)):
@@ -505,13 +511,15 @@
             ref[at + 2 * j + 1 : at + 2 * j + 2, :] = pick[:, 128:]
         for j in range(3):
             ref[at + 6 + j : at + 7 + j, :] = jnp.sum(acc[half][j], axis=0, keepdims=True)
-    return d_normed
 
 
 def adjoint_second_kernel(peers, steps, got, comp, dk, own, oth, keep, nl, x, nrm, cin, sl, dst, dml, win_own, win_oth, skip_row, act, dl, dg,
                           g_own, g_oth, small_own, small_oth, dn, stats, packed, held, proj, dp):
-    dn[...] = adjoint_part(peers, steps, 16, 1, 0, False, got, comp, dk, own, oth, keep, nl, x, nrm,
-                           cin, sl, dst, dml, win_own, win_oth, skip_row, small_own, small_oth, 0, packed, held, proj, dp)
+    def keep_tile(rows, d_normed):
+        dn[rows, :] = d_normed
+
+    adjoint_part(peers, steps, 16, 1, 0, False, got, comp, dk, own, oth, keep, nl, x, nrm,
+                 cin, sl, dst, dml, win_own, win_oth, skip_row, small_own, small_oth, 0, packed, held, proj, dp, keep_tile)
     spread(stats, packed)
     mixer_grads(act, dl, dg, sl, dml, g_own, g_oth)
     in_grads(nl, dp, g_own.at[1536:], g_oth.at[1536:])
@@ -522,10 +530,14 @@
                       act, sl, d_out, dml, g_own, g_oth, skip_row, dst, comp, summ, packed, dl, dg):
     sums = sum_peers(got)
     bias_row, gain_row = row_of_tiles(sums[0:4]), row_of_tiles(sums[4:8])
-    xhat, _ = normalized(x2[...], nrm2)
-    gain = nrm2[2:3, :]
-    d_in = d_out2[...].astype(f32) + nrm2[1:2, :] * (dn[...] * gain - gain * bias_row / count - xhat * (gain * gain_row / count))
-    d_out[...] = d_in
+    mean, inv, gain = nrm2[0:1, :], nrm2[1:2, :], nrm2[2:3, :]
+    scaled, shift, slope = inv * gain, inv * gain * bias_row / count, inv * inv * gain * gain_row / count
+
+    def d_in(rows):
+        value = d_out2[rows, :].astype(f32) + scaled * dn[rows, :] - shift - slope * (x2[rows, :] - mean)
+        d_out[rows, :] = value
+        return value
+
     glu_backward(steps, 0, 1, True, place()[1], d_in, nrm, x, gp, sig, qv, own, oth, keep, wout_own, wout_oth,
                  lin_own, lin_oth, gate_own, gate_oth, skip_row, dst, comp, summ, packed, dl, dg, dml)
     mixer_grads(act, dl, dg, sl, dml, g_own, g_oth)
@@ -535,18 +547,21 @@
                          d_out, perm, small1_own, small1_oth,
                          g_own, g_oth, small_own, small_oth, a_own, a_oth, packed, held, proj, tmp, dp):
     _, core = place()
-    d_normed = adjoint_part(peers, steps, 0, 0, 1, True, got, comp, dk, own, oth, keep, nl, x, nrm,
-                            cin, sl, dst, dml, win_own, win_oth, skip_row, small_own, small_oth, 0, packed, held, proj, dp)
+    scaled = nrm[1:2, :] * nrm[2:3, :]
+
+    def keep_tile(rows, d_normed):
+        tmp[rows, :] = (d_out[rows, :] + scaled * d_normed).astype(bf16)
+
+    adjoint_part(peers, steps, 0, 0, 1, True, got, comp, dk, own, oth, keep, nl, x, nrm,
+                 cin, sl, dst, dml, win_own, win_oth, skip_row, small_own, small_oth, 0, packed, held, proj, dp, keep_tile)
     small_own[16:32, :] = small1_own[...]
     small_oth[16:32, :] = small1_oth[...]
-    partial = d_out[...] + nrm[1:2, :] * nrm[2:3, :] * d_normed
-    tmp[...] = mm_tn(perm[...], partial.astype(bf16))
-    a_own[...] = tmp[:, own_cols(core, 256)].astype(bf16)
-    a_oth[...] = tmp[:, oth_cols(core, 256)].astype(bf16)
+    a_own[...] = mm(perm[1], tmp[:, own_cols(core, 256)]).astype(bf16)
+    a_oth[...] = mm(perm[1], tmp[:, oth_cols(core, 256)]).astype(bf16)
     in_grads(nl, dp, g_own, g_oth)
 
 
-def finish_kernel(count, got, a_mine, a_other, tokens, nrm, rate_log, angle_log,
+def finish_kernel(count, got, a_mine, a_other, tokens, nrm, raw,
                   d_in, ngg, bias, skip, rate_grad, angle_grad, packed):
     _, core = place()
     packed[...] = sum_peers(got)
@@ -555,8 +570,9 @@
         for ref, j in ((skip, 0), (bias, 2), (ngg, 4)):
             ref[k : k + 1, :128] = packed[at + j : at + j + 1, :]
             ref[k : k + 1, 128:] = packed[at + j + 1 : at + j + 2, :]
-        rate = jnp.exp(rate_log[...].astype(f32)[k : k + 1, :])
-        angle = jnp.exp(angle_log[...].astype(f32)[k : k + 1, :])
+        values = raw[k : k + 1, :]
+        rate = jnp.exp(values[:, 768:896])
+        angle = jnp.exp(values[:, 896:])
         modulus = jnp.exp(-rate)
         scale = jnp.sqrt(1.0 - modulus * modulus)
         cos, sin = jnp.cos(angle), jnp.sin(angle)
@@ -642,61 +658,88 @@
         out[...] = (held[rows, :].astype(f32) + got[rows, :].astype(f32)).astype(bf16)
 
 
+def axes_orders(*orders):
+    masks, m = [], 1
+    while m < lax.axis_size("seq"):
+        masks.append(m)
+        m *= 2
+    return list(zip(*[[masks[i] for i in o] + masks[4:] for o in orders]))
+
+
 class SeqSum:
-    def __init__(self, pairs):
-        masks, m = [], 1
-        while m < lax.axis_size("seq"):
-            masks.append(m)
-            m *= 2
-        self.masks = list(zip(masks, masks[2:3] + masks[:2] + masks[3:]))
+    def __init__(self, pairs, masks):
+        self.masks, self.at = masks, 0
         rows = sum(a.shape[0] for a, _ in pairs) // 2
         shape = ((rows, pairs[0][0].shape[1]), bf16)
         flat = tuple(v for p in pairs for v in p)
 
         def kernel(refs, mine, other):
-            first_halves_kernel(self.masks[0], [(refs[i], refs[i + 1]) for i in range(0, len(refs), 2)], mine, other)
-
-        self.mine, self.other = run(kernel, [shape, shape], (flat,))
-
-    def down(self, beside):
-        masks = self.masks
-        for i, now in enumerate(masks):
-            if i < len(beside):
-                self.other = tie(self.other, beside[i]())[0]
-            got = partners(self.other, now)
-            if i + 1 < len(masks):
+            first_halves_kernel(masks[0], [(refs[i], refs[i + 1]) for i in range(0, len(refs), 2)], mine, other)
+
+        self.mine, self.send = run(kernel, [shape, shape], (flat,))
+
+    def step(self):
+        count, i = len(self.masks), self.at
+        self.at += 1
+        if i + 1 < count:
+            got = partners(self.send, self.masks[i])
+            if i + 2 < count:
                 shape = ((got.shape[0] // 2, got.shape[1]), bf16)
-                self.mine, self.other = run(functools.partial(next_halves_kernel, masks[i + 1]), [shape, shape], (self.mine, got))
-        self.value = (self.mine.astype(f32) + got.astype(f32)).astype(bf16)
-
-    def up(self, beside):
-        for i, now in enumerate(self.masks[::-1]):
-            if i < len(beside):
-                self.value = tie(self.value, beside[i]())[0]
-            got = partners(self.value, now)
-            if i + 1 < len(self.masks):
-                bit = bit_of(now)
-                self.value = jnp.concatenate([jnp.where(bit == 0, self.value, got), jnp.where(bit == 0, got, self.value)], axis=0)
-        return self.value, got
-
-
-def unpack_kernel(masks, mine, got, lin, gate, out, entry):
-    bit = bit_of(masks)
-    cut = 1024
-    for ref, which in ((mine, bit), (got, 1 - bit)):
-        def piece(at, rows):
-            return ref[at : at + rows, :].astype(f32)
-
-        @pl.when(which == 0)
-        def _():
-            lin[1], gate[1] = piece(0, 512), piece(512, 512)
-            lin[0], gate[0, :256], entry[0, :256] = piece(cut, 512), piece(cut + 512, 256), piece(cut + 768, 256)
-
-        @pl.when(which == 1)
-        def _():
-            out[1, :, :256], out[1, :, 256:], entry[1] = piece(0, 256), piece(256, 256), piece(512, 512)
-            gate[0, 256:] = piece(cut, 256)
-            out[0, :, :256], out[0, :, 256:], entry[0, 256:] = piece(cut + 256, 256), piece(cut + 512, 256), piece(cut + 768, 256)
+                self.mine, self.send = run(functools.partial(next_halves_kernel, self.masks[i + 1]), [shape, shape], (self.mine, got))
+            else:
+                self.send = (self.mine.astype(f32) + got.astype(f32)).astype(bf16)
+            return False
+        if i + 1 == count:
+            self.send = (self.send.astype(f32) + partners(self.send, self.masks[i]).astype(f32)).astype(bf16)
+            return False
+        mask = self.masks[2 * count - 2 - i]
+        got = partners(self.send, mask)
+        if i + 2 == 2 * count:
+            self.result = (self.send, got)
+            return True
+        bit = bit_of(mask)
+        self.send = jnp.concatenate([jnp.where(bit == 0, self.send, got), jnp.where(bit == 0, got, self.send)], axis=0)
+        return False
+
+    def after(self, values):
+        self.send = tie(self.send, values)[0]
+
+    def before(self, value):
+        value, self.send = tie(value, self.send)
+        return value
+
+
+def unpack_kernel(masks0, masks1, mine0, got0, mine1, got1, lin, gate, out, entry):
+    for k, mine, got, masks in ((0, mine0, got0, masks0), (1, mine1, got1, masks1)):
+        bit = bit_of(masks)
+        for ref, which in ((mine, bit), (got, 1 - bit)):
+
+            def piece(at, rows):
+                return ref[at : at + rows, :].astype(f32)
+
+            def put_entry(at, start, rows):
+                value = piece(at, rows)
+                entry[k, pl.ds(2 * start, rows, stride=2), :] = value[:, :128]
+                entry[k, pl.ds(2 * start + 1, rows, stride=2), :] = value[:, 128:]
+
+            @pl.when(which == 0)
+            def _():
+                lin[k] = piece(0, 512)
+                if k == 1:
+                    gate[1] = piece(512, 512)
+                else:
+                    gate[0, :256] = piece(512, 256)
+                    put_entry(768, 0, 256)
+
+            @pl.when(which == 1)
+            def _():
+                if k == 1:
+                    out[1, :, :256], out[1, :, 256:] = piece(0, 256), piece(256, 256)
+                    put_entry(512, 0, 512)
+                else:
+                    gate[0, 256:] = piece(0, 256)
+                    put_entry(768, 256, 256)
+                    out[0, :, :256], out[0, :, 256:] = piece(256, 256), piece(512, 256)
 
 
 class Far:
@@ -725,39 +768,19 @@
         return self.ref[index]
 
 
-class Drained:
-    def __init__(self, ref, target, sem):
-        self.ref, self.copy, self.sent = ref, pltpu.make_async_copy(ref, target, sem), False
-        self.shape, self.dtype = ref.shape, ref.dtype
-
-    def __getitem__(self, index):
-        return self.ref[index]
-
-    def __setitem__(self, index, value):
-        self.ref[index] = value
-
-    def send(self):
-        if not self.sent:
-            self.copy.start()
-            self.sent = True
-
-
 def run(kernel, outs, groups, scratch=(), limit=24, flops=0):
     args = [a for g in groups for a in (g if isinstance(g, tuple) else (g,))]
     far_in = [i for i, a in enumerate(args) if isinstance(a, Far)]
-    far_out = [i for i, o in enumerate(outs) if len(o) == 3]
     moved = sum(a.value.size * a.value.dtype.itemsize if isinstance(a, Far) else a.size * a.dtype.itemsize for a in args)
 
     def whole(*refs):
         ins, results = list(refs[: len(args)]), list(refs[len(args) : len(args) + len(outs)])
         rest = refs[len(args) + len(outs) :]
         own = rest[: len(scratch)]
-        if far_in or far_out:
+        if far_in:
             buffers, sem = rest[len(scratch) : -1], rest[-1]
         for j, i in enumerate(far_in):
             ins[i] = Held(args[i].source(ins[i]), buffers[j], sem.at[j])
-        for j, i in enumerate(far_out, len(far_in)):
-            results[i] = Drained(buffers[j], results[i], sem.at[j])
         grouped, at = [], 0
         for g in groups:
             if isinstance(g, tuple):
@@ -769,23 +792,18 @@
         kernel(*grouped, *results, *own)
         for i in far_in:
             ins[i].ready()
-        for i in far_out:
-            results[i].send()
-        for i in far_out:
-            results[i].copy.wait()
 
     def space(far):
         return pl.BlockSpec(memory_space=pltpu.HBM if far else pltpu.VMEM)
 
     held = [(pltpu.SMEM if args[i].smem else pltpu.VMEM)(args[i].shape, args[i].value.dtype) for i in far_in]
-    held += [pltpu.VMEM(outs[i][0], outs[i][1]) for i in far_out]
     if held:
         held.append(pltpu.SemaphoreType.DMA((len(held),)))
     return pl.pallas_call(
         whole,
         out_shape=[jax.ShapeDtypeStruct(o[0], o[1]) for o in outs],
         in_specs=[space(isinstance(a, Far)) for a in args],
-        out_specs=[space(len(o) == 3) for o in outs],
+        out_specs=[space(False)] * len(outs),
         scratch_shapes=[pltpu.VMEM(*s) for s in scratch] + held,
         compiler_params=pltpu.CompilerParams(vmem_limit_bytes=limit * 2**20),
         cost_estimate=pl.CostEstimate(flops=flops, bytes_accessed=moved, transcendentals=0),
@@ -801,33 +819,35 @@
     count = float(rows * span * peers)
     packed = ((8, 128), f32)
     one = 2 * n * 512 * 512
-    far = ((n, 512), bf16, "far")
     low = ((n, 512), bf16)
     full = ((n, 512), f32)
 
+    (stats,) = run(stats_kernel, [((2 * peers, 4, 128), f32)], (Far(tokens),))
+    raw, at = 0.0, 0
+    for v in (gain, bias, skip, rate_log, angle_log):
+        raw, at = raw + jnp.pad(v.astype(f32), ((0, 0), (at, 1024 - at - v.shape[1]))), at + v.shape[1]
     w_in = in_proj.reshape(2, 512, 256)
     w_out = out_proj.reshape(2, 256, 512)
     x_oth, cot_oth, in_oth, out_oth, lin_oth, gate_oth = (swap(w) for w in (tokens, cotangent, w_in, w_out, glu_lin, glu_gate))
     enter = [(Far(w_in, k), Far(in_oth, k)) for k in range(2)]
-
-    stats, own, keep, dk, perm = run(
-        functools.partial(prep_kernel, peers, steps),
-        [((2 * peers, 4, 128), f32), ((32, 128), f32), ((2, n, 128), f32), ((2, peers, 8, 128), f32), ((n, n), bf16)],
-        (Far(positions, smem=True),) + tuple(Far(v) for v in (tokens, gain, bias, skip, rate_log, angle_log)))
+    own, keep, dk, perm = run(
+        functools.partial(prep_kernel, peers, steps, span),
+        [((32, 128), f32), ((2, n, 128), f32), ((2, peers, 8, 128), f32), ((2, n, n), bf16)],
+        (Far(positions, smem=True), raw))
     oth = swap(own)
     ordered = ((peers, 8, 128), f32)
 
     for_seq, for_all = ((peers, 8, 128), f32), ((2 * peers, 8, 128), f32)
     scan_outs = [full, ((16, 8, 128), f32), for_seq, ((8, 512), f32)]
     xp, nl0, proj, comp, summ, nrm0 = run(
-        functools.partial(enter_first_kernel, peers, steps, count), [far, far] + scan_outs,
+        functools.partial(enter_first_kernel, peers, steps, count), [low, low] + scan_outs,
         (lax.all_to_all(stats, ("seq", "state"), 0, 0), Far(tokens, "rows"), Far(x_oth, "rows"), perm, own, oth, keep) + enter[0], [packed], flops=2 * one)
     got, (cot_oth, out_oth, lin_oth, gate_oth) = blocking(summ, "seq", (cot_oth, out_oth, lin_oth, gate_oth))
     glu = [tuple(Far(w, k) for w in (w_out, out_oth, glu_lin, lin_oth, glu_gate, gate_oth)) for k in range(2)]
     cin0, sl0, gp0, act0, sig0, qv0, y0, stats = run(
         functools.partial(leave_first_kernel, peers, steps),
-        [((SLAB, 512), f32), far, far, far, far, far, full, for_all],
-        (got, comp, dk, own, oth, keep, proj, Far(xp), nrm0) + glu[0], [packed, ordered], flops=3 * one)
+        [((SLAB, 512), f32), low, low, low, low, low, full, for_all],
+        (got, comp, dk, own, oth, keep, proj, xp, nrm0) + glu[0], [packed, ordered], flops=3 * one)
     got, _ = blocking(stats, ("seq", "state"), ())
     nl1, proj, comp, summ, nrm1 = run(
         functools.partial(enter_second_kernel, peers, steps, count), [low] + scan_outs,
@@ -836,7 +856,7 @@
     turn_outs = [((8, 512), f32), full, ((16, 8, 128), f32)]
     cin1, bo_own, bo_oth, d_out1, act1, dl1, dg1, sl1, dml1, skip1, dst, comp, summ = run(
         functools.partial(turn_kernel, peers, steps),
-        [((SLAB, 512), f32), ((n, 256), bf16, "far"), ((n, 256), bf16, "far"), low, low, low, low, low, low] + turn_outs + [for_seq],
+        [((SLAB, 512), f32), ((n, 256), bf16), ((n, 256), bf16), low, low, low, low, low, low] + turn_outs + [for_seq],
         (got, comp, dk, own, oth, keep, proj, y0, nrm1) + glu[1] + (perm, Far(cotangent, "rows"), Far(cot_oth, "rows")),
         [packed, ordered, full, full, full, full], flops=8 * one)
     got, (bo_oth,) = blocking(summ, "seq", (bo_oth,))
@@ -850,18 +870,20 @@
     d_out0, dml0, g0_own, g0_oth, skip0, dst, comp, summ = run(
         functools.partial(back_first_kernel, steps, count),
         [full, low, ((1536, 256), f32), ((1536, 256), bf16)] + turn_outs + [for_seq],
-        (got, dn, y0, nrm1, d_out1, own, oth, keep, Far(xp), nrm0, Far(gp0), Far(sig0), Far(qv0)) + glu[0] + (Far(act0), Far(sl0)),
+        (got, dn, y0, nrm1, d_out1, own, oth, keep, xp, nrm0, gp0, sig0, qv0) + glu[0] + (act0, sl0),
         [packed, low, low], flops=6 * one)
     got, (g0_oth, bo_got, g1_got) = blocking(summ, "seq", (g0_oth, bo_got, g1_got))
+    bulk1 = SeqSum([(g1_own, g1_got)], axes_orders((0, 1, 2, 3), (1, 0, 2, 3)))
+    got = (bulk1.before(got[0]),)
     g0_got = swap(g0_oth)
     i0_own, i0_oth, s_own, s_oth, a_own, a_oth = run(
         functools.partial(adjoint_first_kernel, peers, steps),
         [((512, 256), f32), ((512, 256), bf16), ((32, 128), f32), ((32, 128), f32), ((n, 256), bf16), ((n, 256), bf16)],
-        (got, comp, dk, own, oth, keep, Far(nl0), Far(xp), nrm0, cin0, Far(sl0), dst, dml0) + enter[0]
+        (got, comp, dk, own, oth, keep, nl0, xp, nrm0, cin0, sl0, dst, dml0) + enter[0]
         + (skip0, d_out0, perm, s1_own, s1_oth),
-        [packed, ordered, full, full, low], flops=4 * one)
+        [packed, ordered, full, low, low], flops=4 * one)
     i0_got = swap(i0_oth)
-    bulk = SeqSum([(g1_own, g1_got), (g0_own, g0_got), (i0_own, i0_got)])
+    bulk0 = SeqSum([(g0_own, g0_got), (i0_own, i0_got)], axes_orders((2, 0, 1, 3), (2, 1, 0, 3)))
     s_got, a_got = swap(s_oth), swap(a_oth)
     s_all = jnp.broadcast_to((s_own + s_got)[None], (peers, 32, 128))
     got = lax.all_to_all(s_all, "seq", 0, 0)
@@ -869,14 +891,22 @@
     d_in, ngg, bias_grad, skip_grad, rate_grad, angle_grad = run(
         functools.partial(finish_kernel, count),
         [((rows, span, width), f32), ((2, 256), f32), ((2, 256), f32), ((2, 256), f32), ((2, 128), f32), ((2, 128), f32)],
-        ((got,), a_own.reshape(pair), a_got.reshape(pair), Far(tokens), nrm0, Far(rate_log), Far(angle_log)),
+        ((got,), a_own.reshape(pair), a_got.reshape(pair), Far(tokens), nrm0, raw),
         [((32, 128), f32)])
-    bulk.down([lambda: (), lambda: s_all, lambda: got, lambda: d_in])
-    mine, other = bulk.up([])
+    while not bulk1.step():
+        pass
+    bulk0.step()
+    bulk0.after(s_all)
+    bulk0.step()
+    bulk0.after(got)
+    bulk0.step()
+    bulk0.after(d_in)
+    while not bulk0.step():
+        pass
     lin_grad, gate_grad, out_grad, in_grad = run(
-        functools.partial(unpack_kernel, bulk.masks[0]),
-        [((2, 512, 256), f32), ((2, 512, 256), f32), ((2, 256, 512), f32), ((2, 512, 256), f32)],
-        (mine, other))
+        functools.partial(unpack_kernel, bulk0.masks[0], bulk1.masks[0]),
+        [((2, 512, 256), f32), ((2, 512, 256), f32), ((2, 256, 512), f32), ((2, 1024, 128), f32)],
+        bulk0.result + bulk1.result)
     out_grad, in_grad = out_grad.reshape(2, 2, 128, 512), in_grad.reshape(2, 512, 2, 128)
     mine, other = bo_own.reshape(pair), bo_got.reshape(pair)
     block_out = jnp.concatenate([jnp.where(core == 0, mine, other), jnp.where(core == 0, other, mine)], axis=0)

time: 203 us -> 173 us (0.85)
  waiting for transfers between devices: 69.5 us -> 46.4 us
  local copies, waits for them, and re-layouts: 9.83 us -> 3.87 us
  Pallas kernels: 32.2 us -> 29.2 us
    ppermute x8 -> x14, waiting for transfers between devices: 64.2 us -> 44.6 us  [partners(): lax.ppermute(value, ('seq', 'state'), [(2 * i + c, 2 * (i ^ masks[c]) + c...]
    unnamed x34 -> x20, local copies, waits for them, and re-layouts: 6.16 us -> 1.77 us
    pallas_call x14 -> x17, Pallas kernels: 32.2 us -> 29.2 us  [run(): pl.pallas_call(whole, out_shape=[jax.ShapeDtypeStruct(o[0], o[1]) for o i...]
    all_to_all x1, waiting for transfers between devices: 2.63 us -> 0.08 us  [body(): got = lax.all_to_all(s_all, 'seq', 0, 0)]
    ppermute x8 -> x14, starting transfers between devices: 6.89 us -> 7.68 us  [partners(): lax.ppermute(value, ('seq', 'state'), [(2 * i + c, 2 * (i ^ masks[c]) + c...]
  transfers between devices with their start and end apart: 22 -> 28, of which waited for: 12 -> 15; matrix products, arithmetic and copies ran while one was open for 1% -> 2% of each run, Pallas kernels for 7% -> 8%
where the time goes in v3:
time: 173 us; the launch traced here: 172 us
  blocking collectives  75.1 us (43%)
  waiting for transfers between devices  46.4 us (27%)
  Pallas kernels  29.2 us (17%)
  starting transfers between devices  14.6 us (8%)
  local copies, waits for them, and re-layouts  3.87 us (2%)
  other arithmetic  2.13 us (1%)
    all_to_all x6, blocking collectives, blocking(): lax.all_to_all(value, axes, 0, 0)  60.7 us
    ppermute x14, waiting for transfers between devices, partners(): lax.ppermute(value, ('seq', 'state'), [(2 * i + c, 2 * (i ^ masks[c]) + c...  44.6 us
    pallas_call x17, Pallas kernels, run(): pl.pallas_call(whole, out_shape=[jax.ShapeDtypeStruct(o[0], o[1]) for o i...  29.2 us
    all_to_all x1, blocking collectives, body(): lax.all_to_all(stats, ('seq', 'state'), 0, 0)  14.4 us
    ppermute x14, starting transfers between devices, partners(): lax.ppermute(value, ('seq', 'state'), [(2 * i + c, 2 * (i ^ masks[c]) + c...  7.68 us
    all_to_all x1, starting transfers between devices, body(): got = lax.all_to_all(s_all, 'seq', 0, 0)  3.53 us
  transfers between devices with their start and end apart: 28, of which 15 were waited for; matrix products, arithmetic and copies ran while one was open for 2% of the time, Pallas kernels for 8%

profile of v3, /device:TPU:0, one launch (start us, length us, event | category | flops | bytes accessed | tf_op | source)
XLA Modules:
  0.0 172.3 jit_solution(1311602694854059885)
XLA Ops:
  0.6 0.5 collective-permute-start
  1.2 1.4 reshape.47.refs_7_.refs_5_.refs_13_
  2.7 0.7 convert_add_fusion.refs_1_.refs_5_
  3.4 0.7 copy-done.6
  4.1 1.4 shard_map.204
  5.5 0.5 collective-permute-start.1
  7.4 1.0 copy-done
  8.6 14.4 %all_to_all.40.refs_0_ = f32[32,4,128]{2,1,0:T(4,128)S(1)} all-to-all(f32[32,4,128]{2,1,0:T(4,128)S(1)} %shard_map.203), channel_id=1, replica_groups=mesh['seq'=16,'state'=2] {'seq','state'}, dimensions={0} | all-to-all | bytes 131072 | tf_op jit(solution)/shard_map/all_to_all | solution.py:844
  23.1 2.1 %shard_map.205 = (bf16[512,512]{1,0:T(8,128)(2,1)S(1)}, bf16[512,512]{1,0:T(8,128)(2,1)S(1)}, f32[512,512]{1,0:T(8,128)S(1)}, f32[16,8,128]{2,1,0:T(8,128)S(1)},...) custom-call(f32[32,4,128]{2,1,0:T(4,128)S(1)} %all_to_all.40.refs_0_, bf16[4,256,256]{2,1,0:T(8,128)(2,1)S(1)} %copy-done, ...), custom_call_target="tpu_custom_call" | custom-call | flops 536870912 | bytes 3768320 | tf_op jit(solution)/shard_map/pallas_call | solution.py:802
  25.2 10.1 %all_to_all.41.refs_0_ = f32[16,8,128]{2,1,0:T(8,128)S(1)} all-to-all(f32[16,8,128]{2,1,0:T(8,128)S(1)} %get-tuple-element.126), channel_id=1, replica_groups=mesh['seq'=16,'state'=2] {'seq'}, dimensions={0} | all-to-all | bytes 131072 | tf_op jit(solution)/shard_map/all_to_all | solution.py:606
  35.3 3.3 %shard_map.206 = (f32[16,512]{1,0:T(8,128)S(1)}, bf16[512,512]{1,0:T(8,128)(2,1)S(1)}, bf16[512,512]{1,0:T(8,128)(2,1)S(1)}, bf16[512,512]{1,0:T(8,128)(2,1)S(1)...) custom-call(f32[16,8,128]{2,1,0:T(8,128)S(1)} %all_to_all.41.refs_0_, ...), custom_call_target="tpu_custom_call" | custom-call | flops 805306368 | bytes 5554176 | tf_op jit(solution)/shard_map/pallas_call | solution.py:802
  38.7 10.1 %all_to_all.42.refs_0_ = f32[32,8,128]{2,1,0:T(8,128)S(1)} all-to-all(f32[32,8,128]{2,1,0:T(8,128)S(1)} %get-tuple-element.140), channel_id=1, replica_groups=mesh['seq'=16,'state'=2] {'seq','state'}, dimensions={0} | all-to-all | bytes 262144 | tf_op jit(solution)/shard_map/all_to_all | solution.py:606
  48.7 1.6 shard_map.207
  50.4 10.2 %all_to_all.43.refs_0_ = f32[16,8,128]{2,1,0:T(8,128)S(1)} all-to-all(f32[16,8,128]{2,1,0:T(8,128)S(1)} %get-tuple-element.142), channel_id=1, replica_groups=mesh['seq'=16,'state'=2] {'seq'}, dimensions={0} | all-to-all | bytes 131072 | tf_op jit(solution)/shard_map/all_to_all | solution.py:606
  60.6 5.9 %shard_map.208 = (f32[16,512]{1,0:T(8,128)S(1)}, bf16[512,256]{1,0:T(8,128)(2,1)S(1)}, bf16[512,256]{1,0:T(8,128)(2,1)S(1)}, bf16[512,512]{1,0:T(8,128)(2,1)S(1)...) custom-call(f32[16,8,128]{2,1,0:T(8,128)S(1)} %all_to_all.43.refs_0_, ...), custom_call_target="tpu_custom_call" | custom-call | flops 2147483648 | bytes 8175616 | tf_op jit(solution)/shard_map/pallas_call | solution.py:802
  66.5 10.1 %all_to_all.44.refs_0_ = f32[16,8,128]{2,1,0:T(8,128)S(1)} all-to-all(f32[16,8,128]{2,1,0:T(8,128)S(1)} %get-tuple-element.150), channel_id=1, replica_groups=mesh['seq'=16,'state'=2] {'seq'}, dimensions={0} | all-to-all | bytes 131072 | tf_op jit(solution)/shard_map/all_to_all | solution.py:606
  76.6 2.8 %shard_map.209 = (f32[2048,256]{1,0:T(8,128)S(1)}, bf16[2048,256]{1,0:T(8,128)(2,1)S(1)}, f32[16,128]{1,0:T(8,128)S(1)}, f32[16,128]{1,0:T(8,128)S(1)}, f32[512,...) custom-call(f32[16,8,128]{2,1,0:T(8,128)S(1)} %all_to_all.44.refs_0_, f32[16,8,128]{2,1,0:T(8,128)S(1)} %get-tuple-element.153.refs_1_, ...), custom_call_target="tpu_custom_call" | custom-call | flops 1610612736 | bytes 7176192 | tf_op jit(solution)/shard_map/pallas_call | solution.py:802
  79.5 9.9 %all_to_all.45.refs_0_ = f32[32,8,128]{2,1,0:T(8,128)S(1)} all-to-all(f32[32,8,128]{2,1,0:T(8,128)S(1)} %get-tuple-element.166), channel_id=1, replica_groups=mesh['seq'=16,'state'=2] {'seq','state'}, dimensions={0} | all-to-all | bytes 262144 | tf_op jit(solution)/shard_map/all_to_all | solution.py:606
  89.9 3.4 %shard_map.210 = (f32[512,512]{1,0:T(8,128)S(1)}, bf16[512,512]{1,0:T(8,128)(2,1)S(1)}, f32[1536,256]{1,0:T(8,128)S(1)}, bf16[1536,256]{1,0:T(8,128)(2,1)S(1)}, ...) custom-call(f32[32,8,128]{2,1,0:T(8,128)S(1)} %all_to_all.45.refs_0_, ...), custom_call_target="tpu_custom_call" | custom-call | flops 1610612736 | bytes 9633792 | tf_op jit(solution)/shard_map/pallas_call | solution.py:802
  93.4 10.2 %all_to_all.46.refs_0_ = f32[16,8,128]{2,1,0:T(8,128)S(1)} all-to-all(f32[16,8,128]{2,1,0:T(8,128)S(1)} %get-tuple-element.181), channel_id=1, replica_groups=mesh['seq'=16,'state'=2] {'seq'}, dimensions={0} | all-to-all | bytes 131072 | tf_op jit(solution)/shard_map/all_to_all | solution.py:606
  103.6 0.9 shard_map.211
  104.5 2.4 %shard_map.212 = (f32[512,256]{1,0:T(8,128)S(1)}, bf16[512,256]{1,0:T(8,128)(2,1)S(1)}, f32[32,128]{1,0:T(8,128)S(1)}, f32[32,128]{1,0:T(8,128)S(1)}, bf16[512,2...) custom-call(f32[16,8,128]{2,1,0:T(8,128)S(1)} %all_to_all.46.refs_0_, f32[16,8,128]{2,1,0:T(8,128)S(1)} %get-tuple-element.191.refs_1_, ...), custom_call_target="tpu_custom_call" | custom-call | flops 1073741824 | bytes 7192576 | tf_op jit(solution)/shard_map/pallas_call | solution.py:802
  107.0 0.6 collective-permute-start.12
  107.5 0.8 collective-permute-start.20
  108.7 0.9 shard_map.214
  109.6 0.7 collective-permute-start.13
  110.4 1.1 collective-permute-done.9
  111.5 0.7 broadcast_in_dim.2
  112.2 3.5 %all-to-all-start.7 = ((f32[16,32,128]{2,1,0:T(8,128)}), f32[16,32,128]{2,1,0:T(8,128)S(1)}, u32[]{:S(2)}, u32[]{:S(2)}) async-start(f32[16,32,128]{2,1,0:T(8,128)} %broadcast_in_dim.2), calls=%async_computation.7 | async-start | bytes 524288 | tf_op jit(solution)/shard_map/all_to_all | solution.py:889
  115.8 1.2 collective-permute-done.20.refs_1_
  117.1 0.7 collective-permute-start.21
  117.8 9.4 %collective-permute-done.13.refs_1_ = bf16[1024,256]{1,0:T(8,128)(2,1)S(1)} collective-permute-done((bf16[1024,256]{1,0:T(8,128)(2,1)}, bf16[1024,256]{1,0:T(8,128)(2,1)S(1)}, u32[]{:S(2)}, u32[]{:S(2)}) %collective-permute-start.13) | collective-permute-done | bytes 524320 | tf_op jit(solution)/shard_map/ppermute | solution.py:632
  127.4 0.9 collective-permute-start.14
  128.6 1.4 shard_map.213
  130.0 3.8 %collective-permute-done.14.refs_1_ = bf16[512,256]{1,0:T(8,128)(2,1)S(1)} collective-permute-done((bf16[512,256]{1,0:T(8,128)(2,1)S(1)}, bf16[512,256]{1,0:T(8,128)(2,1)S(1)}, u32[]{:S(2)}, u32[]{:S(2)}) %collective-permute-start.14) | collective-permute-done | bytes 262176 | tf_op jit(solution)/shard_map/ppermute | solution.py:632
  134.3 4.5 %collective-permute-done.15 = bf16[256,256]{1,0:T(8,128)(2,1)S(1)} collective-permute-done((bf16[256,256]{1,0:T(8,128)(2,1)S(1)}, bf16[256,256]{1,0:T(8,128)(2,1)S(1)}, u32[]{:S(2)}, u32[]{:S(2)}) %collective-permute-start.15) | collective-permute-done | bytes 131104 | tf_op jit(solution)/shard_map/ppermute | solution.py:632
  139.0 5.8 %collective-permute-done.23 = bf16[256,256]{1,0:T(8,128)(2,1)S(1)} collective-permute-done((bf16[256,256]{1,0:T(8,128)(2,1)S(1)}, bf16[256,256]{1,0:T(8,128)(2,1)S(1)}, u32[]{:S(2)}, u32[]{:S(2)}) %collective-permute-start.23) | collective-permute-done | bytes 131104 | tf_op jit(solution)/shard_map/ppermute | solution.py:632
  145.0 1.3 collective-permute-done.16
  146.4 0.8 collective-permute-start.17
  147.2 2.7 %collective-permute-done.24 = bf16[256,256]{1,0:T(8,128)(2,1)S(1)} collective-permute-done((bf16[256,256]{1,0:T(8,128)(2,1)S(1)}, bf16[256,256]{1,0:T(8,128)(2,1)S(1)}, u32[]{:S(2)}, u32[]{:S(2)}) %collective-permute-start.24) | collective-permute-done | bytes 131104 | tf_op jit(solution)/shard_map/ppermute | solution.py:632
  150.0 0.9 collective-permute-start.25
  151.5 1.2 collective-permute-start.18
  152.7 6.6 %collective-permute-done.25 = bf16[512,256]{1,0:T(8,128)(2,1)S(1)} collective-permute-done((bf16[512,256]{1,0:T(8,128)(2,1)S(1)}, bf16[512,256]{1,0:T(8,128)(2,1)S(1)}, u32[]{:S(2)}, u32[]{:S(2)}) %collective-permute-start.25) | collective-permute-done | bytes 262176 | tf_op jit(solution)/shard_map/ppermute | solution.py:632
  159.4 0.8 collective-permute-start.26
  160.6 0.8 pad_maximum_fusion
  161.4 7.3 %collective-permute-done.26.refs_3_ = bf16[1024,256]{1,0:T(8,128)(2,1)S(1)} collective-permute-done((bf16[1024,256]{1,0:T(8,128)(2,1)S(1)}, bf16[1024,256]{1,0:T(8,128)(2,1)S(1)}, u32[]{:S(2)}, u32[]{:S(2)}) %collective-permute-start.26) | collective-permute-done | bytes 524320 | tf_op jit(solution)/shard_map/ppermute | solution.py:632
  168.7 1.3 collective-permute-done.19.refs_1_
  170.0 2.3 %shard_map.219 = (f32[2,512,256]{2,1,0:T(8,128)}, f32[2,512,256]{2,1,0:T(8,128)}, f32[2,256,512]{2,1,0:T(8,128)}, f32[2,1024,128]{2,1,0:T(8,128)}) custom-call(bf16[1024,256]{1,0:T(8,128)(2,1)S(1)} %pad_maximum_fusion.1.refs_0_, bf16[1024,256]{1,0:T(8,128)(2,1)S(1)} %collective-permute-done.19.refs_1_, bf16[1024,256]{1,0:T(8,128)(2,1)S(1)} %pad_maximum_fusion.2.refs_2_, ...), custom_call_target="tpu_custom_call" | custom-call | bytes 2097152 | tf_op jit(solution)/shard_map/pallas_call | solution.py:802
  (70 shorter events, 4.9 us)
Async XLA Ops:
  0.6 6.6 %collective-permute-start = (bf16[4,256,256]{2,1,0:T(8,128)(2,1)}, bf16[4,256,256]{2,1,0:T(8,128)(2,1)S(1)}, u32[]{:S(2)}, u32[]{:S(2)}) collective-permute-start(bf16[4,256,256]{2,1,0:T(8,128)(2,1)} %refs_3_.1), channel_id=1, source_target_pairs={{0,1},{1,0},{2,3},{3,2},{4,5},{5,4},{6,7},{7,6},{8,9},{9,8},{10,11... | collective-permute-start | bytes 1572872 | tf_op jit(solution)/shard_map/ppermute | solution.py:594
  2.5 20.5 %collective-permute-start.2 = (bf16[2,512,256]{2,1,0:T(8,128)(2,1)S(1)}, bf16[2,512,256]{2,1,0:T(8,128)(2,1)S(1)}, u32[]{:S(2)}, u32[]{:S(2)}) collective-permute-start(bf16[2,512,256]{2,1,0:T(8,128)(2,1)S(1)} %reshape.47.refs_7_.refs_5_.refs_13_), channel_id=1, source_target_pairs={{0,1},{1,0},{2,3},{3,2},{4,5},{5,4},{6,7},{7,6},{8,9},{9,8},{10,11... | collective-permute-start | bytes 1572872 | tf_op jit(solution)/shard_map/ppermute | solution.py:594
  3.4 0.7 copy-start.6
  5.5 1.4 collective-permute-start.1
  6.0 19.1 %collective-permute-start.3 = (bf16[4,256,256]{2,1,0:T(8,128)(2,1)}, bf16[4,256,256]{2,1,0:T(8,128)(2,1)S(1)}, u32[]{:S(2)}, u32[]{:S(2)}) collective-permute-start(bf16[4,256,256]{2,1,0:T(8,128)(2,1)} %refs_16_.1), channel_id=1, source_target_pairs={{0,1},{1,0},{2,3},{3,2},{4,5},{5,4},{6,7},{7,6},{8,9},{9,8},{10,11... | collective-permute-start | bytes 1572872 | tf_op jit(solution)/shard_map/ppermute | solution.py:594
  6.1 19.1 %collective-permute-start.4 = (bf16[2,256,512]{2,1,0:T(8,128)(2,1)}, bf16[2,256,512]{2,1,0:T(8,128)(2,1)S(1)}, u32[]{:S(2)}, u32[]{:S(2)}) collective-permute-start(bf16[2,256,512]{2,1,0:T(8,128)(2,1)} %bitcast.7), channel_id=1, source_target_pairs={{0,1},{1,0},{2,3},{3,2},{4,5},{5,4},{6,7},{7,6},{8,9},{9,8},{10,11... | collective-permute-start | bytes 1572872 | tf_op jit(solution)/shard_map/ppermute | solution.py:594
  6.9 18.3 %collective-permute-start.5 = (bf16[2,512,256]{2,1,0:T(8,128)(2,1)}, bf16[2,512,256]{2,1,0:T(8,128)(2,1)S(1)}, u32[]{:S(2)}, u32[]{:S(2)}) collective-permute-start(bf16[2,512,256]{2,1,0:T(8,128)(2,1)} %refs_15_.1), channel_id=1, source_target_pairs={{0,1},{1,0},{2,3},{3,2},{4,5},{5,4},{6,7},{7,6},{8,9},{9,8},{10,11... | collective-permute-start | bytes 1572872 | tf_op jit(solution)/shard_map/ppermute | solution.py:594
  7.2 18.0 %collective-permute-start.6 = (bf16[2,512,256]{2,1,0:T(8,128)(2,1)}, bf16[2,512,256]{2,1,0:T(8,128)(2,1)S(1)}, u32[]{:S(2)}, u32[]{:S(2)}) collective-permute-start(bf16[2,512,256]{2,1,0:T(8,128)(2,1)} %refs_17_.1), channel_id=1, source_target_pairs={{0,1},{1,0},{2,3},{3,2},{4,5},{5,4},{6,7},{7,6},{8,9},{9,8},{10,11... | collective-permute-start | bytes 1572872 | tf_op jit(solution)/shard_map/ppermute | solution.py:594
  7.4 1.0 copy-start
  8.6 26.7 %copy-start.2 = (bf16[2,2,128,512]{3,2,1,0:T(8,128)(2,1)S(1)}, bf16[2,2,128,512]{3,2,1,0:T(8,128)(2,1)}, u32[]{:S(2)}) copy-start(bf16[2,2,128,512]{3,2,1,0:T(8,128)(2,1)} %param.16) | copy-start | bytes 1572868
  8.6 26.7 %copy-start.3 = (bf16[2,512,256]{2,1,0:T(8,128)(2,1)S(1)}, bf16[2,512,256]{2,1,0:T(8,128)(2,1)}, u32[]{:S(2)}) copy-start(bf16[2,512,256]{2,1,0:T(8,128)(2,1)} %refs_15_.1) | copy-start | bytes 1572868
  8.6 26.7 %copy-start.4 = (bf16[2,512,256]{2,1,0:T(8,128)(2,1)S(1)}, bf16[2,512,256]{2,1,0:T(8,128)(2,1)}, u32[]{:S(2)}) copy-start(bf16[2,512,256]{2,1,0:T(8,128)(2,1)} %refs_17_.1) | copy-start | bytes 1572868
  38.7 21.9 %copy-start.5 = (bf16[4,256,256]{2,1,0:T(8,128)(2,1)S(1)}, bf16[4,256,256]{2,1,0:T(8,128)(2,1)}, u32[]{:S(2)}) copy-start(bf16[4,256,256]{2,1,0:T(8,128)(2,1)} %refs_16_.1) | copy-start | bytes 1572868
  89.4 4.0 %collective-permute-start.8 = (bf16[2048,256]{1,0:T(8,128)(2,1)S(1)}, bf16[2048,256]{1,0:T(8,128)(2,1)S(1)}, u32[]{:S(2)}, u32[]{:S(2)}) collective-permute-start(bf16[2048,256]{1,0:T(8,128)(2,1)S(1)} %get-tuple-element.180), channel_id=1, source_target_pairs={{0,1},{1,0},{2,3},{3,2},{4,5},{5,4},{6,7},{7,6},{8,9},{9,8},{10,11... | collective-permute-start | bytes 3145736 | tf_op jit(solution)/shard_map/ppermute | solution.py:594
  89.6 3.7 %collective-permute-start.7 = (bf16[512,256]{1,0:T(8,128)(2,1)S(1)}, bf16[512,256]{1,0:T(8,128)(2,1)S(1)}, u32[]{:S(2)}, u32[]{:S(2)}) collective-permute-start(bf16[512,256]{1,0:T(8,128)(2,1)S(1)} %get-tuple-element.179), channel_id=1, source_target_pairs={{0,1},{1,0},{2,3},{3,2},{4,5},{5,4},{6,7},{7,6},{8,9},{9,8},{10,11... | collective-permute-start | bytes 786440 | tf_op jit(solution)/shard_map/ppermute | solution.py:594
  93.3 13.6 %copy-start.8 = (bf16[512,256]{1,0:T(8,128)(2,1)}, bf16[512,256]{1,0:T(8,128)(2,1)S(1)}, u32[]{:S(2)}) copy-start(bf16[512,256]{1,0:T(8,128)(2,1)S(1)} %collective-permute-done.7) | copy-start | bytes 786436
  103.6 5.1 %collective-permute-start.11 = (bf16[1536,256]{1,0:T(8,128)(2,1)S(1)}, bf16[1536,256]{1,0:T(8,128)(2,1)S(1)}, u32[]{:S(2)}, u32[]{:S(2)}) collective-permute-start(bf16[1536,256]{1,0:T(8,128)(2,1)S(1)} %get-tuple-element.208), channel_id=1, source_target_pairs={{0,1},{1,0},{2,3},{3,2},{4,5},{5,4},{6,7},{7,6},{8,9},{9,8},{10,11... | collective-permute-start | bytes 2359304 | tf_op jit(solution)/shard_map/ppermute | solution.py:594
  106.9 4.6 %copy-start.7 = (bf16[512,256]{1,0:T(8,128)(2,1)}, bf16[512,256]{1,0:T(8,128)(2,1)S(1)}, u32[]{:S(2)}) copy-start(bf16[512,256]{1,0:T(8,128)(2,1)S(1)} %get-tuple-element.203) | copy-start | bytes 786436
  107.0 1.8 %collective-permute-start.12 = (bf16[512,256]{1,0:T(8,128)(2,1)S(1)}, bf16[512,256]{1,0:T(8,128)(2,1)S(1)}, u32[]{:S(2)}, u32[]{:S(2)}) collective-permute-start(bf16[512,256]{1,0:T(8,128)(2,1)S(1)} %get-tuple-element.210), channel_id=1, source_target_pairs={{0,1},{1,0},{2,3},{3,2},{4,5},{5,4},{6,7},{7,6},{8,9},{9,8},{10,11... | collective-permute-start | bytes 786440 | tf_op jit(solution)/shard_map/ppermute | solution.py:594
  107.5 9.4 %collective-permute-start.20 = (bf16[1024,256]{1,0:T(8,128)(2,1)}, bf16[1024,256]{1,0:T(8,128)(2,1)S(1)}, u32[]{:S(2)}, u32[]{:S(2)}) collective-permute-start(bf16[1024,256]{1,0:T(8,128)(2,1)} %get-tuple-element.221), channel_id=1, source_target_pairs={{0,2},{1,5},{2,0},{3,7},{4,6},{5,1},{6,4},{7,3},{8,10},{9,13},{10,... | collective-permute-start | bytes 1572872 | tf_op jit(solution)/shard_map/ppermute | solution.py:632
  109.6 18.9 %copy-start.1 = (bf16[4,256,256]{2,1,0:T(8,128)(2,1)S(1)}, bf16[4,256,256]{2,1,0:T(8,128)(2,1)}, u32[]{:S(2)}) copy-start(bf16[4,256,256]{2,1,0:T(8,128)(2,1)} %refs_3_.1) | copy-start | bytes 1572868
  109.6 17.6 %collective-permute-start.13 = (bf16[1024,256]{1,0:T(8,128)(2,1)}, bf16[1024,256]{1,0:T(8,128)(2,1)S(1)}, u32[]{:S(2)}, u32[]{:S(2)}) collective-permute-start(bf16[1024,256]{1,0:T(8,128)(2,1)} %get-tuple-element.212), channel_id=1, source_target_pairs={{0,8},{1,9},{2,10},{3,11},{4,12},{5,13},{6,14},{7,15},{8,0},{9,1},... | collective-permute-start | bytes 1572872 | tf_op jit(solution)/shard_map/ppermute | solution.py:632
  110.3 1.2 collective-permute-start.9
  112.2 16.3 %all-to-all-start.7 = ((f32[16,32,128]{2,1,0:T(8,128)}), f32[16,32,128]{2,1,0:T(8,128)S(1)}, u32[]{:S(2)}, u32[]{:S(2)}) async-start(f32[16,32,128]{2,1,0:T(8,128)} %broadcast_in_dim.2), calls=%async_computation.7 | async-start | bytes 524288 | tf_op jit(solution)/shard_map/all_to_all | solution.py:889
  117.1 11.2 %collective-permute-start.21 = (bf16[512,256]{1,0:T(8,128)(2,1)S(1)}, bf16[512,256]{1,0:T(8,128)(2,1)S(1)}, u32[]{:S(2)}, u32[]{:S(2)}) collective-permute-start(bf16[512,256]{1,0:T(8,128)(2,1)S(1)} %get-tuple-element.223), channel_id=1, source_target_pairs={{0,4},{1,3},{2,6},{3,1},{4,0},{5,7},{6,2},{7,5},{8,12},{9,11},{10,... | collective-permute-start | bytes 786440 | tf_op jit(solution)/shard_map/ppermute | solution.py:632
  117.8 10.7 %collective-permute-start.10 = (bf16[512,256]{1,0:T(8,128)(2,1)}, bf16[512,256]{1,0:T(8,128)(2,1)S(1)}, u32[]{:S(2)}, u32[]{:S(2)}) collective-permute-start(bf16[512,256]{1,0:T(8,128)(2,1)} %copy-done.7), channel_id=1, source_target_pairs={{0,1},{1,0},{2,3},{3,2},{4,5},{5,4},{6,7},{7,6},{8,9},{9,8},{10,11... | collective-permute-start | bytes 786440 | tf_op jit(solution)/shard_map/ppermute | solution.py:594
  127.4 6.4 %collective-permute-start.14 = (bf16[512,256]{1,0:T(8,128)(2,1)S(1)}, bf16[512,256]{1,0:T(8,128)(2,1)S(1)}, u32[]{:S(2)}, u32[]{:S(2)}) collective-permute-start(bf16[512,256]{1,0:T(8,128)(2,1)S(1)} %get-tuple-element.215), channel_id=1, source_target_pairs={{0,2},{1,5},{2,0},{3,7},{4,6},{5,1},{6,4},{7,3},{8,10},{9,13},{10,... | collective-permute-start | bytes 786440 | tf_op jit(solution)/shard_map/ppermute | solution.py:632
  128.3 5.9 %collective-permute-start.22 = (bf16[256,256]{1,0:T(8,128)(2,1)S(1)}, bf16[256,256]{1,0:T(8,128)(2,1)S(1)}, u32[]{:S(2)}, u32[]{:S(2)}) collective-permute-start(bf16[256,256]{1,0:T(8,128)(2,1)S(1)} %get-tuple-element.225), channel_id=1, source_target_pairs={{0,8},{1,9},{2,10},{3,11},{4,12},{5,13},{6,14},{7,15},{8,0},{9,1},... | collective-permute-start | bytes 393224 | tf_op jit(solution)/shard_map/ppermute | solution.py:632
  133.9 5.0 %collective-permute-start.15 = (bf16[256,256]{1,0:T(8,128)(2,1)S(1)}, bf16[256,256]{1,0:T(8,128)(2,1)S(1)}, u32[]{:S(2)}, u32[]{:S(2)}) collective-permute-start(bf16[256,256]{1,0:T(8,128)(2,1)S(1)} %get-tuple-element.218), channel_id=1, source_target_pairs={{0,4},{1,3},{2,6},{3,1},{4,0},{5,7},{6,2},{7,5},{8,12},{9,11},{10,... | collective-permute-start | bytes 393224 | tf_op jit(solution)/shard_map/ppermute | solution.py:632
  134.3 10.6 %collective-permute-start.23 = (bf16[256,256]{1,0:T(8,128)(2,1)S(1)}, bf16[256,256]{1,0:T(8,128)(2,1)S(1)}, u32[]{:S(2)}, u32[]{:S(2)}) collective-permute-start(bf16[256,256]{1,0:T(8,128)(2,1)S(1)} %add_convert_fusion.1), channel_id=1, source_target_pairs={{0,16},{1,17},{2,18},{3,19},{4,20},{5,21},{6,22},{7,23},{8,24},{9,... | collective-permute-start | bytes 393224 | tf_op jit(solution)/shard_map/ppermute | solution.py:632
  138.9 7.4 %collective-permute-start.16 = (bf16[256,256]{1,0:T(8,128)(2,1)S(1)}, bf16[256,256]{1,0:T(8,128)(2,1)S(1)}, u32[]{:S(2)}, u32[]{:S(2)}) collective-permute-start(bf16[256,256]{1,0:T(8,128)(2,1)S(1)} %add_convert_fusion.3), channel_id=1, source_target_pairs={{0,16},{1,17},{2,18},{3,19},{4,20},{5,21},{6,22},{7,23},{8,24},{9,... | collective-permute-start | bytes 393224 | tf_op jit(solution)/shard_map/ppermute | solution.py:632
  144.9 5.0 %collective-permute-start.24 = (bf16[256,256]{1,0:T(8,128)(2,1)S(1)}, bf16[256,256]{1,0:T(8,128)(2,1)S(1)}, u32[]{:S(2)}, u32[]{:S(2)}) collective-permute-start(bf16[256,256]{1,0:T(8,128)(2,1)S(1)} %add_convert_fusion), channel_id=1, source_target_pairs={{0,8},{1,9},{2,10},{3,11},{4,12},{5,13},{6,14},{7,15},{8,0},{9,1},... | collective-permute-start | bytes 393224 | tf_op jit(solution)/shard_map/ppermute | solution.py:632
  146.4 5.0 %collective-permute-start.17 = (bf16[256,256]{1,0:T(8,128)(2,1)S(1)}, bf16[256,256]{1,0:T(8,128)(2,1)S(1)}, u32[]{:S(2)}, u32[]{:S(2)}) collective-permute-start(bf16[256,256]{1,0:T(8,128)(2,1)S(1)} %add_convert_fusion.2), channel_id=1, source_target_pairs={{0,4},{1,3},{2,6},{3,1},{4,0},{5,7},{6,2},{7,5},{8,12},{9,11},{10,... | collective-permute-start | bytes 393224 | tf_op jit(solution)/shard_map/ppermute | solution.py:632
  150.0 9.3 %collective-permute-start.25 = (bf16[512,256]{1,0:T(8,128)(2,1)S(1)}, bf16[512,256]{1,0:T(8,128)(2,1)S(1)}, u32[]{:S(2)}, u32[]{:S(2)}) collective-permute-start(bf16[512,256]{1,0:T(8,128)(2,1)S(1)} %pad_maximum_fusion.4), channel_id=1, source_target_pairs={{0,4},{1,3},{2,6},{3,1},{4,0},{5,7},{6,2},{7,5},{8,12},{9,11},{10,... | collective-permute-start | bytes 786440 | tf_op jit(solution)/shard_map/ppermute | solution.py:632
  151.4 9.1 %copy-start.9 = (bf16[512,256]{1,0:T(8,128)(2,1)S(1)}, bf16[512,256]{1,0:T(8,128)(2,1)}, u32[]{:S(2)}) copy-start(bf16[512,256]{1,0:T(8,128)(2,1)} %copy-done.8) | copy-start | bytes 786436
  151.5 8.8 %collective-permute-start.18 = (bf16[512,256]{1,0:T(8,128)(2,1)S(1)}, bf16[512,256]{1,0:T(8,128)(2,1)S(1)}, u32[]{:S(2)}, u32[]{:S(2)}) collective-permute-start(bf16[512,256]{1,0:T(8,128)(2,1)S(1)} %pad_maximum_fusion.3), channel_id=1, source_target_pairs={{0,2},{1,5},{2,0},{3,7},{4,6},{5,1},{6,4},{7,3},{8,10},{9,13},{10,... | collective-permute-start | bytes 786440 | tf_op jit(solution)/shard_map/ppermute | solution.py:632
  159.4 9.2 %collective-permute-start.26 = (bf16[1024,256]{1,0:T(8,128)(2,1)S(1)}, bf16[1024,256]{1,0:T(8,128)(2,1)S(1)}, u32[]{:S(2)}, u32[]{:S(2)}) collective-permute-start(bf16[1024,256]{1,0:T(8,128)(2,1)S(1)} %pad_maximum_fusion.2.refs_2_), channel_id=1, source_target_pairs={{0,2},{1,5},{2,0},{3,7},{4,6},{5,1},{6,4},{7,3},{8,10},{9,13},{10,... | collective-permute-start | bytes 1572872 | tf_op jit(solution)/shard_map/ppermute | solution.py:632
  160.4 9.6 %collective-permute-start.19 = (bf16[1024,256]{1,0:T(8,128)(2,1)S(1)}, bf16[1024,256]{1,0:T(8,128)(2,1)S(1)}, u32[]{:S(2)}, u32[]{:S(2)}) collective-permute-start(bf16[1024,256]{1,0:T(8,128)(2,1)S(1)} %pad_maximum_fusion.1.refs_0_), channel_id=1, source_target_pairs={{0,8},{1,9},{2,10},{3,11},{4,12},{5,13},{6,14},{7,15},{8,0},{9,1},... | collective-permute-start | bytes 1572872 | tf_op jit(solution)/shard_map/ppermute | solution.py:632

commit v4 on v3

--- a/solution.py
+++ b/solution.py
@@ -421,17 +421,18 @@
     spread(summ, packed)
 
 
-def mixer_grads(act, dl, dg, sl, dml, g_own, g_oth):
+def mixer_grads(act, dl, dg, sl, dml, l_own, l_oth, g_own, g_oth):
     _, core = place()
     mine, other = own_cols(core, 256), oth_cols(core, 256)
     left = act[...].T
-    for ref, at in ((dl, 0), (dg, 512)):
-        g_own[at : at + 512, :] = mm(left, ref[:, mine])
-        g_oth[at : at + 512, :] = mm(left, ref[:, other]).astype(bf16)
+    l_own[...] = mm(left, dl[:, mine])
+    l_oth[...] = mm(left, dl[:, other]).astype(bf16)
+    g_own[0:512, :] = mm(left, dg[:, mine])
+    g_oth[0:512, :] = mm(left, dg[:, other]).astype(bf16)
     for ref, cut in ((g_own, slice(0, 256)), (g_oth, slice(256, 512))):
         left = sl[:, cut].T
         for i in range(2):
-            ref[1024 + 256 * i : 1280 + 256 * i, :] = mm(left, dml[:, 256 * i : 256 * (i + 1)]).astype(ref.dtype)
+            ref[512 + 256 * i : 768 + 256 * i, :] = mm(left, dml[:, 256 * i : 256 * (i + 1)]).astype(ref.dtype)
 
 
 def in_grads(nl, dp, g_own, g_oth):
@@ -442,14 +443,13 @@
 
 def turn_kernel(peers, steps, got, comp_in, dk, own, oth, keep, proj, x, nrm, wout_own, wout_oth,
                 lin_own, lin_oth, gate_own, gate_oth, perm, cot_own, cot_oth,
-                cin, bo_own, bo_oth, d_out, act, dl, dg, sl, dml, skip_row, dst, comp, summ,
+                cin, result, d_out, act, dl, dg, sl, dml, skip_row, dst, comp, summ,
                 packed, held, gp, sig, qv, y):
     _, core = place()
     states_of(peers, steps, 16, 1, True, got, comp_in, dk, own, oth, keep, proj, cin, sl, packed, held)
     for _ in mix_and_gate(core, x, nrm, sl, wout_own, wout_oth, lin_own, lin_oth, gate_own, gate_oth, gp, act, sig, qv, y):
         pass
-    bo_own[...] = mm(perm[1], y[:, own_cols(core, 256)].astype(bf16)).astype(bf16)
-    bo_oth[...] = mm(perm[1], y[:, oth_cols(core, 256)].astype(bf16)).astype(bf16)
+    result[...] = y[...].astype(bf16)
     d_out[:, own_cols(core, 256)] = mm(perm[0], flat_rows(cot_own)).astype(bf16)
     d_out[:, oth_cols(core, 256)] = mm(perm[0], flat_rows(cot_oth)).astype(bf16)
     glu_backward(steps, 16, 0, False, core, lambda rows: d_out[rows, :].astype(f32), nrm, x, gp, sig, qv, own, oth, keep, wout_own, wout_oth,
@@ -457,7 +457,7 @@
 
 
 def adjoint_part(peers, steps, base, keep_which, adj_which, adj_reverse, got, comp, dk, own, oth, keep, nl, x, nrm,
-                 cin, sl, dst, dml, win_own, win_oth, skip_row, small_own, small_oth, at, packed, held, proj, dp, keep_tile):
+                 cin, sl, dst, dml, win_own, win_oth, skip_row, small_own, small_oth, all_rows, packed, held, proj, dp, keep_tile):
     _, core = place()
     device_carry(place()[0], peers, got, held, dk, adj_which, own, oth, base, True, adj_reverse, packed)
     start = entries(comp, packed)
@@ -502,15 +502,17 @@
         keep_tile(rows, d_normed)
     pack_two(bias_row, gain_row, packed)
 
-    for ref, half, flip in ((small_own, 0, 0), (small_oth, 1, 1)):
-        ref[at : at + 16, :] = jnp.zeros((16, 128), f32)
-        for j, row in enumerate((skip_row[0:1, :], bias_row, gain_row)):
-            low = (core == 0) if flip == 0 else (core == 1)
-            pick = jnp.where(low, row[:, :256], row[:, 256:])
-            ref[at + 2 * j : at + 2 * j + 1, :] = pick[:, :128]
-            ref[at + 2 * j + 1 : at + 2 * j + 2, :] = pick[:, 128:]
+    wanted = (skip_row[0:1, :], bias_row, gain_row) if all_rows else (skip_row[0:1, :],)
+    for ref, half in ((small_own, 0), (small_oth, 1)):
+        ref[...] = jnp.zeros_like(ref)
+        at = 0
+        for row in wanted:
+            pick = jnp.where(core == half, row[:, :256], row[:, 256:])
+            ref[at : at + 1, :] = pick[:, :128]
+            ref[at + 1 : at + 2, :] = pick[:, 128:]
+            at += 2
         for j in range(3):
-            ref[at + 6 + j : at + 7 + j, :] = jnp.sum(acc[half][j], axis=0, keepdims=True)
+            ref[at + j : at + j + 1, :] = jnp.sum(acc[half][j], axis=0, keepdims=True)
 
 
 def adjoint_second_kernel(peers, steps, got, comp, dk, own, oth, keep, nl, x, nrm, cin, sl, dst, dml, win_own, win_oth, skip_row, act, dl, dg,
@@ -519,17 +521,19 @@
         dn[rows, :] = d_normed
 
     adjoint_part(peers, steps, 16, 1, 0, False, got, comp, dk, own, oth, keep, nl, x, nrm,
-                 cin, sl, dst, dml, win_own, win_oth, skip_row, small_own, small_oth, 0, packed, held, proj, dp, keep_tile)
+                 cin, sl, dst, dml, win_own, win_oth, skip_row, small_own, small_oth, False, packed, held, proj, dp, keep_tile)
     spread(stats, packed)
-    mixer_grads(act, dl, dg, sl, dml, g_own, g_oth)
+    mixer_grads(act, dl, dg, sl, dml, g_own.at[:512], g_oth.at[:512], g_own.at[512:1536], g_oth.at[512:1536])
     in_grads(nl, dp, g_own.at[1536:], g_oth.at[1536:])
 
 
 def back_first_kernel(steps, count, got, dn, x2, nrm2, d_out2, own, oth, keep, x, nrm, gp, sig, qv,
                       wout_own, wout_oth, lin_own, lin_oth, gate_own, gate_oth,
-                      act, sl, d_out, dml, g_own, g_oth, skip_row, dst, comp, summ, packed, dl, dg):
+                      act, sl, d_out, dml, totals, l_own, l_oth, g_own, g_oth, skip_row, dst, comp, summ, packed, dl, dg):
     sums = sum_peers(got)
     bias_row, gain_row = row_of_tiles(sums[0:4]), row_of_tiles(sums[4:8])
+    totals[...] = jnp.zeros_like(totals)
+    totals[0:1, :], totals[1:2, :] = bias_row, gain_row
     mean, inv, gain = nrm2[0:1, :], nrm2[1:2, :], nrm2[2:3, :]
     scaled, shift, slope = inv * gain, inv * gain * bias_row / count, inv * inv * gain * gain_row / count
 
@@ -540,43 +544,49 @@
 
     glu_backward(steps, 0, 1, True, place()[1], d_in, nrm, x, gp, sig, qv, own, oth, keep, wout_own, wout_oth,
                  lin_own, lin_oth, gate_own, gate_oth, skip_row, dst, comp, summ, packed, dl, dg, dml)
-    mixer_grads(act, dl, dg, sl, dml, g_own, g_oth)
+    mixer_grads(act, dl, dg, sl, dml, l_own, l_oth, g_own, g_oth)
 
 
 def adjoint_first_kernel(peers, steps, got, comp, dk, own, oth, keep, nl, x, nrm, cin, sl, dst, dml, win_own, win_oth, skip_row,
-                         d_out, perm, small1_own, small1_oth,
-                         g_own, g_oth, small_own, small_oth, a_own, a_oth, packed, held, proj, tmp, dp):
+                         d_out, small1_own, small1_oth,
+                         g_own, g_oth, small_own, partial, packed, held, proj, dp, small_oth):
     _, core = place()
     scaled = nrm[1:2, :] * nrm[2:3, :]
 
     def keep_tile(rows, d_normed):
-        tmp[rows, :] = (d_out[rows, :] + scaled * d_normed).astype(bf16)
+        partial[rows, :] = (d_out[rows, :] + scaled * d_normed).astype(bf16)
 
     adjoint_part(peers, steps, 0, 0, 1, True, got, comp, dk, own, oth, keep, nl, x, nrm,
-                 cin, sl, dst, dml, win_own, win_oth, skip_row, small_own, small_oth, 0, packed, held, proj, dp, keep_tile)
-    small_own[16:32, :] = small1_own[...]
-    small_oth[16:32, :] = small1_oth[...]
-    a_own[...] = mm(perm[1], tmp[:, own_cols(core, 256)]).astype(bf16)
-    a_oth[...] = mm(perm[1], tmp[:, oth_cols(core, 256)]).astype(bf16)
-    in_grads(nl, dp, g_own, g_oth)
-
-
-def finish_kernel(count, got, a_mine, a_other, tokens, nrm, raw,
-                  d_in, ngg, bias, skip, rate_grad, angle_grad, packed):
+                 cin, sl, dst, dml, win_own, win_oth, skip_row, small_own, small_oth, True, packed, held, proj, dp, keep_tile)
+    small_own[9:14, :] = small1_own[0:5, :]
+    small_oth[9:14, :] = small1_oth[0:5, :]
+    in_grads(nl, dp, g_own, g_oth.at[:512])
+    put_small(g_oth, 512, small_oth[...])
+
+
+def order_kernel(perm, result, partial, own, oth):
     _, core = place()
-    packed[...] = sum_peers(got)
-    for k in range(2):
-        at = 16 * k
-        for ref, j in ((skip, 0), (bias, 2), (ngg, 4)):
-            ref[k : k + 1, :128] = packed[at + j : at + j + 1, :]
-            ref[k : k + 1, 128:] = packed[at + j + 1 : at + j + 2, :]
+    for i, ref in enumerate((result, partial)):
+        own[i] = mm(perm[1], ref[:, own_cols(core, 256)]).astype(bf16)
+        oth[i] = mm(perm[1], ref[:, oth_cols(core, 256)]).astype(bf16)
+
+
+def finish_kernel(count, packed, totals1, mine_parts, other_parts, tokens, nrm, raw,
+                  block_out, d_in, ngg, bias, skip, rate_grad, angle_grad):
+    _, core = place()
+    for ref, j in ((skip, 0), (bias, 2), (ngg, 4)):
+        ref[0:1, :128], ref[0:1, 128:] = packed[j : j + 1, :], packed[j + 1 : j + 2, :]
+    skip[1:2, :128], skip[1:2, 128:] = packed[9:10, :], packed[10:11, :]
+    bias[1:2, :] = totals1[0:1, own_cols(core, 256)]
+    ngg[1:2, :] = totals1[1:2, own_cols(core, 256)]
+    for k, at in ((0, 6), (1, 11)):
         values = raw[k : k + 1, :]
         rate = jnp.exp(values[:, 768:896])
         angle = jnp.exp(values[:, 896:])
         modulus = jnp.exp(-rate)
         scale = jnp.sqrt(1.0 - modulus * modulus)
         cos, sin = jnp.cos(angle), jnp.sin(angle)
-        dr, di, ds = (packed[at + j : at + j + 1, :] for j in (6, 7, 8))
+        dr, di, ds = (packed[at + j : at + j + 1, :] for j in range(3))
         g_mod = dr * cos + di * sin - ds * modulus / scale
         rate_grad[k : k + 1, :] = -g_mod * modulus * rate
         angle_grad[k : k + 1, :] = modulus * (di * cos - dr * sin) * angle
@@ -585,7 +595,8 @@
     bias_row, gain_row = bias[0:1, :], ngg[0:1, :]
     flat = inv * gain / count
     for r in range(4):
-        held_rows = jnp.where(core == r // 2, a_mine[r % 2].astype(f32), a_other[r % 2].astype(f32))
+        block_out[r] = jnp.where(core == r // 2, mine_parts[0, r % 2], other_parts[0, r % 2])
+        held_rows = jnp.where(core == r // 2, mine_parts[1, r % 2].astype(f32), other_parts[1, r % 2].astype(f32))
         xhat = (tokens[r].astype(f32) - mean) * inv
         d_in[r] = held_rows - flat * (bias_row + xhat * gain_row)
 
@@ -641,7 +652,20 @@
     return (me // jnp.where(core == 0, masks[0], masks[1])) & 1
 
 
-def first_halves_kernel(masks, pairs, mine, other):
+def put_small(out, at, value):
+    high = value.astype(bf16)
+    rest = value - high.astype(f32)
+    middle = rest.astype(bf16)
+    low = (rest - middle.astype(f32)).astype(bf16)
+    out[at : at + 16, :128], out[at : at + 16, 128:] = high, middle
+    out[at + 16 : at + 32, :128], out[at + 16 : at + 32, 128:] = low, jnp.zeros_like(low)
+
+
+def get_small(ref, at):
+    return (ref[at : at + 16, :128].astype(f32) + ref[at : at + 16, 128:].astype(f32)) + ref[at + 16 : at + 32, :128].astype(f32)
+
+
+def first_halves_kernel(masks, pairs, small, mine, other):
     bit, at = bit_of(masks), 0
     for own, got in pairs:
         half = own.shape[0] // 2
@@ -649,13 +673,32 @@
             rows = pl.ds(pl.multiple_of(which * half, half), half)
             out[at : at + half, :] = (own[rows, :] + got[rows, :].astype(f32)).astype(bf16)
         at += half
-
-
-def next_halves_kernel(masks, held, got, mine, other):
-    bit, half = bit_of(masks), mine.shape[0]
+    if small is not None:
+        total = small[...] + get_small(pairs[-1][1], pairs[-1][0].shape[0])
+        put_small(mine, at, total)
+        put_small(other, at, total)
+
+
+def next_halves_kernel(masks, extra, held, got, mine, other):
+    bit, half = bit_of(masks), mine.shape[0] - extra
     for out, which in ((mine, bit), (other, 1 - bit)):
         rows = pl.ds(pl.multiple_of(which * half, half), half)
-        out[...] = (held[rows, :].astype(f32) + got[rows, :].astype(f32)).astype(bf16)
+        out[:half, :] = (held[rows, :].astype(f32) + got[rows, :].astype(f32)).astype(bf16)
+    if extra:
+        total = get_small(held, 2 * half) + get_small(got, 2 * half)
+        put_small(mine, half, total)
+        put_small(other, half, total)
+
+
+def add_kernel(extra, held, got, total, *small):
+    rows = held.shape[0] - extra
+    total[:rows, :] = (held[:rows, :].astype(f32) + got[:rows, :].astype(f32)).astype(bf16)
+    if extra:
+        value = get_small(held, rows) + get_small(got, rows)
+        if small:
+            small[0][...] = value
+        else:
+            put_small(total, rows, value)
 
 
 def axes_orders(*orders):
@@ -667,30 +710,34 @@
 
 
 class SeqSum:
-    def __init__(self, pairs, masks):
-        self.masks, self.at = masks, 0
-        rows = sum(a.shape[0] for a, _ in pairs) // 2
+    def __init__(self, pairs, masks, small=None):
+        self.masks, self.at, self.small, self.extra = masks, 0, (), 0 if small is None else 32
+        rows = sum(a.shape[0] for a, _ in pairs) // 2 + self.extra
         shape = ((rows, pairs[0][0].shape[1]), bf16)
-        flat = tuple(v for p in pairs for v in p)
+        flat = tuple(v for p in pairs for v in p) + (() if small is None else (small,))
 
         def kernel(refs, mine, other):
-            first_halves_kernel(masks[0], [(refs[i], refs[i + 1]) for i in range(0, len(refs), 2)], mine, other)
+            count = 2 * len(pairs)
+            first_halves_kernel(masks[0], [(refs[i], refs[i + 1]) for i in range(0, count, 2)],
+                                None if small is None else refs[count], mine, other)
 
         self.mine, self.send = run(kernel, [shape, shape], (flat,))
 
     def step(self):
         count, i = len(self.masks), self.at
         self.at += 1
-        if i + 1 < count:
+        if i < count:
             got = partners(self.send, self.masks[i])
+            rows, width = got.shape
+            rows -= self.extra
             if i + 2 < count:
-                shape = ((got.shape[0] // 2, got.shape[1]), bf16)
-                self.mine, self.send = run(functools.partial(next_halves_kernel, self.masks[i + 1]), [shape, shape], (self.mine, got))
+                shape = ((rows // 2 + self.extra, width), bf16)
+                self.mine, self.send = run(functools.partial(next_halves_kernel, self.masks[i + 1], self.extra), [shape, shape], (self.mine, got))
+            elif i + 2 == count:
+                (self.send,) = run(functools.partial(add_kernel, self.extra), [((rows + self.extra, width), bf16)], (self.mine, got))
             else:
-                self.send = (self.mine.astype(f32) + got.astype(f32)).astype(bf16)
-            return False
-        if i + 1 == count:
-            self.send = (self.send.astype(f32) + partners(self.send, self.masks[i]).astype(f32)).astype(bf16)
+                outs = [((rows, width), bf16)] + ([((16, 128), f32)] if self.extra else [])
+                self.send, *self.small = run(functools.partial(add_kernel, self.extra), outs, (self.send, got))
             return False
         mask = self.masks[2 * count - 2 - i]
         got = partners(self.send, mask)
@@ -710,36 +757,34 @@
 
 
 def unpack_kernel(masks0, masks1, mine0, got0, mine1, got1, lin, gate, out, entry):
-    for k, mine, got, masks in ((0, mine0, got0, masks0), (1, mine1, got1, masks1)):
+    def put_entry(ref, at, k, start, rows):
+        value = ref[at : at + rows, :].astype(f32)
+        entry[k, pl.ds(2 * start, rows, stride=2), :] = value[:, :128]
+        entry[k, pl.ds(2 * start + 1, rows, stride=2), :] = value[:, 128:]
+
+    for mine, got, masks, second in ((mine0, got0, masks0, False), (mine1, got1, masks1, True)):
         bit = bit_of(masks)
         for ref, which in ((mine, bit), (got, 1 - bit)):
 
             def piece(at, rows):
                 return ref[at : at + rows, :].astype(f32)
 
-            def put_entry(at, start, rows):
-                value = piece(at, rows)
-                entry[k, pl.ds(2 * start, rows, stride=2), :] = value[:, :128]
-                entry[k, pl.ds(2 * start + 1, rows, stride=2), :] = value[:, 128:]
-
             @pl.when(which == 0)
             def _():
-                lin[k] = piece(0, 512)
-                if k == 1:
-                    gate[1] = piece(512, 512)
+                if second:
+                    lin[1], gate[1], lin[0, :256] = piece(0, 512), piece(512, 512), piece(1024, 256)
                 else:
-                    gate[0, :256] = piece(512, 256)
-                    put_entry(768, 0, 256)
+                    gate[0] = piece(0, 512)
+                    put_entry(ref, 512, 0, 0, 256)
 
             @pl.when(which == 1)
             def _():
-                if k == 1:
-                    out[1, :, :256], out[1, :, 256:] = piece(0, 256), piece(256, 256)
-                    put_entry(512, 0, 512)
+                if second:
+                    out[1, :, :256], out[1, :, 256:], lin[0, 256:] = piece(0, 256), piece(256, 256), piece(1024, 256)
+                    put_entry(ref, 512, 1, 0, 512)
                 else:
-                    gate[0, 256:] = piece(0, 256)
-                    put_entry(768, 256, 256)
-                    out[0, :, :256], out[0, :, 256:] = piece(256, 256), piece(512, 256)
+                    out[0, :, :256], out[0, :, 256:] = piece(0, 256), piece(256, 256)
+                    put_entry(ref, 512, 0, 256, 256)
 
 
 class Far:
@@ -854,53 +899,46 @@
         (got, y0, own, oth, keep) + enter[1], [packed], flops=one)
     got, _ = blocking(summ, "seq", ())
     turn_outs = [((8, 512), f32), full, ((16, 8, 128), f32)]
-    cin1, bo_own, bo_oth, d_out1, act1, dl1, dg1, sl1, dml1, skip1, dst, comp, summ = run(
+    cin1, result, d_out1, act1, dl1, dg1, sl1, dml1, skip1, dst, comp, summ = run(
         functools.partial(turn_kernel, peers, steps),
-        [((SLAB, 512), f32), ((n, 256), bf16), ((n, 256), bf16), low, low, low, low, low, low] + turn_outs + [for_seq],
+        [((SLAB, 512), f32), low, low, low, low, low, low, low] + turn_outs + [for_seq],
         (got, comp, dk, own, oth, keep, proj, y0, nrm1) + glu[1] + (perm, Far(cotangent, "rows"), Far(cot_oth, "rows")),
         [packed, ordered, full, full, full, full], flops=8 * one)
-    got, (bo_oth,) = blocking(summ, "seq", (bo_oth,))
+    got, _ = blocking(summ, "seq", ())
     g1_own, g1_oth, s1_own, s1_oth, dn, stats = run(
         functools.partial(adjoint_second_kernel, peers, steps),
-        [((2048, 256), f32), ((2048, 256), bf16), ((16, 128), f32), ((16, 128), f32), full, for_all],
+        [((2048, 256), f32), ((2048, 256), bf16), ((8, 128), f32), ((8, 128), f32), full, for_all],
         (got, comp, dk, own, oth, keep, nl1, y0, nrm1, cin1, sl1, dst, dml1) + enter[1] + (skip1, act1, dl1, dg1),
         [packed, ordered, full, low], flops=6 * one)
-    got, (bo_oth, g1_oth) = blocking(stats, ("seq", "state"), (bo_oth, g1_oth))
-    bo_got, g1_got = swap(bo_oth), swap(g1_oth)
-    d_out0, dml0, g0_own, g0_oth, skip0, dst, comp, summ = run(
+    got, (g1_oth,) = blocking(stats, ("seq", "state"), (g1_oth,))
+    g1_got = swap(g1_oth)
+    d_out0, dml0, totals1, l0_own, l0_oth, g0_own, g0_oth, skip0, dst, comp, summ = run(
         functools.partial(back_first_kernel, steps, count),
-        [full, low, ((1536, 256), f32), ((1536, 256), bf16)] + turn_outs + [for_seq],
+        [full, low, ((8, 512), f32), ((512, 256), f32), ((512, 256), bf16), ((1024, 256), f32), ((1024, 256), bf16)] + turn_outs + [for_seq],
         (got, dn, y0, nrm1, d_out1, own, oth, keep, xp, nrm0, gp0, sig0, qv0) + glu[0] + (act0, sl0),
         [packed, low, low], flops=6 * one)
-    got, (g0_oth, bo_got, g1_got) = blocking(summ, "seq", (g0_oth, bo_got, g1_got))
-    bulk1 = SeqSum([(g1_own, g1_got)], axes_orders((0, 1, 2, 3), (1, 0, 2, 3)))
-    got = (bulk1.before(got[0]),)
-    g0_got = swap(g0_oth)
-    i0_own, i0_oth, s_own, s_oth, a_own, a_oth = run(
+    got, (l0_oth, g0_oth, g1_got, result) = blocking(summ, "seq", (l0_oth, g0_oth, g1_got, result))
+    l0_got, g0_got = swap(l0_oth), swap(g0_oth)
+    i0_own, i0_oth, s_own, partial = run(
         functools.partial(adjoint_first_kernel, peers, steps),
-        [((512, 256), f32), ((512, 256), bf16), ((32, 128), f32), ((32, 128), f32), ((n, 256), bf16), ((n, 256), bf16)],
+        [((512, 256), f32), ((544, 256), bf16), ((16, 128), f32), low],
         (got, comp, dk, own, oth, keep, nl0, xp, nrm0, cin0, sl0, dst, dml0) + enter[0]
-        + (skip0, d_out0, perm, s1_own, s1_oth),
-        [packed, ordered, full, low, low], flops=4 * one)
+        + (skip0, d_out0, s1_own, s1_oth),
+        [packed, ordered, full, low, ((16, 128), f32)], flops=3 * one)
     i0_got = swap(i0_oth)
-    bulk0 = SeqSum([(g0_own, g0_got), (i0_own, i0_got)], axes_orders((2, 0, 1, 3), (2, 1, 0, 3)))
-    s_got, a_got = swap(s_oth), swap(a_oth)
-    s_all = jnp.broadcast_to((s_own + s_got)[None], (peers, 32, 128))
-    got = lax.all_to_all(s_all, "seq", 0, 0)
-    pair = (2, span, width)
-    d_in, ngg, bias_grad, skip_grad, rate_grad, angle_grad = run(
-        functools.partial(finish_kernel, count),
-        [((rows, span, width), f32), ((2, 256), f32), ((2, 256), f32), ((2, 256), f32), ((2, 128), f32), ((2, 128), f32)],
-        ((got,), a_own.reshape(pair), a_got.reshape(pair), Far(tokens), nrm0, raw),
-        [((32, 128), f32)])
+    bulk1 = SeqSum([(g1_own, g1_got), (l0_own, l0_got)], axes_orders((0, 1, 2, 3), (1, 0, 2, 3)))
+    bulk0 = SeqSum([(g0_own, g0_got), (i0_own, i0_got)], axes_orders((2, 1, 0, 3), (2, 0, 1, 3)), s_own)
+    own_parts, oth_parts = run(order_kernel, [((2, n, 256), bf16)] * 2, (perm, result, partial), flops=2 * one)
+    got_parts = swap(oth_parts)
     while not bulk1.step():
         pass
-    bulk0.step()
-    bulk0.after(s_all)
-    bulk0.step()
-    bulk0.after(got)
-    bulk0.step()
-    bulk0.after(d_in)
+    while not bulk0.small:
+        bulk0.step()
+    quad = (2, 2, span, width)
+    block_out, d_in, ngg, bias_grad, skip_grad, rate_grad, angle_grad = run(
+        functools.partial(finish_kernel, count),
+        [((rows, span, width), bf16), ((rows, span, width), f32), ((2, 256), f32), ((2, 256), f32), ((2, 256), f32), ((2, 128), f32), ((2, 128), f32)],
+        (bulk0.small[0], totals1, own_parts.reshape(quad), got_parts.reshape(quad), Far(tokens), nrm0, raw))
     while not bulk0.step():
         pass
     lin_grad, gate_grad, out_grad, in_grad = run(
@@ -908,8 +946,6 @@
         [((2, 512, 256), f32), ((2, 512, 256), f32), ((2, 256, 512), f32), ((2, 1024, 128), f32)],
         bulk0.result + bulk1.result)
     out_grad, in_grad = out_grad.reshape(2, 2, 128, 512), in_grad.reshape(2, 512, 2, 128)
-    mine, other = bo_own.reshape(pair), bo_got.reshape(pair)
-    block_out = jnp.concatenate([jnp.where(core == 0, mine, other), jnp.where(core == 0, other, mine)], axis=0)
     return (block_out, d_in, ngg, bias_grad, in_grad, out_grad, rate_grad, angle_grad, skip_grad, lin_grad, gate_grad)
 
 

time: 173 us -> 167 us (0.965)
  waiting for transfers between devices: 46.4 us -> 42.3 us
  starting transfers between devices: 14.6 us -> 17 us
  local copies, waits for them, and re-layouts: 3.87 us -> 2.13 us
    ppermute x14, starting transfers between devices: 7.68 us -> 14 us  [partners(): lax.ppermute(value, ('seq', 'state'), [(2 * i + c, 2 * (i ^ masks[c]) + c...]
    ppermute x14, waiting for transfers between devices: 44.6 us -> 39.3 us  [partners(): lax.ppermute(value, ('seq', 'state'), [(2 * i + c, 2 * (i ^ masks[c]) + c...]
    all_to_all x1 -> x0, starting transfers between devices: 3.53 us -> none  [body(): got = lax.all_to_all(s_all, 'seq', 0, 0)]
    pallas_call x17 -> x22, Pallas kernels: 29.2 us -> 28 us  [run(): pl.pallas_call(whole, out_shape=[jax.ShapeDtypeStruct(o[0], o[1]) for o i...]
  transfers between devices with their start and end apart: 28 -> 26, of which waited for: 15 -> 13; matrix products, arithmetic and copies ran while one was open for 2% -> 1% of each run, Pallas kernels for 8% -> 7%
where the time goes in v4:
time: 167 us; the launch traced here: 166 us
  blocking collectives  74.9 us (45%)
  waiting for transfers between devices  42.3 us (25%)
  Pallas kernels  28 us (17%)
  starting transfers between devices  17 us (10%)
  local copies, waits for them, and re-layouts  2.13 us (1%)
    all_to_all x6, blocking collectives, blocking(): lax.all_to_all(value, axes, 0, 0)  60.4 us
    ppermute x14, waiting for transfers between devices, partners(): lax.ppermute(value, ('seq', 'state'), [(2 * i + c, 2 * (i ^ masks[c]) + c...  39.3 us
    pallas_call x22, Pallas kernels, run(): pl.pallas_call(whole, out_shape=[jax.ShapeDtypeStruct(o[0], o[1]) for o i...  28 us
    all_to_all x1, blocking collectives, body(): lax.all_to_all(stats, ('seq', 'state'), 0, 0)  14.4 us
    ppermute x14, starting transfers between devices, partners(): lax.ppermute(value, ('seq', 'state'), [(2 * i + c, 2 * (i ^ masks[c]) + c...  14 us
  transfers between devices with their start and end apart: 26, of which 13 were waited for; matrix products, arithmetic and copies ran while one was open for 1% of the time, Pallas kernels for 7%

profile of v4, /device:TPU:0, one launch (start us, length us, event | category | flops | bytes accessed | tf_op | source)
XLA Modules:
  0.0 166.3 jit_solution(11931186480326340687)
XLA Ops:
  0.7 1.4 reshape.40.refs_7_.refs_5_.refs_13_
  2.1 0.5 collective-permute-start.2
  2.7 0.7 convert_add_fusion.refs_1_.refs_6_
  3.4 0.7 copy-done.5
  4.1 1.4 shard_map.204
  5.5 0.5 collective-permute-start.1
  7.6 14.4 %all_to_all.35.refs_0_ = f32[32,4,128]{2,1,0:T(4,128)S(1)} all-to-all(f32[32,4,128]{2,1,0:T(4,128)S(1)} %shard_map.203), channel_id=1, replica_groups=mesh['seq'=16,'state'=2] {'seq','state'}, dimensions={0} | all-to-all | bytes 131072 | tf_op jit(solution)/shard_map/all_to_all | solution.py:889
  22.0 2.1 %shard_map.205 = (bf16[512,512]{1,0:T(8,128)(2,1)S(1)}, bf16[512,512]{1,0:T(8,128)(2,1)S(1)}, f32[512,512]{1,0:T(8,128)S(1)}, f32[16,8,128]{2,1,0:T(8,128)S(1)},...) custom-call(f32[32,4,128]{2,1,0:T(4,128)S(1)} %all_to_all.35.refs_0_, bf16[4,256,256]{2,1,0:T(8,128)(2,1)S(1)} %copy-done, ...), custom_call_target="tpu_custom_call" | custom-call | flops 536870912 | bytes 3768320 | tf_op jit(solution)/shard_map/pallas_call | solution.py:847
  24.2 10.1 %all_to_all.36.refs_0_ = f32[16,8,128]{2,1,0:T(8,128)S(1)} all-to-all(f32[16,8,128]{2,1,0:T(8,128)S(1)} %get-tuple-element.122), channel_id=1, replica_groups=mesh['seq'=16,'state'=2] {'seq'}, dimensions={0} | all-to-all | bytes 131072 | tf_op jit(solution)/shard_map/all_to_all | solution.py:617
  34.3 3.3 %shard_map.206 = (f32[16,512]{1,0:T(8,128)S(1)}, bf16[512,512]{1,0:T(8,128)(2,1)S(1)}, bf16[512,512]{1,0:T(8,128)(2,1)S(1)}, bf16[512,512]{1,0:T(8,128)(2,1)S(1)...) custom-call(f32[16,8,128]{2,1,0:T(8,128)S(1)} %all_to_all.36.refs_0_, ...), custom_call_target="tpu_custom_call" | custom-call | flops 805306368 | bytes 5554176 | tf_op jit(solution)/shard_map/pallas_call | solution.py:847
  37.6 9.9 %all_to_all.37.refs_0_ = f32[32,8,128]{2,1,0:T(8,128)S(1)} all-to-all(f32[32,8,128]{2,1,0:T(8,128)S(1)} %get-tuple-element.136), channel_id=1, replica_groups=mesh['seq'=16,'state'=2] {'seq','state'}, dimensions={0} | all-to-all | bytes 262144 | tf_op jit(solution)/shard_map/all_to_all | solution.py:617
  47.5 1.6 shard_map.207
  49.1 10.2 %all_to_all.38.refs_0_ = f32[16,8,128]{2,1,0:T(8,128)S(1)} all-to-all(f32[16,8,128]{2,1,0:T(8,128)S(1)} %get-tuple-element.138), channel_id=1, replica_groups=mesh['seq'=16,'state'=2] {'seq'}, dimensions={0} | all-to-all | bytes 131072 | tf_op jit(solution)/shard_map/all_to_all | solution.py:617
  59.4 5.6 %shard_map.208 = (f32[16,512]{1,0:T(8,128)S(1)}, bf16[512,512]{1,0:T(8,128)(2,1)S(1)}, bf16[512,512]{1,0:T(8,128)(2,1)S(1)}, bf16[512,512]{1,0:T(8,128)(2,1)S(1)...) custom-call(f32[16,8,128]{2,1,0:T(8,128)S(1)} %all_to_all.38.refs_0_, ...), custom_call_target="tpu_custom_call" | custom-call | flops 2147483648 | bytes 8175616 | tf_op jit(solution)/shard_map/pallas_call | solution.py:847
  65.0 10.1 %all_to_all.39.refs_0_ = f32[16,8,128]{2,1,0:T(8,128)S(1)} all-to-all(f32[16,8,128]{2,1,0:T(8,128)S(1)} %get-tuple-element.143), channel_id=1, replica_groups=mesh['seq'=16,'state'=2] {'seq'}, dimensions={0} | all-to-all | bytes 131072 | tf_op jit(solution)/shard_map/all_to_all | solution.py:617
  75.1 2.8 %shard_map.209 = (f32[2048,256]{1,0:T(8,128)S(1)}, bf16[2048,256]{1,0:T(8,128)(2,1)S(1)}, f32[8,128]{1,0:T(8,128)S(1)}, f32[8,128]{1,0:T(8,128)S(1)}, f32[512,512]{1,0:T(8,128)S(1)}, /*index=5*/f32[32,8,128]{2,1,0:T(8,128)S(1)}) custom-call(f32[16,8,128]{2,1,0:T(8,128)S(1)} %all_to_all.39.refs_0_, f32[16,8,128]{2,1,0:T(8,128)S(1)} %get-tuple-element.144.refs_1_, ...), custom_call_target="tpu_custom_call" | custom-call | flops 1610612736 | bytes 7176192 | tf_op jit(solution)/shard_map/pallas_call | solution.py:847
  78.0 9.9 %all_to_all.40.refs_0_ = f32[32,8,128]{2,1,0:T(8,128)S(1)} all-to-all(f32[32,8,128]{2,1,0:T(8,128)S(1)} %get-tuple-element.156), channel_id=1, replica_groups=mesh['seq'=16,'state'=2] {'seq','state'}, dimensions={0} | all-to-all | bytes 262144 | tf_op jit(solution)/shard_map/all_to_all | solution.py:617
  88.1 3.3 %shard_map.210 = (f32[512,512]{1,0:T(8,128)S(1)}, bf16[512,512]{1,0:T(8,128)(2,1)S(1)}, f32[8,512]{1,0:T(8,128)S(1)}, f32[512,256]{1,0:T(8,128)S(1)}, bf16[512,2...) custom-call(f32[32,8,128]{2,1,0:T(8,128)S(1)} %all_to_all.40.refs_0_, ...), custom_call_target="tpu_custom_call" | custom-call | flops 1610612736 | bytes 9633792 | tf_op jit(solution)/shard_map/pallas_call | solution.py:847
  91.5 10.1 %all_to_all.41.refs_0_ = f32[16,8,128]{2,1,0:T(8,128)S(1)} all-to-all(f32[16,8,128]{2,1,0:T(8,128)S(1)} %get-tuple-element.172), channel_id=1, replica_groups=mesh['seq'=16,'state'=2] {'seq'}, dimensions={0} | all-to-all | bytes 131072 | tf_op jit(solution)/shard_map/all_to_all | solution.py:617
  101.6 1.5 collective-permute-done.18.refs_3_
  103.3 0.9 collective-permute-start.19
  104.2 2.0 %shard_map.211 = (f32[512,256]{1,0:T(8,128)S(1)}, bf16[544,256]{1,0:T(8,128)(2,1)S(1)}, f32[16,128]{1,0:T(8,128)S(1)}, bf16[512,512]{1,0:T(8,128)(2,1)S(1)}) custom-call(f32[16,8,128]{2,1,0:T(8,128)S(1)} %all_to_all.41.refs_0_, f32[16,8,128]{2,1,0:T(8,128)S(1)} %get-tuple-element.179.refs_1_, f32[2,16,8,128]{3,2,1,0:T(8,128)S(1)} %get-tuple-element.129.refs_2_, ...), custom_call_target="tpu_custom_call" | custom-call | flops 805306368 | bytes 6135808 | tf_op jit(solution)/shard_map/pallas_call | solution.py:847
  106.2 0.6 collective-permute-start.9
  106.8 1.2 collective-permute-done.9.refs_3_
  108.6 5.4 %collective-permute-done.19.refs_1_ = bf16[1280,256]{1,0:T(8,128)(2,1)S(1)} collective-permute-done((bf16[1280,256]{1,0:T(8,128)(2,1)S(1)}, bf16[1280,256]{1,0:T(8,128)(2,1)S(1)}, u32[]{:S(2)}, u32[]{:S(2)}) %collective-permute-start.19) | collective-permute-done | bytes 655392 | tf_op jit(solution)/shard_map/ppermute | solution.py:643
  114.1 0.7 collective-permute-start.20
  114.8 6.4 %collective-permute-done.20.refs_1_ = bf16[640,256]{1,0:T(8,128)(2,1)S(1)} collective-permute-done((bf16[640,256]{1,0:T(8,128)(2,1)S(1)}, bf16[640,256]{1,0:T(8,128)(2,1)S(1)}, u32[]{:S(2)}, u32[]{:S(2)}) %collective-permute-start.20) | collective-permute-done | bytes 327712 | tf_op jit(solution)/shard_map/ppermute | solution.py:643
  121.4 0.7 collective-permute-start.21
  122.2 0.7 collective-permute-start.11
  122.9 3.9 %collective-permute-done.21.refs_1_ = bf16[320,256]{1,0:T(8,128)(2,1)S(1)} collective-permute-done((bf16[320,256]{1,0:T(8,128)(2,1)S(1)}, bf16[320,256]{1,0:T(8,128)(2,1)S(1)}, u32[]{:S(2)}, u32[]{:S(2)}) %collective-permute-start.21) | collective-permute-done | bytes 163872 | tf_op jit(solution)/shard_map/ppermute | solution.py:643
  126.8 0.8 collective-permute-start.22
  127.6 0.5 collective-permute-done.11.refs_1_
  128.2 0.6 collective-permute-start.12
  128.8 6.2 %collective-permute-done.22.refs_1_ = bf16[320,256]{1,0:T(8,128)(2,1)S(1)} collective-permute-done((bf16[320,256]{1,0:T(8,128)(2,1)S(1)}, bf16[320,256]{1,0:T(8,128)(2,1)S(1)}, u32[]{:S(2)}, u32[]{:S(2)}) %collective-permute-start.22) | collective-permute-done | bytes 163872 | tf_op jit(solution)/shard_map/ppermute | solution.py:643
  135.2 1.4 collective-permute-start.13
  136.6 0.7 shard_map.217
  137.4 3.6 %collective-permute-done.13.refs_1_ = bf16[224,256]{1,0:T(8,128)(2,1)S(1)} collective-permute-done((bf16[224,256]{1,0:T(8,128)(2,1)S(1)}, bf16[224,256]{1,0:T(8,128)(2,1)S(1)}, u32[]{:S(2)}, u32[]{:S(2)}) %collective-permute-start.13) | collective-permute-done | bytes 114720 | tf_op jit(solution)/shard_map/ppermute | solution.py:643
  141.1 0.7 collective-permute-start.15
  141.8 0.6 collective-permute-start.24
  142.5 4.4 %collective-permute-done.15 = bf16[192,256]{1,0:T(8,128)(2,1)S(1)} collective-permute-done((bf16[192,256]{1,0:T(8,128)(2,1)S(1)}, bf16[192,256]{1,0:T(8,128)(2,1)S(1)}, u32[]{:S(2)}, u32[]{:S(2)}) %collective-permute-start.15) | collective-permute-done | bytes 98336 | tf_op jit(solution)/shard_map/ppermute | solution.py:643
  146.9 0.7 collective-permute-start.16
  147.6 2.5 %collective-permute-done.24 = bf16[640,256]{1,0:T(8,128)(2,1)S(1)} collective-permute-done((bf16[640,256]{1,0:T(8,128)(2,1)S(1)}, bf16[640,256]{1,0:T(8,128)(2,1)S(1)}, u32[]{:S(2)}, u32[]{:S(2)}) %collective-permute-start.24) | collective-permute-done | bytes 327712 | tf_op jit(solution)/shard_map/ppermute | solution.py:643
  150.3 2.3 %collective-permute-start.25 = (bf16[1280,256]{1,0:T(8,128)(2,1)S(1)}, bf16[1280,256]{1,0:T(8,128)(2,1)S(1)}, u32[]{:S(2)}, u32[]{:S(2)}) collective-permute-start(bf16[1280,256]{1,0:T(8,128)(2,1)S(1)} %pad_maximum_fusion.refs_2_), channel_id=1, source_target_pairs={{0,2},{1,5},{2,0},{3,7},{4,6},{5,1},{6,4},{7,3},{8,10},{9,13},{10,... | collective-permute-start | bytes 1966088 | tf_op jit(solution)/shard_map/ppermute | solution.py:643
  152.5 2.3 %collective-permute-done.16 = bf16[384,256]{1,0:T(8,128)(2,1)S(1)} collective-permute-done((bf16[384,256]{1,0:T(8,128)(2,1)S(1)}, bf16[384,256]{1,0:T(8,128)(2,1)S(1)}, u32[]{:S(2)}, u32[]{:S(2)}) %collective-permute-start.16) | collective-permute-done | bytes 196640 | tf_op jit(solution)/shard_map/ppermute | solution.py:643
  154.9 3.3 %collective-permute-start.17 = (bf16[768,256]{1,0:T(8,128)(2,1)S(1)}, bf16[768,256]{1,0:T(8,128)(2,1)S(1)}, u32[]{:S(2)}, u32[]{:S(2)}) collective-permute-start(bf16[768,256]{1,0:T(8,128)(2,1)S(1)} %pad_maximum_fusion.1.refs_0_), channel_id=1, source_target_pairs={{0,8},{1,9},{2,10},{3,11},{4,12},{5,13},{6,14},{7,15},{8,0},{9,1},... | collective-permute-start | bytes 1179656 | tf_op jit(solution)/shard_map/ppermute | solution.py:643
  158.2 1.6 shard_map.218
  159.9 4.1 %collective-permute-done.17.refs_1_ = bf16[768,256]{1,0:T(8,128)(2,1)S(1)} collective-permute-done((bf16[768,256]{1,0:T(8,128)(2,1)S(1)}, bf16[768,256]{1,0:T(8,128)(2,1)S(1)}, u32[]{:S(2)}, u32[]{:S(2)}) %collective-permute-start.17) | collective-permute-done | bytes 393248 | tf_op jit(solution)/shard_map/ppermute | solution.py:643
  164.0 2.3 %shard_map.224 = (f32[2,512,256]{2,1,0:T(8,128)}, f32[2,512,256]{2,1,0:T(8,128)}, f32[2,256,512]{2,1,0:T(8,128)}, f32[2,1024,128]{2,1,0:T(8,128)}) custom-call(bf16[768,256]{1,0:T(8,128)(2,1)S(1)} %pad_maximum_fusion.1.refs_0_, bf16[768,256]{1,0:T(8,128)(2,1)S(1)} %collective-permute-done.17.refs_1_, bf16[1280,256]{1,0:T(8,128)(2,1)S(1)} %pad_maximum_fusion.refs_2_, ...), custom_call_target="tpu_custom_call" | custom-call | bytes 2097152 | tf_op jit(solution)/shard_map/pallas_call | solution.py:847
  (55 shorter events, 3.7 us)
Async XLA Ops:
  0.6 6.8 %copy-start = (bf16[4,256,256]{2,1,0:T(8,128)(2,1)S(1)}, bf16[4,256,256]{2,1,0:T(8,128)(2,1)}, u32[]{:S(2)}) copy-start(bf16[4,256,256]{2,1,0:T(8,128)(2,1)} %refs_4_.1) | copy-start | bytes 1572868
  2.1 5.1 %collective-permute-start.2 = (bf16[2,512,256]{2,1,0:T(8,128)(2,1)S(1)}, bf16[2,512,256]{2,1,0:T(8,128)(2,1)S(1)}, u32[]{:S(2)}, u32[]{:S(2)}) collective-permute-start(bf16[2,512,256]{2,1,0:T(8,128)(2,1)S(1)} %reshape.40.refs_7_.refs_5_.refs_13_), channel_id=1, source_target_pairs={{0,1},{1,0},{2,3},{3,2},{4,5},{5,4},{6,7},{7,6},{8,9},{9,8},{10,11... | collective-permute-start | bytes 1572872 | tf_op jit(solution)/shard_map/ppermute | solution.py:605
  2.6 19.4 %collective-permute-start = (bf16[4,256,256]{2,1,0:T(8,128)(2,1)}, bf16[4,256,256]{2,1,0:T(8,128)(2,1)S(1)}, u32[]{:S(2)}, u32[]{:S(2)}) collective-permute-start(bf16[4,256,256]{2,1,0:T(8,128)(2,1)} %refs_4_.1), channel_id=1, source_target_pairs={{0,1},{1,0},{2,3},{3,2},{4,5},{5,4},{6,7},{7,6},{8,9},{9,8},{10,11... | collective-permute-start | bytes 1572872 | tf_op jit(solution)/shard_map/ppermute | solution.py:605
  3.4 0.7 copy-start.5
  5.5 1.3 collective-permute-start.1
  6.0 18.1 %collective-permute-start.4 = (bf16[2,256,512]{2,1,0:T(8,128)(2,1)}, bf16[2,256,512]{2,1,0:T(8,128)(2,1)S(1)}, u32[]{:S(2)}, u32[]{:S(2)}) collective-permute-start(bf16[2,256,512]{2,1,0:T(8,128)(2,1)} %bitcast.5), channel_id=1, source_target_pairs={{0,1},{1,0},{2,3},{3,2},{4,5},{5,4},{6,7},{7,6},{8,9},{9,8},{10,11... | collective-permute-start | bytes 1572872 | tf_op jit(solution)/shard_map/ppermute | solution.py:605
  6.1 18.0 %collective-permute-start.3 = (bf16[4,256,256]{2,1,0:T(8,128)(2,1)}, bf16[4,256,256]{2,1,0:T(8,128)(2,1)S(1)}, u32[]{:S(2)}, u32[]{:S(2)}) collective-permute-start(bf16[4,256,256]{2,1,0:T(8,128)(2,1)} %refs_16_.1), channel_id=1, source_target_pairs={{0,1},{1,0},{2,3},{3,2},{4,5},{5,4},{6,7},{7,6},{8,9},{9,8},{10,11... | collective-permute-start | bytes 1572872 | tf_op jit(solution)/shard_map/ppermute | solution.py:605
  6.9 17.3 %collective-permute-start.5 = (bf16[2,512,256]{2,1,0:T(8,128)(2,1)}, bf16[2,512,256]{2,1,0:T(8,128)(2,1)S(1)}, u32[]{:S(2)}, u32[]{:S(2)}) collective-permute-start(bf16[2,512,256]{2,1,0:T(8,128)(2,1)} %refs_15_.1), channel_id=1, source_target_pairs={{0,1},{1,0},{2,3},{3,2},{4,5},{5,4},{6,7},{7,6},{8,9},{9,8},{10,11... | collective-permute-start | bytes 1572872 | tf_op jit(solution)/shard_map/ppermute | solution.py:605
  7.2 16.9 %collective-permute-start.6 = (bf16[2,512,256]{2,1,0:T(8,128)(2,1)}, bf16[2,512,256]{2,1,0:T(8,128)(2,1)S(1)}, u32[]{:S(2)}, u32[]{:S(2)}) collective-permute-start(bf16[2,512,256]{2,1,0:T(8,128)(2,1)} %refs_17_.1), channel_id=1, source_target_pairs={{0,1},{1,0},{2,3},{3,2},{4,5},{5,4},{6,7},{7,6},{8,9},{9,8},{10,11... | collective-permute-start | bytes 1572872 | tf_op jit(solution)/shard_map/ppermute | solution.py:605
  22.0 12.3 %copy-start.1 = (bf16[2,2,128,512]{3,2,1,0:T(8,128)(2,1)S(1)}, bf16[2,2,128,512]{3,2,1,0:T(8,128)(2,1)}, u32[]{:S(2)}) copy-start(bf16[2,2,128,512]{3,2,1,0:T(8,128)(2,1)} %param.16) | copy-start | bytes 1572868
  22.0 12.3 %copy-start.2 = (bf16[2,512,256]{2,1,0:T(8,128)(2,1)S(1)}, bf16[2,512,256]{2,1,0:T(8,128)(2,1)}, u32[]{:S(2)}) copy-start(bf16[2,512,256]{2,1,0:T(8,128)(2,1)} %refs_15_.1) | copy-start | bytes 1572868
  22.0 12.3 %copy-start.3 = (bf16[2,512,256]{2,1,0:T(8,128)(2,1)S(1)}, bf16[2,512,256]{2,1,0:T(8,128)(2,1)}, u32[]{:S(2)}) copy-start(bf16[2,512,256]{2,1,0:T(8,128)(2,1)} %refs_17_.1) | copy-start | bytes 1572868
  47.5 11.8 %copy-start.4 = (bf16[4,256,256]{2,1,0:T(8,128)(2,1)S(1)}, bf16[4,256,256]{2,1,0:T(8,128)(2,1)}, u32[]{:S(2)}) copy-start(bf16[4,256,256]{2,1,0:T(8,128)(2,1)} %refs_16_.1) | copy-start | bytes 1572868
  87.9 3.6 %collective-permute-start.7 = (bf16[2048,256]{1,0:T(8,128)(2,1)S(1)}, bf16[2048,256]{1,0:T(8,128)(2,1)S(1)}, u32[]{:S(2)}, u32[]{:S(2)}) collective-permute-start(bf16[2048,256]{1,0:T(8,128)(2,1)S(1)} %get-tuple-element.170), channel_id=1, source_target_pairs={{0,1},{1,0},{2,3},{3,2},{4,5},{5,4},{6,7},{7,6},{8,9},{9,8},{10,11... | collective-permute-start | bytes 3145736 | tf_op jit(solution)/shard_map/ppermute | solution.py:605
  101.6 1.5 collective-permute-start.18
  103.3 10.7 %collective-permute-start.19 = (bf16[1280,256]{1,0:T(8,128)(2,1)S(1)}, bf16[1280,256]{1,0:T(8,128)(2,1)S(1)}, u32[]{:S(2)}, u32[]{:S(2)}) collective-permute-start(bf16[1280,256]{1,0:T(8,128)(2,1)S(1)} %get-tuple-element.213), channel_id=1, source_target_pairs={{0,2},{1,5},{2,0},{3,7},{4,6},{5,1},{6,4},{7,3},{8,10},{9,13},{10,... | collective-permute-start | bytes 1966088 | tf_op jit(solution)/shard_map/ppermute | solution.py:643
  104.2 3.8 %collective-permute-start.8 = (bf16[1024,256]{1,0:T(8,128)(2,1)S(1)}, bf16[1024,256]{1,0:T(8,128)(2,1)S(1)}, u32[]{:S(2)}, u32[]{:S(2)}) collective-permute-start(bf16[1024,256]{1,0:T(8,128)(2,1)S(1)} %get-tuple-element.177), channel_id=1, source_target_pairs={{0,1},{1,0},{2,3},{3,2},{4,5},{5,4},{6,7},{7,6},{8,9},{9,8},{10,11... | collective-permute-start | bytes 1572872 | tf_op jit(solution)/shard_map/ppermute | solution.py:605
  106.2 1.8 %collective-permute-start.9 = (bf16[544,256]{1,0:T(8,128)(2,1)S(1)}, bf16[544,256]{1,0:T(8,128)(2,1)S(1)}, u32[]{:S(2)}, u32[]{:S(2)}) collective-permute-start(bf16[544,256]{1,0:T(8,128)(2,1)S(1)} %get-tuple-element.189), channel_id=1, source_target_pairs={{0,1},{1,0},{2,3},{3,2},{4,5},{5,4},{6,7},{7,6},{8,9},{9,8},{10,11... | collective-permute-start | bytes 835592 | tf_op jit(solution)/shard_map/ppermute | solution.py:605
  108.2 13.9 %collective-permute-start.10 = (bf16[800,256]{1,0:T(8,128)(2,1)S(1)}, bf16[800,256]{1,0:T(8,128)(2,1)S(1)}, u32[]{:S(2)}, u32[]{:S(2)}) collective-permute-start(bf16[800,256]{1,0:T(8,128)(2,1)S(1)} %get-tuple-element.192), channel_id=1, source_target_pairs={{0,8},{1,9},{2,10},{3,11},{4,12},{5,13},{6,14},{7,15},{8,0},{9,1},... | collective-permute-start | bytes 1228808 | tf_op jit(solution)/shard_map/ppermute | solution.py:643
  114.1 7.1 %collective-permute-start.20 = (bf16[640,256]{1,0:T(8,128)(2,1)S(1)}, bf16[640,256]{1,0:T(8,128)(2,1)S(1)}, u32[]{:S(2)}, u32[]{:S(2)}) collective-permute-start(bf16[640,256]{1,0:T(8,128)(2,1)S(1)} %get-tuple-element.215), channel_id=1, source_target_pairs={{0,4},{1,3},{2,6},{3,1},{4,0},{5,7},{6,2},{7,5},{8,12},{9,11},{10,... | collective-permute-start | bytes 983048 | tf_op jit(solution)/shard_map/ppermute | solution.py:643
  121.4 5.4 %collective-permute-start.21 = (bf16[320,256]{1,0:T(8,128)(2,1)S(1)}, bf16[320,256]{1,0:T(8,128)(2,1)S(1)}, u32[]{:S(2)}, u32[]{:S(2)}) collective-permute-start(bf16[320,256]{1,0:T(8,128)(2,1)S(1)} %get-tuple-element.217), channel_id=1, source_target_pairs={{0,8},{1,9},{2,10},{3,11},{4,12},{5,13},{6,14},{7,15},{8,0},{9,1},... | collective-permute-start | bytes 491528 | tf_op jit(solution)/shard_map/ppermute | solution.py:643
  122.2 5.9 %collective-permute-start.11 = (bf16[416,256]{1,0:T(8,128)(2,1)S(1)}, bf16[416,256]{1,0:T(8,128)(2,1)S(1)}, u32[]{:S(2)}, u32[]{:S(2)}) collective-permute-start(bf16[416,256]{1,0:T(8,128)(2,1)S(1)} %get-tuple-element.194), channel_id=1, source_target_pairs={{0,4},{1,3},{2,6},{3,1},{4,0},{5,7},{6,2},{7,5},{8,12},{9,11},{10,... | collective-permute-start | bytes 638984 | tf_op jit(solution)/shard_map/ppermute | solution.py:643
  126.8 8.2 %collective-permute-start.22 = (bf16[320,256]{1,0:T(8,128)(2,1)S(1)}, bf16[320,256]{1,0:T(8,128)(2,1)S(1)}, u32[]{:S(2)}, u32[]{:S(2)}) collective-permute-start(bf16[320,256]{1,0:T(8,128)(2,1)S(1)} %shard_map.222.refs_0_), channel_id=1, source_target_pairs={{0,16},{1,17},{2,18},{3,19},{4,20},{5,21},{6,22},{7,23},{8,24},{9,... | collective-permute-start | bytes 491528 | tf_op jit(solution)/shard_map/ppermute | solution.py:643
  128.2 7.0 %collective-permute-start.12 = (bf16[224,256]{1,0:T(8,128)(2,1)S(1)}, bf16[224,256]{1,0:T(8,128)(2,1)S(1)}, u32[]{:S(2)}, u32[]{:S(2)}) collective-permute-start(bf16[224,256]{1,0:T(8,128)(2,1)S(1)} %get-tuple-element.196), channel_id=1, source_target_pairs={{0,2},{1,5},{2,0},{3,7},{4,6},{5,1},{6,4},{7,3},{8,10},{9,13},{10,... | collective-permute-start | bytes 344072 | tf_op jit(solution)/shard_map/ppermute | solution.py:643
  135.0 6.7 %collective-permute-start.23 = (bf16[320,256]{1,0:T(8,128)(2,1)S(1)}, bf16[320,256]{1,0:T(8,128)(2,1)S(1)}, u32[]{:S(2)}, u32[]{:S(2)}) collective-permute-start(bf16[320,256]{1,0:T(8,128)(2,1)S(1)} %shard_map.223), channel_id=1, source_target_pairs={{0,8},{1,9},{2,10},{3,11},{4,12},{5,13},{6,14},{7,15},{8,0},{9,1},... | collective-permute-start | bytes 491528 | tf_op jit(solution)/shard_map/ppermute | solution.py:643
  135.2 5.9 %collective-permute-start.13 = (bf16[224,256]{1,0:T(8,128)(2,1)S(1)}, bf16[224,256]{1,0:T(8,128)(2,1)S(1)}, u32[]{:S(2)}, u32[]{:S(2)}) collective-permute-start(bf16[224,256]{1,0:T(8,128)(2,1)S(1)} %shard_map.215.refs_0_), channel_id=1, source_target_pairs={{0,16},{1,17},{2,18},{3,19},{4,20},{5,21},{6,22},{7,23},{8,24},{9,... | collective-permute-start | bytes 344072 | tf_op jit(solution)/shard_map/ppermute | solution.py:643
  137.3 20.9 %collective-permute-start.14 = (bf16[2,512,256]{2,1,0:T(8,128)(2,1)S(1)}, bf16[2,512,256]{2,1,0:T(8,128)(2,1)S(1)}, u32[]{:S(2)}, u32[]{:S(2)}) collective-permute-start(bf16[2,512,256]{2,1,0:T(8,128)(2,1)S(1)} %get-tuple-element.202), channel_id=1, source_target_pairs={{0,1},{1,0},{2,3},{3,2},{4,5},{5,4},{6,7},{7,6},{8,9},{9,8},{10,11... | collective-permute-start | bytes 1572872 | tf_op jit(solution)/shard_map/ppermute | solution.py:605
  141.1 5.8 %collective-permute-start.15 = (bf16[192,256]{1,0:T(8,128)(2,1)S(1)}, bf16[192,256]{1,0:T(8,128)(2,1)S(1)}, u32[]{:S(2)}, u32[]{:S(2)}) collective-permute-start(bf16[192,256]{1,0:T(8,128)(2,1)S(1)} %get-tuple-element.207), channel_id=1, source_target_pairs={{0,2},{1,5},{2,0},{3,7},{4,6},{5,1},{6,4},{7,3},{8,10},{9,13},{10,... | collective-permute-start | bytes 294920 | tf_op jit(solution)/shard_map/ppermute | solution.py:643
  141.8 8.3 %collective-permute-start.24 = (bf16[640,256]{1,0:T(8,128)(2,1)S(1)}, bf16[640,256]{1,0:T(8,128)(2,1)S(1)}, u32[]{:S(2)}, u32[]{:S(2)}) collective-permute-start(bf16[640,256]{1,0:T(8,128)(2,1)S(1)} %pad_maximum_fusion.2), channel_id=1, source_target_pairs={{0,4},{1,3},{2,6},{3,1},{4,0},{5,7},{6,2},{7,5},{8,12},{9,11},{10,... | collective-permute-start | bytes 983048 | tf_op jit(solution)/shard_map/ppermute | solution.py:643
  146.9 7.9 %collective-permute-start.16 = (bf16[384,256]{1,0:T(8,128)(2,1)S(1)}, bf16[384,256]{1,0:T(8,128)(2,1)S(1)}, u32[]{:S(2)}, u32[]{:S(2)}) collective-permute-start(bf16[384,256]{1,0:T(8,128)(2,1)S(1)} %pad_maximum_fusion.3), channel_id=1, source_target_pairs={{0,4},{1,3},{2,6},{3,1},{4,0},{5,7},{6,2},{7,5},{8,12},{9,11},{10,... | collective-permute-start | bytes 589832 | tf_op jit(solution)/shard_map/ppermute | solution.py:643
  150.3 13.7 %collective-permute-start.25 = (bf16[1280,256]{1,0:T(8,128)(2,1)S(1)}, bf16[1280,256]{1,0:T(8,128)(2,1)S(1)}, u32[]{:S(2)}, u32[]{:S(2)}) collective-permute-start(bf16[1280,256]{1,0:T(8,128)(2,1)S(1)} %pad_maximum_fusion.refs_2_), channel_id=1, source_target_pairs={{0,2},{1,5},{2,0},{3,7},{4,6},{5,1},{6,4},{7,3},{8,10},{9,13},{10,... | collective-permute-start | bytes 1966088 | tf_op jit(solution)/shard_map/ppermute | solution.py:643
  154.9 9.1 %collective-permute-start.17 = (bf16[768,256]{1,0:T(8,128)(2,1)S(1)}, bf16[768,256]{1,0:T(8,128)(2,1)S(1)}, u32[]{:S(2)}, u32[]{:S(2)}) collective-permute-start(bf16[768,256]{1,0:T(8,128)(2,1)S(1)} %pad_maximum_fusion.1.refs_0_), channel_id=1, source_target_pairs={{0,8},{1,9},{2,10},{3,11},{4,12},{5,13},{6,14},{7,15},{8,0},{9,1},... | collective-permute-start | bytes 1179656 | tf_op jit(solution)/shard_map/ppermute | solution.py:643

commit v5 on v4

--- a/solution.py
+++ b/solution.py
@@ -425,9 +425,9 @@
     _, core = place()
     mine, other = own_cols(core, 256), oth_cols(core, 256)
     left = act[...].T
-    l_own[...] = mm(left, dl[:, mine])
+    l_own[...] = mm(left, dl[:, mine]).astype(bf16)
     l_oth[...] = mm(left, dl[:, other]).astype(bf16)
-    g_own[0:512, :] = mm(left, dg[:, mine])
+    g_own[0:512, :] = mm(left, dg[:, mine]).astype(bf16)
     g_oth[0:512, :] = mm(left, dg[:, other]).astype(bf16)
     for ref, cut in ((g_own, slice(0, 256)), (g_oth, slice(256, 512))):
         left = sl[:, cut].T
@@ -437,7 +437,7 @@
 
 def in_grads(nl, dp, g_own, g_oth):
     left = nl[...].T
-    g_own[...] = mm(left, dp[:, :256])
+    g_own[...] = mm(left, dp[:, :256]).astype(bf16)
     g_oth[...] = mm(left, dp[:, 256:]).astype(bf16)
 
 
@@ -671,7 +671,7 @@
         half = own.shape[0] // 2
         for out, which in ((mine, bit), (other, 1 - bit)):
             rows = pl.ds(pl.multiple_of(which * half, half), half)
-            out[at : at + half, :] = (own[rows, :] + got[rows, :].astype(f32)).astype(bf16)
+            out[at : at + half, :] = (own[rows, :].astype(f32) + got[rows, :].astype(f32)).astype(bf16)
         at += half
     if small is not None:
         total = small[...] + get_small(pairs[-1][1], pairs[-1][0].shape[0])
@@ -798,6 +798,14 @@
         return ref.at[pl.ds(lax.axis_index("state") * 2, 2)] if self.at == "rows" else ref.at[self.at]
 
 
+class Part:
+    def __init__(self, value, at):
+        self.value, self.at = value, at
+
+    def view(self, ref):
+        return ref.at[pl.ds(lax.axis_index("state") * 2, 2)] if self.at == "rows" else ref.at[self.at]
+
+
 class Held:
     def __init__(self, source, ref, sem):
         self.ref, self.copy, self.shape, self.dtype = ref, pltpu.make_async_copy(source, ref, sem), ref.shape, ref.dtype
@@ -816,7 +824,8 @@
 def run(kernel, outs, groups, scratch=(), limit=24, flops=0):
     args = [a for g in groups for a in (g if isinstance(g, tuple) else (g,))]
     far_in = [i for i, a in enumerate(args) if isinstance(a, Far)]
-    moved = sum(a.value.size * a.value.dtype.itemsize if isinstance(a, Far) else a.size * a.dtype.itemsize for a in args)
+    arrays = [a.value if isinstance(a, (Far, Part)) else a for a in args]
+    moved = sum(a.size * a.dtype.itemsize for a in arrays)
 
     def whole(*refs):
         ins, results = list(refs[: len(args)]), list(refs[len(args) : len(args) + len(outs)])
@@ -826,6 +835,7 @@
             buffers, sem = rest[len(scratch) : -1], rest[-1]
         for j, i in enumerate(far_in):
             ins[i] = Held(args[i].source(ins[i]), buffers[j], sem.at[j])
+        ins = [a.view(r) if isinstance(a, Part) else r for r, a in zip(ins, args)]
         grouped, at = [], 0
         for g in groups:
             if isinstance(g, tuple):
@@ -852,7 +862,7 @@
         scratch_shapes=[pltpu.VMEM(*s) for s in scratch] + held,
         compiler_params=pltpu.CompilerParams(vmem_limit_bytes=limit * 2**20),
         cost_estimate=pl.CostEstimate(flops=flops, bytes_accessed=moved, transcendentals=0),
-    )(*[a.value if isinstance(a, Far) else a for a in args])
+    )(*arrays)
 
 
 def body(tokens, gain, bias, in_proj, out_proj, rate_log, angle_log, skip, glu_lin, glu_gate, positions, cotangent):
@@ -867,14 +877,14 @@
     low = ((n, 512), bf16)
     full = ((n, 512), f32)
 
-    (stats,) = run(stats_kernel, [((2 * peers, 4, 128), f32)], (Far(tokens),))
+    (stats,) = run(stats_kernel, [((2 * peers, 4, 128), f32)], (tokens,))
     raw, at = 0.0, 0
     for v in (gain, bias, skip, rate_log, angle_log):
         raw, at = raw + jnp.pad(v.astype(f32), ((0, 0), (at, 1024 - at - v.shape[1]))), at + v.shape[1]
     w_in = in_proj.reshape(2, 512, 256)
     w_out = out_proj.reshape(2, 256, 512)
     x_oth, cot_oth, in_oth, out_oth, lin_oth, gate_oth = (swap(w) for w in (tokens, cotangent, w_in, w_out, glu_lin, glu_gate))
-    enter = [(Far(w_in, k), Far(in_oth, k)) for k in range(2)]
+    enter = [(Part(w_in, k), Part(in_oth, k)) for k in range(2)]
     own, keep, dk, perm = run(
         functools.partial(prep_kernel, peers, steps, span),
         [((32, 128), f32), ((2, n, 128), f32), ((2, peers, 8, 128), f32), ((2, n, n), bf16)],
@@ -886,9 +896,9 @@
     scan_outs = [full, ((16, 8, 128), f32), for_seq, ((8, 512), f32)]
     xp, nl0, proj, comp, summ, nrm0 = run(
         functools.partial(enter_first_kernel, peers, steps, count), [low, low] + scan_outs,
-        (lax.all_to_all(stats, ("seq", "state"), 0, 0), Far(tokens, "rows"), Far(x_oth, "rows"), perm, own, oth, keep) + enter[0], [packed], flops=2 * one)
+        (lax.all_to_all(stats, ("seq", "state"), 0, 0), Part(tokens, "rows"), Part(x_oth, "rows"), perm, own, oth, keep) + enter[0], [packed], flops=2 * one)
     got, (cot_oth, out_oth, lin_oth, gate_oth) = blocking(summ, "seq", (cot_oth, out_oth, lin_oth, gate_oth))
-    glu = [tuple(Far(w, k) for w in (w_out, out_oth, glu_lin, lin_oth, glu_gate, gate_oth)) for k in range(2)]
+    glu = [tuple((Part if i % 2 else Part)(w, k) for i, w in enumerate((w_out, out_oth, glu_lin, lin_oth, glu_gate, gate_oth))) for k in range(2)]
     cin0, sl0, gp0, act0, sig0, qv0, y0, stats = run(
         functools.partial(leave_first_kernel, peers, steps),
         [((SLAB, 512), f32), low, low, low, low, low, full, for_all],
@@ -902,26 +912,26 @@
     cin1, result, d_out1, act1, dl1, dg1, sl1, dml1, skip1, dst, comp, summ = run(
         functools.partial(turn_kernel, peers, steps),
         [((SLAB, 512), f32), low, low, low, low, low, low, low] + turn_outs + [for_seq],
-        (got, comp, dk, own, oth, keep, proj, y0, nrm1) + glu[1] + (perm, Far(cotangent, "rows"), Far(cot_oth, "rows")),
+        (got, comp, dk, own, oth, keep, proj, y0, nrm1) + glu[1] + (perm, Part(cotangent, "rows"), Part(cot_oth, "rows")),
         [packed, ordered, full, full, full, full], flops=8 * one)
     got, _ = blocking(summ, "seq", ())
     g1_own, g1_oth, s1_own, s1_oth, dn, stats = run(
         functools.partial(adjoint_second_kernel, peers, steps),
-        [((2048, 256), f32), ((2048, 256), bf16), ((8, 128), f32), ((8, 128), f32), full, for_all],
+        [((2048, 256), bf16), ((2048, 256), bf16), ((8, 128), f32), ((8, 128), f32), full, for_all],
         (got, comp, dk, own, oth, keep, nl1, y0, nrm1, cin1, sl1, dst, dml1) + enter[1] + (skip1, act1, dl1, dg1),
         [packed, ordered, full, low], flops=6 * one)
     got, (g1_oth,) = blocking(stats, ("seq", "state"), (g1_oth,))
     g1_got = swap(g1_oth)
     d_out0, dml0, totals1, l0_own, l0_oth, g0_own, g0_oth, skip0, dst, comp, summ = run(
         functools.partial(back_first_kernel, steps, count),
-        [full, low, ((8, 512), f32), ((512, 256), f32), ((512, 256), bf16), ((1024, 256), f32), ((1024, 256), bf16)] + turn_outs + [for_seq],
+        [full, low, ((8, 512), f32), ((512, 256), bf16), ((512, 256), bf16), ((1024, 256), bf16), ((1024, 256), bf16)] + turn_outs + [for_seq],
         (got, dn, y0, nrm1, d_out1, own, oth, keep, xp, nrm0, gp0, sig0, qv0) + glu[0] + (act0, sl0),
         [packed, low, low], flops=6 * one)
     got, (l0_oth, g0_oth, g1_got, result) = blocking(summ, "seq", (l0_oth, g0_oth, g1_got, result))
     l0_got, g0_got = swap(l0_oth), swap(g0_oth)
     i0_own, i0_oth, s_own, partial = run(
         functools.partial(adjoint_first_kernel, peers, steps),
-        [((512, 256), f32), ((544, 256), bf16), ((16, 128), f32), low],
+        [((512, 256), bf16), ((544, 256), bf16), ((16, 128), f32), low],
         (got, comp, dk, own, oth, keep, nl0, xp, nrm0, cin0, sl0, dst, dml0) + enter[0]
         + (skip0, d_out0, s1_own, s1_oth),
         [packed, ordered, full, low, ((16, 128), f32)], flops=3 * one)
@@ -930,17 +940,20 @@
     bulk0 = SeqSum([(g0_own, g0_got), (i0_own, i0_got)], axes_orders((2, 1, 0, 3), (2, 0, 1, 3)), s_own)
     own_parts, oth_parts = run(order_kernel, [((2, n, 256), bf16)] * 2, (perm, result, partial), flops=2 * one)
     got_parts = swap(oth_parts)
-    while not bulk1.step():
-        pass
-    while not bulk0.small:
-        bulk0.step()
+    for _ in range(3):
+        bulk1.step()
+    ended = False
+    while not bulk0.step():
+        if not ended:
+            bulk1.after(bulk0.send)
+            ended = bulk1.step()
+    while not ended:
+        ended = bulk1.step()
     quad = (2, 2, span, width)
     block_out, d_in, ngg, bias_grad, skip_grad, rate_grad, angle_grad = run(
         functools.partial(finish_kernel, count),
         [((rows, span, width), bf16), ((rows, span, width), f32), ((2, 256), f32), ((2, 256), f32), ((2, 256), f32), ((2, 128), f32), ((2, 128), f32)],
-        (bulk0.small[0], totals1, own_parts.reshape(quad), got_parts.reshape(quad), Far(tokens), nrm0, raw))
-    while not bulk0.step():
-        pass
+        (bulk0.small[0], totals1, own_parts.reshape(quad), got_parts.reshape(quad), tokens, nrm0, raw))
     lin_grad, gate_grad, out_grad, in_grad = run(
         functools.partial(unpack_kernel, bulk0.masks[0], bulk1.masks[0]),
         [((2, 512, 256), f32), ((2, 512, 256), f32), ((2, 256, 512), f32), ((2, 1024, 128), f32)],

time: 167 us -> 159 us (0.952)
  Pallas kernels: 28 us -> 21.2 us
    pallas_call x22, Pallas kernels: 28 us -> 21.2 us  [run(): pl.pallas_call(whole, out_shape=[jax.ShapeDtypeStruct(o[0], o[1]) for o i...]
  transfers between devices with their start and end apart: 26 -> 26, of which waited for: 13 -> 13; matrix products, arithmetic and copies ran while one was open for 1% -> 0% of each run, Pallas kernels for 7% -> 6%
where the time goes in v5:
time: 159 us
  blocking collectives  74.9 us (47%)
  waiting for transfers between devices  42.7 us (27%)
  Pallas kernels  21.2 us (13%)
  starting transfers between devices  17.1 us (11%)
    all_to_all x6, blocking collectives, blocking(): lax.all_to_all(value, axes, 0, 0)  60.5 us
    ppermute x14, waiting for transfers between devices, partners(): lax.ppermute(value, ('seq', 'state'), [(2 * i + c, 2 * (i ^ masks[c]) + c...  39.7 us
    pallas_call x22, Pallas kernels, run(): pl.pallas_call(whole, out_shape=[jax.ShapeDtypeStruct(o[0], o[1]) for o i...  21.2 us
    all_to_all x1, blocking collectives, body(): lax.all_to_all(stats, ('seq', 'state'), 0, 0)  14.4 us
    ppermute x14, starting transfers between devices, partners(): lax.ppermute(value, ('seq', 'state'), [(2 * i + c, 2 * (i ^ masks[c]) + c...  14.2 us
  transfers between devices with their start and end apart: 26, of which 13 were waited for; matrix products, arithmetic and copies ran while one was open for 0% of the time, Pallas kernels for 6%

profile of v5, /device:TPU:0, one launch (start us, length us, event | category | flops | bytes accessed | tf_op | source)
XLA Modules:
  0.0 158.7 jit_solution(14895473278027587162)
XLA Ops:
  0.7 1.4 reshape.40.refs_7_.refs_5_.refs_13_
  2.2 0.5 collective-permute-start.2
  2.8 1.4 shard_map.204
  4.3 0.5 collective-permute-start.1
  4.8 0.4 collective-permute-start.3
  6.2 14.4 %all_to_all.35.refs_0_ = f32[32,4,128]{2,1,0:T(4,128)S(1)} all-to-all(f32[32,4,128]{2,1,0:T(4,128)S(1)} %shard_map.203), channel_id=1, replica_groups=mesh['seq'=16,'state'=2] {'seq','state'}, dimensions={0} | all-to-all | bytes 131072 | tf_op jit(solution)/shard_map/all_to_all | solution.py:899
  20.6 1.0 shard_map.205
  21.7 10.1 %all_to_all.36.refs_0_ = f32[16,8,128]{2,1,0:T(8,128)S(1)} all-to-all(f32[16,8,128]{2,1,0:T(8,128)S(1)} %get-tuple-element.126), channel_id=1, replica_groups=mesh['seq'=16,'state'=2] {'seq'}, dimensions={0} | all-to-all | bytes 131072 | tf_op jit(solution)/shard_map/all_to_all | solution.py:617
  31.8 2.1 %shard_map.206 = (f32[16,512]{1,0:T(8,128)S(1)}, bf16[512,512]{1,0:T(8,128)(2,1)S(1)}, bf16[512,512]{1,0:T(8,128)(2,1)S(1)}, bf16[512,512]{1,0:T(8,128)(2,1)S(1)...) custom-call(f32[16,8,128]{2,1,0:T(8,128)S(1)} %all_to_all.36.refs_0_, ...), custom_call_target="tpu_custom_call" | custom-call | flops 805306368 | bytes 5554176 | tf_op jit(solution)/shard_map/pallas_call | solution.py:857
  33.9 9.9 %all_to_all.37.refs_0_ = f32[32,8,128]{2,1,0:T(8,128)S(1)} all-to-all(f32[32,8,128]{2,1,0:T(8,128)S(1)} %get-tuple-element.140), channel_id=1, replica_groups=mesh['seq'=16,'state'=2] {'seq','state'}, dimensions={0} | all-to-all | bytes 262144 | tf_op jit(solution)/shard_map/all_to_all | solution.py:617
  43.9 0.8 shard_map.207
  44.7 10.2 %all_to_all.38.refs_0_ = f32[16,8,128]{2,1,0:T(8,128)S(1)} all-to-all(f32[16,8,128]{2,1,0:T(8,128)S(1)} %get-tuple-element.142), channel_id=1, replica_groups=mesh['seq'=16,'state'=2] {'seq'}, dimensions={0} | all-to-all | bytes 131072 | tf_op jit(solution)/shard_map/all_to_all | solution.py:617
  54.9 3.8 %shard_map.208 = (f32[16,512]{1,0:T(8,128)S(1)}, bf16[512,512]{1,0:T(8,128)(2,1)S(1)}, bf16[512,512]{1,0:T(8,128)(2,1)S(1)}, bf16[512,512]{1,0:T(8,128)(2,1)S(1)...) custom-call(f32[16,8,128]{2,1,0:T(8,128)S(1)} %all_to_all.38.refs_0_, ...), custom_call_target="tpu_custom_call" | custom-call | flops 2147483648 | bytes 8175616 | tf_op jit(solution)/shard_map/pallas_call | solution.py:857
  58.7 10.1 %all_to_all.39.refs_0_ = f32[16,8,128]{2,1,0:T(8,128)S(1)} all-to-all(f32[16,8,128]{2,1,0:T(8,128)S(1)} %get-tuple-element.147), channel_id=1, replica_groups=mesh['seq'=16,'state'=2] {'seq'}, dimensions={0} | all-to-all | bytes 131072 | tf_op jit(solution)/shard_map/all_to_all | solution.py:617
  68.8 2.2 %shard_map.209 = (bf16[2048,256]{1,0:T(8,128)(2,1)S(1)}, bf16[2048,256]{1,0:T(8,128)(2,1)S(1)}, f32[8,128]{1,0:T(8,128)S(1)}, f32[8,128]{1,0:T(8,128)S(1)}, f32[...) custom-call(f32[16,8,128]{2,1,0:T(8,128)S(1)} %all_to_all.39.refs_0_, f32[16,8,128]{2,1,0:T(8,128)S(1)} %get-tuple-element.148.refs_1_, ...), custom_call_target="tpu_custom_call" | custom-call | flops 1610612736 | bytes 7176192 | tf_op jit(solution)/shard_map/pallas_call | solution.py:857
  71.0 9.9 %all_to_all.40.refs_0_ = f32[32,8,128]{2,1,0:T(8,128)S(1)} all-to-all(f32[32,8,128]{2,1,0:T(8,128)S(1)} %get-tuple-element.160), channel_id=1, replica_groups=mesh['seq'=16,'state'=2] {'seq','state'}, dimensions={0} | all-to-all | bytes 262144 | tf_op jit(solution)/shard_map/all_to_all | solution.py:617
  81.2 2.4 %shard_map.210 = (f32[512,512]{1,0:T(8,128)S(1)}, bf16[512,512]{1,0:T(8,128)(2,1)S(1)}, f32[8,512]{1,0:T(8,128)S(1)}, bf16[512,256]{1,0:T(8,128)(2,1)S(1)}, bf16...) custom-call(f32[32,8,128]{2,1,0:T(8,128)S(1)} %all_to_all.40.refs_0_, ...), custom_call_target="tpu_custom_call" | custom-call | flops 1610612736 | bytes 9633792 | tf_op jit(solution)/shard_map/pallas_call | solution.py:857
  83.6 10.2 %all_to_all.41.refs_0_ = f32[16,8,128]{2,1,0:T(8,128)S(1)} all-to-all(f32[16,8,128]{2,1,0:T(8,128)S(1)} %get-tuple-element.176), channel_id=1, replica_groups=mesh['seq'=16,'state'=2] {'seq'}, dimensions={0} | all-to-all | bytes 131072 | tf_op jit(solution)/shard_map/all_to_all | solution.py:617
  93.8 1.5 collective-permute-done.18.refs_3_
  95.7 0.9 collective-permute-start.19
  96.6 1.6 shard_map.211
  98.2 0.6 collective-permute-start.9
  98.7 1.2 collective-permute-done.9.refs_3_
  100.1 0.5 collective-permute-start.10
  100.6 5.7 %collective-permute-done.19.refs_1_ = bf16[1280,256]{1,0:T(8,128)(2,1)S(1)} collective-permute-done((bf16[1280,256]{1,0:T(8,128)(2,1)S(1)}, bf16[1280,256]{1,0:T(8,128)(2,1)S(1)}, u32[]{:S(2)}, u32[]{:S(2)}) %collective-permute-start.19) | collective-permute-done | bytes 655392 | tf_op jit(solution)/shard_map/ppermute | solution.py:643
  106.5 0.7 collective-permute-start.20
  107.2 6.4 %collective-permute-done.20.refs_1_ = bf16[640,256]{1,0:T(8,128)(2,1)S(1)} collective-permute-done((bf16[640,256]{1,0:T(8,128)(2,1)S(1)}, bf16[640,256]{1,0:T(8,128)(2,1)S(1)}, u32[]{:S(2)}, u32[]{:S(2)}) %collective-permute-start.20) | collective-permute-done | bytes 327712 | tf_op jit(solution)/shard_map/ppermute | solution.py:643
  113.7 0.7 collective-permute-start.21
  114.5 0.7 collective-permute-start.11
  115.2 3.8 %collective-permute-done.21.refs_1_ = bf16[320,256]{1,0:T(8,128)(2,1)S(1)} collective-permute-done((bf16[320,256]{1,0:T(8,128)(2,1)S(1)}, bf16[320,256]{1,0:T(8,128)(2,1)S(1)}, u32[]{:S(2)}, u32[]{:S(2)}) %collective-permute-start.21) | collective-permute-done | bytes 163872 | tf_op jit(solution)/shard_map/ppermute | solution.py:643
  119.1 0.8 collective-permute-start.22
  119.9 0.5 collective-permute-done.11.refs_1_
  120.5 0.6 collective-permute-start.12
  121.1 6.2 %collective-permute-done.22.refs_1_ = bf16[320,256]{1,0:T(8,128)(2,1)S(1)} collective-permute-done((bf16[320,256]{1,0:T(8,128)(2,1)S(1)}, bf16[320,256]{1,0:T(8,128)(2,1)S(1)}, u32[]{:S(2)}, u32[]{:S(2)}) %collective-permute-start.22) | collective-permute-done | bytes 163872 | tf_op jit(solution)/shard_map/ppermute | solution.py:643
  127.5 1.5 collective-permute-start.13
  129.0 0.7 shard_map.217
  129.7 3.6 %collective-permute-done.13.refs_1_ = bf16[224,256]{1,0:T(8,128)(2,1)S(1)} collective-permute-done((bf16[224,256]{1,0:T(8,128)(2,1)S(1)}, bf16[224,256]{1,0:T(8,128)(2,1)S(1)}, u32[]{:S(2)}, u32[]{:S(2)}) %collective-permute-start.13) | collective-permute-done | bytes 114720 | tf_op jit(solution)/shard_map/ppermute | solution.py:643
  133.4 0.7 collective-permute-start.15
  134.2 0.6 collective-permute-start.24
  134.8 4.4 %collective-permute-done.15 = bf16[192,256]{1,0:T(8,128)(2,1)S(1)} collective-permute-done((bf16[192,256]{1,0:T(8,128)(2,1)S(1)}, bf16[192,256]{1,0:T(8,128)(2,1)S(1)}, u32[]{:S(2)}, u32[]{:S(2)}) %collective-permute-start.15) | collective-permute-done | bytes 98336 | tf_op jit(solution)/shard_map/ppermute | solution.py:643
  139.2 0.7 collective-permute-start.16
  140.0 2.6 %collective-permute-done.24 = bf16[640,256]{1,0:T(8,128)(2,1)S(1)} collective-permute-done((bf16[640,256]{1,0:T(8,128)(2,1)S(1)}, bf16[640,256]{1,0:T(8,128)(2,1)S(1)}, u32[]{:S(2)}, u32[]{:S(2)}) %collective-permute-start.24) | collective-permute-done | bytes 327712 | tf_op jit(solution)/shard_map/ppermute | solution.py:643
  142.6 2.3 %collective-permute-start.25 = (bf16[1280,256]{1,0:T(8,128)(2,1)S(1)}, bf16[1280,256]{1,0:T(8,128)(2,1)S(1)}, u32[]{:S(2)}, u32[]{:S(2)}) collective-permute-start(bf16[1280,256]{1,0:T(8,128)(2,1)S(1)} %pad_maximum_fusion.refs_2_), channel_id=1, source_target_pairs={{0,2},{1,5},{2,0},{3,7},{4,6},{5,1},{6,4},{7,3},{8,10},{9,13},{10,... | collective-permute-start | bytes 1966088 | tf_op jit(solution)/shard_map/ppermute | solution.py:643
  144.9 2.3 %collective-permute-done.16 = bf16[384,256]{1,0:T(8,128)(2,1)S(1)} collective-permute-done((bf16[384,256]{1,0:T(8,128)(2,1)S(1)}, bf16[384,256]{1,0:T(8,128)(2,1)S(1)}, u32[]{:S(2)}, u32[]{:S(2)}) %collective-permute-start.16) | collective-permute-done | bytes 196640 | tf_op jit(solution)/shard_map/ppermute | solution.py:643
  147.3 3.4 %collective-permute-start.17 = (bf16[768,256]{1,0:T(8,128)(2,1)S(1)}, bf16[768,256]{1,0:T(8,128)(2,1)S(1)}, u32[]{:S(2)}, u32[]{:S(2)}) collective-permute-start(bf16[768,256]{1,0:T(8,128)(2,1)S(1)} %pad_maximum_fusion.1.refs_0_), channel_id=1, source_target_pairs={{0,8},{1,9},{2,10},{3,11},{4,12},{5,13},{6,14},{7,15},{8,0},{9,1},... | collective-permute-start | bytes 1179656 | tf_op jit(solution)/shard_map/ppermute | solution.py:643
  150.6 1.6 %shard_map.218 = (bf16[4,256,256]{2,1,0:T(8,128)(2,1)}, f32[4,256,256]{2,1,0:T(8,128)}, f32[2,256]{1,0:T(2,128)}, f32[2,256]{1,0:T(2,128)}, f32[2,256]{1,0:T(2,1...) custom-call(f32[16,128]{1,0:T(8,128)S(1)} %get-tuple-element.201.refs_0_, f32[8,512]{1,0:T(8,128)S(1)} %get-tuple-element.202.refs_1_, ...), custom_call_target="tpu_custom_call" | custom-call | bytes 1622016 | tf_op jit(solution)/shard_map/pallas_call | solution.py:857
  152.2 4.1 %collective-permute-done.17.refs_1_ = bf16[768,256]{1,0:T(8,128)(2,1)S(1)} collective-permute-done((bf16[768,256]{1,0:T(8,128)(2,1)S(1)}, bf16[768,256]{1,0:T(8,128)(2,1)S(1)}, u32[]{:S(2)}, u32[]{:S(2)}) %collective-permute-start.17) | collective-permute-done | bytes 393248 | tf_op jit(solution)/shard_map/ppermute | solution.py:643
  156.4 2.3 %shard_map.224 = (f32[2,512,256]{2,1,0:T(8,128)}, f32[2,512,256]{2,1,0:T(8,128)}, f32[2,256,512]{2,1,0:T(8,128)}, f32[2,1024,128]{2,1,0:T(8,128)}) custom-call(bf16[768,256]{1,0:T(8,128)(2,1)S(1)} %pad_maximum_fusion.1.refs_0_, bf16[768,256]{1,0:T(8,128)(2,1)S(1)} %collective-permute-done.17.refs_1_, bf16[1280,256]{1,0:T(8,128)(2,1)S(1)} %pad_maximum_fusion.refs_2_, ...), custom_call_target="tpu_custom_call" | custom-call | bytes 2097152 | tf_op jit(solution)/shard_map/pallas_call | solution.py:857
  (65 shorter events, 2.9 us)
Async XLA Ops:
  0.6 2.1 %copy-start = (bf16[4,256,256]{2,1,0:T(8,128)(2,1)S(1)}, bf16[4,256,256]{2,1,0:T(8,128)(2,1)}, u32[]{:S(2)}) copy-start(bf16[4,256,256]{2,1,0:T(8,128)(2,1)} %refs_4_.1) | copy-start | bytes 1572868
  0.7 2.1 %copy-start.8 = (bf16[2,256]{1,0:T(2,128)(2,1)S(1)}, bf16[2,256]{1,0:T(2,128)(2,1)}, u32[]{:S(2)}) copy-start(bf16[2,256]{1,0:T(2,128)(2,1)} %param.13) | copy-start | bytes 3076
  0.7 2.1 %copy-start.7 = (bf16[2,256]{1,0:T(2,128)(2,1)S(1)}, bf16[2,256]{1,0:T(2,128)(2,1)}, u32[]{:S(2)}) copy-start(bf16[2,256]{1,0:T(2,128)(2,1)} %param.14) | copy-start | bytes 3076
  0.7 2.1 %copy-start.10 = (bf16[2,128]{1,0:T(2,128)(2,1)S(1)}, bf16[2,128]{1,0:T(2,128)(2,1)}, u32[]{:S(2)}) copy-start(bf16[2,128]{1,0:T(2,128)(2,1)} %param.17) | copy-start | bytes 1540
  0.7 2.1 %copy-start.9 = (bf16[2,128]{1,0:T(2,128)(2,1)S(1)}, bf16[2,128]{1,0:T(2,128)(2,1)}, u32[]{:S(2)}) copy-start(bf16[2,128]{1,0:T(2,128)(2,1)} %param.18) | copy-start | bytes 1540
  0.7 2.1 %copy-start.6 = (bf16[2,256]{1,0:T(2,128)(2,1)S(1)}, bf16[2,256]{1,0:T(2,128)(2,1)}, u32[]{:S(2)}) copy-start(bf16[2,256]{1,0:T(2,128)(2,1)} %param.19) | copy-start | bytes 3076
  0.7 2.1 %copy-start.5 = (s32[4,16]{1,0:T(4,128)S(1)}, s32[4,16]{1,0:T(4,128)}, u32[]{:S(2)}) copy-start(s32[4,16]{1,0:T(4,128)} %refs_0_.3) | copy-start | bytes 772
  0.7 4.0 %copy-start.1 = (bf16[2,2,128,512]{3,2,1,0:T(8,128)(2,1)S(1)}, bf16[2,2,128,512]{3,2,1,0:T(8,128)(2,1)}, u32[]{:S(2)}) copy-start(bf16[2,2,128,512]{3,2,1,0:T(8,128)(2,1)} %param.16) | copy-start | bytes 1572868
  2.2 3.8 %collective-permute-start.2 = (bf16[2,512,256]{2,1,0:T(8,128)(2,1)S(1)}, bf16[2,512,256]{2,1,0:T(8,128)(2,1)S(1)}, u32[]{:S(2)}, u32[]{:S(2)}) collective-permute-start(bf16[2,512,256]{2,1,0:T(8,128)(2,1)S(1)} %reshape.40.refs_7_.refs_5_.refs_13_), channel_id=1, source_target_pairs={{0,1},{1,0},{2,3},{3,2},{4,5},{5,4},{6,7},{7,6},{8,9},{9,8},{10,11... | collective-permute-start | bytes 1572872 | tf_op jit(solution)/shard_map/ppermute | solution.py:605
  2.7 17.9 %collective-permute-start = (bf16[4,256,256]{2,1,0:T(8,128)(2,1)S(1)}, bf16[4,256,256]{2,1,0:T(8,128)(2,1)S(1)}, u32[]{:S(2)}, u32[]{:S(2)}) collective-permute-start(bf16[4,256,256]{2,1,0:T(8,128)(2,1)S(1)} %copy-done), channel_id=1, source_target_pairs={{0,1},{1,0},{2,3},{3,2},{4,5},{5,4},{6,7},{7,6},{8,9},{9,8},{10,11... | collective-permute-start | bytes 1572872 | tf_op jit(solution)/shard_map/ppermute | solution.py:605
  4.3 1.3 collective-permute-start.1
  4.8 16.9 %collective-permute-start.4 = (bf16[2,256,512]{2,1,0:T(8,128)(2,1)S(1)}, bf16[2,256,512]{2,1,0:T(8,128)(2,1)S(1)}, u32[]{:S(2)}, u32[]{:S(2)}) collective-permute-start(bf16[2,256,512]{2,1,0:T(8,128)(2,1)S(1)} %bitcast.5), channel_id=1, source_target_pairs={{0,1},{1,0},{2,3},{3,2},{4,5},{5,4},{6,7},{7,6},{8,9},{9,8},{10,11... | collective-permute-start | bytes 1572872 | tf_op jit(solution)/shard_map/ppermute | solution.py:605
  4.8 16.8 %collective-permute-start.3 = (bf16[4,256,256]{2,1,0:T(8,128)(2,1)}, bf16[4,256,256]{2,1,0:T(8,128)(2,1)S(1)}, u32[]{:S(2)}, u32[]{:S(2)}) collective-permute-start(bf16[4,256,256]{2,1,0:T(8,128)(2,1)} %refs_16_.1), channel_id=1, source_target_pairs={{0,1},{1,0},{2,3},{3,2},{4,5},{5,4},{6,7},{7,6},{8,9},{9,8},{10,11... | collective-permute-start | bytes 1572872 | tf_op jit(solution)/shard_map/ppermute | solution.py:605
  5.6 16.1 %collective-permute-start.5 = (bf16[2,512,256]{2,1,0:T(8,128)(2,1)}, bf16[2,512,256]{2,1,0:T(8,128)(2,1)S(1)}, u32[]{:S(2)}, u32[]{:S(2)}) collective-permute-start(bf16[2,512,256]{2,1,0:T(8,128)(2,1)} %refs_15_.1), channel_id=1, source_target_pairs={{0,1},{1,0},{2,3},{3,2},{4,5},{5,4},{6,7},{7,6},{8,9},{9,8},{10,11... | collective-permute-start | bytes 1572872 | tf_op jit(solution)/shard_map/ppermute | solution.py:605
  5.9 15.8 %collective-permute-start.6 = (bf16[2,512,256]{2,1,0:T(8,128)(2,1)}, bf16[2,512,256]{2,1,0:T(8,128)(2,1)S(1)}, u32[]{:S(2)}, u32[]{:S(2)}) collective-permute-start(bf16[2,512,256]{2,1,0:T(8,128)(2,1)} %refs_17_.1), channel_id=1, source_target_pairs={{0,1},{1,0},{2,3},{3,2},{4,5},{5,4},{6,7},{7,6},{8,9},{9,8},{10,11... | collective-permute-start | bytes 1572872 | tf_op jit(solution)/shard_map/ppermute | solution.py:605
  20.6 11.2 %copy-start.2 = (bf16[2,512,256]{2,1,0:T(8,128)(2,1)S(1)}, bf16[2,512,256]{2,1,0:T(8,128)(2,1)}, u32[]{:S(2)}) copy-start(bf16[2,512,256]{2,1,0:T(8,128)(2,1)} %refs_15_.1) | copy-start | bytes 1572868
  20.6 11.2 %copy-start.3 = (bf16[2,512,256]{2,1,0:T(8,128)(2,1)S(1)}, bf16[2,512,256]{2,1,0:T(8,128)(2,1)}, u32[]{:S(2)}) copy-start(bf16[2,512,256]{2,1,0:T(8,128)(2,1)} %refs_17_.1) | copy-start | bytes 1572868
  43.8 11.0 %copy-start.4 = (bf16[4,256,256]{2,1,0:T(8,128)(2,1)S(1)}, bf16[4,256,256]{2,1,0:T(8,128)(2,1)}, u32[]{:S(2)}) copy-start(bf16[4,256,256]{2,1,0:T(8,128)(2,1)} %refs_16_.1) | copy-start | bytes 1572868
  81.0 2.7 %collective-permute-start.7 = (bf16[2048,256]{1,0:T(8,128)(2,1)S(1)}, bf16[2048,256]{1,0:T(8,128)(2,1)S(1)}, u32[]{:S(2)}, u32[]{:S(2)}) collective-permute-start(bf16[2048,256]{1,0:T(8,128)(2,1)S(1)} %get-tuple-element.174), channel_id=1, source_target_pairs={{0,1},{1,0},{2,3},{3,2},{4,5},{5,4},{6,7},{7,6},{8,9},{9,8},{10,11... | collective-permute-start | bytes 3145736 | tf_op jit(solution)/shard_map/ppermute | solution.py:605
  93.8 1.5 collective-permute-start.18
  95.7 10.7 %collective-permute-start.19 = (bf16[1280,256]{1,0:T(8,128)(2,1)S(1)}, bf16[1280,256]{1,0:T(8,128)(2,1)S(1)}, u32[]{:S(2)}, u32[]{:S(2)}) collective-permute-start(bf16[1280,256]{1,0:T(8,128)(2,1)S(1)} %get-tuple-element.217), channel_id=1, source_target_pairs={{0,2},{1,5},{2,0},{3,7},{4,6},{5,1},{6,4},{7,3},{8,10},{9,13},{10,... | collective-permute-start | bytes 1966088 | tf_op jit(solution)/shard_map/ppermute | solution.py:643
  96.6 3.4 %collective-permute-start.8 = (bf16[1024,256]{1,0:T(8,128)(2,1)S(1)}, bf16[1024,256]{1,0:T(8,128)(2,1)S(1)}, u32[]{:S(2)}, u32[]{:S(2)}) collective-permute-start(bf16[1024,256]{1,0:T(8,128)(2,1)S(1)} %get-tuple-element.181), channel_id=1, source_target_pairs={{0,1},{1,0},{2,3},{3,2},{4,5},{5,4},{6,7},{7,6},{8,9},{9,8},{10,11... | collective-permute-start | bytes 1572872 | tf_op jit(solution)/shard_map/ppermute | solution.py:605
  98.2 1.8 %collective-permute-start.9 = (bf16[544,256]{1,0:T(8,128)(2,1)S(1)}, bf16[544,256]{1,0:T(8,128)(2,1)S(1)}, u32[]{:S(2)}, u32[]{:S(2)}) collective-permute-start(bf16[544,256]{1,0:T(8,128)(2,1)S(1)} %get-tuple-element.193), channel_id=1, source_target_pairs={{0,1},{1,0},{2,3},{3,2},{4,5},{5,4},{6,7},{7,6},{8,9},{9,8},{10,11... | collective-permute-start | bytes 835592 | tf_op jit(solution)/shard_map/ppermute | solution.py:605
  100.1 14.3 %collective-permute-start.10 = (bf16[800,256]{1,0:T(8,128)(2,1)S(1)}, bf16[800,256]{1,0:T(8,128)(2,1)S(1)}, u32[]{:S(2)}, u32[]{:S(2)}) collective-permute-start(bf16[800,256]{1,0:T(8,128)(2,1)S(1)} %get-tuple-element.196), channel_id=1, source_target_pairs={{0,8},{1,9},{2,10},{3,11},{4,12},{5,13},{6,14},{7,15},{8,0},{9,1},... | collective-permute-start | bytes 1228808 | tf_op jit(solution)/shard_map/ppermute | solution.py:643
  106.5 7.1 %collective-permute-start.20 = (bf16[640,256]{1,0:T(8,128)(2,1)S(1)}, bf16[640,256]{1,0:T(8,128)(2,1)S(1)}, u32[]{:S(2)}, u32[]{:S(2)}) collective-permute-start(bf16[640,256]{1,0:T(8,128)(2,1)S(1)} %get-tuple-element.219), channel_id=1, source_target_pairs={{0,4},{1,3},{2,6},{3,1},{4,0},{5,7},{6,2},{7,5},{8,12},{9,11},{10,... | collective-permute-start | bytes 983048 | tf_op jit(solution)/shard_map/ppermute | solution.py:643
  113.7 5.4 %collective-permute-start.21 = (bf16[320,256]{1,0:T(8,128)(2,1)S(1)}, bf16[320,256]{1,0:T(8,128)(2,1)S(1)}, u32[]{:S(2)}, u32[]{:S(2)}) collective-permute-start(bf16[320,256]{1,0:T(8,128)(2,1)S(1)} %get-tuple-element.221), channel_id=1, source_target_pairs={{0,8},{1,9},{2,10},{3,11},{4,12},{5,13},{6,14},{7,15},{8,0},{9,1},... | collective-permute-start | bytes 491528 | tf_op jit(solution)/shard_map/ppermute | solution.py:643
  114.5 5.9 %collective-permute-start.11 = (bf16[416,256]{1,0:T(8,128)(2,1)S(1)}, bf16[416,256]{1,0:T(8,128)(2,1)S(1)}, u32[]{:S(2)}, u32[]{:S(2)}) collective-permute-start(bf16[416,256]{1,0:T(8,128)(2,1)S(1)} %get-tuple-element.198), channel_id=1, source_target_pairs={{0,4},{1,3},{2,6},{3,1},{4,0},{5,7},{6,2},{7,5},{8,12},{9,11},{10,... | collective-permute-start | bytes 638984 | tf_op jit(solution)/shard_map/ppermute | solution.py:643
  119.1 8.2 %collective-permute-start.22 = (bf16[320,256]{1,0:T(8,128)(2,1)S(1)}, bf16[320,256]{1,0:T(8,128)(2,1)S(1)}, u32[]{:S(2)}, u32[]{:S(2)}) collective-permute-start(bf16[320,256]{1,0:T(8,128)(2,1)S(1)} %shard_map.222.refs_0_), channel_id=1, source_target_pairs={{0,16},{1,17},{2,18},{3,19},{4,20},{5,21},{6,22},{7,23},{8,24},{9,... | collective-permute-start | bytes 491528 | tf_op jit(solution)/shard_map/ppermute | solution.py:643
  120.5 7.0 %collective-permute-start.12 = (bf16[224,256]{1,0:T(8,128)(2,1)S(1)}, bf16[224,256]{1,0:T(8,128)(2,1)S(1)}, u32[]{:S(2)}, u32[]{:S(2)}) collective-permute-start(bf16[224,256]{1,0:T(8,128)(2,1)S(1)} %get-tuple-element.200), channel_id=1, source_target_pairs={{0,2},{1,5},{2,0},{3,7},{4,6},{5,1},{6,4},{7,3},{8,10},{9,13},{10,... | collective-permute-start | bytes 344072 | tf_op jit(solution)/shard_map/ppermute | solution.py:643
  127.4 6.7 %collective-permute-start.23 = (bf16[320,256]{1,0:T(8,128)(2,1)S(1)}, bf16[320,256]{1,0:T(8,128)(2,1)S(1)}, u32[]{:S(2)}, u32[]{:S(2)}) collective-permute-start(bf16[320,256]{1,0:T(8,128)(2,1)S(1)} %shard_map.223), channel_id=1, source_target_pairs={{0,8},{1,9},{2,10},{3,11},{4,12},{5,13},{6,14},{7,15},{8,0},{9,1},... | collective-permute-start | bytes 491528 | tf_op jit(solution)/shard_map/ppermute | solution.py:643
  127.5 5.9 %collective-permute-start.13 = (bf16[224,256]{1,0:T(8,128)(2,1)S(1)}, bf16[224,256]{1,0:T(8,128)(2,1)S(1)}, u32[]{:S(2)}, u32[]{:S(2)}) collective-permute-start(bf16[224,256]{1,0:T(8,128)(2,1)S(1)} %shard_map.215.refs_0_), channel_id=1, source_target_pairs={{0,16},{1,17},{2,18},{3,19},{4,20},{5,21},{6,22},{7,23},{8,24},{9,... | collective-permute-start | bytes 344072 | tf_op jit(solution)/shard_map/ppermute | solution.py:643
  129.7 21.0 %collective-permute-start.14 = (bf16[2,512,256]{2,1,0:T(8,128)(2,1)S(1)}, bf16[2,512,256]{2,1,0:T(8,128)(2,1)S(1)}, u32[]{:S(2)}, u32[]{:S(2)}) collective-permute-start(bf16[2,512,256]{2,1,0:T(8,128)(2,1)S(1)} %get-tuple-element.206), channel_id=1, source_target_pairs={{0,1},{1,0},{2,3},{3,2},{4,5},{5,4},{6,7},{7,6},{8,9},{9,8},{10,11... | collective-permute-start | bytes 1572872 | tf_op jit(solution)/shard_map/ppermute | solution.py:605
  133.4 5.8 %collective-permute-start.15 = (bf16[192,256]{1,0:T(8,128)(2,1)S(1)}, bf16[192,256]{1,0:T(8,128)(2,1)S(1)}, u32[]{:S(2)}, u32[]{:S(2)}) collective-permute-start(bf16[192,256]{1,0:T(8,128)(2,1)S(1)} %get-tuple-element.211), channel_id=1, source_target_pairs={{0,2},{1,5},{2,0},{3,7},{4,6},{5,1},{6,4},{7,3},{8,10},{9,13},{10,... | collective-permute-start | bytes 294920 | tf_op jit(solution)/shard_map/ppermute | solution.py:643
  134.2 8.3 %collective-permute-start.24 = (bf16[640,256]{1,0:T(8,128)(2,1)S(1)}, bf16[640,256]{1,0:T(8,128)(2,1)S(1)}, u32[]{:S(2)}, u32[]{:S(2)}) collective-permute-start(bf16[640,256]{1,0:T(8,128)(2,1)S(1)} %pad_maximum_fusion.2), channel_id=1, source_target_pairs={{0,4},{1,3},{2,6},{3,1},{4,0},{5,7},{6,2},{7,5},{8,12},{9,11},{10,... | collective-permute-start | bytes 983048 | tf_op jit(solution)/shard_map/ppermute | solution.py:643
  139.2 7.9 %collective-permute-start.16 = (bf16[384,256]{1,0:T(8,128)(2,1)S(1)}, bf16[384,256]{1,0:T(8,128)(2,1)S(1)}, u32[]{:S(2)}, u32[]{:S(2)}) collective-permute-start(bf16[384,256]{1,0:T(8,128)(2,1)S(1)} %pad_maximum_fusion.3), channel_id=1, source_target_pairs={{0,4},{1,3},{2,6},{3,1},{4,0},{5,7},{6,2},{7,5},{8,12},{9,11},{10,... | collective-permute-start | bytes 589832 | tf_op jit(solution)/shard_map/ppermute | solution.py:643
  142.6 13.8 %collective-permute-start.25 = (bf16[1280,256]{1,0:T(8,128)(2,1)S(1)}, bf16[1280,256]{1,0:T(8,128)(2,1)S(1)}, u32[]{:S(2)}, u32[]{:S(2)}) collective-permute-start(bf16[1280,256]{1,0:T(8,128)(2,1)S(1)} %pad_maximum_fusion.refs_2_), channel_id=1, source_target_pairs={{0,2},{1,5},{2,0},{3,7},{4,6},{5,1},{6,4},{7,3},{8,10},{9,13},{10,... | collective-permute-start | bytes 1966088 | tf_op jit(solution)/shard_map/ppermute | solution.py:643
  147.3 9.1 %collective-permute-start.17 = (bf16[768,256]{1,0:T(8,128)(2,1)S(1)}, bf16[768,256]{1,0:T(8,128)(2,1)S(1)}, u32[]{:S(2)}, u32[]{:S(2)}) collective-permute-start(bf16[768,256]{1,0:T(8,128)(2,1)S(1)} %pad_maximum_fusion.1.refs_0_), channel_id=1, source_target_pairs={{0,8},{1,9},{2,10},{3,11},{4,12},{5,13},{6,14},{7,15},{8,0},{9,1},... | collective-permute-start | bytes 1179656 | tf_op jit(solution)/shard_map/ppermute | solution.py:643

commit v6 on v5

--- a/solution.py
+++ b/solution.py
@@ -756,35 +756,90 @@
         return value
 
 
-def unpack_kernel(masks0, masks1, mine0, got0, mine1, got1, lin, gate, out, entry):
-    def put_entry(ref, at, k, start, rows):
-        value = ref[at : at + rows, :].astype(f32)
-        entry[k, pl.ds(2 * start, rows, stride=2), :] = value[:, :128]
-        entry[k, pl.ds(2 * start + 1, rows, stride=2), :] = value[:, 128:]
-
-    for mine, got, masks, second in ((mine0, got0, masks0, False), (mine1, got1, masks1, True)):
-        bit = bit_of(masks)
-        for ref, which in ((mine, bit), (got, 1 - bit)):
-
-            def piece(at, rows):
-                return ref[at : at + rows, :].astype(f32)
-
-            @pl.when(which == 0)
-            def _():
-                if second:
-                    lin[1], gate[1], lin[0, :256] = piece(0, 512), piece(512, 512), piece(1024, 256)
-                else:
-                    gate[0] = piece(0, 512)
-                    put_entry(ref, 512, 0, 0, 256)
-
-            @pl.when(which == 1)
-            def _():
-                if second:
-                    out[1, :, :256], out[1, :, 256:], lin[0, 256:] = piece(0, 256), piece(256, 256), piece(1024, 256)
-                    put_entry(ref, 512, 1, 0, 512)
-                else:
-                    out[0, :, :256], out[0, :, 256:] = piece(0, 256), piece(256, 256)
-                    put_entry(ref, 512, 0, 256, 256)
+class Leaving:
+    def __init__(self, sem):
+        self.sem, self.copies = sem, []
+
+    def send(self, source, target):
+        copy = pltpu.make_async_copy(source, target, self.sem.at[len(self.copies)])
+        copy.start()
+        self.copies.append(copy)
+
+    def wait(self):
+        for copy in self.copies:
+            copy.wait()
+
+
+def put_entry(entry, ref, at, start, rows):
+    value = ref[at : at + rows, :].astype(f32)
+    entry[pl.ds(2 * start, rows, stride=2), :] = value[:, :128]
+    entry[pl.ds(2 * start + 1, rows, stride=2), :] = value[:, 128:]
+
+
+def on_half(mine, got, masks, half, put):
+    bit = bit_of(masks)
+    for ref, which in ((mine, bit), (got, 1 - bit)):
+
+        @pl.when(which == half)
+        def _():
+            put(ref, lambda at, rows: ref[at : at + rows, :].astype(f32))
+
+
+def unpack_second_kernel(masks, mine, got, lin_out, gate_out, out_out, entry_out, lin, gate, out, entry, sem):
+    leaving = Leaving(sem)
+
+    def low(ref, piece):
+        lin[1], gate[...], lin[0, :256] = piece(0, 512), piece(512, 512), piece(1024, 256)
+
+    def high(ref, piece):
+        out[:, :256], out[:, 256:], lin[0, 256:] = piece(0, 256), piece(256, 256), piece(1024, 256)
+        put_entry(entry, ref, 512, 0, 512)
+
+    on_half(mine, got, masks, 0, low)
+    leaving.send(gate, gate_out.at[1])
+    on_half(mine, got, masks, 1, high)
+    leaving.send(lin, lin_out)
+    leaving.send(out, out_out.at[1])
+    leaving.send(entry, entry_out.at[1])
+    leaving.wait()
+
+
+def unpack_first_kernel(masks, mine, got, gate_in, out_in, entry_in, gate_out, out_out, entry_out, gate, out, entry, sem):
+    leaving = Leaving(sem)
+
+    def low(ref, piece):
+        gate[...] = piece(0, 512)
+        put_entry(entry, ref, 512, 0, 256)
+
+    def high(ref, piece):
+        out[:, :256], out[:, 256:] = piece(0, 256), piece(256, 256)
+        put_entry(entry, ref, 512, 256, 256)
+
+    on_half(mine, got, masks, 0, low)
+    leaving.send(gate, gate_out.at[0])
+    on_half(mine, got, masks, 1, high)
+    leaving.send(out, out_out.at[0])
+    leaving.send(entry, entry_out.at[0])
+    leaving.wait()
+
+
+def unpack(second, second_masks, first, first_masks):
+    far, near = pl.BlockSpec(memory_space=pltpu.HBM), pl.BlockSpec(memory_space=pltpu.VMEM)
+    lin, gate, out, entry = (jax.ShapeDtypeStruct(s, f32) for s in ((2, 512, 256), (2, 512, 256), (2, 256, 512), (2, 1024, 128)))
+    parts = [pltpu.VMEM(a.shape[1:], f32) for a in (gate, out, entry)]
+    params = pltpu.CompilerParams(vmem_limit_bytes=24 * 2**20)
+    lin_grad, *rest = pl.pallas_call(
+        functools.partial(unpack_second_kernel, second_masks),
+        out_shape=[lin, gate, out, entry], in_specs=[near] * 2, out_specs=[far] * 4,
+        scratch_shapes=[pltpu.VMEM(lin.shape, f32)] + parts + [pltpu.SemaphoreType.DMA((4,))],
+        compiler_params=params)(*second)
+    rest = pl.pallas_call(
+        functools.partial(unpack_first_kernel, first_masks),
+        out_shape=[gate, out, entry], in_specs=[near] * 2 + [far] * 3, out_specs=[far] * 3,
+        scratch_shapes=parts + [pltpu.SemaphoreType.DMA((3,))],
+        input_output_aliases={2: 0, 3: 1, 4: 2},
+        compiler_params=params)(*first, *rest)
+    return [lin_grad, *rest]
 
 
 class Far:
@@ -940,24 +995,15 @@
     bulk0 = SeqSum([(g0_own, g0_got), (i0_own, i0_got)], axes_orders((2, 1, 0, 3), (2, 0, 1, 3)), s_own)
     own_parts, oth_parts = run(order_kernel, [((2, n, 256), bf16)] * 2, (perm, result, partial), flops=2 * one)
     got_parts = swap(oth_parts)
-    for _ in range(3):
-        bulk1.step()
-    ended = False
-    while not bulk0.step():
-        if not ended:
-            bulk1.after(bulk0.send)
-            ended = bulk1.step()
-    while not ended:
-        ended = bulk1.step()
+    for bulk in (bulk1, bulk0):
+        while not bulk.step():
+            pass
     quad = (2, 2, span, width)
     block_out, d_in, ngg, bias_grad, skip_grad, rate_grad, angle_grad = run(
         functools.partial(finish_kernel, count),
         [((rows, span, width), bf16), ((rows, span, width), f32), ((2, 256), f32), ((2, 256), f32), ((2, 256), f32), ((2, 128), f32), ((2, 128), f32)],
         (bulk0.small[0], totals1, own_parts.reshape(quad), got_parts.reshape(quad), tokens, nrm0, raw))
-    lin_grad, gate_grad, out_grad, in_grad = run(
-        functools.partial(unpack_kernel, bulk0.masks[0], bulk1.masks[0]),
-        [((2, 512, 256), f32), ((2, 512, 256), f32), ((2, 256, 512), f32), ((2, 1024, 128), f32)],
-        bulk0.result + bulk1.result)
+    lin_grad, gate_grad, out_grad, in_grad = unpack(bulk1.result, bulk1.masks[0], bulk0.result, bulk0.masks[0])
     out_grad, in_grad = out_grad.reshape(2, 2, 128, 512), in_grad.reshape(2, 512, 2, 128)
     return (block_out, d_in, ngg, bias_grad, in_grad, out_grad, rate_grad, angle_grad, skip_grad, lin_grad, gate_grad)
 

time: 159 us -> 158 us (level)
  waiting for transfers between devices: 42.7 us -> 41.1 us
    pallas_call x0 -> x2, Pallas kernels: none -> 2.82 us  [the longest x1 1.6 us: unpack(): pl.pallas_call(functools.partial(unpack_second_kernel, second_masks), out...]
    pallas_call x22 -> x21, Pallas kernels: 21.2 us -> 18.8 us  [run(): pl.pallas_call(whole, out_shape=[jax.ShapeDtypeStruct(o[0], o[1]) for o i...]
    ppermute x14, waiting for transfers between devices: 39.7 us -> 38 us  [partners(): lax.ppermute(value, ('seq', 'state'), [(2 * i + c, 2 * (i ^ masks[c]) + c...]
  transfers between devices with their start and end apart: 26 -> 26, of which waited for: 13 -> 14; matrix products, arithmetic and copies ran while one was open for 0% -> 0% of each run, Pallas kernels for 6% -> 7%
where the time goes in v6:
time: 158 us
  blocking collectives  74.9 us (47%)
  waiting for transfers between devices  41.1 us (26%)
  Pallas kernels  21.7 us (14%)
  starting transfers between devices  17 us (11%)
    all_to_all x6, blocking collectives, blocking(): lax.all_to_all(value, axes, 0, 0)  60.5 us
    ppermute x14, waiting for transfers between devices, partners(): lax.ppermute(value, ('seq', 'state'), [(2 * i + c, 2 * (i ^ masks[c]) + c...  38 us
    pallas_call x21, Pallas kernels, run(): pl.pallas_call(whole, out_shape=[jax.ShapeDtypeStruct(o[0], o[1]) for o i...  18.8 us
    all_to_all x1, blocking collectives, body(): lax.all_to_all(stats, ('seq', 'state'), 0, 0)  14.4 us
    ppermute x14, starting transfers between devices, partners(): lax.ppermute(value, ('seq', 'state'), [(2 * i + c, 2 * (i ^ masks[c]) + c...  14.1 us
  transfers between devices with their start and end apart: 26, of which 14 were waited for; matrix products, arithmetic and copies ran while one was open for 0% of the time, Pallas kernels for 7%

profile of v6, /device:TPU:0, one launch (start us, length us, event | category | flops | bytes accessed | tf_op | source)
XLA Modules:
  0.0 157.7 jit_solution(6740431171057235526)
XLA Ops:
  0.7 1.4 reshape.40.refs_7_.refs_5_.refs_13_
  2.2 0.5 collective-permute-start.2
  2.8 1.4 shard_map.204
  4.3 0.5 collective-permute-start.1
  6.2 14.4 %all_to_all.35.refs_0_ = f32[32,4,128]{2,1,0:T(4,128)S(1)} all-to-all(f32[32,4,128]{2,1,0:T(4,128)S(1)} %shard_map.203), channel_id=1, replica_groups=mesh['seq'=16,'state'=2] {'seq','state'}, dimensions={0} | all-to-all | bytes 131072 | tf_op jit(solution)/shard_map/all_to_all | solution.py:954
  20.6 1.0 shard_map.205
  21.7 10.1 %all_to_all.36.refs_0_ = f32[16,8,128]{2,1,0:T(8,128)S(1)} all-to-all(f32[16,8,128]{2,1,0:T(8,128)S(1)} %get-tuple-element.125), channel_id=1, replica_groups=mesh['seq'=16,'state'=2] {'seq'}, dimensions={0} | all-to-all | bytes 131072 | tf_op jit(solution)/shard_map/all_to_all | solution.py:617
  31.8 2.1 %shard_map.206 = (f32[16,512]{1,0:T(8,128)S(1)}, bf16[512,512]{1,0:T(8,128)(2,1)S(1)}, bf16[512,512]{1,0:T(8,128)(2,1)S(1)}, bf16[512,512]{1,0:T(8,128)(2,1)S(1)...) custom-call(f32[16,8,128]{2,1,0:T(8,128)S(1)} %all_to_all.36.refs_0_, ...), custom_call_target="tpu_custom_call" | custom-call | flops 805306368 | bytes 5554176 | tf_op jit(solution)/shard_map/pallas_call | solution.py:912
  33.9 9.9 %all_to_all.37.refs_0_ = f32[32,8,128]{2,1,0:T(8,128)S(1)} all-to-all(f32[32,8,128]{2,1,0:T(8,128)S(1)} %get-tuple-element.139), channel_id=1, replica_groups=mesh['seq'=16,'state'=2] {'seq','state'}, dimensions={0} | all-to-all | bytes 262144 | tf_op jit(solution)/shard_map/all_to_all | solution.py:617
  43.9 0.8 shard_map.207
  44.7 10.2 %all_to_all.38.refs_0_ = f32[16,8,128]{2,1,0:T(8,128)S(1)} all-to-all(f32[16,8,128]{2,1,0:T(8,128)S(1)} %get-tuple-element.141), channel_id=1, replica_groups=mesh['seq'=16,'state'=2] {'seq'}, dimensions={0} | all-to-all | bytes 131072 | tf_op jit(solution)/shard_map/all_to_all | solution.py:617
  54.9 3.8 %shard_map.208 = (f32[16,512]{1,0:T(8,128)S(1)}, bf16[512,512]{1,0:T(8,128)(2,1)S(1)}, bf16[512,512]{1,0:T(8,128)(2,1)S(1)}, bf16[512,512]{1,0:T(8,128)(2,1)S(1)...) custom-call(f32[16,8,128]{2,1,0:T(8,128)S(1)} %all_to_all.38.refs_0_, ...), custom_call_target="tpu_custom_call" | custom-call | flops 2147483648 | bytes 8175616 | tf_op jit(solution)/shard_map/pallas_call | solution.py:912
  58.7 10.1 %all_to_all.39.refs_0_ = f32[16,8,128]{2,1,0:T(8,128)S(1)} all-to-all(f32[16,8,128]{2,1,0:T(8,128)S(1)} %get-tuple-element.146), channel_id=1, replica_groups=mesh['seq'=16,'state'=2] {'seq'}, dimensions={0} | all-to-all | bytes 131072 | tf_op jit(solution)/shard_map/all_to_all | solution.py:617
  68.8 2.2 %shard_map.209 = (bf16[2048,256]{1,0:T(8,128)(2,1)S(1)}, bf16[2048,256]{1,0:T(8,128)(2,1)S(1)}, f32[8,128]{1,0:T(8,128)S(1)}, f32[8,128]{1,0:T(8,128)S(1)}, f32[...) custom-call(f32[16,8,128]{2,1,0:T(8,128)S(1)} %all_to_all.39.refs_0_, f32[16,8,128]{2,1,0:T(8,128)S(1)} %get-tuple-element.147.refs_1_, ...), custom_call_target="tpu_custom_call" | custom-call | flops 1610612736 | bytes 7176192 | tf_op jit(solution)/shard_map/pallas_call | solution.py:912
  71.0 9.9 %all_to_all.40.refs_0_ = f32[32,8,128]{2,1,0:T(8,128)S(1)} all-to-all(f32[32,8,128]{2,1,0:T(8,128)S(1)} %get-tuple-element.159), channel_id=1, replica_groups=mesh['seq'=16,'state'=2] {'seq','state'}, dimensions={0} | all-to-all | bytes 262144 | tf_op jit(solution)/shard_map/all_to_all | solution.py:617
  81.2 2.4 %shard_map.210 = (f32[512,512]{1,0:T(8,128)S(1)}, bf16[512,512]{1,0:T(8,128)(2,1)S(1)}, f32[8,512]{1,0:T(8,128)S(1)}, bf16[512,256]{1,0:T(8,128)(2,1)S(1)}, bf16...) custom-call(f32[32,8,128]{2,1,0:T(8,128)S(1)} %all_to_all.40.refs_0_, ...), custom_call_target="tpu_custom_call" | custom-call | flops 1610612736 | bytes 9633792 | tf_op jit(solution)/shard_map/pallas_call | solution.py:912
  83.6 10.2 %all_to_all.41.refs_0_ = f32[16,8,128]{2,1,0:T(8,128)S(1)} all-to-all(f32[16,8,128]{2,1,0:T(8,128)S(1)} %get-tuple-element.175), channel_id=1, replica_groups=mesh['seq'=16,'state'=2] {'seq'}, dimensions={0} | all-to-all | bytes 131072 | tf_op jit(solution)/shard_map/all_to_all | solution.py:617
  93.8 1.5 collective-permute-done.18.refs_3_
  95.7 0.9 collective-permute-start.19
  96.6 1.6 %shard_map.211 = (bf16[512,256]{1,0:T(8,128)(2,1)S(1)}, bf16[544,256]{1,0:T(8,128)(2,1)S(1)}, f32[16,128]{1,0:T(8,128)S(1)}, bf16[512,512]{1,0:T(8,128)(2,1)S(1)}) custom-call(f32[16,8,128]{2,1,0:T(8,128)S(1)} %all_to_all.41.refs_0_, f32[16,8,128]{2,1,0:T(8,128)S(1)} %get-tuple-element.182.refs_1_, f32[2,16,8,128]{3,2,1,0:T(8,128)S(1)} %get-tuple-element.132.refs_2_, ...), custom_call_target="tpu_custom_call" | custom-call | flops 805306368 | bytes 6135808 | tf_op jit(solution)/shard_map/pallas_call | solution.py:912
  98.2 0.6 collective-permute-start.9
  98.7 1.2 collective-permute-done.9.refs_3_
  100.6 5.7 %collective-permute-done.19.refs_1_ = bf16[1280,256]{1,0:T(8,128)(2,1)S(1)} collective-permute-done((bf16[1280,256]{1,0:T(8,128)(2,1)S(1)}, bf16[1280,256]{1,0:T(8,128)(2,1)S(1)}, u32[]{:S(2)}, u32[]{:S(2)}) %collective-permute-start.19) | collective-permute-done | bytes 655392 | tf_op jit(solution)/shard_map/ppermute | solution.py:643
  106.5 0.7 collective-permute-start.20
  107.2 6.4 %collective-permute-done.20.refs_1_ = bf16[640,256]{1,0:T(8,128)(2,1)S(1)} collective-permute-done((bf16[640,256]{1,0:T(8,128)(2,1)S(1)}, bf16[640,256]{1,0:T(8,128)(2,1)S(1)}, u32[]{:S(2)}, u32[]{:S(2)}) %collective-permute-start.20) | collective-permute-done | bytes 327712 | tf_op jit(solution)/shard_map/ppermute | solution.py:643
  113.7 0.7 collective-permute-start.21
  114.5 0.7 collective-permute-start.11
  115.2 3.8 %collective-permute-done.21.refs_1_ = bf16[320,256]{1,0:T(8,128)(2,1)S(1)} collective-permute-done((bf16[320,256]{1,0:T(8,128)(2,1)S(1)}, bf16[320,256]{1,0:T(8,128)(2,1)S(1)}, u32[]{:S(2)}, u32[]{:S(2)}) %collective-permute-start.21) | collective-permute-done | bytes 163872 | tf_op jit(solution)/shard_map/ppermute | solution.py:643
  119.1 0.8 collective-permute-start.22
  119.9 0.5 collective-permute-done.11.refs_1_
  120.5 0.6 collective-permute-start.12
  121.1 6.2 %collective-permute-done.22.refs_1_ = bf16[320,256]{1,0:T(8,128)(2,1)S(1)} collective-permute-done((bf16[320,256]{1,0:T(8,128)(2,1)S(1)}, bf16[320,256]{1,0:T(8,128)(2,1)S(1)}, u32[]{:S(2)}, u32[]{:S(2)}) %collective-permute-start.22) | collective-permute-done | bytes 163872 | tf_op jit(solution)/shard_map/ppermute | solution.py:643
  127.5 1.5 collective-permute-start.13
  129.0 0.7 shard_map.217
  129.7 3.6 %collective-permute-done.13.refs_1_ = bf16[224,256]{1,0:T(8,128)(2,1)S(1)} collective-permute-done((bf16[224,256]{1,0:T(8,128)(2,1)S(1)}, bf16[224,256]{1,0:T(8,128)(2,1)S(1)}, u32[]{:S(2)}, u32[]{:S(2)}) %collective-permute-start.13) | collective-permute-done | bytes 114720 | tf_op jit(solution)/shard_map/ppermute | solution.py:643
  133.4 0.7 collective-permute-start.15
  134.2 0.6 collective-permute-start.24
  134.8 4.4 %collective-permute-done.15 = bf16[192,256]{1,0:T(8,128)(2,1)S(1)} collective-permute-done((bf16[192,256]{1,0:T(8,128)(2,1)S(1)}, bf16[192,256]{1,0:T(8,128)(2,1)S(1)}, u32[]{:S(2)}, u32[]{:S(2)}) %collective-permute-start.15) | collective-permute-done | bytes 98336 | tf_op jit(solution)/shard_map/ppermute | solution.py:643
  139.2 0.7 collective-permute-start.16
  140.0 2.5 %collective-permute-done.24 = bf16[640,256]{1,0:T(8,128)(2,1)S(1)} collective-permute-done((bf16[640,256]{1,0:T(8,128)(2,1)S(1)}, bf16[640,256]{1,0:T(8,128)(2,1)S(1)}, u32[]{:S(2)}, u32[]{:S(2)}) %collective-permute-start.24) | collective-permute-done | bytes 327712 | tf_op jit(solution)/shard_map/ppermute | solution.py:643
  142.6 2.3 %collective-permute-start.25 = (bf16[1280,256]{1,0:T(8,128)(2,1)S(1)}, bf16[1280,256]{1,0:T(8,128)(2,1)S(1)}, u32[]{:S(2)}, u32[]{:S(2)}) collective-permute-start(bf16[1280,256]{1,0:T(8,128)(2,1)S(1)} %pad_maximum_fusion.mine), channel_id=1, source_target_pairs={{0,2},{1,5},{2,0},{3,7},{4,6},{5,1},{6,4},{7,3},{8,10},{9,13},{10,... | collective-permute-start | bytes 1966088 | tf_op jit(solution)/shard_map/ppermute | solution.py:643
  144.9 2.3 %collective-permute-done.16 = bf16[384,256]{1,0:T(8,128)(2,1)S(1)} collective-permute-done((bf16[384,256]{1,0:T(8,128)(2,1)S(1)}, bf16[384,256]{1,0:T(8,128)(2,1)S(1)}, u32[]{:S(2)}, u32[]{:S(2)}) %collective-permute-start.16) | collective-permute-done | bytes 196640 | tf_op jit(solution)/shard_map/ppermute | solution.py:643
  147.3 3.3 %collective-permute-start.17 = (bf16[768,256]{1,0:T(8,128)(2,1)S(1)}, bf16[768,256]{1,0:T(8,128)(2,1)S(1)}, u32[]{:S(2)}, u32[]{:S(2)}) collective-permute-start(bf16[768,256]{1,0:T(8,128)(2,1)S(1)} %pad_maximum_fusion.1.mine), channel_id=1, source_target_pairs={{0,8},{1,9},{2,10},{3,11},{4,12},{5,13},{6,14},{7,15},{8,0},{9,1},... | collective-permute-start | bytes 1179656 | tf_op jit(solution)/shard_map/ppermute | solution.py:643
  150.5 1.6 %shard_map.218 = (bf16[4,256,256]{2,1,0:T(8,128)(2,1)}, f32[4,256,256]{2,1,0:T(8,128)}, f32[2,256]{1,0:T(2,128)}, f32[2,256]{1,0:T(2,128)}, f32[2,256]{1,0:T(2,1...) custom-call(f32[16,128]{1,0:T(8,128)S(1)} %get-tuple-element.200.refs_0_, f32[8,512]{1,0:T(8,128)S(1)} %get-tuple-element.201.refs_1_, ...), custom_call_target="tpu_custom_call" | custom-call | bytes 1622016 | tf_op jit(solution)/shard_map/pallas_call | solution.py:912
  152.2 1.3 collective-permute-done.25.got
  153.4 1.6 %shard_map.224 = (f32[2,512,256]{2,1,0:T(8,128)}, f32[2,512,256]{2,1,0:T(8,128)}, f32[2,256,512]{2,1,0:T(8,128)}, f32[2,1024,128]{2,1,0:T(8,128)}) custom-call(bf16[1280,256]{1,0:T(8,128)(2,1)S(1)} %pad_maximum_fusion.mine, bf16[1280,256]{1,0:T(8,128)(2,1)S(1)} %collective-permute-done.25.got), custom_call_target="tpu_custom_call" | custom-call | tf_op jit(solution)/shard_map/pallas_call | solution.py:831
  155.1 1.2 collective-permute-done.17.got
  156.3 1.2 shard_map.225
  (66 shorter events, 3.8 us)
Async XLA Ops:
  0.6 2.1 %copy-start = (bf16[4,256,256]{2,1,0:T(8,128)(2,1)S(1)}, bf16[4,256,256]{2,1,0:T(8,128)(2,1)}, u32[]{:S(2)}) copy-start(bf16[4,256,256]{2,1,0:T(8,128)(2,1)} %refs_4_.1) | copy-start | bytes 1572868
  0.7 2.1 %copy-start.8 = (bf16[2,256]{1,0:T(2,128)(2,1)S(1)}, bf16[2,256]{1,0:T(2,128)(2,1)}, u32[]{:S(2)}) copy-start(bf16[2,256]{1,0:T(2,128)(2,1)} %param.13) | copy-start | bytes 3076
  0.7 2.1 %copy-start.7 = (bf16[2,256]{1,0:T(2,128)(2,1)S(1)}, bf16[2,256]{1,0:T(2,128)(2,1)}, u32[]{:S(2)}) copy-start(bf16[2,256]{1,0:T(2,128)(2,1)} %param.14) | copy-start | bytes 3076
  0.7 2.1 %copy-start.10 = (bf16[2,128]{1,0:T(2,128)(2,1)S(1)}, bf16[2,128]{1,0:T(2,128)(2,1)}, u32[]{:S(2)}) copy-start(bf16[2,128]{1,0:T(2,128)(2,1)} %param.17) | copy-start | bytes 1540
  0.7 2.1 %copy-start.9 = (bf16[2,128]{1,0:T(2,128)(2,1)S(1)}, bf16[2,128]{1,0:T(2,128)(2,1)}, u32[]{:S(2)}) copy-start(bf16[2,128]{1,0:T(2,128)(2,1)} %param.18) | copy-start | bytes 1540
  0.7 2.1 %copy-start.6 = (bf16[2,256]{1,0:T(2,128)(2,1)S(1)}, bf16[2,256]{1,0:T(2,128)(2,1)}, u32[]{:S(2)}) copy-start(bf16[2,256]{1,0:T(2,128)(2,1)} %param.19) | copy-start | bytes 3076
  0.7 2.1 %copy-start.5 = (s32[4,16]{1,0:T(4,128)S(1)}, s32[4,16]{1,0:T(4,128)}, u32[]{:S(2)}) copy-start(s32[4,16]{1,0:T(4,128)} %refs_0_.3) | copy-start | bytes 772
  0.7 4.0 %copy-start.1 = (bf16[2,2,128,512]{3,2,1,0:T(8,128)(2,1)S(1)}, bf16[2,2,128,512]{3,2,1,0:T(8,128)(2,1)}, u32[]{:S(2)}) copy-start(bf16[2,2,128,512]{3,2,1,0:T(8,128)(2,1)} %param.16) | copy-start | bytes 1572868
  2.2 3.8 %collective-permute-start.2 = (bf16[2,512,256]{2,1,0:T(8,128)(2,1)S(1)}, bf16[2,512,256]{2,1,0:T(8,128)(2,1)S(1)}, u32[]{:S(2)}, u32[]{:S(2)}) collective-permute-start(bf16[2,512,256]{2,1,0:T(8,128)(2,1)S(1)} %reshape.40.refs_7_.refs_5_.refs_13_), channel_id=1, source_target_pairs={{0,1},{1,0},{2,3},{3,2},{4,5},{5,4},{6,7},{7,6},{8,9},{9,8},{10,11... | collective-permute-start | bytes 1572872 | tf_op jit(solution)/shard_map/ppermute | solution.py:605
  2.7 17.9 %collective-permute-start = (bf16[4,256,256]{2,1,0:T(8,128)(2,1)S(1)}, bf16[4,256,256]{2,1,0:T(8,128)(2,1)S(1)}, u32[]{:S(2)}, u32[]{:S(2)}) collective-permute-start(bf16[4,256,256]{2,1,0:T(8,128)(2,1)S(1)} %copy-done), channel_id=1, source_target_pairs={{0,1},{1,0},{2,3},{3,2},{4,5},{5,4},{6,7},{7,6},{8,9},{9,8},{10,11... | collective-permute-start | bytes 1572872 | tf_op jit(solution)/shard_map/ppermute | solution.py:605
  4.3 1.3 collective-permute-start.1
  4.8 16.9 %collective-permute-start.4 = (bf16[2,256,512]{2,1,0:T(8,128)(2,1)S(1)}, bf16[2,256,512]{2,1,0:T(8,128)(2,1)S(1)}, u32[]{:S(2)}, u32[]{:S(2)}) collective-permute-start(bf16[2,256,512]{2,1,0:T(8,128)(2,1)S(1)} %bitcast.5), channel_id=1, source_target_pairs={{0,1},{1,0},{2,3},{3,2},{4,5},{5,4},{6,7},{7,6},{8,9},{9,8},{10,11... | collective-permute-start | bytes 1572872 | tf_op jit(solution)/shard_map/ppermute | solution.py:605
  4.8 16.8 %collective-permute-start.3 = (bf16[4,256,256]{2,1,0:T(8,128)(2,1)}, bf16[4,256,256]{2,1,0:T(8,128)(2,1)S(1)}, u32[]{:S(2)}, u32[]{:S(2)}) collective-permute-start(bf16[4,256,256]{2,1,0:T(8,128)(2,1)} %refs_16_.1), channel_id=1, source_target_pairs={{0,1},{1,0},{2,3},{3,2},{4,5},{5,4},{6,7},{7,6},{8,9},{9,8},{10,11... | collective-permute-start | bytes 1572872 | tf_op jit(solution)/shard_map/ppermute | solution.py:605
  5.6 16.1 %collective-permute-start.5 = (bf16[2,512,256]{2,1,0:T(8,128)(2,1)}, bf16[2,512,256]{2,1,0:T(8,128)(2,1)S(1)}, u32[]{:S(2)}, u32[]{:S(2)}) collective-permute-start(bf16[2,512,256]{2,1,0:T(8,128)(2,1)} %refs_15_.1), channel_id=1, source_target_pairs={{0,1},{1,0},{2,3},{3,2},{4,5},{5,4},{6,7},{7,6},{8,9},{9,8},{10,11... | collective-permute-start | bytes 1572872 | tf_op jit(solution)/shard_map/ppermute | solution.py:605
  5.9 15.8 %collective-permute-start.6 = (bf16[2,512,256]{2,1,0:T(8,128)(2,1)}, bf16[2,512,256]{2,1,0:T(8,128)(2,1)S(1)}, u32[]{:S(2)}, u32[]{:S(2)}) collective-permute-start(bf16[2,512,256]{2,1,0:T(8,128)(2,1)} %refs_17_.1), channel_id=1, source_target_pairs={{0,1},{1,0},{2,3},{3,2},{4,5},{5,4},{6,7},{7,6},{8,9},{9,8},{10,11... | collective-permute-start | bytes 1572872 | tf_op jit(solution)/shard_map/ppermute | solution.py:605
  20.6 11.2 %copy-start.2 = (bf16[2,512,256]{2,1,0:T(8,128)(2,1)S(1)}, bf16[2,512,256]{2,1,0:T(8,128)(2,1)}, u32[]{:S(2)}) copy-start(bf16[2,512,256]{2,1,0:T(8,128)(2,1)} %refs_15_.1) | copy-start | bytes 1572868
  20.6 11.2 %copy-start.3 = (bf16[2,512,256]{2,1,0:T(8,128)(2,1)S(1)}, bf16[2,512,256]{2,1,0:T(8,128)(2,1)}, u32[]{:S(2)}) copy-start(bf16[2,512,256]{2,1,0:T(8,128)(2,1)} %refs_17_.1) | copy-start | bytes 1572868
  43.8 11.0 %copy-start.4 = (bf16[4,256,256]{2,1,0:T(8,128)(2,1)S(1)}, bf16[4,256,256]{2,1,0:T(8,128)(2,1)}, u32[]{:S(2)}) copy-start(bf16[4,256,256]{2,1,0:T(8,128)(2,1)} %refs_16_.1) | copy-start | bytes 1572868
  81.0 2.7 %collective-permute-start.7 = (bf16[2048,256]{1,0:T(8,128)(2,1)S(1)}, bf16[2048,256]{1,0:T(8,128)(2,1)S(1)}, u32[]{:S(2)}, u32[]{:S(2)}) collective-permute-start(bf16[2048,256]{1,0:T(8,128)(2,1)S(1)} %get-tuple-element.173), channel_id=1, source_target_pairs={{0,1},{1,0},{2,3},{3,2},{4,5},{5,4},{6,7},{7,6},{8,9},{9,8},{10,11... | collective-permute-start | bytes 3145736 | tf_op jit(solution)/shard_map/ppermute | solution.py:605
  93.8 1.5 collective-permute-start.18
  95.7 10.7 %collective-permute-start.19 = (bf16[1280,256]{1,0:T(8,128)(2,1)S(1)}, bf16[1280,256]{1,0:T(8,128)(2,1)S(1)}, u32[]{:S(2)}, u32[]{:S(2)}) collective-permute-start(bf16[1280,256]{1,0:T(8,128)(2,1)S(1)} %get-tuple-element.216), channel_id=1, source_target_pairs={{0,2},{1,5},{2,0},{3,7},{4,6},{5,1},{6,4},{7,3},{8,10},{9,13},{10,... | collective-permute-start | bytes 1966088 | tf_op jit(solution)/shard_map/ppermute | solution.py:643
  96.6 3.4 %collective-permute-start.8 = (bf16[1024,256]{1,0:T(8,128)(2,1)S(1)}, bf16[1024,256]{1,0:T(8,128)(2,1)S(1)}, u32[]{:S(2)}, u32[]{:S(2)}) collective-permute-start(bf16[1024,256]{1,0:T(8,128)(2,1)S(1)} %get-tuple-element.180), channel_id=1, source_target_pairs={{0,1},{1,0},{2,3},{3,2},{4,5},{5,4},{6,7},{7,6},{8,9},{9,8},{10,11... | collective-permute-start | bytes 1572872 | tf_op jit(solution)/shard_map/ppermute | solution.py:605
  98.2 1.8 %collective-permute-start.9 = (bf16[544,256]{1,0:T(8,128)(2,1)S(1)}, bf16[544,256]{1,0:T(8,128)(2,1)S(1)}, u32[]{:S(2)}, u32[]{:S(2)}) collective-permute-start(bf16[544,256]{1,0:T(8,128)(2,1)S(1)} %get-tuple-element.192), channel_id=1, source_target_pairs={{0,1},{1,0},{2,3},{3,2},{4,5},{5,4},{6,7},{7,6},{8,9},{9,8},{10,11... | collective-permute-start | bytes 835592 | tf_op jit(solution)/shard_map/ppermute | solution.py:605
  100.1 14.3 %collective-permute-start.10 = (bf16[800,256]{1,0:T(8,128)(2,1)S(1)}, bf16[800,256]{1,0:T(8,128)(2,1)S(1)}, u32[]{:S(2)}, u32[]{:S(2)}) collective-permute-start(bf16[800,256]{1,0:T(8,128)(2,1)S(1)} %get-tuple-element.195), channel_id=1, source_target_pairs={{0,8},{1,9},{2,10},{3,11},{4,12},{5,13},{6,14},{7,15},{8,0},{9,1},... | collective-permute-start | bytes 1228808 | tf_op jit(solution)/shard_map/ppermute | solution.py:643
  106.5 7.1 %collective-permute-start.20 = (bf16[640,256]{1,0:T(8,128)(2,1)S(1)}, bf16[640,256]{1,0:T(8,128)(2,1)S(1)}, u32[]{:S(2)}, u32[]{:S(2)}) collective-permute-start(bf16[640,256]{1,0:T(8,128)(2,1)S(1)} %get-tuple-element.218), channel_id=1, source_target_pairs={{0,4},{1,3},{2,6},{3,1},{4,0},{5,7},{6,2},{7,5},{8,12},{9,11},{10,... | collective-permute-start | bytes 983048 | tf_op jit(solution)/shard_map/ppermute | solution.py:643
  113.7 5.4 %collective-permute-start.21 = (bf16[320,256]{1,0:T(8,128)(2,1)S(1)}, bf16[320,256]{1,0:T(8,128)(2,1)S(1)}, u32[]{:S(2)}, u32[]{:S(2)}) collective-permute-start(bf16[320,256]{1,0:T(8,128)(2,1)S(1)} %get-tuple-element.220), channel_id=1, source_target_pairs={{0,8},{1,9},{2,10},{3,11},{4,12},{5,13},{6,14},{7,15},{8,0},{9,1},... | collective-permute-start | bytes 491528 | tf_op jit(solution)/shard_map/ppermute | solution.py:643
  114.5 5.9 %collective-permute-start.11 = (bf16[416,256]{1,0:T(8,128)(2,1)S(1)}, bf16[416,256]{1,0:T(8,128)(2,1)S(1)}, u32[]{:S(2)}, u32[]{:S(2)}) collective-permute-start(bf16[416,256]{1,0:T(8,128)(2,1)S(1)} %get-tuple-element.197), channel_id=1, source_target_pairs={{0,4},{1,3},{2,6},{3,1},{4,0},{5,7},{6,2},{7,5},{8,12},{9,11},{10,... | collective-permute-start | bytes 638984 | tf_op jit(solution)/shard_map/ppermute | solution.py:643
  119.1 8.2 %collective-permute-start.22 = (bf16[320,256]{1,0:T(8,128)(2,1)S(1)}, bf16[320,256]{1,0:T(8,128)(2,1)S(1)}, u32[]{:S(2)}, u32[]{:S(2)}) collective-permute-start(bf16[320,256]{1,0:T(8,128)(2,1)S(1)} %shard_map.222.refs_0_), channel_id=1, source_target_pairs={{0,16},{1,17},{2,18},{3,19},{4,20},{5,21},{6,22},{7,23},{8,24},{9,... | collective-permute-start | bytes 491528 | tf_op jit(solution)/shard_map/ppermute | solution.py:643
  120.5 7.0 %collective-permute-start.12 = (bf16[224,256]{1,0:T(8,128)(2,1)S(1)}, bf16[224,256]{1,0:T(8,128)(2,1)S(1)}, u32[]{:S(2)}, u32[]{:S(2)}) collective-permute-start(bf16[224,256]{1,0:T(8,128)(2,1)S(1)} %get-tuple-element.199), channel_id=1, source_target_pairs={{0,2},{1,5},{2,0},{3,7},{4,6},{5,1},{6,4},{7,3},{8,10},{9,13},{10,... | collective-permute-start | bytes 344072 | tf_op jit(solution)/shard_map/ppermute | solution.py:643
  127.4 6.7 %collective-permute-start.23 = (bf16[320,256]{1,0:T(8,128)(2,1)S(1)}, bf16[320,256]{1,0:T(8,128)(2,1)S(1)}, u32[]{:S(2)}, u32[]{:S(2)}) collective-permute-start(bf16[320,256]{1,0:T(8,128)(2,1)S(1)} %shard_map.223), channel_id=1, source_target_pairs={{0,8},{1,9},{2,10},{3,11},{4,12},{5,13},{6,14},{7,15},{8,0},{9,1},... | collective-permute-start | bytes 491528 | tf_op jit(solution)/shard_map/ppermute | solution.py:643
  127.5 5.9 %collective-permute-start.13 = (bf16[224,256]{1,0:T(8,128)(2,1)S(1)}, bf16[224,256]{1,0:T(8,128)(2,1)S(1)}, u32[]{:S(2)}, u32[]{:S(2)}) collective-permute-start(bf16[224,256]{1,0:T(8,128)(2,1)S(1)} %shard_map.215.refs_0_), channel_id=1, source_target_pairs={{0,16},{1,17},{2,18},{3,19},{4,20},{5,21},{6,22},{7,23},{8,24},{9,... | collective-permute-start | bytes 344072 | tf_op jit(solution)/shard_map/ppermute | solution.py:643
  129.7 20.9 %collective-permute-start.14 = (bf16[2,512,256]{2,1,0:T(8,128)(2,1)S(1)}, bf16[2,512,256]{2,1,0:T(8,128)(2,1)S(1)}, u32[]{:S(2)}, u32[]{:S(2)}) collective-permute-start(bf16[2,512,256]{2,1,0:T(8,128)(2,1)S(1)} %get-tuple-element.205), channel_id=1, source_target_pairs={{0,1},{1,0},{2,3},{3,2},{4,5},{5,4},{6,7},{7,6},{8,9},{9,8},{10,11... | collective-permute-start | bytes 1572872 | tf_op jit(solution)/shard_map/ppermute | solution.py:605
  133.4 5.8 %collective-permute-start.15 = (bf16[192,256]{1,0:T(8,128)(2,1)S(1)}, bf16[192,256]{1,0:T(8,128)(2,1)S(1)}, u32[]{:S(2)}, u32[]{:S(2)}) collective-permute-start(bf16[192,256]{1,0:T(8,128)(2,1)S(1)} %get-tuple-element.210), channel_id=1, source_target_pairs={{0,2},{1,5},{2,0},{3,7},{4,6},{5,1},{6,4},{7,3},{8,10},{9,13},{10,... | collective-permute-start | bytes 294920 | tf_op jit(solution)/shard_map/ppermute | solution.py:643
  134.2 8.3 %collective-permute-start.24 = (bf16[640,256]{1,0:T(8,128)(2,1)S(1)}, bf16[640,256]{1,0:T(8,128)(2,1)S(1)}, u32[]{:S(2)}, u32[]{:S(2)}) collective-permute-start(bf16[640,256]{1,0:T(8,128)(2,1)S(1)} %pad_maximum_fusion.2), channel_id=1, source_target_pairs={{0,4},{1,3},{2,6},{3,1},{4,0},{5,7},{6,2},{7,5},{8,12},{9,11},{10,... | collective-permute-start | bytes 983048 | tf_op jit(solution)/shard_map/ppermute | solution.py:643
  139.2 7.9 %collective-permute-start.16 = (bf16[384,256]{1,0:T(8,128)(2,1)S(1)}, bf16[384,256]{1,0:T(8,128)(2,1)S(1)}, u32[]{:S(2)}, u32[]{:S(2)}) collective-permute-start(bf16[384,256]{1,0:T(8,128)(2,1)S(1)} %pad_maximum_fusion.3), channel_id=1, source_target_pairs={{0,4},{1,3},{2,6},{3,1},{4,0},{5,7},{6,2},{7,5},{8,12},{9,11},{10,... | collective-permute-start | bytes 589832 | tf_op jit(solution)/shard_map/ppermute | solution.py:643
  142.6 10.8 %collective-permute-start.25 = (bf16[1280,256]{1,0:T(8,128)(2,1)S(1)}, bf16[1280,256]{1,0:T(8,128)(2,1)S(1)}, u32[]{:S(2)}, u32[]{:S(2)}) collective-permute-start(bf16[1280,256]{1,0:T(8,128)(2,1)S(1)} %pad_maximum_fusion.mine), channel_id=1, source_target_pairs={{0,2},{1,5},{2,0},{3,7},{4,6},{5,1},{6,4},{7,3},{8,10},{9,13},{10,... | collective-permute-start | bytes 1966088 | tf_op jit(solution)/shard_map/ppermute | solution.py:643
  147.3 9.1 %collective-permute-start.17 = (bf16[768,256]{1,0:T(8,128)(2,1)S(1)}, bf16[768,256]{1,0:T(8,128)(2,1)S(1)}, u32[]{:S(2)}, u32[]{:S(2)}) collective-permute-start(bf16[768,256]{1,0:T(8,128)(2,1)S(1)} %pad_maximum_fusion.1.mine), channel_id=1, source_target_pairs={{0,8},{1,9},{2,10},{3,11},{4,12},{5,13},{6,14},{7,15},{8,0},{9,1},... | collective-permute-start | bytes 1179656 | tf_op jit(solution)/shard_map/ppermute | solution.py:643

commit v7 on v6

--- a/solution.py
+++ b/solution.py
@@ -11,7 +11,7 @@
 norm_eps = 1e-05
 CHUNKS = 8
 SLAB = 2 * CHUNKS
-TILE = 256
+TILE = 512
 
 
 def mm(a, b):

time: 158 us -> 158 us (level)
  transfers between devices with their start and end apart: 26 -> 26, of which waited for: 14 -> 15; matrix products, arithmetic and copies ran while one was open for 0% -> 0% of each run, Pallas kernels for 7% -> 7%
where the time goes in v7:
time: 158 us; the launch traced here: 157 us
  blocking collectives  74.9 us (47%)
  waiting for transfers between devices  41.1 us (26%)
  Pallas kernels  21.4 us (14%)
  starting transfers between devices  17.1 us (11%)
    all_to_all x6, blocking collectives, blocking(): lax.all_to_all(value, axes, 0, 0)  60.5 us
    ppermute x14, waiting for transfers between devices, partners(): lax.ppermute(value, ('seq', 'state'), [(2 * i + c, 2 * (i ^ masks[c]) + c...  38 us
    pallas_call x21, Pallas kernels, run(): pl.pallas_call(whole, out_shape=[jax.ShapeDtypeStruct(o[0], o[1]) for o i...  18.6 us
    all_to_all x1, blocking collectives, body(): lax.all_to_all(stats, ('seq', 'state'), 0, 0)  14.4 us
    ppermute x14, starting transfers between devices, partners(): lax.ppermute(value, ('seq', 'state'), [(2 * i + c, 2 * (i ^ masks[c]) + c...  14.1 us
  transfers between devices with their start and end apart: 26, of which 15 were waited for; matrix products, arithmetic and copies ran while one was open for 0% of the time, Pallas kernels for 7%

profile of v7, /device:TPU:0, one launch (start us, length us, event | category | flops | bytes accessed | tf_op | source)
XLA Modules:
  0.0 157.5 jit_solution(5819455777109315467)
XLA Ops:
  0.7 1.4 reshape.40.refs_7_.refs_5_.refs_13_
  2.2 0.5 collective-permute-start.2
  2.8 1.4 shard_map.204
  4.3 0.5 collective-permute-start.1
  6.2 14.4 %all_to_all.35.refs_0_ = f32[32,4,128]{2,1,0:T(4,128)S(1)} all-to-all(f32[32,4,128]{2,1,0:T(4,128)S(1)} %shard_map.203), channel_id=1, replica_groups=mesh['seq'=16,'state'=2] {'seq','state'}, dimensions={0} | all-to-all | bytes 131072 | tf_op jit(solution)/shard_map/all_to_all | solution.py:954
  20.6 1.0 shard_map.205
  21.7 10.1 %all_to_all.36.refs_0_ = f32[16,8,128]{2,1,0:T(8,128)S(1)} all-to-all(f32[16,8,128]{2,1,0:T(8,128)S(1)} %get-tuple-element.125), channel_id=1, replica_groups=mesh['seq'=16,'state'=2] {'seq'}, dimensions={0} | all-to-all | bytes 131072 | tf_op jit(solution)/shard_map/all_to_all | solution.py:617
  31.8 2.1 %shard_map.206 = (f32[16,512]{1,0:T(8,128)S(1)}, bf16[512,512]{1,0:T(8,128)(2,1)S(1)}, bf16[512,512]{1,0:T(8,128)(2,1)S(1)}, bf16[512,512]{1,0:T(8,128)(2,1)S(1)...) custom-call(f32[16,8,128]{2,1,0:T(8,128)S(1)} %all_to_all.36.refs_0_, ...), custom_call_target="tpu_custom_call" | custom-call | flops 805306368 | bytes 5554176 | tf_op jit(solution)/shard_map/pallas_call | solution.py:912
  33.9 9.9 %all_to_all.37.refs_0_ = f32[32,8,128]{2,1,0:T(8,128)S(1)} all-to-all(f32[32,8,128]{2,1,0:T(8,128)S(1)} %get-tuple-element.139), channel_id=1, replica_groups=mesh['seq'=16,'state'=2] {'seq','state'}, dimensions={0} | all-to-all | bytes 262144 | tf_op jit(solution)/shard_map/all_to_all | solution.py:617
  43.8 0.8 shard_map.207
  44.7 10.2 %all_to_all.38.refs_0_ = f32[16,8,128]{2,1,0:T(8,128)S(1)} all-to-all(f32[16,8,128]{2,1,0:T(8,128)S(1)} %get-tuple-element.141), channel_id=1, replica_groups=mesh['seq'=16,'state'=2] {'seq'}, dimensions={0} | all-to-all | bytes 131072 | tf_op jit(solution)/shard_map/all_to_all | solution.py:617
  54.9 3.5 %shard_map.208 = (f32[16,512]{1,0:T(8,128)S(1)}, bf16[512,512]{1,0:T(8,128)(2,1)S(1)}, bf16[512,512]{1,0:T(8,128)(2,1)S(1)}, bf16[512,512]{1,0:T(8,128)(2,1)S(1)...) custom-call(f32[16,8,128]{2,1,0:T(8,128)S(1)} %all_to_all.38.refs_0_, ...), custom_call_target="tpu_custom_call" | custom-call | flops 2147483648 | bytes 8175616 | tf_op jit(solution)/shard_map/pallas_call | solution.py:912
  58.4 10.1 %all_to_all.39.refs_0_ = f32[16,8,128]{2,1,0:T(8,128)S(1)} all-to-all(f32[16,8,128]{2,1,0:T(8,128)S(1)} %get-tuple-element.146), channel_id=1, replica_groups=mesh['seq'=16,'state'=2] {'seq'}, dimensions={0} | all-to-all | bytes 131072 | tf_op jit(solution)/shard_map/all_to_all | solution.py:617
  68.5 2.2 %shard_map.209 = (bf16[2048,256]{1,0:T(8,128)(2,1)S(1)}, bf16[2048,256]{1,0:T(8,128)(2,1)S(1)}, f32[8,128]{1,0:T(8,128)S(1)}, f32[8,128]{1,0:T(8,128)S(1)}, f32[...) custom-call(f32[16,8,128]{2,1,0:T(8,128)S(1)} %all_to_all.39.refs_0_, f32[16,8,128]{2,1,0:T(8,128)S(1)} %get-tuple-element.147.refs_1_, ...), custom_call_target="tpu_custom_call" | custom-call | flops 1610612736 | bytes 7176192 | tf_op jit(solution)/shard_map/pallas_call | solution.py:912
  70.8 9.9 %all_to_all.40.refs_0_ = f32[32,8,128]{2,1,0:T(8,128)S(1)} all-to-all(f32[32,8,128]{2,1,0:T(8,128)S(1)} %get-tuple-element.159), channel_id=1, replica_groups=mesh['seq'=16,'state'=2] {'seq','state'}, dimensions={0} | all-to-all | bytes 262144 | tf_op jit(solution)/shard_map/all_to_all | solution.py:617
  80.9 2.4 %shard_map.210 = (f32[512,512]{1,0:T(8,128)S(1)}, bf16[512,512]{1,0:T(8,128)(2,1)S(1)}, f32[8,512]{1,0:T(8,128)S(1)}, bf16[512,256]{1,0:T(8,128)(2,1)S(1)}, bf16...) custom-call(f32[32,8,128]{2,1,0:T(8,128)S(1)} %all_to_all.40.refs_0_, ...), custom_call_target="tpu_custom_call" | custom-call | flops 1610612736 | bytes 9633792 | tf_op jit(solution)/shard_map/pallas_call | solution.py:912
  83.4 10.2 %all_to_all.41.refs_0_ = f32[16,8,128]{2,1,0:T(8,128)S(1)} all-to-all(f32[16,8,128]{2,1,0:T(8,128)S(1)} %get-tuple-element.175), channel_id=1, replica_groups=mesh['seq'=16,'state'=2] {'seq'}, dimensions={0} | all-to-all | bytes 131072 | tf_op jit(solution)/shard_map/all_to_all | solution.py:617
  93.6 1.5 collective-permute-done.18.refs_3_
  95.4 0.9 collective-permute-start.19
  96.3 1.6 %shard_map.211 = (bf16[512,256]{1,0:T(8,128)(2,1)S(1)}, bf16[544,256]{1,0:T(8,128)(2,1)S(1)}, f32[16,128]{1,0:T(8,128)S(1)}, bf16[512,512]{1,0:T(8,128)(2,1)S(1)}) custom-call(f32[16,8,128]{2,1,0:T(8,128)S(1)} %all_to_all.41.refs_0_, f32[16,8,128]{2,1,0:T(8,128)S(1)} %get-tuple-element.182.refs_1_, f32[2,16,8,128]{3,2,1,0:T(8,128)S(1)} %get-tuple-element.132.refs_2_, ...), custom_call_target="tpu_custom_call" | custom-call | flops 805306368 | bytes 6135808 | tf_op jit(solution)/shard_map/pallas_call | solution.py:912
  97.9 0.6 collective-permute-start.9
  98.5 1.2 collective-permute-done.9.refs_3_
  100.3 5.7 %collective-permute-done.19.refs_1_ = bf16[1280,256]{1,0:T(8,128)(2,1)S(1)} collective-permute-done((bf16[1280,256]{1,0:T(8,128)(2,1)S(1)}, bf16[1280,256]{1,0:T(8,128)(2,1)S(1)}, u32[]{:S(2)}, u32[]{:S(2)}) %collective-permute-start.19) | collective-permute-done | bytes 655392 | tf_op jit(solution)/shard_map/ppermute | solution.py:643
  106.2 0.7 collective-permute-start.20
  107.0 6.4 %collective-permute-done.20.refs_1_ = bf16[640,256]{1,0:T(8,128)(2,1)S(1)} collective-permute-done((bf16[640,256]{1,0:T(8,128)(2,1)S(1)}, bf16[640,256]{1,0:T(8,128)(2,1)S(1)}, u32[]{:S(2)}, u32[]{:S(2)}) %collective-permute-start.20) | collective-permute-done | bytes 327712 | tf_op jit(solution)/shard_map/ppermute | solution.py:643
  113.5 0.7 collective-permute-start.21
  114.3 0.7 collective-permute-start.11
  115.0 3.8 %collective-permute-done.21.refs_1_ = bf16[320,256]{1,0:T(8,128)(2,1)S(1)} collective-permute-done((bf16[320,256]{1,0:T(8,128)(2,1)S(1)}, bf16[320,256]{1,0:T(8,128)(2,1)S(1)}, u32[]{:S(2)}, u32[]{:S(2)}) %collective-permute-start.21) | collective-permute-done | bytes 163872 | tf_op jit(solution)/shard_map/ppermute | solution.py:643
  118.9 0.8 collective-permute-start.22
  119.7 0.5 collective-permute-done.11.refs_1_
  120.3 0.6 collective-permute-start.12
  120.9 6.2 %collective-permute-done.22.refs_1_ = bf16[320,256]{1,0:T(8,128)(2,1)S(1)} collective-permute-done((bf16[320,256]{1,0:T(8,128)(2,1)S(1)}, bf16[320,256]{1,0:T(8,128)(2,1)S(1)}, u32[]{:S(2)}, u32[]{:S(2)}) %collective-permute-start.22) | collective-permute-done | bytes 163872 | tf_op jit(solution)/shard_map/ppermute | solution.py:643
  127.3 1.5 collective-permute-start.13
  128.7 0.7 shard_map.217
  129.5 3.6 %collective-permute-done.13.refs_1_ = bf16[224,256]{1,0:T(8,128)(2,1)S(1)} collective-permute-done((bf16[224,256]{1,0:T(8,128)(2,1)S(1)}, bf16[224,256]{1,0:T(8,128)(2,1)S(1)}, u32[]{:S(2)}, u32[]{:S(2)}) %collective-permute-start.13) | collective-permute-done | bytes 114720 | tf_op jit(solution)/shard_map/ppermute | solution.py:643
  133.2 0.7 collective-permute-start.15
  133.9 0.6 collective-permute-start.24
  134.6 4.4 %collective-permute-done.15 = bf16[192,256]{1,0:T(8,128)(2,1)S(1)} collective-permute-done((bf16[192,256]{1,0:T(8,128)(2,1)S(1)}, bf16[192,256]{1,0:T(8,128)(2,1)S(1)}, u32[]{:S(2)}, u32[]{:S(2)}) %collective-permute-start.15) | collective-permute-done | bytes 98336 | tf_op jit(solution)/shard_map/ppermute | solution.py:643
  139.0 0.7 collective-permute-start.16
  139.7 2.5 %collective-permute-done.24 = bf16[640,256]{1,0:T(8,128)(2,1)S(1)} collective-permute-done((bf16[640,256]{1,0:T(8,128)(2,1)S(1)}, bf16[640,256]{1,0:T(8,128)(2,1)S(1)}, u32[]{:S(2)}, u32[]{:S(2)}) %collective-permute-start.24) | collective-permute-done | bytes 327712 | tf_op jit(solution)/shard_map/ppermute | solution.py:643
  142.4 2.3 %collective-permute-start.25 = (bf16[1280,256]{1,0:T(8,128)(2,1)S(1)}, bf16[1280,256]{1,0:T(8,128)(2,1)S(1)}, u32[]{:S(2)}, u32[]{:S(2)}) collective-permute-start(bf16[1280,256]{1,0:T(8,128)(2,1)S(1)} %pad_maximum_fusion.mine), channel_id=1, source_target_pairs={{0,2},{1,5},{2,0},{3,7},{4,6},{5,1},{6,4},{7,3},{8,10},{9,13},{10,... | collective-permute-start | bytes 1966088 | tf_op jit(solution)/shard_map/ppermute | solution.py:643
  144.6 2.3 %collective-permute-done.16 = bf16[384,256]{1,0:T(8,128)(2,1)S(1)} collective-permute-done((bf16[384,256]{1,0:T(8,128)(2,1)S(1)}, bf16[384,256]{1,0:T(8,128)(2,1)S(1)}, u32[]{:S(2)}, u32[]{:S(2)}) %collective-permute-start.16) | collective-permute-done | bytes 196640 | tf_op jit(solution)/shard_map/ppermute | solution.py:643
  147.0 3.3 %collective-permute-start.17 = (bf16[768,256]{1,0:T(8,128)(2,1)S(1)}, bf16[768,256]{1,0:T(8,128)(2,1)S(1)}, u32[]{:S(2)}, u32[]{:S(2)}) collective-permute-start(bf16[768,256]{1,0:T(8,128)(2,1)S(1)} %pad_maximum_fusion.1.mine), channel_id=1, source_target_pairs={{0,8},{1,9},{2,10},{3,11},{4,12},{5,13},{6,14},{7,15},{8,0},{9,1},... | collective-permute-start | bytes 1179656 | tf_op jit(solution)/shard_map/ppermute | solution.py:643
  150.3 1.6 %shard_map.218 = (bf16[4,256,256]{2,1,0:T(8,128)(2,1)}, f32[4,256,256]{2,1,0:T(8,128)}, f32[2,256]{1,0:T(2,128)}, f32[2,256]{1,0:T(2,128)}, f32[2,256]{1,0:T(2,1...) custom-call(f32[16,128]{1,0:T(8,128)S(1)} %get-tuple-element.200.refs_0_, f32[8,512]{1,0:T(8,128)S(1)} %get-tuple-element.201.refs_1_, ...), custom_call_target="tpu_custom_call" | custom-call | bytes 1622016 | tf_op jit(solution)/shard_map/pallas_call | solution.py:912
  151.9 1.3 collective-permute-done.25.got
  153.2 1.6 %shard_map.224 = (f32[2,512,256]{2,1,0:T(8,128)}, f32[2,512,256]{2,1,0:T(8,128)}, f32[2,256,512]{2,1,0:T(8,128)}, f32[2,1024,128]{2,1,0:T(8,128)}) custom-call(bf16[1280,256]{1,0:T(8,128)(2,1)S(1)} %pad_maximum_fusion.mine, bf16[1280,256]{1,0:T(8,128)(2,1)S(1)} %collective-permute-done.25.got), custom_call_target="tpu_custom_call" | custom-call | tf_op jit(solution)/shard_map/pallas_call | solution.py:831
  154.8 1.3 collective-permute-done.17.got
  156.1 1.2 shard_map.225
  (66 shorter events, 3.9 us)
Async XLA Ops:
  0.6 2.1 %copy-start = (bf16[4,256,256]{2,1,0:T(8,128)(2,1)S(1)}, bf16[4,256,256]{2,1,0:T(8,128)(2,1)}, u32[]{:S(2)}) copy-start(bf16[4,256,256]{2,1,0:T(8,128)(2,1)} %refs_4_.1) | copy-start | bytes 1572868
  0.7 2.1 %copy-start.8 = (bf16[2,256]{1,0:T(2,128)(2,1)S(1)}, bf16[2,256]{1,0:T(2,128)(2,1)}, u32[]{:S(2)}) copy-start(bf16[2,256]{1,0:T(2,128)(2,1)} %param.13) | copy-start | bytes 3076
  0.7 2.1 %copy-start.7 = (bf16[2,256]{1,0:T(2,128)(2,1)S(1)}, bf16[2,256]{1,0:T(2,128)(2,1)}, u32[]{:S(2)}) copy-start(bf16[2,256]{1,0:T(2,128)(2,1)} %param.14) | copy-start | bytes 3076
  0.7 2.1 %copy-start.10 = (bf16[2,128]{1,0:T(2,128)(2,1)S(1)}, bf16[2,128]{1,0:T(2,128)(2,1)}, u32[]{:S(2)}) copy-start(bf16[2,128]{1,0:T(2,128)(2,1)} %param.17) | copy-start | bytes 1540
  0.7 2.1 %copy-start.9 = (bf16[2,128]{1,0:T(2,128)(2,1)S(1)}, bf16[2,128]{1,0:T(2,128)(2,1)}, u32[]{:S(2)}) copy-start(bf16[2,128]{1,0:T(2,128)(2,1)} %param.18) | copy-start | bytes 1540
  0.7 2.1 %copy-start.6 = (bf16[2,256]{1,0:T(2,128)(2,1)S(1)}, bf16[2,256]{1,0:T(2,128)(2,1)}, u32[]{:S(2)}) copy-start(bf16[2,256]{1,0:T(2,128)(2,1)} %param.19) | copy-start | bytes 3076
  0.7 2.1 %copy-start.5 = (s32[4,16]{1,0:T(4,128)S(1)}, s32[4,16]{1,0:T(4,128)}, u32[]{:S(2)}) copy-start(s32[4,16]{1,0:T(4,128)} %refs_0_.3) | copy-start | bytes 772
  0.7 4.0 %copy-start.1 = (bf16[2,2,128,512]{3,2,1,0:T(8,128)(2,1)S(1)}, bf16[2,2,128,512]{3,2,1,0:T(8,128)(2,1)}, u32[]{:S(2)}) copy-start(bf16[2,2,128,512]{3,2,1,0:T(8,128)(2,1)} %param.16) | copy-start | bytes 1572868
  2.2 3.8 %collective-permute-start.2 = (bf16[2,512,256]{2,1,0:T(8,128)(2,1)S(1)}, bf16[2,512,256]{2,1,0:T(8,128)(2,1)S(1)}, u32[]{:S(2)}, u32[]{:S(2)}) collective-permute-start(bf16[2,512,256]{2,1,0:T(8,128)(2,1)S(1)} %reshape.40.refs_7_.refs_5_.refs_13_), channel_id=1, source_target_pairs={{0,1},{1,0},{2,3},{3,2},{4,5},{5,4},{6,7},{7,6},{8,9},{9,8},{10,11... | collective-permute-start | bytes 1572872 | tf_op jit(solution)/shard_map/ppermute | solution.py:605
  2.7 17.9 %collective-permute-start = (bf16[4,256,256]{2,1,0:T(8,128)(2,1)S(1)}, bf16[4,256,256]{2,1,0:T(8,128)(2,1)S(1)}, u32[]{:S(2)}, u32[]{:S(2)}) collective-permute-start(bf16[4,256,256]{2,1,0:T(8,128)(2,1)S(1)} %copy-done), channel_id=1, source_target_pairs={{0,1},{1,0},{2,3},{3,2},{4,5},{5,4},{6,7},{7,6},{8,9},{9,8},{10,11... | collective-permute-start | bytes 1572872 | tf_op jit(solution)/shard_map/ppermute | solution.py:605
  4.3 1.3 collective-permute-start.1
  4.8 16.9 %collective-permute-start.4 = (bf16[2,256,512]{2,1,0:T(8,128)(2,1)S(1)}, bf16[2,256,512]{2,1,0:T(8,128)(2,1)S(1)}, u32[]{:S(2)}, u32[]{:S(2)}) collective-permute-start(bf16[2,256,512]{2,1,0:T(8,128)(2,1)S(1)} %bitcast.5), channel_id=1, source_target_pairs={{0,1},{1,0},{2,3},{3,2},{4,5},{5,4},{6,7},{7,6},{8,9},{9,8},{10,11... | collective-permute-start | bytes 1572872 | tf_op jit(solution)/shard_map/ppermute | solution.py:605
  4.8 16.8 %collective-permute-start.3 = (bf16[4,256,256]{2,1,0:T(8,128)(2,1)}, bf16[4,256,256]{2,1,0:T(8,128)(2,1)S(1)}, u32[]{:S(2)}, u32[]{:S(2)}) collective-permute-start(bf16[4,256,256]{2,1,0:T(8,128)(2,1)} %refs_16_.1), channel_id=1, source_target_pairs={{0,1},{1,0},{2,3},{3,2},{4,5},{5,4},{6,7},{7,6},{8,9},{9,8},{10,11... | collective-permute-start | bytes 1572872 | tf_op jit(solution)/shard_map/ppermute | solution.py:605
  5.6 16.1 %collective-permute-start.5 = (bf16[2,512,256]{2,1,0:T(8,128)(2,1)}, bf16[2,512,256]{2,1,0:T(8,128)(2,1)S(1)}, u32[]{:S(2)}, u32[]{:S(2)}) collective-permute-start(bf16[2,512,256]{2,1,0:T(8,128)(2,1)} %refs_15_.1), channel_id=1, source_target_pairs={{0,1},{1,0},{2,3},{3,2},{4,5},{5,4},{6,7},{7,6},{8,9},{9,8},{10,11... | collective-permute-start | bytes 1572872 | tf_op jit(solution)/shard_map/ppermute | solution.py:605
  5.9 15.8 %collective-permute-start.6 = (bf16[2,512,256]{2,1,0:T(8,128)(2,1)}, bf16[2,512,256]{2,1,0:T(8,128)(2,1)S(1)}, u32[]{:S(2)}, u32[]{:S(2)}) collective-permute-start(bf16[2,512,256]{2,1,0:T(8,128)(2,1)} %refs_17_.1), channel_id=1, source_target_pairs={{0,1},{1,0},{2,3},{3,2},{4,5},{5,4},{6,7},{7,6},{8,9},{9,8},{10,11... | collective-permute-start | bytes 1572872 | tf_op jit(solution)/shard_map/ppermute | solution.py:605
  20.6 11.2 %copy-start.2 = (bf16[2,512,256]{2,1,0:T(8,128)(2,1)S(1)}, bf16[2,512,256]{2,1,0:T(8,128)(2,1)}, u32[]{:S(2)}) copy-start(bf16[2,512,256]{2,1,0:T(8,128)(2,1)} %refs_15_.1) | copy-start | bytes 1572868
  20.6 11.2 %copy-start.3 = (bf16[2,512,256]{2,1,0:T(8,128)(2,1)S(1)}, bf16[2,512,256]{2,1,0:T(8,128)(2,1)}, u32[]{:S(2)}) copy-start(bf16[2,512,256]{2,1,0:T(8,128)(2,1)} %refs_17_.1) | copy-start | bytes 1572868
  43.8 11.0 %copy-start.4 = (bf16[4,256,256]{2,1,0:T(8,128)(2,1)S(1)}, bf16[4,256,256]{2,1,0:T(8,128)(2,1)}, u32[]{:S(2)}) copy-start(bf16[4,256,256]{2,1,0:T(8,128)(2,1)} %refs_16_.1) | copy-start | bytes 1572868
  80.7 2.7 %collective-permute-start.7 = (bf16[2048,256]{1,0:T(8,128)(2,1)S(1)}, bf16[2048,256]{1,0:T(8,128)(2,1)S(1)}, u32[]{:S(2)}, u32[]{:S(2)}) collective-permute-start(bf16[2048,256]{1,0:T(8,128)(2,1)S(1)} %get-tuple-element.173), channel_id=1, source_target_pairs={{0,1},{1,0},{2,3},{3,2},{4,5},{5,4},{6,7},{7,6},{8,9},{9,8},{10,11... | collective-permute-start | bytes 3145736 | tf_op jit(solution)/shard_map/ppermute | solution.py:605
  93.6 1.5 collective-permute-start.18
  95.4 10.7 %collective-permute-start.19 = (bf16[1280,256]{1,0:T(8,128)(2,1)S(1)}, bf16[1280,256]{1,0:T(8,128)(2,1)S(1)}, u32[]{:S(2)}, u32[]{:S(2)}) collective-permute-start(bf16[1280,256]{1,0:T(8,128)(2,1)S(1)} %get-tuple-element.216), channel_id=1, source_target_pairs={{0,2},{1,5},{2,0},{3,7},{4,6},{5,1},{6,4},{7,3},{8,10},{9,13},{10,... | collective-permute-start | bytes 1966088 | tf_op jit(solution)/shard_map/ppermute | solution.py:643
  96.3 3.3 %collective-permute-start.8 = (bf16[1024,256]{1,0:T(8,128)(2,1)S(1)}, bf16[1024,256]{1,0:T(8,128)(2,1)S(1)}, u32[]{:S(2)}, u32[]{:S(2)}) collective-permute-start(bf16[1024,256]{1,0:T(8,128)(2,1)S(1)} %get-tuple-element.180), channel_id=1, source_target_pairs={{0,1},{1,0},{2,3},{3,2},{4,5},{5,4},{6,7},{7,6},{8,9},{9,8},{10,11... | collective-permute-start | bytes 1572872 | tf_op jit(solution)/shard_map/ppermute | solution.py:605
  97.9 1.8 %collective-permute-start.9 = (bf16[544,256]{1,0:T(8,128)(2,1)S(1)}, bf16[544,256]{1,0:T(8,128)(2,1)S(1)}, u32[]{:S(2)}, u32[]{:S(2)}) collective-permute-start(bf16[544,256]{1,0:T(8,128)(2,1)S(1)} %get-tuple-element.192), channel_id=1, source_target_pairs={{0,1},{1,0},{2,3},{3,2},{4,5},{5,4},{6,7},{7,6},{8,9},{9,8},{10,11... | collective-permute-start | bytes 835592 | tf_op jit(solution)/shard_map/ppermute | solution.py:605
  99.9 14.3 %collective-permute-start.10 = (bf16[800,256]{1,0:T(8,128)(2,1)S(1)}, bf16[800,256]{1,0:T(8,128)(2,1)S(1)}, u32[]{:S(2)}, u32[]{:S(2)}) collective-permute-start(bf16[800,256]{1,0:T(8,128)(2,1)S(1)} %get-tuple-element.195), channel_id=1, source_target_pairs={{0,8},{1,9},{2,10},{3,11},{4,12},{5,13},{6,14},{7,15},{8,0},{9,1},... | collective-permute-start | bytes 1228808 | tf_op jit(solution)/shard_map/ppermute | solution.py:643
  106.2 7.1 %collective-permute-start.20 = (bf16[640,256]{1,0:T(8,128)(2,1)S(1)}, bf16[640,256]{1,0:T(8,128)(2,1)S(1)}, u32[]{:S(2)}, u32[]{:S(2)}) collective-permute-start(bf16[640,256]{1,0:T(8,128)(2,1)S(1)} %get-tuple-element.218), channel_id=1, source_target_pairs={{0,4},{1,3},{2,6},{3,1},{4,0},{5,7},{6,2},{7,5},{8,12},{9,11},{10,... | collective-permute-start | bytes 983048 | tf_op jit(solution)/shard_map/ppermute | solution.py:643
  113.5 5.4 %collective-permute-start.21 = (bf16[320,256]{1,0:T(8,128)(2,1)S(1)}, bf16[320,256]{1,0:T(8,128)(2,1)S(1)}, u32[]{:S(2)}, u32[]{:S(2)}) collective-permute-start(bf16[320,256]{1,0:T(8,128)(2,1)S(1)} %get-tuple-element.220), channel_id=1, source_target_pairs={{0,8},{1,9},{2,10},{3,11},{4,12},{5,13},{6,14},{7,15},{8,0},{9,1},... | collective-permute-start | bytes 491528 | tf_op jit(solution)/shard_map/ppermute | solution.py:643
  114.3 5.9 %collective-permute-start.11 = (bf16[416,256]{1,0:T(8,128)(2,1)S(1)}, bf16[416,256]{1,0:T(8,128)(2,1)S(1)}, u32[]{:S(2)}, u32[]{:S(2)}) collective-permute-start(bf16[416,256]{1,0:T(8,128)(2,1)S(1)} %get-tuple-element.197), channel_id=1, source_target_pairs={{0,4},{1,3},{2,6},{3,1},{4,0},{5,7},{6,2},{7,5},{8,12},{9,11},{10,... | collective-permute-start | bytes 638984 | tf_op jit(solution)/shard_map/ppermute | solution.py:643
  118.9 8.2 %collective-permute-start.22 = (bf16[320,256]{1,0:T(8,128)(2,1)S(1)}, bf16[320,256]{1,0:T(8,128)(2,1)S(1)}, u32[]{:S(2)}, u32[]{:S(2)}) collective-permute-start(bf16[320,256]{1,0:T(8,128)(2,1)S(1)} %shard_map.222.refs_0_), channel_id=1, source_target_pairs={{0,16},{1,17},{2,18},{3,19},{4,20},{5,21},{6,22},{7,23},{8,24},{9,... | collective-permute-start | bytes 491528 | tf_op jit(solution)/shard_map/ppermute | solution.py:643
  120.3 7.0 %collective-permute-start.12 = (bf16[224,256]{1,0:T(8,128)(2,1)S(1)}, bf16[224,256]{1,0:T(8,128)(2,1)S(1)}, u32[]{:S(2)}, u32[]{:S(2)}) collective-permute-start(bf16[224,256]{1,0:T(8,128)(2,1)S(1)} %get-tuple-element.199), channel_id=1, source_target_pairs={{0,2},{1,5},{2,0},{3,7},{4,6},{5,1},{6,4},{7,3},{8,10},{9,13},{10,... | collective-permute-start | bytes 344072 | tf_op jit(solution)/shard_map/ppermute | solution.py:643
  127.1 6.7 %collective-permute-start.23 = (bf16[320,256]{1,0:T(8,128)(2,1)S(1)}, bf16[320,256]{1,0:T(8,128)(2,1)S(1)}, u32[]{:S(2)}, u32[]{:S(2)}) collective-permute-start(bf16[320,256]{1,0:T(8,128)(2,1)S(1)} %shard_map.223), channel_id=1, source_target_pairs={{0,8},{1,9},{2,10},{3,11},{4,12},{5,13},{6,14},{7,15},{8,0},{9,1},... | collective-permute-start | bytes 491528 | tf_op jit(solution)/shard_map/ppermute | solution.py:643
  127.3 5.9 %collective-permute-start.13 = (bf16[224,256]{1,0:T(8,128)(2,1)S(1)}, bf16[224,256]{1,0:T(8,128)(2,1)S(1)}, u32[]{:S(2)}, u32[]{:S(2)}) collective-permute-start(bf16[224,256]{1,0:T(8,128)(2,1)S(1)} %shard_map.215.refs_0_), channel_id=1, source_target_pairs={{0,16},{1,17},{2,18},{3,19},{4,20},{5,21},{6,22},{7,23},{8,24},{9,... | collective-permute-start | bytes 344072 | tf_op jit(solution)/shard_map/ppermute | solution.py:643
  129.4 20.9 %collective-permute-start.14 = (bf16[2,512,256]{2,1,0:T(8,128)(2,1)S(1)}, bf16[2,512,256]{2,1,0:T(8,128)(2,1)S(1)}, u32[]{:S(2)}, u32[]{:S(2)}) collective-permute-start(bf16[2,512,256]{2,1,0:T(8,128)(2,1)S(1)} %get-tuple-element.205), channel_id=1, source_target_pairs={{0,1},{1,0},{2,3},{3,2},{4,5},{5,4},{6,7},{7,6},{8,9},{9,8},{10,11... | collective-permute-start | bytes 1572872 | tf_op jit(solution)/shard_map/ppermute | solution.py:605
  133.2 5.8 %collective-permute-start.15 = (bf16[192,256]{1,0:T(8,128)(2,1)S(1)}, bf16[192,256]{1,0:T(8,128)(2,1)S(1)}, u32[]{:S(2)}, u32[]{:S(2)}) collective-permute-start(bf16[192,256]{1,0:T(8,128)(2,1)S(1)} %get-tuple-element.210), channel_id=1, source_target_pairs={{0,2},{1,5},{2,0},{3,7},{4,6},{5,1},{6,4},{7,3},{8,10},{9,13},{10,... | collective-permute-start | bytes 294920 | tf_op jit(solution)/shard_map/ppermute | solution.py:643
  133.9 8.3 %collective-permute-start.24 = (bf16[640,256]{1,0:T(8,128)(2,1)S(1)}, bf16[640,256]{1,0:T(8,128)(2,1)S(1)}, u32[]{:S(2)}, u32[]{:S(2)}) collective-permute-start(bf16[640,256]{1,0:T(8,128)(2,1)S(1)} %pad_maximum_fusion.2), channel_id=1, source_target_pairs={{0,4},{1,3},{2,6},{3,1},{4,0},{5,7},{6,2},{7,5},{8,12},{9,11},{10,... | collective-permute-start | bytes 983048 | tf_op jit(solution)/shard_map/ppermute | solution.py:643
  139.0 7.9 %collective-permute-start.16 = (bf16[384,256]{1,0:T(8,128)(2,1)S(1)}, bf16[384,256]{1,0:T(8,128)(2,1)S(1)}, u32[]{:S(2)}, u32[]{:S(2)}) collective-permute-start(bf16[384,256]{1,0:T(8,128)(2,1)S(1)} %pad_maximum_fusion.3), channel_id=1, source_target_pairs={{0,4},{1,3},{2,6},{3,1},{4,0},{5,7},{6,2},{7,5},{8,12},{9,11},{10,... | collective-permute-start | bytes 589832 | tf_op jit(solution)/shard_map/ppermute | solution.py:643
  142.4 10.8 %collective-permute-start.25 = (bf16[1280,256]{1,0:T(8,128)(2,1)S(1)}, bf16[1280,256]{1,0:T(8,128)(2,1)S(1)}, u32[]{:S(2)}, u32[]{:S(2)}) collective-permute-start(bf16[1280,256]{1,0:T(8,128)(2,1)S(1)} %pad_maximum_fusion.mine), channel_id=1, source_target_pairs={{0,2},{1,5},{2,0},{3,7},{4,6},{5,1},{6,4},{7,3},{8,10},{9,13},{10,... | collective-permute-start | bytes 1966088 | tf_op jit(solution)/shard_map/ppermute | solution.py:643
  147.0 9.1 %collective-permute-start.17 = (bf16[768,256]{1,0:T(8,128)(2,1)S(1)}, bf16[768,256]{1,0:T(8,128)(2,1)S(1)}, u32[]{:S(2)}, u32[]{:S(2)}) collective-permute-start(bf16[768,256]{1,0:T(8,128)(2,1)S(1)} %pad_maximum_fusion.1.mine), channel_id=1, source_target_pairs={{0,8},{1,9},{2,10},{3,11},{4,12},{5,13},{6,14},{7,15},{8,0},{9,1},... | collective-permute-start | bytes 1179656 | tf_op jit(solution)/shard_map/ppermute | solution.py:643

commit v8 on v7

--- a/solution.py
+++ b/solution.py
@@ -876,7 +876,7 @@
         return self.ref[index]
 
 
-def run(kernel, outs, groups, scratch=(), limit=24, flops=0):
+def run(kernel, outs, groups, scratch=(), limit=24, flops=0, smem=None):
     args = [a for g in groups for a in (g if isinstance(g, tuple) else (g,))]
     far_in = [i for i, a in enumerate(args) if isinstance(a, Far)]
     arrays = [a.value if isinstance(a, (Far, Part)) else a for a in args]
@@ -912,7 +912,7 @@
     return pl.pallas_call(
         whole,
         out_shape=[jax.ShapeDtypeStruct(o[0], o[1]) for o in outs],
-        in_specs=[space(isinstance(a, Far)) for a in args],
+        in_specs=[pl.BlockSpec(memory_space=pltpu.SMEM) if a is smem else space(isinstance(a, Far)) for a in args],
         out_specs=[space(False)] * len(outs),
         scratch_shapes=[pltpu.VMEM(*s) for s in scratch] + held,
         compiler_params=pltpu.CompilerParams(vmem_limit_bytes=limit * 2**20),
@@ -943,7 +943,7 @@
     own, keep, dk, perm = run(
         functools.partial(prep_kernel, peers, steps, span),
         [((32, 128), f32), ((2, n, 128), f32), ((2, peers, 8, 128), f32), ((2, n, n), bf16)],
-        (Far(positions, smem=True), raw))
+        (positions, raw), smem=positions)
     oth = swap(own)
     ordered = ((peers, 8, 128), f32)
 

time: 158 us -> 158 us (level)
  no operation moved by 1% of the time
where the time goes in v8:
time: 158 us
  blocking collectives  74.9 us (47%)
  waiting for transfers between devices  41.1 us (26%)
  Pallas kernels  21.7 us (14%)
  starting transfers between devices  17.1 us (11%)
    all_to_all x6, blocking collectives, blocking(): lax.all_to_all(value, axes, 0, 0)  60.5 us
    ppermute x14, waiting for transfers between devices, partners(): lax.ppermute(value, ('seq', 'state'), [(2 * i + c, 2 * (i ^ masks[c]) + c...  38 us
    pallas_call x21, Pallas kernels, run(): pl.pallas_call(whole, out_shape=[jax.ShapeDtypeStruct(o[0], o[1]) for o i...  18.9 us
    all_to_all x1, blocking collectives, body(): lax.all_to_all(stats, ('seq', 'state'), 0, 0)  14.4 us
    ppermute x14, starting transfers between devices, partners(): lax.ppermute(value, ('seq', 'state'), [(2 * i + c, 2 * (i ^ masks[c]) + c...  14.1 us
  transfers between devices with their start and end apart: 26, of which 15 were waited for; matrix products, arithmetic and copies ran while one was open for 0% of the time, Pallas kernels for 7%

profile of v8, /device:TPU:0, one launch (start us, length us, event | category | flops | bytes accessed | tf_op | source)
XLA Modules:
  0.0 157.8 jit_solution(16834041863432816705)
XLA Ops:
  0.7 1.4 reshape.40.refs_7_.refs_5_.refs_13_
  2.2 0.5 collective-permute-start.2
  2.8 1.7 %shard_map.204 = (f32[32,128]{1,0:T(8,128)S(1)}, f32[2,512,128]{2,1,0:T(8,128)S(1)}, f32[2,16,8,128]{3,2,1,0:T(8,128)S(1)}, bf16[2,512,512]{2,1,0:T(8,128)(2,1)S(1)}) custom-call(s32[4,16]{1,0:T(4,128)S(1)} %copy-done.5, f32[2,1024]{1,0:T(2,128)S(1)} %convert_add_fusion.refs_1_.refs_6_), custom_call_target="tpu_custom_call" | custom-call | bytes 8448 | tf_op jit(solution)/shard_map/pallas_call | solution.py:912
  4.6 0.5 collective-permute-start.1
  6.5 14.4 %all_to_all.35.refs_0_ = f32[32,4,128]{2,1,0:T(4,128)S(1)} all-to-all(f32[32,4,128]{2,1,0:T(4,128)S(1)} %shard_map.203), channel_id=1, replica_groups=mesh['seq'=16,'state'=2] {'seq','state'}, dimensions={0} | all-to-all | bytes 131072 | tf_op jit(solution)/shard_map/all_to_all | solution.py:954
  20.9 1.0 shard_map.205
  22.0 10.1 %all_to_all.36.refs_0_ = f32[16,8,128]{2,1,0:T(8,128)S(1)} all-to-all(f32[16,8,128]{2,1,0:T(8,128)S(1)} %get-tuple-element.125), channel_id=1, replica_groups=mesh['seq'=16,'state'=2] {'seq'}, dimensions={0} | all-to-all | bytes 131072 | tf_op jit(solution)/shard_map/all_to_all | solution.py:617
  32.1 2.1 %shard_map.206 = (f32[16,512]{1,0:T(8,128)S(1)}, bf16[512,512]{1,0:T(8,128)(2,1)S(1)}, bf16[512,512]{1,0:T(8,128)(2,1)S(1)}, bf16[512,512]{1,0:T(8,128)(2,1)S(1)...) custom-call(f32[16,8,128]{2,1,0:T(8,128)S(1)} %all_to_all.36.refs_0_, ...), custom_call_target="tpu_custom_call" | custom-call | flops 805306368 | bytes 5554176 | tf_op jit(solution)/shard_map/pallas_call | solution.py:912
  34.2 9.9 %all_to_all.37.refs_0_ = f32[32,8,128]{2,1,0:T(8,128)S(1)} all-to-all(f32[32,8,128]{2,1,0:T(8,128)S(1)} %get-tuple-element.139), channel_id=1, replica_groups=mesh['seq'=16,'state'=2] {'seq','state'}, dimensions={0} | all-to-all | bytes 262144 | tf_op jit(solution)/shard_map/all_to_all | solution.py:617
  44.1 0.8 shard_map.207
  45.0 10.2 %all_to_all.38.refs_0_ = f32[16,8,128]{2,1,0:T(8,128)S(1)} all-to-all(f32[16,8,128]{2,1,0:T(8,128)S(1)} %get-tuple-element.141), channel_id=1, replica_groups=mesh['seq'=16,'state'=2] {'seq'}, dimensions={0} | all-to-all | bytes 131072 | tf_op jit(solution)/shard_map/all_to_all | solution.py:617
  55.2 3.5 %shard_map.208 = (f32[16,512]{1,0:T(8,128)S(1)}, bf16[512,512]{1,0:T(8,128)(2,1)S(1)}, bf16[512,512]{1,0:T(8,128)(2,1)S(1)}, bf16[512,512]{1,0:T(8,128)(2,1)S(1)...) custom-call(f32[16,8,128]{2,1,0:T(8,128)S(1)} %all_to_all.38.refs_0_, ...), custom_call_target="tpu_custom_call" | custom-call | flops 2147483648 | bytes 8175616 | tf_op jit(solution)/shard_map/pallas_call | solution.py:912
  58.7 10.1 %all_to_all.39.refs_0_ = f32[16,8,128]{2,1,0:T(8,128)S(1)} all-to-all(f32[16,8,128]{2,1,0:T(8,128)S(1)} %get-tuple-element.146), channel_id=1, replica_groups=mesh['seq'=16,'state'=2] {'seq'}, dimensions={0} | all-to-all | bytes 131072 | tf_op jit(solution)/shard_map/all_to_all | solution.py:617
  68.8 2.2 %shard_map.209 = (bf16[2048,256]{1,0:T(8,128)(2,1)S(1)}, bf16[2048,256]{1,0:T(8,128)(2,1)S(1)}, f32[8,128]{1,0:T(8,128)S(1)}, f32[8,128]{1,0:T(8,128)S(1)}, f32[...) custom-call(f32[16,8,128]{2,1,0:T(8,128)S(1)} %all_to_all.39.refs_0_, f32[16,8,128]{2,1,0:T(8,128)S(1)} %get-tuple-element.147.refs_1_, ...), custom_call_target="tpu_custom_call" | custom-call | flops 1610612736 | bytes 7176192 | tf_op jit(solution)/shard_map/pallas_call | solution.py:912
  71.1 9.9 %all_to_all.40.refs_0_ = f32[32,8,128]{2,1,0:T(8,128)S(1)} all-to-all(f32[32,8,128]{2,1,0:T(8,128)S(1)} %get-tuple-element.159), channel_id=1, replica_groups=mesh['seq'=16,'state'=2] {'seq','state'}, dimensions={0} | all-to-all | bytes 262144 | tf_op jit(solution)/shard_map/all_to_all | solution.py:617
  81.2 2.4 %shard_map.210 = (f32[512,512]{1,0:T(8,128)S(1)}, bf16[512,512]{1,0:T(8,128)(2,1)S(1)}, f32[8,512]{1,0:T(8,128)S(1)}, bf16[512,256]{1,0:T(8,128)(2,1)S(1)}, bf16...) custom-call(f32[32,8,128]{2,1,0:T(8,128)S(1)} %all_to_all.40.refs_0_, ...), custom_call_target="tpu_custom_call" | custom-call | flops 1610612736 | bytes 9633792 | tf_op jit(solution)/shard_map/pallas_call | solution.py:912
  83.7 10.2 %all_to_all.41.refs_0_ = f32[16,8,128]{2,1,0:T(8,128)S(1)} all-to-all(f32[16,8,128]{2,1,0:T(8,128)S(1)} %get-tuple-element.175), channel_id=1, replica_groups=mesh['seq'=16,'state'=2] {'seq'}, dimensions={0} | all-to-all | bytes 131072 | tf_op jit(solution)/shard_map/all_to_all | solution.py:617
  93.9 1.5 collective-permute-done.18.refs_3_
  95.7 0.9 collective-permute-start.19
  96.6 1.6 %shard_map.211 = (bf16[512,256]{1,0:T(8,128)(2,1)S(1)}, bf16[544,256]{1,0:T(8,128)(2,1)S(1)}, f32[16,128]{1,0:T(8,128)S(1)}, bf16[512,512]{1,0:T(8,128)(2,1)S(1)}) custom-call(f32[16,8,128]{2,1,0:T(8,128)S(1)} %all_to_all.41.refs_0_, f32[16,8,128]{2,1,0:T(8,128)S(1)} %get-tuple-element.182.refs_1_, f32[2,16,8,128]{3,2,1,0:T(8,128)S(1)} %get-tuple-element.132.refs_2_, ...), custom_call_target="tpu_custom_call" | custom-call | flops 805306368 | bytes 6135808 | tf_op jit(solution)/shard_map/pallas_call | solution.py:912
  98.2 0.6 collective-permute-start.9
  98.8 1.2 collective-permute-done.9.refs_3_
  100.6 5.7 %collective-permute-done.19.refs_1_ = bf16[1280,256]{1,0:T(8,128)(2,1)S(1)} collective-permute-done((bf16[1280,256]{1,0:T(8,128)(2,1)S(1)}, bf16[1280,256]{1,0:T(8,128)(2,1)S(1)}, u32[]{:S(2)}, u32[]{:S(2)}) %collective-permute-start.19) | collective-permute-done | bytes 655392 | tf_op jit(solution)/shard_map/ppermute | solution.py:643
  106.5 0.7 collective-permute-start.20
  107.3 6.4 %collective-permute-done.20.refs_1_ = bf16[640,256]{1,0:T(8,128)(2,1)S(1)} collective-permute-done((bf16[640,256]{1,0:T(8,128)(2,1)S(1)}, bf16[640,256]{1,0:T(8,128)(2,1)S(1)}, u32[]{:S(2)}, u32[]{:S(2)}) %collective-permute-start.20) | collective-permute-done | bytes 327712 | tf_op jit(solution)/shard_map/ppermute | solution.py:643
  113.8 0.7 collective-permute-start.21
  114.6 0.7 collective-permute-start.11
  115.3 3.8 %collective-permute-done.21.refs_1_ = bf16[320,256]{1,0:T(8,128)(2,1)S(1)} collective-permute-done((bf16[320,256]{1,0:T(8,128)(2,1)S(1)}, bf16[320,256]{1,0:T(8,128)(2,1)S(1)}, u32[]{:S(2)}, u32[]{:S(2)}) %collective-permute-start.21) | collective-permute-done | bytes 163872 | tf_op jit(solution)/shard_map/ppermute | solution.py:643
  119.2 0.8 collective-permute-start.22
  120.0 0.5 collective-permute-done.11.refs_1_
  120.6 0.6 collective-permute-start.12
  121.2 6.2 %collective-permute-done.22.refs_1_ = bf16[320,256]{1,0:T(8,128)(2,1)S(1)} collective-permute-done((bf16[320,256]{1,0:T(8,128)(2,1)S(1)}, bf16[320,256]{1,0:T(8,128)(2,1)S(1)}, u32[]{:S(2)}, u32[]{:S(2)}) %collective-permute-start.22) | collective-permute-done | bytes 163872 | tf_op jit(solution)/shard_map/ppermute | solution.py:643
  127.6 1.5 collective-permute-start.13
  129.0 0.7 shard_map.217
  129.8 3.6 %collective-permute-done.13.refs_1_ = bf16[224,256]{1,0:T(8,128)(2,1)S(1)} collective-permute-done((bf16[224,256]{1,0:T(8,128)(2,1)S(1)}, bf16[224,256]{1,0:T(8,128)(2,1)S(1)}, u32[]{:S(2)}, u32[]{:S(2)}) %collective-permute-start.13) | collective-permute-done | bytes 114720 | tf_op jit(solution)/shard_map/ppermute | solution.py:643
  133.5 0.7 collective-permute-start.15
  134.2 0.6 collective-permute-start.24
  134.9 4.4 %collective-permute-done.15 = bf16[192,256]{1,0:T(8,128)(2,1)S(1)} collective-permute-done((bf16[192,256]{1,0:T(8,128)(2,1)S(1)}, bf16[192,256]{1,0:T(8,128)(2,1)S(1)}, u32[]{:S(2)}, u32[]{:S(2)}) %collective-permute-start.15) | collective-permute-done | bytes 98336 | tf_op jit(solution)/shard_map/ppermute | solution.py:643
  139.3 0.7 collective-permute-start.16
  140.0 2.5 %collective-permute-done.24 = bf16[640,256]{1,0:T(8,128)(2,1)S(1)} collective-permute-done((bf16[640,256]{1,0:T(8,128)(2,1)S(1)}, bf16[640,256]{1,0:T(8,128)(2,1)S(1)}, u32[]{:S(2)}, u32[]{:S(2)}) %collective-permute-start.24) | collective-permute-done | bytes 327712 | tf_op jit(solution)/shard_map/ppermute | solution.py:643
  142.7 2.3 %collective-permute-start.25 = (bf16[1280,256]{1,0:T(8,128)(2,1)S(1)}, bf16[1280,256]{1,0:T(8,128)(2,1)S(1)}, u32[]{:S(2)}, u32[]{:S(2)}) collective-permute-start(bf16[1280,256]{1,0:T(8,128)(2,1)S(1)} %pad_maximum_fusion.mine), channel_id=1, source_target_pairs={{0,2},{1,5},{2,0},{3,7},{4,6},{5,1},{6,4},{7,3},{8,10},{9,13},{10,... | collective-permute-start | bytes 1966088 | tf_op jit(solution)/shard_map/ppermute | solution.py:643
  144.9 2.3 %collective-permute-done.16 = bf16[384,256]{1,0:T(8,128)(2,1)S(1)} collective-permute-done((bf16[384,256]{1,0:T(8,128)(2,1)S(1)}, bf16[384,256]{1,0:T(8,128)(2,1)S(1)}, u32[]{:S(2)}, u32[]{:S(2)}) %collective-permute-start.16) | collective-permute-done | bytes 196640 | tf_op jit(solution)/shard_map/ppermute | solution.py:643
  147.3 3.3 %collective-permute-start.17 = (bf16[768,256]{1,0:T(8,128)(2,1)S(1)}, bf16[768,256]{1,0:T(8,128)(2,1)S(1)}, u32[]{:S(2)}, u32[]{:S(2)}) collective-permute-start(bf16[768,256]{1,0:T(8,128)(2,1)S(1)} %pad_maximum_fusion.1.mine), channel_id=1, source_target_pairs={{0,8},{1,9},{2,10},{3,11},{4,12},{5,13},{6,14},{7,15},{8,0},{9,1},... | collective-permute-start | bytes 1179656 | tf_op jit(solution)/shard_map/ppermute | solution.py:643
  150.6 1.6 %shard_map.218 = (bf16[4,256,256]{2,1,0:T(8,128)(2,1)}, f32[4,256,256]{2,1,0:T(8,128)}, f32[2,256]{1,0:T(2,128)}, f32[2,256]{1,0:T(2,128)}, f32[2,256]{1,0:T(2,1...) custom-call(f32[16,128]{1,0:T(8,128)S(1)} %get-tuple-element.200.refs_0_, f32[8,512]{1,0:T(8,128)S(1)} %get-tuple-element.201.refs_1_, ...), custom_call_target="tpu_custom_call" | custom-call | bytes 1622016 | tf_op jit(solution)/shard_map/pallas_call | solution.py:912
  152.2 1.3 collective-permute-done.25.got
  153.5 1.6 %shard_map.224 = (f32[2,512,256]{2,1,0:T(8,128)}, f32[2,512,256]{2,1,0:T(8,128)}, f32[2,256,512]{2,1,0:T(8,128)}, f32[2,1024,128]{2,1,0:T(8,128)}) custom-call(bf16[1280,256]{1,0:T(8,128)(2,1)S(1)} %pad_maximum_fusion.mine, bf16[1280,256]{1,0:T(8,128)(2,1)S(1)} %collective-permute-done.25.got), custom_call_target="tpu_custom_call" | custom-call | tf_op jit(solution)/shard_map/pallas_call | solution.py:831
  155.1 1.3 collective-permute-done.17.got
  156.4 1.2 shard_map.225
  (66 shorter events, 3.9 us)
Async XLA Ops:
  0.6 2.1 %copy-start = (bf16[4,256,256]{2,1,0:T(8,128)(2,1)S(1)}, bf16[4,256,256]{2,1,0:T(8,128)(2,1)}, u32[]{:S(2)}) copy-start(bf16[4,256,256]{2,1,0:T(8,128)(2,1)} %refs_4_.1) | copy-start | bytes 1572868
  0.7 2.1 %copy-start.8 = (bf16[2,256]{1,0:T(2,128)(2,1)S(1)}, bf16[2,256]{1,0:T(2,128)(2,1)}, u32[]{:S(2)}) copy-start(bf16[2,256]{1,0:T(2,128)(2,1)} %param.13) | copy-start | bytes 3076
  0.7 2.1 %copy-start.7 = (bf16[2,256]{1,0:T(2,128)(2,1)S(1)}, bf16[2,256]{1,0:T(2,128)(2,1)}, u32[]{:S(2)}) copy-start(bf16[2,256]{1,0:T(2,128)(2,1)} %param.14) | copy-start | bytes 3076
  0.7 2.1 %copy-start.10 = (bf16[2,128]{1,0:T(2,128)(2,1)S(1)}, bf16[2,128]{1,0:T(2,128)(2,1)}, u32[]{:S(2)}) copy-start(bf16[2,128]{1,0:T(2,128)(2,1)} %param.17) | copy-start | bytes 1540
  0.7 2.1 %copy-start.9 = (bf16[2,128]{1,0:T(2,128)(2,1)S(1)}, bf16[2,128]{1,0:T(2,128)(2,1)}, u32[]{:S(2)}) copy-start(bf16[2,128]{1,0:T(2,128)(2,1)} %param.18) | copy-start | bytes 1540
  0.7 2.1 %copy-start.6 = (bf16[2,256]{1,0:T(2,128)(2,1)S(1)}, bf16[2,256]{1,0:T(2,128)(2,1)}, u32[]{:S(2)}) copy-start(bf16[2,256]{1,0:T(2,128)(2,1)} %param.19) | copy-start | bytes 3076
  0.7 2.1 %copy-start.5 = (s32[4,16]{1,0:T(4,128)S(1)}, s32[4,16]{1,0:T(4,128)}, u32[]{:S(2)}) copy-start(s32[4,16]{1,0:T(4,128)} %refs_0_.3) | copy-start | bytes 772
  0.7 4.3 %copy-start.1 = (bf16[2,2,128,512]{3,2,1,0:T(8,128)(2,1)S(1)}, bf16[2,2,128,512]{3,2,1,0:T(8,128)(2,1)}, u32[]{:S(2)}) copy-start(bf16[2,2,128,512]{3,2,1,0:T(8,128)(2,1)} %param.16) | copy-start | bytes 1572868
  2.2 4.1 %collective-permute-start.2 = (bf16[2,512,256]{2,1,0:T(8,128)(2,1)S(1)}, bf16[2,512,256]{2,1,0:T(8,128)(2,1)S(1)}, u32[]{:S(2)}, u32[]{:S(2)}) collective-permute-start(bf16[2,512,256]{2,1,0:T(8,128)(2,1)S(1)} %reshape.40.refs_7_.refs_5_.refs_13_), channel_id=1, source_target_pairs={{0,1},{1,0},{2,3},{3,2},{4,5},{5,4},{6,7},{7,6},{8,9},{9,8},{10,11... | collective-permute-start | bytes 1572872 | tf_op jit(solution)/shard_map/ppermute | solution.py:605
  2.7 18.2 %collective-permute-start = (bf16[4,256,256]{2,1,0:T(8,128)(2,1)S(1)}, bf16[4,256,256]{2,1,0:T(8,128)(2,1)S(1)}, u32[]{:S(2)}, u32[]{:S(2)}) collective-permute-start(bf16[4,256,256]{2,1,0:T(8,128)(2,1)S(1)} %copy-done), channel_id=1, source_target_pairs={{0,1},{1,0},{2,3},{3,2},{4,5},{5,4},{6,7},{7,6},{8,9},{9,8},{10,11... | collective-permute-start | bytes 1572872 | tf_op jit(solution)/shard_map/ppermute | solution.py:605
  4.6 1.3 collective-permute-start.1
  5.1 16.9 %collective-permute-start.4 = (bf16[2,256,512]{2,1,0:T(8,128)(2,1)S(1)}, bf16[2,256,512]{2,1,0:T(8,128)(2,1)S(1)}, u32[]{:S(2)}, u32[]{:S(2)}) collective-permute-start(bf16[2,256,512]{2,1,0:T(8,128)(2,1)S(1)} %bitcast.5), channel_id=1, source_target_pairs={{0,1},{1,0},{2,3},{3,2},{4,5},{5,4},{6,7},{7,6},{8,9},{9,8},{10,11... | collective-permute-start | bytes 1572872 | tf_op jit(solution)/shard_map/ppermute | solution.py:605
  5.1 16.8 %collective-permute-start.3 = (bf16[4,256,256]{2,1,0:T(8,128)(2,1)}, bf16[4,256,256]{2,1,0:T(8,128)(2,1)S(1)}, u32[]{:S(2)}, u32[]{:S(2)}) collective-permute-start(bf16[4,256,256]{2,1,0:T(8,128)(2,1)} %refs_16_.1), channel_id=1, source_target_pairs={{0,1},{1,0},{2,3},{3,2},{4,5},{5,4},{6,7},{7,6},{8,9},{9,8},{10,11... | collective-permute-start | bytes 1572872 | tf_op jit(solution)/shard_map/ppermute | solution.py:605
  5.9 16.1 %collective-permute-start.5 = (bf16[2,512,256]{2,1,0:T(8,128)(2,1)}, bf16[2,512,256]{2,1,0:T(8,128)(2,1)S(1)}, u32[]{:S(2)}, u32[]{:S(2)}) collective-permute-start(bf16[2,512,256]{2,1,0:T(8,128)(2,1)} %refs_15_.1), channel_id=1, source_target_pairs={{0,1},{1,0},{2,3},{3,2},{4,5},{5,4},{6,7},{7,6},{8,9},{9,8},{10,11... | collective-permute-start | bytes 1572872 | tf_op jit(solution)/shard_map/ppermute | solution.py:605
  6.2 15.8 %collective-permute-start.6 = (bf16[2,512,256]{2,1,0:T(8,128)(2,1)}, bf16[2,512,256]{2,1,0:T(8,128)(2,1)S(1)}, u32[]{:S(2)}, u32[]{:S(2)}) collective-permute-start(bf16[2,512,256]{2,1,0:T(8,128)(2,1)} %refs_17_.1), channel_id=1, source_target_pairs={{0,1},{1,0},{2,3},{3,2},{4,5},{5,4},{6,7},{7,6},{8,9},{9,8},{10,11... | collective-permute-start | bytes 1572872 | tf_op jit(solution)/shard_map/ppermute | solution.py:605
  20.9 11.2 %copy-start.2 = (bf16[2,512,256]{2,1,0:T(8,128)(2,1)S(1)}, bf16[2,512,256]{2,1,0:T(8,128)(2,1)}, u32[]{:S(2)}) copy-start(bf16[2,512,256]{2,1,0:T(8,128)(2,1)} %refs_15_.1) | copy-start | bytes 1572868
  20.9 11.2 %copy-start.3 = (bf16[2,512,256]{2,1,0:T(8,128)(2,1)S(1)}, bf16[2,512,256]{2,1,0:T(8,128)(2,1)}, u32[]{:S(2)}) copy-start(bf16[2,512,256]{2,1,0:T(8,128)(2,1)} %refs_17_.1) | copy-start | bytes 1572868
  44.1 11.0 %copy-start.4 = (bf16[4,256,256]{2,1,0:T(8,128)(2,1)S(1)}, bf16[4,256,256]{2,1,0:T(8,128)(2,1)}, u32[]{:S(2)}) copy-start(bf16[4,256,256]{2,1,0:T(8,128)(2,1)} %refs_16_.1) | copy-start | bytes 1572868
  81.0 2.7 %collective-permute-start.7 = (bf16[2048,256]{1,0:T(8,128)(2,1)S(1)}, bf16[2048,256]{1,0:T(8,128)(2,1)S(1)}, u32[]{:S(2)}, u32[]{:S(2)}) collective-permute-start(bf16[2048,256]{1,0:T(8,128)(2,1)S(1)} %get-tuple-element.173), channel_id=1, source_target_pairs={{0,1},{1,0},{2,3},{3,2},{4,5},{5,4},{6,7},{7,6},{8,9},{9,8},{10,11... | collective-permute-start | bytes 3145736 | tf_op jit(solution)/shard_map/ppermute | solution.py:605
  93.9 1.5 collective-permute-start.18
  95.7 10.7 %collective-permute-start.19 = (bf16[1280,256]{1,0:T(8,128)(2,1)S(1)}, bf16[1280,256]{1,0:T(8,128)(2,1)S(1)}, u32[]{:S(2)}, u32[]{:S(2)}) collective-permute-start(bf16[1280,256]{1,0:T(8,128)(2,1)S(1)} %get-tuple-element.216), channel_id=1, source_target_pairs={{0,2},{1,5},{2,0},{3,7},{4,6},{5,1},{6,4},{7,3},{8,10},{9,13},{10,... | collective-permute-start | bytes 1966088 | tf_op jit(solution)/shard_map/ppermute | solution.py:643
  96.6 3.3 %collective-permute-start.8 = (bf16[1024,256]{1,0:T(8,128)(2,1)S(1)}, bf16[1024,256]{1,0:T(8,128)(2,1)S(1)}, u32[]{:S(2)}, u32[]{:S(2)}) collective-permute-start(bf16[1024,256]{1,0:T(8,128)(2,1)S(1)} %get-tuple-element.180), channel_id=1, source_target_pairs={{0,1},{1,0},{2,3},{3,2},{4,5},{5,4},{6,7},{7,6},{8,9},{9,8},{10,11... | collective-permute-start | bytes 1572872 | tf_op jit(solution)/shard_map/ppermute | solution.py:605
  98.2 1.8 %collective-permute-start.9 = (bf16[544,256]{1,0:T(8,128)(2,1)S(1)}, bf16[544,256]{1,0:T(8,128)(2,1)S(1)}, u32[]{:S(2)}, u32[]{:S(2)}) collective-permute-start(bf16[544,256]{1,0:T(8,128)(2,1)S(1)} %get-tuple-element.192), channel_id=1, source_target_pairs={{0,1},{1,0},{2,3},{3,2},{4,5},{5,4},{6,7},{7,6},{8,9},{9,8},{10,11... | collective-permute-start | bytes 835592 | tf_op jit(solution)/shard_map/ppermute | solution.py:605
  100.2 14.3 %collective-permute-start.10 = (bf16[800,256]{1,0:T(8,128)(2,1)S(1)}, bf16[800,256]{1,0:T(8,128)(2,1)S(1)}, u32[]{:S(2)}, u32[]{:S(2)}) collective-permute-start(bf16[800,256]{1,0:T(8,128)(2,1)S(1)} %get-tuple-element.195), channel_id=1, source_target_pairs={{0,8},{1,9},{2,10},{3,11},{4,12},{5,13},{6,14},{7,15},{8,0},{9,1},... | collective-permute-start | bytes 1228808 | tf_op jit(solution)/shard_map/ppermute | solution.py:643
  106.5 7.1 %collective-permute-start.20 = (bf16[640,256]{1,0:T(8,128)(2,1)S(1)}, bf16[640,256]{1,0:T(8,128)(2,1)S(1)}, u32[]{:S(2)}, u32[]{:S(2)}) collective-permute-start(bf16[640,256]{1,0:T(8,128)(2,1)S(1)} %get-tuple-element.218), channel_id=1, source_target_pairs={{0,4},{1,3},{2,6},{3,1},{4,0},{5,7},{6,2},{7,5},{8,12},{9,11},{10,... | collective-permute-start | bytes 983048 | tf_op jit(solution)/shard_map/ppermute | solution.py:643
  113.8 5.4 %collective-permute-start.21 = (bf16[320,256]{1,0:T(8,128)(2,1)S(1)}, bf16[320,256]{1,0:T(8,128)(2,1)S(1)}, u32[]{:S(2)}, u32[]{:S(2)}) collective-permute-start(bf16[320,256]{1,0:T(8,128)(2,1)S(1)} %get-tuple-element.220), channel_id=1, source_target_pairs={{0,8},{1,9},{2,10},{3,11},{4,12},{5,13},{6,14},{7,15},{8,0},{9,1},... | collective-permute-start | bytes 491528 | tf_op jit(solution)/shard_map/ppermute | solution.py:643
  114.6 5.9 %collective-permute-start.11 = (bf16[416,256]{1,0:T(8,128)(2,1)S(1)}, bf16[416,256]{1,0:T(8,128)(2,1)S(1)}, u32[]{:S(2)}, u32[]{:S(2)}) collective-permute-start(bf16[416,256]{1,0:T(8,128)(2,1)S(1)} %get-tuple-element.197), channel_id=1, source_target_pairs={{0,4},{1,3},{2,6},{3,1},{4,0},{5,7},{6,2},{7,5},{8,12},{9,11},{10,... | collective-permute-start | bytes 638984 | tf_op jit(solution)/shard_map/ppermute | solution.py:643
  119.2 8.2 %collective-permute-start.22 = (bf16[320,256]{1,0:T(8,128)(2,1)S(1)}, bf16[320,256]{1,0:T(8,128)(2,1)S(1)}, u32[]{:S(2)}, u32[]{:S(2)}) collective-permute-start(bf16[320,256]{1,0:T(8,128)(2,1)S(1)} %shard_map.222.refs_0_), channel_id=1, source_target_pairs={{0,16},{1,17},{2,18},{3,19},{4,20},{5,21},{6,22},{7,23},{8,24},{9,... | collective-permute-start | bytes 491528 | tf_op jit(solution)/shard_map/ppermute | solution.py:643
  120.6 7.0 %collective-permute-start.12 = (bf16[224,256]{1,0:T(8,128)(2,1)S(1)}, bf16[224,256]{1,0:T(8,128)(2,1)S(1)}, u32[]{:S(2)}, u32[]{:S(2)}) collective-permute-start(bf16[224,256]{1,0:T(8,128)(2,1)S(1)} %get-tuple-element.199), channel_id=1, source_target_pairs={{0,2},{1,5},{2,0},{3,7},{4,6},{5,1},{6,4},{7,3},{8,10},{9,13},{10,... | collective-permute-start | bytes 344072 | tf_op jit(solution)/shard_map/ppermute | solution.py:643
  127.4 6.7 %collective-permute-start.23 = (bf16[320,256]{1,0:T(8,128)(2,1)S(1)}, bf16[320,256]{1,0:T(8,128)(2,1)S(1)}, u32[]{:S(2)}, u32[]{:S(2)}) collective-permute-start(bf16[320,256]{1,0:T(8,128)(2,1)S(1)} %shard_map.223), channel_id=1, source_target_pairs={{0,8},{1,9},{2,10},{3,11},{4,12},{5,13},{6,14},{7,15},{8,0},{9,1},... | collective-permute-start | bytes 491528 | tf_op jit(solution)/shard_map/ppermute | solution.py:643
  127.6 5.9 %collective-permute-start.13 = (bf16[224,256]{1,0:T(8,128)(2,1)S(1)}, bf16[224,256]{1,0:T(8,128)(2,1)S(1)}, u32[]{:S(2)}, u32[]{:S(2)}) collective-permute-start(bf16[224,256]{1,0:T(8,128)(2,1)S(1)} %shard_map.215.refs_0_), channel_id=1, source_target_pairs={{0,16},{1,17},{2,18},{3,19},{4,20},{5,21},{6,22},{7,23},{8,24},{9,... | collective-permute-start | bytes 344072 | tf_op jit(solution)/shard_map/ppermute | solution.py:643
  129.7 20.9 %collective-permute-start.14 = (bf16[2,512,256]{2,1,0:T(8,128)(2,1)S(1)}, bf16[2,512,256]{2,1,0:T(8,128)(2,1)S(1)}, u32[]{:S(2)}, u32[]{:S(2)}) collective-permute-start(bf16[2,512,256]{2,1,0:T(8,128)(2,1)S(1)} %get-tuple-element.205), channel_id=1, source_target_pairs={{0,1},{1,0},{2,3},{3,2},{4,5},{5,4},{6,7},{7,6},{8,9},{9,8},{10,11... | collective-permute-start | bytes 1572872 | tf_op jit(solution)/shard_map/ppermute | solution.py:605
  133.5 5.8 %collective-permute-start.15 = (bf16[192,256]{1,0:T(8,128)(2,1)S(1)}, bf16[192,256]{1,0:T(8,128)(2,1)S(1)}, u32[]{:S(2)}, u32[]{:S(2)}) collective-permute-start(bf16[192,256]{1,0:T(8,128)(2,1)S(1)} %get-tuple-element.210), channel_id=1, source_target_pairs={{0,2},{1,5},{2,0},{3,7},{4,6},{5,1},{6,4},{7,3},{8,10},{9,13},{10,... | collective-permute-start | bytes 294920 | tf_op jit(solution)/shard_map/ppermute | solution.py:643
  134.2 8.3 %collective-permute-start.24 = (bf16[640,256]{1,0:T(8,128)(2,1)S(1)}, bf16[640,256]{1,0:T(8,128)(2,1)S(1)}, u32[]{:S(2)}, u32[]{:S(2)}) collective-permute-start(bf16[640,256]{1,0:T(8,128)(2,1)S(1)} %pad_maximum_fusion.2), channel_id=1, source_target_pairs={{0,4},{1,3},{2,6},{3,1},{4,0},{5,7},{6,2},{7,5},{8,12},{9,11},{10,... | collective-permute-start | bytes 983048 | tf_op jit(solution)/shard_map/ppermute | solution.py:643
  139.3 7.9 %collective-permute-start.16 = (bf16[384,256]{1,0:T(8,128)(2,1)S(1)}, bf16[384,256]{1,0:T(8,128)(2,1)S(1)}, u32[]{:S(2)}, u32[]{:S(2)}) collective-permute-start(bf16[384,256]{1,0:T(8,128)(2,1)S(1)} %pad_maximum_fusion.3), channel_id=1, source_target_pairs={{0,4},{1,3},{2,6},{3,1},{4,0},{5,7},{6,2},{7,5},{8,12},{9,11},{10,... | collective-permute-start | bytes 589832 | tf_op jit(solution)/shard_map/ppermute | solution.py:643
  142.7 10.8 %collective-permute-start.25 = (bf16[1280,256]{1,0:T(8,128)(2,1)S(1)}, bf16[1280,256]{1,0:T(8,128)(2,1)S(1)}, u32[]{:S(2)}, u32[]{:S(2)}) collective-permute-start(bf16[1280,256]{1,0:T(8,128)(2,1)S(1)} %pad_maximum_fusion.mine), channel_id=1, source_target_pairs={{0,2},{1,5},{2,0},{3,7},{4,6},{5,1},{6,4},{7,3},{8,10},{9,13},{10,... | collective-permute-start | bytes 1966088 | tf_op jit(solution)/shard_map/ppermute | solution.py:643
  147.3 9.1 %collective-permute-start.17 = (bf16[768,256]{1,0:T(8,128)(2,1)S(1)}, bf16[768,256]{1,0:T(8,128)(2,1)S(1)}, u32[]{:S(2)}, u32[]{:S(2)}) collective-permute-start(bf16[768,256]{1,0:T(8,128)(2,1)S(1)} %pad_maximum_fusion.1.mine), channel_id=1, source_target_pairs={{0,8},{1,9},{2,10},{3,11},{4,12},{5,13},{6,14},{7,15},{8,0},{9,1},... | collective-permute-start | bytes 1179656 | tf_op jit(solution)/shard_map/ppermute | solution.py:643
